TPU v7x, 32 devices: a whole 2x2x4 slice. The times are simulated.
32 devices in a mesh: heads: 4 (over x, core), cells: 8 (over z, y).
Axes of the slice: x: 2, y: 2, z: 4, core: 2. Of those that a mesh axis runs over, the one named last changes fastest.
Arguments:
- cells_in: bfloat16 [8, 1024, 1024], P(None, ('heads', 'cells')), may hold values from -6 to 6
- gain: float32 [1024], replicated, may hold values from 0.1 to 1.9
- w_qkv: bfloat16 [1024, 3072], replicated
- w_out: bfloat16 [1024, 1024], replicated, may hold values from -0.1875 to 0.1875
- tile_of_cell: int32 [1024], P(('heads', 'cells')), may hold values from 0 to 255
- tile_adjacent: int32 [256, 256], replicated, may hold values from 0 to 1, as said below
Outputs:
- cells_out: bfloat16 [8, 1024, 1024], P(None, ('heads', 'cells'))
Inputs may be any that keep to these rules, and one draw needn't show every extreme that they name: Tiles sit at the places of a 16 x 16 grid in an order drawn from the seed; tile_adjacent is 1 exactly where the two tiles' places differ by at most one in each grid direction, so it is symmetric with ones on the diagonal.
All inputs are finite; a program needn't handle non-finite values.
Results may differ from a plain program's by a relative error of at most 0.011.
Values may be sent and summed in bfloat16 or wider, within the bound.
No kernel may reach another device: no remote copies, remote signals or barrier semaphores. Data moves between devices by JAX's collectives and lax.ppermute only.
A program may use at most 64 MiB of HBM per device.

v0:
```python
import math

import jax
import jax.numpy as jnp
from jax import lax
from jax.sharding import PartitionSpec as P

HEAD_DIM = 64


def tile_rows(tiles, adjacency):
    return jnp.take(adjacency, tiles, axis=0)


def start_carry(batch, rows):
    return (
        jnp.full((batch, rows), -1e30, jnp.float32),
        jnp.zeros((batch, rows), jnp.float32),
        jnp.zeros((batch, rows, HEAD_DIM), jnp.float32),
    )


def update(carry, query_matrix, rowtile, key_matrix, value_matrix, key_tiles):
    allowed = jnp.take(rowtile, key_tiles, axis=1) > 0
    logit_scores = (
        jnp.einsum("hoz,hjz->hoj", query_matrix, key_matrix, preferred_element_type=jnp.float32)
        * 0.125
    )
    masked = jnp.where(allowed[None], logit_scores, -1e30)
    running, total, summed = carry
    newest = jnp.maximum(running, jnp.max(masked, axis=-1))
    softmax_weights = jnp.where(allowed[None], jnp.exp(masked - newest[..., None]), 0.0)
    factor = jnp.exp(running - newest)
    total = total * factor + jnp.sum(softmax_weights, axis=-1)
    summed = summed * factor[..., None] + jnp.einsum(
        "ovn,onr->ovr",
        softmax_weights.astype(jnp.bfloat16),
        value_matrix,
        preferred_element_type=jnp.float32,
    )
    return (newest, total, summed)


def absorb(carry, query_matrix, rowtile, key_vals, key_tiles):
    length = key_vals.shape[1]
    step = math.gcd(length, 512)

    def one_step(index, state):
        kv_block = lax.dynamic_slice_in_dim(key_vals, index * step, step, 1)
        tile_block = lax.dynamic_slice_in_dim(key_tiles, index * step, step, 0)
        return update(
            state,
            query_matrix,
            rowtile,
            kv_block[..., :HEAD_DIM],
            kv_block[..., HEAD_DIM:],
            tile_block,
        )

    return lax.fori_loop(0, length // step, one_step, carry)


def finish(carry):
    running, total, summed = carry
    return (summed / total[..., None]).astype(jnp.bfloat16)


def on_device(cells_in, gain, w_qkv, w_out, tile_of_cell, tile_adjacent):
    genes, cell_dev, width = cells_in.shape
    groups = lax.axis_size("heads")
    group_width = width // groups
    local_heads = group_width // HEAD_DIM
    x32 = cells_in.astype(jnp.float32)
    normed = (x32 * lax.rsqrt(jnp.mean(x32 * x32, axis=-1, keepdims=True) + 1e-05) * gain).astype(
        jnp.bfloat16
    )
    rows_all = lax.all_gather(normed, "heads", axis=1, tiled=True)
    columns = w_qkv.reshape(width, 3, groups, group_width)
    columns = lax.dynamic_slice_in_dim(columns, lax.axis_index("heads"), 1, 2).reshape(
        width, 3 * group_width
    )
    mixed = jnp.dot(rows_all, columns, preferred_element_type=jnp.float32).astype(jnp.bfloat16)
    mixed = mixed.reshape(genes, rows_all.shape[1], 3, group_width)
    rows_here = mixed.shape[1]
    arranged = mixed.reshape(genes, rows_here, 3, local_heads, HEAD_DIM).transpose(0, 3, 1, 2, 4)
    arranged = arranged.reshape(genes * local_heads, rows_here, 3 * HEAD_DIM)
    tiles_here = lax.all_gather(tile_of_cell, "heads", axis=0, tiled=True)
    spread = lax.all_to_all(arranged, "cells", split_axis=0, concat_axis=1, tiled=True)
    tiles_all = lax.all_gather(tiles_here, "cells", axis=0, tiled=True)
    items, total_rows = (spread.shape[0], spread.shape[1])
    block = math.gcd(total_rows, 512)
    rowtile_all = tile_rows(tiles_all, tile_adjacent)
    key_vals = spread[..., HEAD_DIM:]
    query_all = spread[..., :HEAD_DIM]

    def one_block(index):
        query_matrix = lax.dynamic_slice_in_dim(query_all, index * block, block, 1)
        rowtile = lax.dynamic_slice_in_dim(rowtile_all, index * block, block, 0)
        return finish(absorb(start_carry(items, block), query_matrix, rowtile, key_vals, tiles_all))

    blocks_out = lax.map(one_block, jnp.arange(total_rows // block, dtype=jnp.int32))
    attention_output = blocks_out.transpose(1, 0, 2, 3).reshape(
        items, total_rows // 2, 2 * HEAD_DIM
    )
    returned = lax.all_to_all(attention_output, "cells", split_axis=1, concat_axis=0, tiled=True)
    attended = returned.reshape(genes * local_heads, rows_here, HEAD_DIM)
    heads_out = (
        attended.reshape(genes, local_heads, rows_here, HEAD_DIM)
        .transpose(0, 2, 1, 3)
        .reshape(genes, rows_here, group_width)
    )
    merged = lax.all_to_all(heads_out, "heads", split_axis=1, concat_axis=2, tiled=True)
    return jnp.dot(merged, w_out, preferred_element_type=jnp.float32).astype(jnp.bfloat16)


def solution(mesh):
    return jax.shard_map(
        on_device,
        mesh=mesh,
        in_specs=(P(None, ("heads", "cells"), None), P(), P(), P(), P(("heads", "cells")), P()),
        out_specs=P(None, ("heads", "cells"), None),
        check_vma=False,
    )
```

profile of v0, /device:TPU:0, one launch (start us, length us, event | category | flops | bytes accessed | tf_op | source)
XLA Modules:
  0.0 222.6 jit_solution(10566422300952968953)
XLA Ops:
  6.5 1.4 fusion.24
  7.9 2.0 fusion.26
  10.0 8.7 %copy.33 = bf16[1024,3072]{0,1:T(8,128)(2,1)} copy(bf16[1024,3072]{1,0:T(8,128)(2,1)} %param.12) | data formatting | bytes 12582912 | tf_op args[2]
  18.6 2.9 %constant_dynamic-slice_fusion.2 = bf16[1024,3,1,256]{0,3,2,1:T(8,128)(2,1)} fusion(bf16[1024,3,4,256]{0,3,2,1:T(8,128)(2,1)} %bitcast.73, s32[]{:T(128)S(6)} %select_n.62), kind=kLoop, calls=%fused_computation.48 | loop fusion | bytes 3145732 | tf_op jit(solution)/shard_map/dynamic_slice | solution.py:79
  21.5 13.9 %all-gather.3.cloned.1.call-done = bf16[8,128,1024]{2,1,0:T(8,128)(2,1)} async-done(((bf16[8,32,1024]{2,1,0:T(8,128)(2,1)}), bf16[8,128,1024]{2,1,0:T(8,128)(2,1)}) %all-gather.3.cloned.1.call-update) | async-done | bytes 2097168 | tf_op jit(solution)/shard_map/all_gather | solution.py:77
  35.4 5.0 %convolution_convert_fusion = bf16[8,128,768]{2,1,0:T(8,128)(2,1)} fusion(bf16[8,128,1024]{2,1,0:T(8,128)(2,1)} %all-gather.3.cloned.1.call-done, bf16[1024,768,1]{0,1,2:T(8,128)(2,1)} %bitcast.83), kind=kOutput, calls=%fused_computation.34 | convolution fusion | flops 1611399168 | bytes 5242880 | tf_op jit(solution)/shard_map/dot_general | solution.py:82
  40.5 2.6 %copy.35 = bf16[8,128,768]{1,2,0:T(8,128)(2,1)} copy(bf16[8,128,768]{2,1,0:T(8,128)(2,1)} %convolution_convert_fusion) | data formatting | bytes 3145728 | tf_op jit(solution)/shard_map/convert_element_type | solution.py:82
  43.1 2.7 %copy.36 = bf16[8,4,128,3,64]{2,4,3,1,0:T(8,128)(2,1)} copy(bf16[8,4,128,3,64]{2,4,1,3,0:T(8,128)(2,1)} %bitcast.77) | data formatting | bytes 3145728 | tf_op jit(solution)/shard_map/transpose | solution.py:85
  45.8 5.5 %all-to-all-start = ((bf16[32,128,192]{1,2,0:T(8,128)(2,1)}), bf16[32,128,192]{1,2,0:T(8,128)(2,1)}, u32[]{:S(2)}, u32[]{:S(2)}) async-start(bf16[32,128,192]{1,2,0:T(8,128)(2,1)} %bitcast.74), calls=%async_computation | async-start | bytes 3145728 | tf_op jit(solution)/shard_map/all_to_all | solution.py:88
  51.4 0.6 dynamic-slice
  52.5 0.2 dynamic-update-slice
  52.8 4.3 %all-reduce = s32[128]{0:T(128)S(1)} all-reduce(s32[128]{0:T(128)S(1)} %dynamic-update-slice), channel_id=1, replica_groups=mesh['heads'=4,'cells'=8] {'heads'}, use_global_device_ids=true, to_apply=%add | all-reduce | flops 128 | bytes 1024
  57.0 35.9 %all-gather = s32[8,1,128]{2,1,0:T(1,128)S(1)} all-gather(s32[1,1,128]{2,1,0:T(1,128)S(1)} %bitcast.88), channel_id=1, replica_groups=mesh['heads'=4,'cells'=8] {'cells'}, dimensions={0}, use_global_device_ids=true | all-gather | bytes 4608 | tf_op jit(solution)/shard_map/all_gather | solution.py:89
  93.0 3.5 %gather_fusion.1 = s32[1024,256]{1,0:T(8,128)S(1)} fusion(s32[256,256]{1,0:T(8,128)S(1)} %copy-done.1, s32[1024]{0:T(1024)S(1)} %fusion.27), kind=kCustom, calls=%fused_computation.1 | custom fusion | bytes 2101248 | tf_op jit(solution)/shard_map/jit(_take)/gather | solution.py:12
  96.5 1.2 broadcast_select_fusion
  97.7 1.8 copy.54
  99.5 1.1 slice.29
  100.6 0.8 slice.28
  101.4 72.4 %while.29 = (s32[]{:T(128)}, bf16[2,4,512,64]{2,3,1,0:T(8,128)(2,1)}, s32[2]{0:T(128)S(1)}, s32[1024,256]{1,0:T(8,128)}, bf16[4,1024,64]{1,2,0:T(8,128)(2,1)}, /...) while((s32[]{:T(128)}, ...), condition=%wide.region_6.7_spmd, body=%wide.region_1.6_spmd.sunk | while | flops 283260928 | bytes 22173724 | solution.py:101
  101.4 0.6 dynamic_slice.40
  102.7 1.1 constant_dynamic-slice_fusion.5
  103.8 0.2 copy.57
  104.0 1.0 constant_dynamic-slice_fusion.6
  105.0 30.9 %while.30 = (s32[]{:T(128)}, f32[4,512]{1,0:T(4,128)S(1)}, f32[4,512]{1,0:T(4,128)S(1)}, f32[4,512,64]{1,2,0:T(8,128)}, s32[1024]{0:T(1024)S(1)}, /*index=5*/s32...) while((s32[]{:T(128)}, f32[4,512]{1,0:T(4,128)S(1)}, ...), condition=%wide.region_5.5_spmd.clone, body=%wide.region_2.4_spmd.clone.sunk | while | flops 282998784 | bytes 18756820 | solution.py:60
  105.0 0.1 compare_and_fusion.3
  105.1 2.3 %gather_fusion = s32[512,512]{1,0:T(8,128)} fusion(s32[512,256]{0,1:T(8,128)S(1)} %get-tuple-element.430, s32[1024]{0:T(1024)S(1)} %pad_clamp_fusion.2), kind=kCustom, calls=%fused_computation.clone.clone.1 | custom fusion | bytes 2099200 | tf_op jit(solution)/shard_map/while/body/eval_jaxpr/while/body/eval_jaxpr/jit(_take)/gather | solution.py:24
  107.4 1.5 fusion.43
  108.9 3.8 %fusion.44 = (f32[4,512]{1,0:T(4,128)S(1)}, f32[4,512,512]{2,1,0:T(8,128)}) fusion(pred[512,512]{0,1:T(8,128)(4,1)S(1)} %fusion.43, bf16[4,512,64]{1,2,0:T(8,128)(2,1)S(1)} %get-tuple-element.432, bf16[4,1024,128]{1,2,0:T(8,128)(2,1)} %get-tuple-element.431, s32[]{:T(128)S(6)} %select_n.115), kind=kOutput, calls=%fused_computation.4.clone.1 | convolution fusion | flops 137361408 | bytes 4988932 | tf_op jit(solution)/shard_map/while/body/eval_jaxpr/while/body/eval_jaxpr/hoz,hjz->hoj/dot_general | solution.py:26
  112.7 3.2 %fusion.45 = f32[4,512]{1,0:T(4,128)S(1)} fusion(f32[4,512,512]{2,1,0:T(8,128)} %get-tuple-element.396, f32[4,512]{1,0:T(4,128)S(1)} %select_maximum_fusion.2, pred[512,512]{0,1:T(8,128)(4,1)S(1)} %fusion.43), kind=kLoop, calls=%fused_computation.6.clone.1 | loop fusion | flops 5240832 | bytes 4472832 | tf_op jit(solution)/shard_map/while/body/eval_jaxpr/while/body/eval_jaxpr/reduce_sum | solution.py:34
  116.0 4.4 %fusion.47 = f32[4,512,64]{1,2,0:T(8,128)} fusion(f32[4,512,512]{2,1,0:T(8,128)} %get-tuple-element.396, f32[4,512]{1,0:T(4,128)S(1)} %select_maximum_fusion.2, pred[512,512]{0,1:T(8,128)(4,1)S(1)} %fusion.43, f32[4,512,64]{1,2,0:T(8,128)} %get-tuple-element.415, bf16[4,1024,128]{1,2,0:T(8,128)(2,1)} %get-tuple-element.431, s32[]{:T(128)S(6)} %select_n.115, ...), kind=kOutput, calls=%fused_computation.9.clone.1 | convolution fusion | flops 139853824 | bytes 5783561 | tf_op jit(solution)/shard_map/while/body/eval_jaxpr/while/body/eval_jaxpr/ovn,onr->ovr/dot_general | solution.py:35
  120.4 2.3 %gather_fusion = s32[512,512]{1,0:T(8,128)} fusion(s32[512,256]{0,1:T(8,128)S(1)} %get-tuple-element.430, s32[1024]{0:T(1024)S(1)} %pad_clamp_fusion.2), kind=kCustom, calls=%fused_computation.clone.clone.1 | custom fusion | bytes 2099200 | tf_op jit(solution)/shard_map/while/body/eval_jaxpr/while/body/eval_jaxpr/jit(_take)/gather | solution.py:24
  122.8 1.5 fusion.43
  124.3 3.8 %fusion.44 = (f32[4,512]{1,0:T(4,128)S(1)}, f32[4,512,512]{2,1,0:T(8,128)}) fusion(pred[512,512]{0,1:T(8,128)(4,1)S(1)} %fusion.43, bf16[4,512,64]{1,2,0:T(8,128)(2,1)S(1)} %get-tuple-element.432, bf16[4,1024,128]{1,2,0:T(8,128)(2,1)} %get-tuple-element.431, s32[]{:T(128)S(6)} %select_n.115), kind=kOutput, calls=%fused_computation.4.clone.1 | convolution fusion | flops 137361408 | bytes 4988932 | tf_op jit(solution)/shard_map/while/body/eval_jaxpr/while/body/eval_jaxpr/hoz,hjz->hoj/dot_general | solution.py:26
  128.1 3.2 %fusion.45 = f32[4,512]{1,0:T(4,128)S(1)} fusion(f32[4,512,512]{2,1,0:T(8,128)} %get-tuple-element.396, f32[4,512]{1,0:T(4,128)S(1)} %select_maximum_fusion.2, pred[512,512]{0,1:T(8,128)(4,1)S(1)} %fusion.43), kind=kLoop, calls=%fused_computation.6.clone.1 | loop fusion | flops 5240832 | bytes 4472832 | tf_op jit(solution)/shard_map/while/body/eval_jaxpr/while/body/eval_jaxpr/reduce_sum | solution.py:34
  131.3 4.5 %fusion.47 = f32[4,512,64]{1,2,0:T(8,128)} fusion(f32[4,512,512]{2,1,0:T(8,128)} %get-tuple-element.396, f32[4,512]{1,0:T(4,128)S(1)} %select_maximum_fusion.2, pred[512,512]{0,1:T(8,128)(4,1)S(1)} %fusion.43, f32[4,512,64]{1,2,0:T(8,128)} %get-tuple-element.415, bf16[4,1024,128]{1,2,0:T(8,128)(2,1)} %get-tuple-element.431, s32[]{:T(128)S(6)} %select_n.115, ...), kind=kOutput, calls=%fused_computation.9.clone.1 | convolution fusion | flops 139853824 | bytes 5783561 | tf_op jit(solution)/shard_map/while/body/eval_jaxpr/while/body/eval_jaxpr/ovn,onr->ovr/dot_general | solution.py:35
  135.8 1.8 bitcast_dynamic-update-slice_fusion.2
  137.6 0.6 dynamic_slice.40
  138.9 1.1 constant_dynamic-slice_fusion.5
  139.9 0.2 copy.57
  140.1 1.0 constant_dynamic-slice_fusion.6
  141.1 30.9 %while.30 = (s32[]{:T(128)}, f32[4,512]{1,0:T(4,128)S(1)}, f32[4,512]{1,0:T(4,128)S(1)}, f32[4,512,64]{1,2,0:T(8,128)}, s32[1024]{0:T(1024)S(1)}, /*index=5*/s32...) while((s32[]{:T(128)}, f32[4,512]{1,0:T(4,128)S(1)}, ...), condition=%wide.region_5.5_spmd.clone, body=%wide.region_2.4_spmd.clone.sunk | while | flops 282998784 | bytes 18756820 | solution.py:60
  141.3 2.3 %gather_fusion = s32[512,512]{1,0:T(8,128)} fusion(s32[512,256]{0,1:T(8,128)S(1)} %get-tuple-element.430, s32[1024]{0:T(1024)S(1)} %pad_clamp_fusion.2), kind=kCustom, calls=%fused_computation.clone.clone.1 | custom fusion | bytes 2099200 | tf_op jit(solution)/shard_map/while/body/eval_jaxpr/while/body/eval_jaxpr/jit(_take)/gather | solution.py:24
  143.6 1.5 fusion.43
  145.1 3.8 %fusion.44 = (f32[4,512]{1,0:T(4,128)S(1)}, f32[4,512,512]{2,1,0:T(8,128)}) fusion(pred[512,512]{0,1:T(8,128)(4,1)S(1)} %fusion.43, bf16[4,512,64]{1,2,0:T(8,128)(2,1)S(1)} %get-tuple-element.432, bf16[4,1024,128]{1,2,0:T(8,128)(2,1)} %get-tuple-element.431, s32[]{:T(128)S(6)} %select_n.115), kind=kOutput, calls=%fused_computation.4.clone.1 | convolution fusion | flops 137361408 | bytes 4988932 | tf_op jit(solution)/shard_map/while/body/eval_jaxpr/while/body/eval_jaxpr/hoz,hjz->hoj/dot_general | solution.py:26
  148.9 3.2 %fusion.45 = f32[4,512]{1,0:T(4,128)S(1)} fusion(f32[4,512,512]{2,1,0:T(8,128)} %get-tuple-element.396, f32[4,512]{1,0:T(4,128)S(1)} %select_maximum_fusion.2, pred[512,512]{0,1:T(8,128)(4,1)S(1)} %fusion.43), kind=kLoop, calls=%fused_computation.6.clone.1 | loop fusion | flops 5240832 | bytes 4472832 | tf_op jit(solution)/shard_map/while/body/eval_jaxpr/while/body/eval_jaxpr/reduce_sum | solution.py:34
  152.2 4.4 %fusion.47 = f32[4,512,64]{1,2,0:T(8,128)} fusion(f32[4,512,512]{2,1,0:T(8,128)} %get-tuple-element.396, f32[4,512]{1,0:T(4,128)S(1)} %select_maximum_fusion.2, pred[512,512]{0,1:T(8,128)(4,1)S(1)} %fusion.43, f32[4,512,64]{1,2,0:T(8,128)} %get-tuple-element.415, bf16[4,1024,128]{1,2,0:T(8,128)(2,1)} %get-tuple-element.431, s32[]{:T(128)S(6)} %select_n.115, ...), kind=kOutput, calls=%fused_computation.9.clone.1 | convolution fusion | flops 139853824 | bytes 5783561 | tf_op jit(solution)/shard_map/while/body/eval_jaxpr/while/body/eval_jaxpr/ovn,onr->ovr/dot_general | solution.py:35
  156.6 2.3 %gather_fusion = s32[512,512]{1,0:T(8,128)} fusion(s32[512,256]{0,1:T(8,128)S(1)} %get-tuple-element.430, s32[1024]{0:T(1024)S(1)} %pad_clamp_fusion.2), kind=kCustom, calls=%fused_computation.clone.clone.1 | custom fusion | bytes 2099200 | tf_op jit(solution)/shard_map/while/body/eval_jaxpr/while/body/eval_jaxpr/jit(_take)/gather | solution.py:24
  159.0 1.5 fusion.43
  160.5 3.8 %fusion.44 = (f32[4,512]{1,0:T(4,128)S(1)}, f32[4,512,512]{2,1,0:T(8,128)}) fusion(pred[512,512]{0,1:T(8,128)(4,1)S(1)} %fusion.43, bf16[4,512,64]{1,2,0:T(8,128)(2,1)S(1)} %get-tuple-element.432, bf16[4,1024,128]{1,2,0:T(8,128)(2,1)} %get-tuple-element.431, s32[]{:T(128)S(6)} %select_n.115), kind=kOutput, calls=%fused_computation.4.clone.1 | convolution fusion | flops 137361408 | bytes 4988932 | tf_op jit(solution)/shard_map/while/body/eval_jaxpr/while/body/eval_jaxpr/hoz,hjz->hoj/dot_general | solution.py:26
  164.3 3.2 %fusion.45 = f32[4,512]{1,0:T(4,128)S(1)} fusion(f32[4,512,512]{2,1,0:T(8,128)} %get-tuple-element.396, f32[4,512]{1,0:T(4,128)S(1)} %select_maximum_fusion.2, pred[512,512]{0,1:T(8,128)(4,1)S(1)} %fusion.43), kind=kLoop, calls=%fused_computation.6.clone.1 | loop fusion | flops 5240832 | bytes 4472832 | tf_op jit(solution)/shard_map/while/body/eval_jaxpr/while/body/eval_jaxpr/reduce_sum | solution.py:34
  167.5 4.5 %fusion.47 = f32[4,512,64]{1,2,0:T(8,128)} fusion(f32[4,512,512]{2,1,0:T(8,128)} %get-tuple-element.396, f32[4,512]{1,0:T(4,128)S(1)} %select_maximum_fusion.2, pred[512,512]{0,1:T(8,128)(4,1)S(1)} %fusion.43, f32[4,512,64]{1,2,0:T(8,128)} %get-tuple-element.415, bf16[4,1024,128]{1,2,0:T(8,128)(2,1)} %get-tuple-element.431, s32[]{:T(128)S(6)} %select_n.115, ...), kind=kOutput, calls=%fused_computation.9.clone.1 | convolution fusion | flops 139853824 | bytes 5783561 | tf_op jit(solution)/shard_map/while/body/eval_jaxpr/while/body/eval_jaxpr/ovn,onr->ovr/dot_general | solution.py:35
  172.0 1.8 bitcast_dynamic-update-slice_fusion.2
  173.8 1.5 copy.39
  175.3 1.3 reshape.63
  176.6 1.4 copy.40
  178.1 19.0 %all_to_all.51 = bf16[4,512,128]{2,0,1:T(4,128)(2,1)S(1)} all-to-all(bf16[4,512,128]{2,0,1:T(4,128)(2,1)S(1)} %copy.40), channel_id=1, replica_groups=mesh['heads'=4,'cells'=8] {'cells'}, dimensions={1} | all-to-all | bytes 1048576 | tf_op jit(solution)/shard_map/all_to_all | solution.py:105
  197.1 0.9 copy.55
  198.0 1.6 reshape_reshape.7
  199.6 1.1 copy.42
  200.8 1.4 copy.43
  202.2 11.2 %all_to_all.52 = bf16[8,128,256]{2,0,1:T(8,128)(2,1)S(1)} all-to-all(bf16[8,128,256]{2,0,1:T(8,128)(2,1)S(1)} %copy.43), channel_id=1, replica_groups=mesh['heads'=4,'cells'=8] {'heads'}, dimensions={1} | all-to-all | bytes 1048576 | tf_op jit(solution)/shard_map/all_to_all | solution.py:112
  213.4 0.4 copy.45
  213.8 0.4 all_to_all.47
  214.2 1.5 fusion.21
  (42 shorter events, 0.4 us)
Async XLA Ops:
  6.5 207.7 %copy-start = (bf16[1024,1024]{1,0:T(8,128)(2,1)S(1)}, bf16[1024,1024]{1,0:T(8,128)(2,1)}, u32[]{:S(2)}) copy-start(bf16[1024,1024]{1,0:T(8,128)(2,1)} %param.13) | copy-start | bytes 6291460
  6.5 28.9 %all-gather.3.cloned.1.call-start = ((), (), s32[]{:S(2)}) async-start(), calls=%async_computation.3 | async-start | bytes 2621440 | tf_op jit(solution)/shard_map/all_gather | solution.py:77
  40.4 10.9 %copy-start.3 = (u32[32]{0:T(128)S(1)}, u32[32]{0:T(128)}, u32[]{:S(2)}) copy-start(u32[32]{0:T(128)} %constant.135) | copy-start | bytes 388
  40.5 12.1 %copy-start.2 = (s32[32]{0:T(128)S(1)}, s32[32]{0:T(128)}, u32[]{:S(2)}) copy-start(s32[32]{0:T(128)} %param.14) | copy-start | bytes 388
  40.5 52.5 %copy-start.1 = (s32[256,256]{1,0:T(8,128)S(1)}, s32[256,256]{1,0:T(8,128)}, u32[]{:S(2)}) copy-start(s32[256,256]{1,0:T(8,128)} %param.15) | copy-start | bytes 786436
  45.8 51.8 %all-to-all-start = ((bf16[32,128,192]{1,2,0:T(8,128)(2,1)}), bf16[32,128,192]{1,2,0:T(8,128)(2,1)}, u32[]{:S(2)}, u32[]{:S(2)}) async-start(bf16[32,128,192]{1,2,0:T(8,128)(2,1)} %bitcast.74), calls=%async_computation | async-start | bytes 3145728 | tf_op jit(solution)/shard_map/all_to_all | solution.py:88
Sparse Core Ops, SparseCore 0:
  10.1 25.2 all-gather.2
where the time goes:
time: 224 us; the launch traced here: 223 us
  blocking collectives  70.4 us (31%)
  local copies, waits for them, and re-layouts  50.1 us (22%)
  matrix products  39.4 us (18%)
  other arithmetic  27.6 us (12%)
  between operations  14.1 us (6%)
  waiting for transfers between devices  13.9 us (6%)
  starting transfers between devices  5.52 us (2%)
    all_gather x1, blocking collectives, on_device(): tiles_all = lax.all_gather(tiles_here, 'cells', axis=0, tiled=True)  35.9 us
    all_to_all x1, blocking collectives, on_device(): lax.all_to_all(attention_output, 'cells', split_axis=1, concat_axis=0, ti...  19 us
    dot_general x4, matrix products, update(): jnp.einsum('ovn,onr->ovr', softmax_weights.astype(jnp.bfloat16), value_ma...  17.7 us
    dot_general x4, matrix products, update(): jnp.einsum('hoz,hjz->hoj', query_matrix, key_matrix, preferred_element_ty...  15.2 us
    all_gather x1, waiting for transfers between devices, on_device(): rows_all = lax.all_gather(normed, 'heads', axis=1, tiled=True)  13.9 us
    reduce_sum x4, other arithmetic, update(): total = total * factor + jnp.sum(softmax_weights, axis=-1)  13 us
    all_to_all x1, blocking collectives, on_device(): lax.all_to_all(heads_out, 'heads', split_axis=1, concat_axis=2, tiled=True)  11.2 us
    unnamed x12, local copies, waits for them, and re-layouts  9.51 us
  transfers between devices with their start and end apart: 2, of which 1 were waited for; matrix products, arithmetic and copies ran while one was open for 8% of the time, Pallas kernels for 0%

commit v1 on v0

v1 whole, which is shorter than its diff:
```python
import functools
import math

import jax
import jax.numpy as jnp
from jax import lax
from jax.experimental import pallas as pl
from jax.experimental.pallas import tpu as pltpu
from jax.sharding import PartitionSpec as P

HEAD_DIM = 64
PAIR = 2 * HEAD_DIM
VAL_ROWS = HEAD_DIM + 16
ACC_ROWS = HEAD_DIM + 8
MASKED = -1e30
SCALE = 0.125 * math.log2(math.e)
BLOCK = 512


def normalise(rows, gain):
    x32 = rows.astype(jnp.float32)
    mean = jnp.mean(x32 * x32, axis=-1, keepdims=True)
    return (x32 * lax.rsqrt(mean + 1e-05) * gain).astype(jnp.bfloat16)


def dot(a, b, a_dim=1, b_dim=0):
    return lax.dot_general(
        a, b, (((a_dim,), (b_dim,)), ((), ())), preferred_element_type=jnp.float32
    )


def one_hot(tiles, count):
    places = lax.broadcasted_iota(jnp.int32, (count, tiles.shape[1]), 0)
    return (places == tiles).astype(jnp.float32).astype(jnp.bfloat16)


def query_rows(adj_ref, tiles):
    adjacency = adj_ref[...].astype(jnp.float32).astype(jnp.bfloat16)
    return dot(adjacency, one_hot(tiles, adjacency.shape[0])).astype(jnp.bfloat16)


def absorb_block(rows, tiles, near, gain, wk_ref, wvt_ref, query_ref, acc_ref, top_ref, key_ref, val_ref, bias_ref, first):
    width = rows.shape[1]
    heads = width // HEAD_DIM
    normed = normalise(rows, gain)
    for start in range(0, width, 256):
        key_ref[:, start : start + 256] = dot(normed, wk_ref[:, start : start + 256]).astype(
            jnp.bfloat16
        )
    for start in range(0, width, 256):
        values = dot(wvt_ref[start : start + 256, :], normed, 1, 1).astype(jnp.bfloat16)
        for part in range(256 // HEAD_DIM):
            head = start // HEAD_DIM + part
            val_ref[head, :HEAD_DIM, :] = values[part * HEAD_DIM : (part + 1) * HEAD_DIM]
    allowed = dot(one_hot(tiles, near.shape[0]), near, 0, 0)
    bias_ref[...] = (allowed - 1.0) * -MASKED
    for head in range(heads):
        pair = slice(head // 2 * PAIR, head // 2 * PAIR + PAIR)
        query = query_ref[:, pair]
        lane = lax.broadcasted_iota(jnp.int32, query.shape, 1)
        query = jnp.where((lane // HEAD_DIM) == head % 2, query, jnp.zeros_like(query))
        scores = dot(key_ref[:, pair], query, 1, 1) + bias_ref[...]
        top = jnp.max(scores, axis=0, keepdims=True)
        if not first:
            before = top_ref[head : head + 1, :]
            top = jnp.maximum(top, before)
        weights = jnp.exp2(scores - top).astype(jnp.bfloat16)
        summed = dot(val_ref[head], weights)[:ACC_ROWS]
        if not first:
            summed = summed + acc_ref[head] * jnp.exp2(before - top)
        acc_ref[head] = summed
        top_ref[head : head + 1, :] = top


def absorb_all(chunks, tile_refs, near, gain, wk_ref, wvt_ref, query_ref, acc_ref, top_ref, key_ref, val_ref, bias_ref, first):
    block = key_ref.shape[0]
    for chunk, tile_ref in zip(chunks, tile_refs):
        for start in range(0, chunk.shape[0], block):
            absorb_block(
                chunk[start : start + block, :],
                tile_ref[:, start : start + block],
                near,
                gain,
                wk_ref,
                wvt_ref,
                query_ref,
                acc_ref,
                top_ref,
                key_ref,
                val_ref,
                bias_ref,
                first,
            )
            first = False


def set_ones(val_ref):
    heads, _, block = val_ref.shape
    val_ref[:, HEAD_DIM:, :] = jnp.ones((heads, VAL_ROWS - HEAD_DIM, block), jnp.bfloat16)


def first_kernel(count, xq_ref, tq_ref, gain_ref, adj_ref, wq_ref, wk_ref, wvt_ref, *refs):
    chunks, tile_refs, rest = refs[:count], refs[count : 2 * count], refs[2 * count :]
    query_ref, acc_ref, top_ref, key_ref, val_ref, bias_ref = rest
    gain = gain_ref[...]
    width = xq_ref.shape[1]
    set_ones(val_ref)
    normed = normalise(xq_ref[...], gain)
    for start in range(0, width, 256):
        part = dot(normed, wq_ref[:, start : start + 256]) * SCALE
        query_ref[:, start : start + 256] = part.astype(jnp.bfloat16)
    near = query_rows(adj_ref, tq_ref[...])
    absorb_all(chunks, tile_refs, near, gain, wk_ref, wvt_ref, query_ref, acc_ref, top_ref, key_ref, val_ref, bias_ref, True)


def last_kernel(count, query_ref, acc_in, top_in, tq_ref, gain_ref, adj_ref, wk_ref, wvt_ref, wo_ref, *refs):
    chunks, tile_refs, rest = refs[:count], refs[count : 2 * count], refs[2 * count :]
    out_ref, acc_ref, top_ref, key_ref, val_ref, bias_ref, att_ref = rest
    set_ones(val_ref)
    acc_ref[...] = acc_in[...]
    top_ref[...] = top_in[...]
    near = query_rows(adj_ref, tq_ref[...])
    absorb_all(
        chunks, tile_refs, near, gain_ref[...], wk_ref, wvt_ref, query_ref, acc_ref, top_ref, key_ref, val_ref, bias_ref, False
    )
    for head in range(acc_ref.shape[0]):
        total = acc_ref[head, HEAD_DIM : HEAD_DIM + 1, :]
        part = acc_ref[head, :HEAD_DIM, :] / total
        att_ref[head * HEAD_DIM : (head + 1) * HEAD_DIM, :] = part.astype(jnp.bfloat16)
    attended = att_ref[...]
    width = attended.shape[0]
    for start in range(0, width, 256):
        out_ref[:, start : start + 256] = dot(attended, wo_ref[:, start : start + 256], 0, 0).astype(
            jnp.bfloat16
        )


def vmem(count):
    return [pl.BlockSpec(memory_space=pltpu.VMEM)] * count


def scratch(block, queries, heads):
    return [
        pltpu.VMEM((block, heads * HEAD_DIM), jnp.bfloat16),
        pltpu.VMEM((heads, VAL_ROWS, block), jnp.bfloat16),
        pltpu.VMEM((block, queries), jnp.float32),
    ]


PARAMS = pltpu.CompilerParams(vmem_limit_bytes=48 * 1024 * 1024)


def call_first(xq, tq, gain, adjacency, wq, wk, wvt, chunks, tiles):
    queries, width = xq.shape
    heads = width // HEAD_DIM
    block = math.gcd(BLOCK, chunks[0].shape[0])
    operands = (xq, tq, gain, adjacency, wq, wk, wvt, *chunks, *tiles)
    return pl.pallas_call(
        functools.partial(first_kernel, len(chunks)),
        out_shape=(
            jax.ShapeDtypeStruct((queries, width), jnp.bfloat16),
            jax.ShapeDtypeStruct((heads, ACC_ROWS, queries), jnp.float32),
            jax.ShapeDtypeStruct((heads, queries), jnp.float32),
        ),
        in_specs=vmem(len(operands)),
        out_specs=tuple(vmem(3)),
        scratch_shapes=scratch(block, queries, heads),
        compiler_params=PARAMS,
        name="attend_first",
    )(*operands)


def call_last(query, acc, top, tq, gain, adjacency, wk, wvt, wo, chunks, tiles):
    queries, width = query.shape
    heads = width // HEAD_DIM
    block = math.gcd(BLOCK, chunks[0].shape[0])
    operands = (query, acc, top, tq, gain, adjacency, wk, wvt, wo, *chunks, *tiles)
    return pl.pallas_call(
        functools.partial(last_kernel, len(chunks)),
        out_shape=jax.ShapeDtypeStruct((queries, width), jnp.bfloat16),
        in_specs=vmem(len(operands)),
        out_specs=vmem(1)[0],
        scratch_shapes=[
            pltpu.VMEM((heads, ACC_ROWS, queries), jnp.float32),
            pltpu.VMEM((heads, queries), jnp.float32),
            *scratch(block, queries, heads),
            pltpu.VMEM((width, queries), jnp.bfloat16),
        ],
        compiler_params=PARAMS,
        name="attend_last",
    )(*operands)


def on_device(cells_in, gain, w_qkv, w_out, tile_of_cell, tile_adjacent):
    genes, cell_dev, width = cells_in.shape
    head_devs, cell_devs = lax.axis_size("heads"), lax.axis_size("cells")
    sets = cell_devs // genes
    across = [[s * genes + g for g in range(genes)] for s in range(sets)]
    same = [[s * genes + g for s in range(sets)] for g in range(genes)]

    def partner(value, step):
        return lax.ppermute(value, "heads", [(i, i ^ step) for i in range(head_devs)])

    own = lax.all_to_all(cells_in, "cells", 0, 0, axis_index_groups=across, tiled=True)
    own = own.reshape(genes * cell_dev, width)
    spread = jnp.broadcast_to(tile_of_cell[None], (genes, cell_dev))
    tile_own = lax.all_to_all(spread, "cells", 0, 0, axis_index_groups=across, tiled=True)
    tile_own = tile_own.reshape(1, genes * cell_dev)
    held, tile_held = own, tile_own
    if sets > 1:
        held = lax.all_gather(own, "cells", axis=0, axis_index_groups=same, tiled=True)
        tile_held = lax.all_gather(tile_own, "cells", axis=1, axis_index_groups=same, tiled=True)
    chunks, tiles = [held], [tile_held]
    for step in range(2, head_devs, 2):
        chunks.append(partner(held, step))
        tiles.append(partner(tile_held, step))
    beside = [partner(chunk, 1) for chunk in chunks]
    tiles_beside = [partner(tile, 1) for tile in tiles]

    gain = gain.reshape(1, width)
    wq, wk, wvt = w_qkv[:, :width], w_qkv[:, width : 2 * width], w_qkv[:, 2 * width :].T
    query, acc, top = call_first(
        own, tile_own, gain, tile_adjacent, wq, wk, wvt, [chunks[0], beside[0]], [tiles[0], tiles_beside[0]]
    )
    out = call_last(
        query, acc, top, tile_own, gain, tile_adjacent, wk, wvt, w_out,
        [*chunks[1:], *beside[1:]], [*tiles[1:], *tiles_beside[1:]],
    )
    out = out.reshape(genes, cell_dev, width)
    return lax.all_to_all(out, "cells", 0, 0, axis_index_groups=across, tiled=True)


def solution(mesh):
    return jax.shard_map(
        on_device,
        mesh=mesh,
        in_specs=(P(None, ("heads", "cells"), None), P(), P(), P(), P(("heads", "cells")), P()),
        out_specs=P(None, ("heads", "cells"), None),
        check_vma=False,
    )
```

time: 224 us -> 108 us (0.48)
  matrix products: 39.4 us -> 0 us
  local copies, waits for them, and re-layouts: 50.1 us -> 11.7 us
  Pallas kernels: 0 us -> 28.9 us
  other arithmetic: 27.6 us -> 0.66 us
  blocking collectives: 70.4 us -> 50.3 us
  between operations: 14.1 us -> 0.07 us
  starting transfers between devices: 5.52 us -> 3 us
    dot_general x10 -> x0, matrix products: 39.4 us -> none  [the longest x4 17.7 us: update(): jnp.einsum('ovn,onr->ovr', softmax_weights.astype(jnp.bfloat16), value_ma...]
    all_gather x1 -> x0, blocking collectives: 35.9 us -> none  [on_device(): tiles_all = lax.all_gather(tiles_here, 'cells', axis=0, tiled=True)]
    pallas_call x0 -> x2, Pallas kernels: none -> 28.9 us  [the longest x1 14.5 us: call_last(): pl.pallas_call(functools.partial(last_kernel, len(chunks)), out_shape=jax...]
    all_to_all x2 -> x3, blocking collectives: 30.2 us -> 50.3 us  [the longest x1 21.8 us: on_device(): lax.all_to_all(cells_in, 'cells', 0, 0, axis_index_groups=across, tiled=T...]
    reduce_sum x5 -> x0, other arithmetic: 14.3 us -> none  [the longest x4 13 us: update(): total = total * factor + jnp.sum(softmax_weights, axis=-1)]
    all_gather x1 -> x0, waiting for transfers between devices: 13.9 us -> none  [on_device(): rows_all = lax.all_gather(normed, 'heads', axis=1, tiled=True)]
    ppermute x0 -> x6, waiting for transfers between devices: none -> 13.2 us  [partner(): lax.ppermute(value, 'heads', [(i, i ^ step) for i in range(head_devs)])]
    gather x5 -> x0, local copies, waits for them, and re-layouts: 12.8 us -> none  [the longest x4 9.31 us: update(): allowed = jnp.take(rowtile, key_tiles, axis=1) > 0]
  transfers between devices with their start and end apart: 2 -> 6, of which waited for: 1 -> 2; matrix products, arithmetic and copies ran while one was open for 8% -> 11% of each run, Pallas kernels for 0% -> 13%
where the time goes in v1:
time: 108 us
  blocking collectives  50.3 us (47%)
  Pallas kernels  28.9 us (27%)
  waiting for transfers between devices  13.2 us (12%)
  local copies, waits for them, and re-layouts  11.7 us (11%)
  starting transfers between devices  3 us (3%)
    all_to_all x1, blocking collectives, on_device(): lax.all_to_all(cells_in, 'cells', 0, 0, axis_index_groups=across, tiled=T...  21.8 us
    all_to_all x1, blocking collectives, on_device(): lax.all_to_all(out, 'cells', 0, 0, axis_index_groups=across, tiled=True)  17.8 us
    pallas_call x1, Pallas kernels, call_last(): pl.pallas_call(functools.partial(last_kernel, len(chunks)), out_shape=jax...  14.5 us
    pallas_call x1, Pallas kernels, call_first(): pl.pallas_call(functools.partial(first_kernel, len(chunks)), out_shape=(j...  14.4 us
    ppermute x6, waiting for transfers between devices, partner(): lax.ppermute(value, 'heads', [(i, i ^ step) for i in range(head_devs)])  13.2 us
    all_to_all x1, blocking collectives, on_device(): lax.all_to_all(spread, 'cells', 0, 0, axis_index_groups=across, tiled=True)  10.6 us
    slice x1, local copies, waits for them, and re-layouts, on_device(): w_qkv[:, 2 * width:]  5.66 us
    unnamed x8, local copies, waits for them, and re-layouts  4.78 us
  transfers between devices with their start and end apart: 6, of which 2 were waited for; matrix products, arithmetic and copies ran while one was open for 11% of the time, Pallas kernels for 13%

profile of v1, /device:TPU:0, one launch (start us, length us, event | category | flops | bytes accessed | tf_op | source)
XLA Modules:
  0.0 107.9 jit_solution(811851920335966516)
XLA Ops:
  0.0 21.8 %all_to_all.16 = bf16[8,32,1024]{2,1,0:T(8,128)(2,1)S(1)} all-to-all(bf16[8,32,1024]{2,1,0:T(8,128)(2,1)} %param.6), channel_id=1, replica_groups={{0,1,2,3,4,5,6,7},{8,9,10,11,12,13,14,15},{16,17,18,19,20,21,22,23},{24..., dimensions={0} | all-to-all | bytes 1048576 | tf_op jit(solution)/shard_map/all_to_all | solution.py:204
  21.8 1.5 %collective-permute-start.2 = (bf16[256,1024]{1,0:T(8,128)(2,1)S(1)}, bf16[256,1024]{1,0:T(8,128)(2,1)}, u32[]{:S(2)}, u32[]{:S(2)}) collective-permute-start(bf16[256,1024]{1,0:T(8,128)(2,1)S(1)} %bitcast.4), channel_id=1, source_target_pairs={{0,16},{8,24},{16,0},{24,8},{1,17},{9,25},{17,1},{25,9},{2,18},{10... | collective-permute-start | bytes 1572872 | tf_op jit(solution)/shard_map/ppermute | solution.py:202
  23.3 0.0 collective-permute-start
  23.3 11.1 %collective-permute-done.2.refs_0_ = bf16[256,1024]{1,0:T(8,128)(2,1)} collective-permute-done((bf16[256,1024]{1,0:T(8,128)(2,1)S(1)}, bf16[256,1024]{1,0:T(8,128)(2,1)}, u32[]{:S(2)}, u32[]{:S(2)}) %collective-permute-start.2) | collective-permute-done | bytes 524320 | tf_op jit(solution)/shard_map/ppermute | solution.py:202
  34.5 0.0 collective-permute-start.3
  34.5 0.7 broadcast_in_dim.2
  35.1 10.6 %all_to_all.17 = s32[8,1,32]{2,1,0:T(1,128)S(1)} all-to-all(s32[8,1,32]{2,1,0:T(1,128)S(1)} %broadcast_in_dim.2), channel_id=1, replica_groups={{0,1,2,3,4,5,6,7},{8,9,10,11,12,13,14,15},{16,17,18,19,20,21,22,23},{24..., dimensions={0} | all-to-all | bytes 2048 | tf_op jit(solution)/shard_map/all_to_all | solution.py:207
  45.7 0.5 broadcast.6
  46.2 0.7 reduce.3
  46.9 0.1 reshape.20.tq_ref.refs_2_
  47.0 1.5 %collective-permute-start.4 = (s32[1,256]{1,0:T(1,128)S(1)}, s32[1,256]{1,0:T(1,128)S(1)}, u32[]{:S(2)}, u32[]{:S(2)}) collective-permute-start(s32[1,256]{1,0:T(1,128)S(1)} %reshape.20.tq_ref.refs_2_), channel_id=1, source_target_pairs={{0,16},{8,24},{16,0},{24,8},{1,17},{9,25},{17,1},{25,9},{2,18},{10... | collective-permute-start | bytes 3080 | tf_op jit(solution)/shard_map/ppermute | solution.py:202
  48.5 0.0 collective-permute-start.1
  48.5 2.1 %collective-permute-done.4.refs_2_ = s32[1,256]{1,0:T(1,128)S(1)} collective-permute-done((s32[1,256]{1,0:T(1,128)S(1)}, s32[1,256]{1,0:T(1,128)S(1)}, u32[]{:S(2)}, u32[]{:S(2)}) %collective-permute-start.4) | collective-permute-done | bytes 1056 | tf_op jit(solution)/shard_map/ppermute | solution.py:202
  50.6 0.0 collective-permute-start.5
  50.6 5.7 %fusion = (bf16[1024,1024]{1,0:T(8,128)(2,1)}, bf16[1024,1024]{1,0:T(8,128)(2,1)S(1)}, bf16[1024,1024]{1,0:T(8,128)(2,1)}) fusion(bf16[1024,3072]{1,0:T(8,128)(2,1)} %param.8), kind=kLoop, calls=%fused_computation | loop fusion | bytes 12582912 | tf_op jit(solution)/shard_map/slice | solution.py:221
  56.2 0.0 copy-start.1
  56.2 0.0 copy-start.2
  56.2 4.0 %copy.9 = bf16[1024,1024]{0,1:T(8,128)(2,1)} copy(bf16[1024,1024]{1,0:T(8,128)(2,1)} %get-tuple-element.11) | data formatting | bytes 4194304
  60.2 0.0 collective-permute-done.1.refs_3_
  60.2 0.0 collective-permute-done.refs_1_
  60.2 0.0 copy-done.1
  60.2 0.0 copy-done.2
  60.2 0.0 copy-start
  60.2 14.4 %attend_first.1 = (bf16[256,1024]{1,0:T(8,128)(2,1)S(1)}, f32[16,72,256]{2,1,0:T(8,128)S(1)}, f32[16,256]{1,0:T(8,128)S(1)}) custom-call(bf16[256,1024]{1,0:T(8,128)(2,1)S(1)} %bitcast.6, s32[1,256]{1,0:T(1,128)S(1)} %reshape.20.tq_ref.refs_2_, f32[1,1024]{1,0:T(1,128)S(1)} %bitcast.9, s32[256,256]{1,0:T(8,128)S(1)} %copy-done.1, ...), custom_call_target="tpu_custom_call" | custom-call | tf_op jit(solution)/shard_map/attend_first/pallas_call | solution.py:158
  74.7 0.0 collective-permute-done.5.refs_3_
  74.7 0.0 collective-permute-done.3.refs_1_
  74.7 0.0 copy-done
  74.7 14.5 %attend_last.1 = bf16[256,1024]{1,0:T(8,128)(2,1)S(1)} custom-call(bf16[256,1024]{1,0:T(8,128)(2,1)S(1)} %get-tuple-element.8.query_ref, f32[16,72,256]{2,1,0:T(8,128)S(1)} %get-tuple-element.9.acc_in, f32[16,256]{1,0:T(8,128)S(1)} %get-tuple-element.10.top_in, s32[1,256]{1,0:T(1,128)S(1)} %reshape.20.tq_ref.refs_2_, f32[1,1024]{1,0:T(1,128)S(1)} %bitcast.10, ...), custom_call_target="tpu_custom_call" | custom-call | tf_op jit(solution)/shard_map/attend_last/pallas_call | solution.py:178
  89.2 17.8 %all_to_all.18 = bf16[8,32,1024]{2,1,0:T(8,128)(2,1)S(1)} all-to-all(bf16[8,32,1024]{2,1,0:T(8,128)(2,1)S(1)} %bitcast.8), channel_id=1, replica_groups={{0,1,2,3,4,5,6,7},{8,9,10,11,12,13,14,15},{16,17,18,19,20,21,22,23},{24..., dimensions={0} | all-to-all | bytes 1048576 | tf_op jit(solution)/shard_map/all_to_all | solution.py:230
  107.1 0.8 copy.11
Async XLA Ops:
  21.8 12.6 %collective-permute-start.2 = (bf16[256,1024]{1,0:T(8,128)(2,1)S(1)}, bf16[256,1024]{1,0:T(8,128)(2,1)}, u32[]{:S(2)}, u32[]{:S(2)}) collective-permute-start(bf16[256,1024]{1,0:T(8,128)(2,1)S(1)} %bitcast.4), channel_id=1, source_target_pairs={{0,16},{8,24},{16,0},{24,8},{1,17},{9,25},{17,1},{25,9},{2,18},{10... | collective-permute-start | bytes 1572872 | tf_op jit(solution)/shard_map/ppermute | solution.py:202
  23.3 36.9 %collective-permute-start = (bf16[256,1024]{1,0:T(8,128)(2,1)S(1)}, bf16[256,1024]{1,0:T(8,128)(2,1)S(1)}, u32[]{:S(2)}, u32[]{:S(2)}) collective-permute-start(bf16[256,1024]{1,0:T(8,128)(2,1)S(1)} %bitcast.5), channel_id=1, source_target_pairs={{0,8},{8,0},{16,24},{24,16},{1,9},{9,1},{17,25},{25,17},{2,10},{10... | collective-permute-start | bytes 1572872 | tf_op jit(solution)/shard_map/ppermute | solution.py:202
  34.5 40.2 %collective-permute-start.3 = (bf16[256,1024]{1,0:T(8,128)(2,1)}, bf16[256,1024]{1,0:T(8,128)(2,1)}, u32[]{:S(2)}, u32[]{:S(2)}) collective-permute-start(bf16[256,1024]{1,0:T(8,128)(2,1)} %collective-permute-done.2.refs_0_), channel_id=1, source_target_pairs={{0,8},{8,0},{16,24},{24,16},{1,9},{9,1},{17,25},{25,17},{2,10},{10... | collective-permute-start | bytes 1572872 | tf_op jit(solution)/shard_map/ppermute | solution.py:202
  47.0 3.6 %collective-permute-start.4 = (s32[1,256]{1,0:T(1,128)S(1)}, s32[1,256]{1,0:T(1,128)S(1)}, u32[]{:S(2)}, u32[]{:S(2)}) collective-permute-start(s32[1,256]{1,0:T(1,128)S(1)} %reshape.20.tq_ref.refs_2_), channel_id=1, source_target_pairs={{0,16},{8,24},{16,0},{24,8},{1,17},{9,25},{17,1},{25,9},{2,18},{10... | collective-permute-start | bytes 3080 | tf_op jit(solution)/shard_map/ppermute | solution.py:202
  48.5 11.7 %collective-permute-start.1 = (s32[1,256]{1,0:T(1,128)S(1)}, s32[1,256]{1,0:T(1,128)S(1)}, u32[]{:S(2)}, u32[]{:S(2)}) collective-permute-start(s32[1,256]{1,0:T(1,128)S(1)} %reshape.20.tq_ref.refs_2_), channel_id=1, source_target_pairs={{0,8},{8,0},{16,24},{24,16},{1,9},{9,1},{17,25},{25,17},{2,10},{10... | collective-permute-start | bytes 3080 | tf_op jit(solution)/shard_map/ppermute | solution.py:202
  50.6 24.1 %collective-permute-start.5 = (s32[1,256]{1,0:T(1,128)S(1)}, s32[1,256]{1,0:T(1,128)S(1)}, u32[]{:S(2)}, u32[]{:S(2)}) collective-permute-start(s32[1,256]{1,0:T(1,128)S(1)} %collective-permute-done.4.refs_2_), channel_id=1, source_target_pairs={{0,8},{8,0},{16,24},{24,16},{1,9},{9,1},{17,25},{25,17},{2,10},{10... | collective-permute-start | bytes 3080 | tf_op jit(solution)/shard_map/ppermute | solution.py:202
  56.2 4.0 %copy-start.1 = (s32[256,256]{1,0:T(8,128)S(1)}, s32[256,256]{1,0:T(8,128)}, u32[]{:S(2)}) copy-start(s32[256,256]{1,0:T(8,128)} %adj_ref.3) | copy-start | bytes 786436
  56.2 4.0 %copy-start.2 = (f32[1024]{0:T(1024)S(1)}, f32[1024]{0:T(1024)}, u32[]{:S(2)}) copy-start(f32[1024]{0:T(1024)} %param.7) | copy-start | bytes 12292
  60.2 14.4 %copy-start = (bf16[1024,1024]{1,0:T(8,128)(2,1)S(1)}, bf16[1024,1024]{1,0:T(8,128)(2,1)}, u32[]{:S(2)}) copy-start(bf16[1024,1024]{1,0:T(8,128)(2,1)} %get-tuple-element.13.wk_ref) | copy-start | bytes 6291460

commit v2 on v1

v2 whole, which is shorter than its diff:
```python
import functools
import math

import jax
import jax.numpy as jnp
from jax import lax
from jax.experimental import pallas as pl
from jax.experimental.pallas import tpu as pltpu
from jax.sharding import PartitionSpec as P

HEAD_DIM = 64
PAIR = 2 * HEAD_DIM
VAL_ROWS = HEAD_DIM + 16
ACC_ROWS = HEAD_DIM + 8
MASKED = -1e30
SCALE = 0.125 * math.log2(math.e)
BLOCK = 256
COLS = 256


def normalise(rows, gain):
    x32 = rows.astype(jnp.float32)
    mean = jnp.mean(x32 * x32, axis=-1, keepdims=True)
    return (x32 * lax.rsqrt(mean + 1e-05) * gain).astype(jnp.bfloat16)


def dot(a, b, a_dim=1, b_dim=0):
    return lax.dot_general(
        a, b, (((a_dim,), (b_dim,)), ((), ())), preferred_element_type=jnp.float32
    )


def one_hot(tiles, count):
    places = lax.broadcasted_iota(jnp.int32, (count, tiles.shape[1]), 0)
    return (places == tiles).astype(jnp.float32).astype(jnp.bfloat16)


def query_rows(adj_ref, tiles):
    adjacency = adj_ref[...].astype(jnp.float32).astype(jnp.bfloat16)
    return dot(adjacency, one_hot(tiles, adjacency.shape[0])).astype(jnp.bfloat16)


class Work:
    def __init__(self, gain, w_ref, near, query_ref, acc_ref, top_ref, scratch):
        self.gain, self.w_ref, self.near = gain, w_ref, near
        self.query_ref, self.acc_ref, self.top_ref = query_ref, acc_ref, top_ref
        self.norm_ref, self.key_ref, self.val_ref, self.bias_ref, self.weight_ref = scratch
        heads, _, block = self.val_ref.shape
        ones = jnp.ones((heads, VAL_ROWS - HEAD_DIM, block), jnp.bfloat16)
        self.val_ref[:, HEAD_DIM:, :] = ones

    def normal(self, pieces):
        start = 0
        for piece in pieces:
            self.norm_ref[start : start + piece.shape[0], :] = normalise(piece, self.gain)
            start += piece.shape[0]
        return self.norm_ref[...]

    def project_queries(self, pieces):
        normed = self.normal(pieces)
        for start in range(0, normed.shape[1], COLS):
            part = dot(normed, self.w_ref[:, start : start + COLS]) * SCALE
            self.query_ref[:, start : start + COLS] = part.astype(jnp.bfloat16)

    def absorb(self, pieces, tiles, first):
        normed = self.normal(pieces)
        width = normed.shape[1]
        heads = width // HEAD_DIM
        for start in range(0, width, COLS):
            keys = dot(normed, self.w_ref[:, width + start : width + start + COLS])
            self.key_ref[:, start : start + COLS] = keys.astype(jnp.bfloat16)
        allowed = dot(one_hot(tiles, self.near.shape[0]), self.near, 0, 0)
        self.bias_ref[...] = (allowed - 1.0) * -MASKED
        for start in range(0, width, COLS):
            values = dot(normed, self.w_ref[:, 2 * width + start : 2 * width + start + COLS])
            values = values.astype(jnp.bfloat16).T
            for part in range(COLS // HEAD_DIM):
                rows = slice(part * HEAD_DIM, (part + 1) * HEAD_DIM)
                self.val_ref[start // HEAD_DIM + part, :HEAD_DIM, :] = values[rows]
        factors = []
        for head in range(heads):
            pair = slice(head // 2 * PAIR, head // 2 * PAIR + PAIR)
            query = self.query_ref[:, pair]
            lane = lax.broadcasted_iota(jnp.int32, query.shape, 1)
            query = jnp.where((lane // HEAD_DIM) == head % 2, query, jnp.zeros_like(query))
            scores = dot(self.key_ref[:, pair], query, 1, 1) + self.bias_ref[...]
            top = jnp.max(scores, axis=0, keepdims=True)
            if not first:
                before = self.top_ref[head : head + 1, :]
                top = jnp.maximum(top, before)
                factors.append(jnp.exp2(before - top))
            self.weight_ref[head] = jnp.exp2(scores - top).astype(jnp.bfloat16)
            self.top_ref[head : head + 1, :] = top
        for head in range(heads):
            summed = dot(self.val_ref[head], self.weight_ref[head])[:ACC_ROWS]
            if not first:
                summed = summed + self.acc_ref[head] * factors[head]
            self.acc_ref[head] = summed


def blocks_of(chunks, tile_refs, block):
    held = []
    for chunk, tile_ref in zip(chunks, tile_refs):
        step = min(block, chunk.shape[0])
        for start in range(0, chunk.shape[0], step):
            held.append((chunk[start : start + step, :], tile_ref[:, start : start + step]))
    per = block // held[0][0].shape[0]
    for start in range(0, len(held), per):
        group = held[start : start + per]
        yield [rows for rows, _ in group], jnp.concatenate([tiles for _, tiles in group], axis=1)


def first_kernel(queries, count, tq_ref, gain_ref, adj_ref, w_ref, *refs):
    query_x, refs = refs[:queries], refs[queries:]
    chunks, tile_refs, rest = refs[:count], refs[count : 2 * count], refs[2 * count :]
    query_ref, acc_ref, top_ref, *scratch = rest
    near = query_rows(adj_ref, tq_ref[...])
    work = Work(gain_ref[...], w_ref, near, query_ref, acc_ref, top_ref, scratch)
    work.project_queries([ref[...] for ref in query_x])
    first = True
    for pieces, tiles in blocks_of(chunks, tile_refs, scratch[0].shape[0]):
        work.absorb(pieces, tiles, first)
        first = False


def next_kernel(count, query_ref, acc_in, top_in, tq_ref, gain_ref, adj_ref, w_ref, *refs):
    chunks, tile_refs, rest = refs[:count], refs[count : 2 * count], refs[2 * count :]
    acc_ref, top_ref, *scratch = rest
    near = query_rows(adj_ref, tq_ref[...])
    acc_ref[...] = acc_in[...]
    top_ref[...] = top_in[...]
    work = Work(gain_ref[...], w_ref, near, query_ref, acc_ref, top_ref, scratch)
    for pieces, tiles in blocks_of(chunks, tile_refs, scratch[0].shape[0]):
        work.absorb(pieces, tiles, False)


def last_kernel(count, query_ref, acc_in, top_in, tq_ref, gain_ref, adj_ref, w_ref, wo_ref, *refs):
    chunks, tile_refs, rest = refs[:count], refs[count : 2 * count], refs[2 * count :]
    out_ref, acc_ref, top_ref, att_ref, *scratch = rest
    near = query_rows(adj_ref, tq_ref[...])
    acc_ref[...] = acc_in[...]
    top_ref[...] = top_in[...]
    work = Work(gain_ref[...], w_ref, near, query_ref, acc_ref, top_ref, scratch)
    for pieces, tiles in blocks_of(chunks, tile_refs, scratch[0].shape[0]):
        work.absorb(pieces, tiles, False)
    for head in range(acc_ref.shape[0]):
        total = acc_ref[head, HEAD_DIM : HEAD_DIM + 1, :]
        part = acc_ref[head, :HEAD_DIM, :] / total
        att_ref[head * HEAD_DIM : (head + 1) * HEAD_DIM, :] = part.astype(jnp.bfloat16)
    attended = att_ref[...].T
    for start in range(0, attended.shape[1], COLS):
        out = dot(attended, wo_ref[:, start : start + COLS])
        out_ref[:, start : start + COLS] = out.astype(jnp.bfloat16)


def vmem(count):
    return [pl.BlockSpec(memory_space=pltpu.VMEM)] * count


def scratch(queries, heads):
    return [
        pltpu.VMEM((BLOCK, heads * HEAD_DIM), jnp.bfloat16),
        pltpu.VMEM((BLOCK, heads * HEAD_DIM), jnp.bfloat16),
        pltpu.VMEM((heads, VAL_ROWS, BLOCK), jnp.bfloat16),
        pltpu.VMEM((BLOCK, queries), jnp.float32),
        pltpu.VMEM((heads, BLOCK, queries), jnp.bfloat16),
    ]


def cost(queries, keys, width, more):
    flops = 2 * (2 * keys * width * width + 4 * queries * keys * width + more * queries * width * width)
    return pl.CostEstimate(flops=flops, bytes_accessed=8 * width * width, transcendentals=0)


PARAMS = pltpu.CompilerParams(vmem_limit_bytes=32 * 1024 * 1024)


def state_shapes(heads, queries):
    return (
        jax.ShapeDtypeStruct((heads, ACC_ROWS, queries), jnp.float32),
        jax.ShapeDtypeStruct((heads, queries), jnp.float32),
    )


def call_first(query_x, tq, gain, adjacency, w_qkv, chunks, tiles):
    queries, width = tq.shape[1], w_qkv.shape[0]
    heads = width // HEAD_DIM
    operands = (tq, gain, adjacency, w_qkv, *query_x, *chunks, *tiles)
    return pl.pallas_call(
        functools.partial(first_kernel, len(query_x), len(chunks)),
        out_shape=(jax.ShapeDtypeStruct((queries, width), jnp.bfloat16), *state_shapes(heads, queries)),
        in_specs=vmem(len(operands)),
        out_specs=tuple(vmem(3)),
        scratch_shapes=scratch(queries, heads),
        compiler_params=PARAMS,
        cost_estimate=cost(queries, sum(c.shape[0] for c in chunks), width, 1),
        name="attend_first",
    )(*operands)


def call_next(query, acc, top, tq, gain, adjacency, w_qkv, chunks, tiles):
    queries, width = query.shape
    heads = width // HEAD_DIM
    operands = (query, acc, top, tq, gain, adjacency, w_qkv, *chunks, *tiles)
    return pl.pallas_call(
        functools.partial(next_kernel, len(chunks)),
        out_shape=state_shapes(heads, queries),
        in_specs=vmem(len(operands)),
        out_specs=tuple(vmem(2)),
        scratch_shapes=scratch(queries, heads),
        compiler_params=PARAMS,
        cost_estimate=cost(queries, sum(c.shape[0] for c in chunks), width, 0),
        name="attend_next",
    )(*operands)


def call_last(query, acc, top, tq, gain, adjacency, w_qkv, wo, chunks, tiles):
    queries, width = query.shape
    heads = width // HEAD_DIM
    operands = (query, acc, top, tq, gain, adjacency, w_qkv, wo, *chunks, *tiles)
    return pl.pallas_call(
        functools.partial(last_kernel, len(chunks)),
        out_shape=jax.ShapeDtypeStruct((queries, width), jnp.bfloat16),
        in_specs=vmem(len(operands)),
        out_specs=vmem(1)[0],
        scratch_shapes=[
            pltpu.VMEM((heads, ACC_ROWS, queries), jnp.float32),
            pltpu.VMEM((heads, queries), jnp.float32),
            pltpu.VMEM((width, queries), jnp.bfloat16),
            *scratch(queries, heads),
        ],
        compiler_params=PARAMS,
        cost_estimate=cost(queries, sum(c.shape[0] for c in chunks), width, 1),
        name="attend_last",
    )(*operands)


def on_device(cells_in, gain, w_qkv, w_out, tile_of_cell, tile_adjacent):
    genes, cell_dev, width = cells_in.shape
    head_devs, cell_devs = lax.axis_size("heads"), lax.axis_size("cells")
    sets = cell_devs // genes
    half = genes // 2
    gene = lax.rem(lax.axis_index("cells"), genes)
    same = [[s * genes + g for s in range(sets)] for g in range(genes)]

    def over_cells(value, step):
        return lax.ppermute(value, "cells", [(i, i ^ step) for i in range(cell_devs)])

    def over_heads(value, step):
        return lax.ppermute(value, "heads", [(i, i ^ step) for i in range(head_devs)])

    def gather_sets(value, axis):
        if sets == 1:
            return value
        return lax.all_gather(value, "cells", axis=axis, axis_index_groups=same, tiled=True)

    pieces = [lax.dynamic_index_in_dim(cells_in, gene ^ k, 0, keepdims=False) for k in range(genes)]
    tile_own = tile_of_cell.reshape(1, cell_dev)
    step = 1
    while step < genes:
        tile_own = jnp.concatenate([tile_own, over_cells(tile_own, step)], axis=1)
        step *= 2
    arrived = [pieces[0]] + [None] * (genes - 1)
    for k in [*range(half, genes), *range(1, half)]:
        arrived[k] = over_cells(pieces[k], k)
    parts = [jnp.concatenate(arrived[:half], 0), jnp.concatenate(arrived[half:], 0)]
    tile_parts = [tile_own[:, : half * cell_dev], tile_own[:, half * cell_dev :]]
    chunks = [[], []]
    tiles = [[], []]
    for i in range(2):
        held, tile_held = gather_sets(parts[i], 0), gather_sets(tile_parts[i], 1)
        for step in range(0, head_devs, 2):
            chunk = held if step == 0 else over_heads(held, step)
            tile = tile_held if step == 0 else over_heads(tile_held, step)
            chunks[i] += [chunk, over_heads(chunk, 1)]
            tiles[i] += [tile, over_heads(tile, 1)]
    gain = gain.reshape(1, width)
    query, acc, top = call_first(
        parts, tile_own, gain, tile_adjacent, w_qkv, chunks[0][:2] + chunks[1][:2], tiles[0][:2] + tiles[1][:2]
    )
    acc, top = call_next(query, acc, top, tile_own, gain, tile_adjacent, w_qkv, chunks[0][2:], tiles[0][2:])
    out = call_last(
        query, acc, top, tile_own, gain, tile_adjacent, w_qkv, w_out, chunks[1][2:], tiles[1][2:]
    )
    out = out.reshape(genes, cell_dev, width)
    result = jnp.zeros_like(out)
    for k in [*range(half, genes), *range(1, half), 0]:
        piece = out[k] if k == 0 else over_cells(out[k], k)
        result = lax.dynamic_update_index_in_dim(result, piece, gene ^ k, 0)
    return result


def solution(mesh):
    return jax.shard_map(
        on_device,
        mesh=mesh,
        in_specs=(P(None, ("heads", "cells"), None), P(), P(), P(), P(("heads", "cells")), P()),
        out_specs=P(None, ("heads", "cells"), None),
        check_vma=False,
    )
```

time: 108 us -> 75.2 us (0.70)
  blocking collectives: 50.3 us -> 0 us
  starting transfers between devices: 3 us -> 32.1 us
  Pallas kernels: 28.9 us -> 12.1 us
  waiting for transfers between devices: 13.2 us -> 24.8 us
  local copies, waits for them, and re-layouts: 11.7 us -> 5.53 us
    all_to_all x3 -> x0, blocking collectives: 50.3 us -> none  [the longest x1 21.8 us: on_device(): lax.all_to_all(cells_in, 'cells', 0, 0, axis_index_groups=across, tiled=T...]
    ppermute x6 -> x29, starting transfers between devices: 3 us -> 32.1 us  [the longest x17 26.8 us: over_cells(): lax.ppermute(value, 'cells', [(i, i ^ step) for i in range(cell_devs)])]
    ppermute x6 -> x29, waiting for transfers between devices: 13.2 us -> 24.8 us  [the longest x17 16.6 us: over_cells(): lax.ppermute(value, 'cells', [(i, i ^ step) for i in range(cell_devs)])]
    pallas_call x1, Pallas kernels: 14.5 us -> 3.38 us  [call_last(): pl.pallas_call(functools.partial(last_kernel, len(chunks)), out_shape=jax...]
    pallas_call x1 -> x2, Pallas kernels: 14.4 us -> 8.72 us  [the longest x1 5.95 us: call_first(): pl.pallas_call(functools.partial(first_kernel, len(query_x), len(chunks))...]
    slice x1, local copies, waits for them, and re-layouts: 5.66 us -> 0.03 us  [on_device(): piece = out[k] if k == 0 else over_cells(out[k], k)]
    unnamed x8 -> x15, local copies, waits for them, and re-layouts: 4.78 us -> 3.6 us
    squeeze x0 -> x1, local copies, waits for them, and re-layouts: none -> 1.14 us  [on_device(): lax.dynamic_index_in_dim(cells_in, gene ^ k, 0, keepdims=False)]
  transfers between devices with their start and end apart: 6 -> 29, of which waited for: 2 -> 13; matrix products, arithmetic and copies ran while one was open for 11% -> 1% of each run, Pallas kernels for 13% -> 12%
where the time goes in v2:
time: 75.2 us; the launch traced here: 75 us
  starting transfers between devices  32.1 us (43%)
  waiting for transfers between devices  24.8 us (33%)
  Pallas kernels  12.1 us (16%)
  local copies, waits for them, and re-layouts  5.53 us (7%)
    ppermute x17, starting transfers between devices, over_cells(): lax.ppermute(value, 'cells', [(i, i ^ step) for i in range(cell_devs)])  26.8 us
    ppermute x17, waiting for transfers between devices, over_cells(): lax.ppermute(value, 'cells', [(i, i ^ step) for i in range(cell_devs)])  16.6 us
    ppermute x12, waiting for transfers between devices, over_heads(): lax.ppermute(value, 'heads', [(i, i ^ step) for i in range(head_devs)])  8.19 us
    pallas_call x1, Pallas kernels, call_first(): pl.pallas_call(functools.partial(first_kernel, len(query_x), len(chunks))...  5.95 us
    ppermute x12, starting transfers between devices, over_heads(): lax.ppermute(value, 'heads', [(i, i ^ step) for i in range(head_devs)])  5.22 us
    unnamed x15, local copies, waits for them, and re-layouts  3.6 us
    pallas_call x1, Pallas kernels, call_last(): pl.pallas_call(functools.partial(last_kernel, len(chunks)), out_shape=jax...  3.38 us
    pallas_call x1, Pallas kernels, call_next(): pl.pallas_call(functools.partial(next_kernel, len(chunks)), out_shape=sta...  2.77 us
  transfers between devices with their start and end apart: 29, of which 13 were waited for; matrix products, arithmetic and copies ran while one was open for 1% of the time, Pallas kernels for 12%

profile of v2, /device:TPU:0, one launch (start us, length us, event | category | flops | bytes accessed | tf_op | source)
XLA Modules:
  0.0 75.0 jit_solution(4304811217666885231)
XLA Ops:
  0.0 1.1 %dynamic-slice_bitcast_fusion = (bf16[32,1024]{1,0:T(8,128)(2,1)S(1)}, bf16[32,1024]{1,0:T(8,128)(2,1)S(1)}, bf16[32,1024]{1,0:T(8,128)(2,1)S(1)}, bf16[32,1024]...) fusion(bf16[8,32,1024]{2,1,0:T(8,128)(2,1)} %param.6, ...), kind=kLoop, calls=%fused_computation.10 | loop fusion | bytes 1048608 | tf_op jit(solution)/shard_map/jit(dynamic_index_in_dim)/squeeze | solution.py:257
  1.1 3.1 %collective-permute-start.3 = (bf16[32,1024]{1,0:T(8,128)(2,1)S(1)}, bf16[32,1024]{1,0:T(8,128)(2,1)S(1)}, u32[]{:S(2)}, u32[]{:S(2)}) collective-permute-start(bf16[32,1024]{1,0:T(8,128)(2,1)S(1)} %get-tuple-element.27), channel_id=1, source_target_pairs={{0,1},{1,0},{2,3},{3,2},{4,5},{5,4},{6,7},{7,6},{8,9},{9,8},{10,11... | collective-permute-start | bytes 196616 | tf_op jit(solution)/shard_map/ppermute | solution.py:247
  4.2 1.6 %collective-permute-start.4 = (bf16[32,1024]{1,0:T(8,128)(2,1)S(1)}, bf16[32,1024]{1,0:T(8,128)(2,1)S(1)}, u32[]{:S(2)}, u32[]{:S(2)}) collective-permute-start(bf16[32,1024]{1,0:T(8,128)(2,1)S(1)} %get-tuple-element.26), channel_id=1, source_target_pairs={{0,2},{1,3},{2,0},{3,1},{4,6},{5,7},{6,4},{7,5},{8,10},{9,11},{10,... | collective-permute-start | bytes 196616 | tf_op jit(solution)/shard_map/ppermute | solution.py:247
  5.8 0.0 collective-permute-start.5
  5.8 3.0 %collective-permute-start.6 = (bf16[32,1024]{1,0:T(8,128)(2,1)S(1)}, bf16[32,1024]{1,0:T(8,128)(2,1)S(1)}, u32[]{:S(2)}, u32[]{:S(2)}) collective-permute-start(bf16[32,1024]{1,0:T(8,128)(2,1)S(1)} %get-tuple-element.24), channel_id=1, source_target_pairs={{0,4},{1,5},{2,6},{3,7},{4,0},{5,1},{6,2},{7,3},{8,12},{9,13},{10,... | collective-permute-start | bytes 196616 | tf_op jit(solution)/shard_map/ppermute | solution.py:247
  8.8 1.3 %collective-permute-start.7 = (bf16[32,1024]{1,0:T(8,128)(2,1)S(1)}, bf16[32,1024]{1,0:T(8,128)(2,1)S(1)}, u32[]{:S(2)}, u32[]{:S(2)}) collective-permute-start(bf16[32,1024]{1,0:T(8,128)(2,1)S(1)} %get-tuple-element.23), channel_id=1, source_target_pairs={{0,5},{1,4},{2,7},{3,6},{4,1},{5,0},{6,3},{7,2},{8,13},{9,12},{10,... | collective-permute-start | bytes 196616 | tf_op jit(solution)/shard_map/ppermute | solution.py:247
  10.1 0.0 collective-permute-done.3
  10.1 3.6 %collective-permute-start.8 = (bf16[32,1024]{1,0:T(8,128)(2,1)S(1)}, bf16[32,1024]{1,0:T(8,128)(2,1)S(1)}, u32[]{:S(2)}, u32[]{:S(2)}) collective-permute-start(bf16[32,1024]{1,0:T(8,128)(2,1)S(1)} %get-tuple-element.29), channel_id=1, source_target_pairs={{0,6},{1,7},{2,4},{3,5},{4,2},{5,3},{6,0},{7,1},{8,14},{9,15},{10,... | collective-permute-start | bytes 196616 | tf_op jit(solution)/shard_map/ppermute | solution.py:247
  13.7 0.0 collective-permute-done.4
  13.7 0.0 collective-permute-start.9
  13.7 0.0 collective-permute-done.5
  13.7 1.7 %collective-permute-start = (s32[1,32]{1,0:T(1,128)}, s32[1,32]{1,0:T(1,128)S(1)}, u32[]{:S(2)}, u32[]{:S(2)}) collective-permute-start(s32[1,32]{1,0:T(1,128)} %bitcast.39), channel_id=1, source_target_pairs={{0,1},{1,0},{2,3},{3,2},{4,5},{5,4},{6,7},{7,6},{8,9},{9,8},{10,11... | collective-permute-start | bytes 392 | tf_op jit(solution)/shard_map/ppermute | solution.py:247
  15.4 0.0 collective-permute-done.6
  15.4 0.1 collective-permute-start.10
  15.5 3.5 %collective-permute-done.7 = bf16[32,1024]{1,0:T(8,128)(2,1)S(1)} collective-permute-done((bf16[32,1024]{1,0:T(8,128)(2,1)S(1)}, bf16[32,1024]{1,0:T(8,128)(2,1)S(1)}, u32[]{:S(2)}, u32[]{:S(2)}) %collective-permute-start.7) | collective-permute-done | bytes 65568 | tf_op jit(solution)/shard_map/ppermute | solution.py:247
  19.0 1.5 %collective-permute-start.14 = (bf16[128,1024]{1,0:T(8,128)(2,1)S(1)}, bf16[128,1024]{1,0:T(8,128)(2,1)S(1)}, u32[]{:S(2)}, u32[]{:S(2)}) collective-permute-start(bf16[128,1024]{1,0:T(8,128)(2,1)S(1)} %pad_maximum_fusion.refs_0_.refs_2_), channel_id=1, source_target_pairs={{0,16},{8,24},{16,0},{24,8},{1,17},{9,25},{17,1},{25,9},{2,18},{10... | collective-permute-start | bytes 786440 | tf_op jit(solution)/shard_map/ppermute | solution.py:250
  20.5 0.0 collective-permute-done.8
  20.5 0.2 collective-permute-done.9
  20.8 0.0 collective-permute-start.11
  20.8 1.6 %collective-permute-start.18 = (bf16[128,1024]{1,0:T(8,128)(2,1)S(1)}, bf16[128,1024]{1,0:T(8,128)(2,1)S(1)}, u32[]{:S(2)}, u32[]{:S(2)}) collective-permute-start(bf16[128,1024]{1,0:T(8,128)(2,1)S(1)} %constant_dynamic-update-slice_fusion.refs_1_.refs_4_), channel_id=1, source_target_pairs={{0,16},{8,24},{16,0},{24,8},{1,17},{9,25},{17,1},{25,9},{2,18},{10... | collective-permute-start | bytes 786440 | tf_op jit(solution)/shard_map/ppermute | solution.py:250
  22.3 0.1 pad_add_fusion.1
  22.4 1.6 %collective-permute-start.1 = (s32[1,64]{1,0:T(1,128)S(1)}, s32[1,64]{1,0:T(1,128)S(1)}, u32[]{:S(2)}, u32[]{:S(2)}) collective-permute-start(s32[1,64]{1,0:T(1,128)S(1)} %pad_add_fusion.1), channel_id=1, source_target_pairs={{0,2},{1,3},{2,0},{3,1},{4,6},{5,7},{6,4},{7,5},{8,10},{9,11},{10,... | collective-permute-start | bytes 776 | tf_op jit(solution)/shard_map/ppermute | solution.py:247
  24.1 1.9 %collective-permute-done.1 = s32[1,64]{1,0:T(1,128)S(1)} collective-permute-done((s32[1,64]{1,0:T(1,128)S(1)}, s32[1,64]{1,0:T(1,128)S(1)}, u32[]{:S(2)}, u32[]{:S(2)}) %collective-permute-start.1) | collective-permute-done | bytes 288 | tf_op jit(solution)/shard_map/ppermute | solution.py:247
  26.0 0.1 pad_add_fusion.2.refs_6_
  26.0 2.7 %collective-permute-start.2 = (s32[1,128]{1,0:T(1,128)S(1)}, s32[1,128]{1,0:T(1,128)S(1)}, u32[]{:S(2)}, u32[]{:S(2)}) collective-permute-start(s32[1,128]{1,0:T(1,128)S(1)} %pad_add_fusion.2.refs_6_), channel_id=1, source_target_pairs={{0,4},{1,5},{2,6},{3,7},{4,0},{5,1},{6,2},{7,3},{8,12},{9,13},{10,... | collective-permute-start | bytes 1544 | tf_op jit(solution)/shard_map/ppermute | solution.py:247
  28.8 1.7 %collective-permute-done.2.refs_8_ = s32[1,128]{1,0:T(1,128)S(1)} collective-permute-done((s32[1,128]{1,0:T(1,128)S(1)}, s32[1,128]{1,0:T(1,128)S(1)}, u32[]{:S(2)}, u32[]{:S(2)}) %collective-permute-start.2) | collective-permute-done | bytes 544 | tf_op jit(solution)/shard_map/ppermute | solution.py:247
  30.5 0.0 collective-permute-start.12
  30.5 1.1 %collective-permute-done.12.refs_7_ = s32[1,128]{1,0:T(1,128)S(1)} collective-permute-done((s32[1,128]{1,0:T(1,128)S(1)}, s32[1,128]{1,0:T(1,128)S(1)}, u32[]{:S(2)}, u32[]{:S(2)}) %collective-permute-start.12) | collective-permute-done | bytes 544 | tf_op jit(solution)/shard_map/ppermute | solution.py:250
  31.6 0.5 collective-permute-start.16
  32.1 3.0 %collective-permute-done.16.refs_2_ = s32[1,128]{1,0:T(1,128)S(1)} collective-permute-done((s32[1,128]{1,0:T(1,128)S(1)}, s32[1,128]{1,0:T(1,128)S(1)}, u32[]{:S(2)}, u32[]{:S(2)}) %collective-permute-start.16) | collective-permute-done | bytes 544 | tf_op jit(solution)/shard_map/ppermute | solution.py:250
  35.1 0.0 collective-permute-start.13
  35.1 1.1 %collective-permute-done.13.refs_9_ = s32[1,128]{1,0:T(1,128)S(1)} collective-permute-done((s32[1,128]{1,0:T(1,128)S(1)}, s32[1,128]{1,0:T(1,128)S(1)}, u32[]{:S(2)}, u32[]{:S(2)}) %collective-permute-start.13) | collective-permute-done | bytes 544 | tf_op jit(solution)/shard_map/ppermute | solution.py:250
  36.3 0.5 collective-permute-start.20
  36.8 0.1 pad_add_fusion.tq_ref
  36.9 2.9 %collective-permute-done.20.refs_2_ = s32[1,128]{1,0:T(1,128)S(1)} collective-permute-done((s32[1,128]{1,0:T(1,128)S(1)}, s32[1,128]{1,0:T(1,128)S(1)}, u32[]{:S(2)}, u32[]{:S(2)}) %collective-permute-start.20) | collective-permute-done | bytes 544 | tf_op jit(solution)/shard_map/ppermute | solution.py:250
  39.8 0.0 collective-permute-start.17
  39.8 0.5 collective-permute-start.21
  40.3 0.1 collective-permute-start.15
  40.4 0.0 collective-permute-done.18.refs_0_
  40.4 0.4 collective-permute-start.19
  40.8 0.0 copy-start
  40.9 2.8 %copy-done = bf16[1024,3072]{1,0:T(8,128)(2,1)S(1)} copy-done((bf16[1024,3072]{1,0:T(8,128)(2,1)S(1)}, bf16[1024,3072]{1,0:T(8,128)(2,1)}, u32[]{:S(2)}) %copy-start) | copy-done | bytes 6291480
  43.6 6.0 %attend_first.1 = (bf16[256,1024]{1,0:T(8,128)(2,1)S(1)}, f32[16,72,256]{2,1,0:T(8,128)S(1)}, f32[16,256]{1,0:T(8,128)S(1)}) custom-call(s32[1,256]{1,0:T(1,128)S(1)} %pad_add_fusion.tq_ref, f32[1,1024]{1,0:T(1,128)S(1)} %bitcast.36, s32[256,256]{1,0:T(8,128)S(1)} %copy-done.2, bf16[1024,3072]{1,0:T(8,128)(2,1)S(1)} %copy-done, ...), custom_call_target="tpu_custom_call" | custom-call | flops 3758096384 | bytes 8388608 | tf_op jit(solution)/shard_map/attend_first/pallas_call | solution.py:189
  49.6 0.0 collective-permute-done.17.refs_3_
  49.6 0.0 copy-start.1
  49.6 2.8 %attend_next.1 = (f32[16,72,256]{2,1,0:T(8,128)S(1)}, f32[16,256]{1,0:T(8,128)S(1)}) custom-call(bf16[256,1024]{1,0:T(8,128)(2,1)S(1)} %get-tuple-element.10.query_ref, f32[16,72,256]{2,1,0:T(8,128)S(1)} %get-tuple-element.11.acc_in, f32[16,256]{1,0:T(8,128)S(1)} %get-tuple-element.12.top_in, s32[1,256]{1,0:T(1,128)S(1)} %pad_add_fusion.tq_ref, ...), custom_call_target="tpu_custom_call" | custom-call | flops 1610612736 | bytes 8388608 | tf_op jit(solution)/shard_map/attend_next/pallas_call | solution.py:205
  52.4 0.0 collective-permute-done.21.refs_3_
  52.4 3.4 %attend_last.1 = bf16[256,1024]{1,0:T(8,128)(2,1)S(1)} custom-call(bf16[256,1024]{1,0:T(8,128)(2,1)S(1)} %get-tuple-element.10.query_ref, f32[16,72,256]{2,1,0:T(8,128)S(1)} %get-tuple-element.13.acc_in, f32[16,256]{1,0:T(8,128)S(1)} %get-tuple-element.14.top_in, s32[1,256]{1,0:T(1,128)S(1)} %pad_add_fusion.tq_ref, f32[1,1024]{1,0:T(1,128)S(1)} %bitcast.38, ...), custom_call_target="tpu_custom_call" | custom-call | flops 2147483648 | bytes 8388608 | tf_op jit(solution)/shard_map/attend_last/pallas_call | solution.py:221
  55.9 2.8 %collective-permute-start.22 = (bf16[32,1024]{1,0:T(8,128)(2,1)S(1)}, bf16[32,1024]{1,0:T(8,128)(2,1)S(1)}, u32[]{:S(2)}, u32[]{:S(2)}) collective-permute-start(bf16[32,1024]{1,0:T(8,128)(2,1)S(1)} %get-tuple-element.21), channel_id=1, source_target_pairs={{0,4},{1,5},{2,6},{3,7},{4,0},{5,1},{6,2},{7,3},{8,12},{9,13},{10,... | collective-permute-start | bytes 196616 | tf_op jit(solution)/shard_map/ppermute | solution.py:247
  58.7 0.1 collective-permute-start.23
  58.8 2.2 %collective-permute-start.24 = (bf16[32,1024]{1,0:T(8,128)(2,1)S(1)}, bf16[32,1024]{1,0:T(8,128)(2,1)S(1)}, u32[]{:S(2)}, u32[]{:S(2)}) collective-permute-start(bf16[32,1024]{1,0:T(8,128)(2,1)S(1)} %get-tuple-element.19), channel_id=1, source_target_pairs={{0,6},{1,7},{2,4},{3,5},{4,2},{5,3},{6,0},{7,1},{8,14},{9,15},{10,... | collective-permute-start | bytes 196616 | tf_op jit(solution)/shard_map/ppermute | solution.py:247
  61.0 2.6 %collective-permute-start.25 = (bf16[32,1024]{1,0:T(8,128)(2,1)S(1)}, bf16[32,1024]{1,0:T(8,128)(2,1)S(1)}, u32[]{:S(2)}, u32[]{:S(2)}) collective-permute-start(bf16[32,1024]{1,0:T(8,128)(2,1)S(1)} %get-tuple-element.18), channel_id=1, source_target_pairs={{0,7},{1,6},{2,5},{3,4},{4,3},{5,2},{6,1},{7,0},{8,15},{9,14},{10,... | collective-permute-start | bytes 196616 | tf_op jit(solution)/shard_map/ppermute | solution.py:247
  63.6 0.5 collective-permute-start.26
  64.1 2.4 %collective-permute-done.22 = bf16[32,1024]{1,0:T(8,128)(2,1)S(1)} collective-permute-done((bf16[32,1024]{1,0:T(8,128)(2,1)S(1)}, bf16[32,1024]{1,0:T(8,128)(2,1)S(1)}, u32[]{:S(2)}, u32[]{:S(2)}) %collective-permute-start.22) | collective-permute-done | bytes 65568 | tf_op jit(solution)/shard_map/ppermute | solution.py:247
  66.5 0.1 broadcast_in_dim.26
  66.6 1.8 %collective-permute-done.23 = bf16[32,1024]{1,0:T(8,128)(2,1)S(1)} collective-permute-done((bf16[32,1024]{1,0:T(8,128)(2,1)S(1)}, bf16[32,1024]{1,0:T(8,128)(2,1)S(1)}, u32[]{:S(2)}, u32[]{:S(2)}) %collective-permute-start.23) | collective-permute-done | bytes 65568 | tf_op jit(solution)/shard_map/ppermute | solution.py:247
  68.4 0.0 collective-permute-done.24
  68.4 0.0 collective-permute-done.25
  68.5 0.5 collective-permute-done.26
  69.0 2.1 %collective-permute-done.27 = bf16[32,1024]{1,0:T(8,128)(2,1)S(1)} collective-permute-done((bf16[32,1024]{1,0:T(8,128)(2,1)S(1)}, bf16[32,1024]{1,0:T(8,128)(2,1)S(1)}, u32[]{:S(2)}, u32[]{:S(2)}) %collective-permute-start.27) | collective-permute-done | bytes 65568 | tf_op jit(solution)/shard_map/ppermute | solution.py:247
  71.0 2.5 %collective-permute-done.28 = bf16[32,1024]{1,0:T(8,128)(2,1)S(1)} collective-permute-done((bf16[32,1024]{1,0:T(8,128)(2,1)S(1)}, bf16[32,1024]{1,0:T(8,128)(2,1)S(1)}, u32[]{:S(2)}, u32[]{:S(2)}) %collective-permute-start.28) | collective-permute-done | bytes 65568 | tf_op jit(solution)/shard_map/ppermute | solution.py:247
  73.6 0.0 copy-start.4
  73.6 0.8 %copy-done.4 = bf16[8,32,1024]{2,1,0:T(8,128)(2,1)} copy-done((bf16[8,32,1024]{2,1,0:T(8,128)(2,1)}, bf16[8,32,1024]{2,1,0:T(8,128)(2,1)S(1)}, u32[]{:S(2)}) %copy-start.4) | copy-done | bytes 524312
  74.4 0.6 fusion
  (28 shorter events, 0.2 us)
Async XLA Ops:
  0.0 22.3 %copy-start.5 = (s32[32]{0:T(128)S(1)}, s32[32]{0:T(128)}, u32[]{:S(2)}) copy-start(s32[32]{0:T(128)} %param.10) | copy-start | bytes 388
  0.0 40.8 %copy-start.3 = (f32[1024]{0:T(1024)S(1)}, f32[1024]{0:T(1024)}, u32[]{:S(2)}) copy-start(f32[1024]{0:T(1024)} %param.7) | copy-start | bytes 12292
  0.0 40.8 %copy-start.2 = (s32[256,256]{1,0:T(8,128)S(1)}, s32[256,256]{1,0:T(8,128)}, u32[]{:S(2)}) copy-start(s32[256,256]{1,0:T(8,128)} %adj_ref.5) | copy-start | bytes 786436
  1.1 8.9 %collective-permute-start.3 = (bf16[32,1024]{1,0:T(8,128)(2,1)S(1)}, bf16[32,1024]{1,0:T(8,128)(2,1)S(1)}, u32[]{:S(2)}, u32[]{:S(2)}) collective-permute-start(bf16[32,1024]{1,0:T(8,128)(2,1)S(1)} %get-tuple-element.27), channel_id=1, source_target_pairs={{0,1},{1,0},{2,3},{3,2},{4,5},{5,4},{6,7},{7,6},{8,9},{9,8},{10,11... | collective-permute-start | bytes 196616 | tf_op jit(solution)/shard_map/ppermute | solution.py:247
  4.2 9.5 %collective-permute-start.4 = (bf16[32,1024]{1,0:T(8,128)(2,1)S(1)}, bf16[32,1024]{1,0:T(8,128)(2,1)S(1)}, u32[]{:S(2)}, u32[]{:S(2)}) collective-permute-start(bf16[32,1024]{1,0:T(8,128)(2,1)S(1)} %get-tuple-element.26), channel_id=1, source_target_pairs={{0,2},{1,3},{2,0},{3,1},{4,6},{5,7},{6,4},{7,5},{8,10},{9,11},{10,... | collective-permute-start | bytes 196616 | tf_op jit(solution)/shard_map/ppermute | solution.py:247
  5.8 7.9 %collective-permute-start.5 = (bf16[32,1024]{1,0:T(8,128)(2,1)S(1)}, bf16[32,1024]{1,0:T(8,128)(2,1)S(1)}, u32[]{:S(2)}, u32[]{:S(2)}) collective-permute-start(bf16[32,1024]{1,0:T(8,128)(2,1)S(1)} %get-tuple-element.25), channel_id=1, source_target_pairs={{0,3},{1,2},{2,1},{3,0},{4,7},{5,6},{6,5},{7,4},{8,11},{9,10},{10,... | collective-permute-start | bytes 196616 | tf_op jit(solution)/shard_map/ppermute | solution.py:247
  5.8 9.6 %collective-permute-start.6 = (bf16[32,1024]{1,0:T(8,128)(2,1)S(1)}, bf16[32,1024]{1,0:T(8,128)(2,1)S(1)}, u32[]{:S(2)}, u32[]{:S(2)}) collective-permute-start(bf16[32,1024]{1,0:T(8,128)(2,1)S(1)} %get-tuple-element.24), channel_id=1, source_target_pairs={{0,4},{1,5},{2,6},{3,7},{4,0},{5,1},{6,2},{7,3},{8,12},{9,13},{10,... | collective-permute-start | bytes 196616 | tf_op jit(solution)/shard_map/ppermute | solution.py:247
  8.8 10.2 %collective-permute-start.7 = (bf16[32,1024]{1,0:T(8,128)(2,1)S(1)}, bf16[32,1024]{1,0:T(8,128)(2,1)S(1)}, u32[]{:S(2)}, u32[]{:S(2)}) collective-permute-start(bf16[32,1024]{1,0:T(8,128)(2,1)S(1)} %get-tuple-element.23), channel_id=1, source_target_pairs={{0,5},{1,4},{2,7},{3,6},{4,1},{5,0},{6,3},{7,2},{8,13},{9,12},{10,... | collective-permute-start | bytes 196616 | tf_op jit(solution)/shard_map/ppermute | solution.py:247
  10.1 10.4 %collective-permute-start.8 = (bf16[32,1024]{1,0:T(8,128)(2,1)S(1)}, bf16[32,1024]{1,0:T(8,128)(2,1)S(1)}, u32[]{:S(2)}, u32[]{:S(2)}) collective-permute-start(bf16[32,1024]{1,0:T(8,128)(2,1)S(1)} %get-tuple-element.29), channel_id=1, source_target_pairs={{0,6},{1,7},{2,4},{3,5},{4,2},{5,3},{6,0},{7,1},{8,14},{9,15},{10,... | collective-permute-start | bytes 196616 | tf_op jit(solution)/shard_map/ppermute | solution.py:247
  13.7 7.1 %collective-permute-start.9 = (bf16[32,1024]{1,0:T(8,128)(2,1)S(1)}, bf16[32,1024]{1,0:T(8,128)(2,1)S(1)}, u32[]{:S(2)}, u32[]{:S(2)}) collective-permute-start(bf16[32,1024]{1,0:T(8,128)(2,1)S(1)} %get-tuple-element.22), channel_id=1, source_target_pairs={{0,7},{1,6},{2,5},{3,4},{4,3},{5,2},{6,1},{7,0},{8,15},{9,14},{10,... | collective-permute-start | bytes 196616 | tf_op jit(solution)/shard_map/ppermute | solution.py:247
  13.7 8.6 %collective-permute-start = (s32[1,32]{1,0:T(1,128)}, s32[1,32]{1,0:T(1,128)S(1)}, u32[]{:S(2)}, u32[]{:S(2)}) collective-permute-start(s32[1,32]{1,0:T(1,128)} %bitcast.39), channel_id=1, source_target_pairs={{0,1},{1,0},{2,3},{3,2},{4,5},{5,4},{6,7},{7,6},{8,9},{9,8},{10,11... | collective-permute-start | bytes 392 | tf_op jit(solution)/shard_map/ppermute | solution.py:247
  15.4 25.4 %collective-permute-start.10 = (bf16[128,1024]{1,0:T(8,128)(2,1)S(1)}, bf16[128,1024]{1,0:T(8,128)(2,1)S(1)}, u32[]{:S(2)}, u32[]{:S(2)}) collective-permute-start(bf16[128,1024]{1,0:T(8,128)(2,1)S(1)} %pad_maximum_fusion.refs_0_.refs_2_), channel_id=1, source_target_pairs={{0,8},{8,0},{16,24},{24,16},{1,9},{9,1},{17,25},{25,17},{2,10},{10... | collective-permute-start | bytes 786440 | tf_op jit(solution)/shard_map/ppermute | solution.py:250
  19.0 21.3 %collective-permute-start.14 = (bf16[128,1024]{1,0:T(8,128)(2,1)S(1)}, bf16[128,1024]{1,0:T(8,128)(2,1)S(1)}, u32[]{:S(2)}, u32[]{:S(2)}) collective-permute-start(bf16[128,1024]{1,0:T(8,128)(2,1)S(1)} %pad_maximum_fusion.refs_0_.refs_2_), channel_id=1, source_target_pairs={{0,16},{8,24},{16,0},{24,8},{1,17},{9,25},{17,1},{25,9},{2,18},{10... | collective-permute-start | bytes 786440 | tf_op jit(solution)/shard_map/ppermute | solution.py:250
  20.8 19.0 %collective-permute-start.11 = (bf16[128,1024]{1,0:T(8,128)(2,1)S(1)}, bf16[128,1024]{1,0:T(8,128)(2,1)S(1)}, u32[]{:S(2)}, u32[]{:S(2)}) collective-permute-start(bf16[128,1024]{1,0:T(8,128)(2,1)S(1)} %constant_dynamic-update-slice_fusion.refs_1_.refs_4_), channel_id=1, source_target_pairs={{0,8},{8,0},{16,24},{24,16},{1,9},{9,1},{17,25},{25,17},{2,10},{10... | collective-permute-start | bytes 786440 | tf_op jit(solution)/shard_map/ppermute | solution.py:250
  20.8 19.6 %collective-permute-start.18 = (bf16[128,1024]{1,0:T(8,128)(2,1)S(1)}, bf16[128,1024]{1,0:T(8,128)(2,1)S(1)}, u32[]{:S(2)}, u32[]{:S(2)}) collective-permute-start(bf16[128,1024]{1,0:T(8,128)(2,1)S(1)} %constant_dynamic-update-slice_fusion.refs_1_.refs_4_), channel_id=1, source_target_pairs={{0,16},{8,24},{16,0},{24,8},{1,17},{9,25},{17,1},{25,9},{2,18},{10... | collective-permute-start | bytes 786440 | tf_op jit(solution)/shard_map/ppermute | solution.py:250
  22.4 3.5 %collective-permute-start.1 = (s32[1,64]{1,0:T(1,128)S(1)}, s32[1,64]{1,0:T(1,128)S(1)}, u32[]{:S(2)}, u32[]{:S(2)}) collective-permute-start(s32[1,64]{1,0:T(1,128)S(1)} %pad_add_fusion.1), channel_id=1, source_target_pairs={{0,2},{1,3},{2,0},{3,1},{4,6},{5,7},{6,4},{7,5},{8,10},{9,11},{10,... | collective-permute-start | bytes 776 | tf_op jit(solution)/shard_map/ppermute | solution.py:247
  26.0 4.4 %collective-permute-start.2 = (s32[1,128]{1,0:T(1,128)S(1)}, s32[1,128]{1,0:T(1,128)S(1)}, u32[]{:S(2)}, u32[]{:S(2)}) collective-permute-start(s32[1,128]{1,0:T(1,128)S(1)} %pad_add_fusion.2.refs_6_), channel_id=1, source_target_pairs={{0,4},{1,5},{2,6},{3,7},{4,0},{5,1},{6,2},{7,3},{8,12},{9,13},{10,... | collective-permute-start | bytes 1544 | tf_op jit(solution)/shard_map/ppermute | solution.py:247
  30.5 1.1 %collective-permute-start.12 = (s32[1,128]{1,0:T(1,128)S(1)}, s32[1,128]{1,0:T(1,128)S(1)}, u32[]{:S(2)}, u32[]{:S(2)}) collective-permute-start(s32[1,128]{1,0:T(1,128)S(1)} %pad_add_fusion.2.refs_6_), channel_id=1, source_target_pairs={{0,8},{8,0},{16,24},{24,16},{1,9},{9,1},{17,25},{25,17},{2,10},{10... | collective-permute-start | bytes 1544 | tf_op jit(solution)/shard_map/ppermute | solution.py:250
  31.6 3.5 %collective-permute-start.16 = (s32[1,128]{1,0:T(1,128)S(1)}, s32[1,128]{1,0:T(1,128)S(1)}, u32[]{:S(2)}, u32[]{:S(2)}) collective-permute-start(s32[1,128]{1,0:T(1,128)S(1)} %pad_add_fusion.2.refs_6_), channel_id=1, source_target_pairs={{0,16},{8,24},{16,0},{24,8},{1,17},{9,25},{17,1},{25,9},{2,18},{10... | collective-permute-start | bytes 1544 | tf_op jit(solution)/shard_map/ppermute | solution.py:250
  35.1 1.1 %collective-permute-start.13 = (s32[1,128]{1,0:T(1,128)S(1)}, s32[1,128]{1,0:T(1,128)S(1)}, u32[]{:S(2)}, u32[]{:S(2)}) collective-permute-start(s32[1,128]{1,0:T(1,128)S(1)} %collective-permute-done.2.refs_8_), channel_id=1, source_target_pairs={{0,8},{8,0},{16,24},{24,16},{1,9},{9,1},{17,25},{25,17},{2,10},{10... | collective-permute-start | bytes 1544 | tf_op jit(solution)/shard_map/ppermute | solution.py:250
  36.3 3.5 %collective-permute-start.20 = (s32[1,128]{1,0:T(1,128)S(1)}, s32[1,128]{1,0:T(1,128)S(1)}, u32[]{:S(2)}, u32[]{:S(2)}) collective-permute-start(s32[1,128]{1,0:T(1,128)S(1)} %collective-permute-done.2.refs_8_), channel_id=1, source_target_pairs={{0,16},{8,24},{16,0},{24,8},{1,17},{9,25},{17,1},{25,9},{2,18},{10... | collective-permute-start | bytes 1544 | tf_op jit(solution)/shard_map/ppermute | solution.py:250
  39.8 9.8 %collective-permute-start.17 = (s32[1,128]{1,0:T(1,128)S(1)}, s32[1,128]{1,0:T(1,128)S(1)}, u32[]{:S(2)}, u32[]{:S(2)}) collective-permute-start(s32[1,128]{1,0:T(1,128)S(1)} %collective-permute-done.16.refs_2_), channel_id=1, source_target_pairs={{0,8},{8,0},{16,24},{24,16},{1,9},{9,1},{17,25},{25,17},{2,10},{10... | collective-permute-start | bytes 1544 | tf_op jit(solution)/shard_map/ppermute | solution.py:250
  39.8 12.6 %collective-permute-start.21 = (s32[1,128]{1,0:T(1,128)S(1)}, s32[1,128]{1,0:T(1,128)S(1)}, u32[]{:S(2)}, u32[]{:S(2)}) collective-permute-start(s32[1,128]{1,0:T(1,128)S(1)} %collective-permute-done.20.refs_2_), channel_id=1, source_target_pairs={{0,8},{8,0},{16,24},{24,16},{1,9},{9,1},{17,25},{25,17},{2,10},{10... | collective-permute-start | bytes 1544 | tf_op jit(solution)/shard_map/ppermute | solution.py:250
  40.3 9.3 %collective-permute-start.15 = (bf16[128,1024]{1,0:T(8,128)(2,1)S(1)}, bf16[128,1024]{1,0:T(8,128)(2,1)S(1)}, u32[]{:S(2)}, u32[]{:S(2)}) collective-permute-start(bf16[128,1024]{1,0:T(8,128)(2,1)S(1)} %collective-permute-done.14.refs_0_), channel_id=1, source_target_pairs={{0,8},{8,0},{16,24},{24,16},{1,9},{9,1},{17,25},{25,17},{2,10},{10... | collective-permute-start | bytes 786440 | tf_op jit(solution)/shard_map/ppermute | solution.py:250
  40.4 12.0 %collective-permute-start.19 = (bf16[128,1024]{1,0:T(8,128)(2,1)S(1)}, bf16[128,1024]{1,0:T(8,128)(2,1)S(1)}, u32[]{:S(2)}, u32[]{:S(2)}) collective-permute-start(bf16[128,1024]{1,0:T(8,128)(2,1)S(1)} %collective-permute-done.18.refs_0_), channel_id=1, source_target_pairs={{0,8},{8,0},{16,24},{24,16},{1,9},{9,1},{17,25},{25,17},{2,10},{10... | collective-permute-start | bytes 786440 | tf_op jit(solution)/shard_map/ppermute | solution.py:250
  40.8 2.8 %copy-start = (bf16[1024,3072]{1,0:T(8,128)(2,1)S(1)}, bf16[1024,3072]{1,0:T(8,128)(2,1)}, u32[]{:S(2)}) copy-start(bf16[1024,3072]{1,0:T(8,128)(2,1)} %w_ref.5) | copy-start | bytes 18874372
  49.6 2.8 %copy-start.1 = (bf16[1024,1024]{1,0:T(8,128)(2,1)S(1)}, bf16[1024,1024]{1,0:T(8,128)(2,1)}, u32[]{:S(2)}) copy-start(bf16[1024,1024]{1,0:T(8,128)(2,1)} %wo_ref.1) | copy-start | bytes 6291460
  55.9 10.7 %collective-permute-start.22 = (bf16[32,1024]{1,0:T(8,128)(2,1)S(1)}, bf16[32,1024]{1,0:T(8,128)(2,1)S(1)}, u32[]{:S(2)}, u32[]{:S(2)}) collective-permute-start(bf16[32,1024]{1,0:T(8,128)(2,1)S(1)} %get-tuple-element.21), channel_id=1, source_target_pairs={{0,4},{1,5},{2,6},{3,7},{4,0},{5,1},{6,2},{7,3},{8,12},{9,13},{10,... | collective-permute-start | bytes 196616 | tf_op jit(solution)/shard_map/ppermute | solution.py:247
  58.7 9.7 %collective-permute-start.23 = (bf16[32,1024]{1,0:T(8,128)(2,1)S(1)}, bf16[32,1024]{1,0:T(8,128)(2,1)S(1)}, u32[]{:S(2)}, u32[]{:S(2)}) collective-permute-start(bf16[32,1024]{1,0:T(8,128)(2,1)S(1)} %get-tuple-element.20), channel_id=1, source_target_pairs={{0,5},{1,4},{2,7},{3,6},{4,1},{5,0},{6,3},{7,2},{8,13},{9,12},{10,... | collective-permute-start | bytes 196616 | tf_op jit(solution)/shard_map/ppermute | solution.py:247
  58.8 9.6 %collective-permute-start.24 = (bf16[32,1024]{1,0:T(8,128)(2,1)S(1)}, bf16[32,1024]{1,0:T(8,128)(2,1)S(1)}, u32[]{:S(2)}, u32[]{:S(2)}) collective-permute-start(bf16[32,1024]{1,0:T(8,128)(2,1)S(1)} %get-tuple-element.19), channel_id=1, source_target_pairs={{0,6},{1,7},{2,4},{3,5},{4,2},{5,3},{6,0},{7,1},{8,14},{9,15},{10,... | collective-permute-start | bytes 196616 | tf_op jit(solution)/shard_map/ppermute | solution.py:247
  61.0 7.4 %collective-permute-start.25 = (bf16[32,1024]{1,0:T(8,128)(2,1)S(1)}, bf16[32,1024]{1,0:T(8,128)(2,1)S(1)}, u32[]{:S(2)}, u32[]{:S(2)}) collective-permute-start(bf16[32,1024]{1,0:T(8,128)(2,1)S(1)} %get-tuple-element.18), channel_id=1, source_target_pairs={{0,7},{1,6},{2,5},{3,4},{4,3},{5,2},{6,1},{7,0},{8,15},{9,14},{10,... | collective-permute-start | bytes 196616 | tf_op jit(solution)/shard_map/ppermute | solution.py:247
  63.6 5.4 %collective-permute-start.26 = (bf16[32,1024]{1,0:T(8,128)(2,1)S(1)}, bf16[32,1024]{1,0:T(8,128)(2,1)S(1)}, u32[]{:S(2)}, u32[]{:S(2)}) collective-permute-start(bf16[32,1024]{1,0:T(8,128)(2,1)S(1)} %get-tuple-element.17), channel_id=1, source_target_pairs={{0,1},{1,0},{2,3},{3,2},{4,5},{5,4},{6,7},{7,6},{8,9},{9,8},{10,11... | collective-permute-start | bytes 196616 | tf_op jit(solution)/shard_map/ppermute | solution.py:247
  66.5 4.5 %collective-permute-start.27 = (bf16[32,1024]{1,0:T(8,128)(2,1)S(1)}, bf16[32,1024]{1,0:T(8,128)(2,1)S(1)}, u32[]{:S(2)}, u32[]{:S(2)}) collective-permute-start(bf16[32,1024]{1,0:T(8,128)(2,1)S(1)} %get-tuple-element.16), channel_id=1, source_target_pairs={{0,2},{1,3},{2,0},{3,1},{4,6},{5,7},{6,4},{7,5},{8,10},{9,11},{10,... | collective-permute-start | bytes 196616 | tf_op jit(solution)/shard_map/ppermute | solution.py:247
  68.4 5.2 %collective-permute-start.28 = (bf16[32,1024]{1,0:T(8,128)(2,1)S(1)}, bf16[32,1024]{1,0:T(8,128)(2,1)S(1)}, u32[]{:S(2)}, u32[]{:S(2)}) collective-permute-start(bf16[32,1024]{1,0:T(8,128)(2,1)S(1)} %get-tuple-element.15), channel_id=1, source_target_pairs={{0,3},{1,2},{2,1},{3,0},{4,7},{5,6},{6,5},{7,4},{8,11},{9,10},{10,... | collective-permute-start | bytes 196616 | tf_op jit(solution)/shard_map/ppermute | solution.py:247
  73.6 0.8 %copy-start.4 = (bf16[8,32,1024]{2,1,0:T(8,128)(2,1)}, bf16[8,32,1024]{2,1,0:T(8,128)(2,1)S(1)}, u32[]{:S(2)}) copy-start(bf16[8,32,1024]{2,1,0:T(8,128)(2,1)S(1)} %bitcast_dynamic-update-slice_fusion) | copy-start | bytes 1572868

commit v3 on v2

v3 whole, which is shorter than its diff:
```python
import functools
import math

import jax
import jax.numpy as jnp
from jax import lax
from jax.experimental import pallas as pl
from jax.experimental.pallas import tpu as pltpu
from jax.sharding import PartitionSpec as P

HEAD_DIM = 64
PAIR = 2 * HEAD_DIM
VAL_ROWS = HEAD_DIM + 16
ACC_ROWS = HEAD_DIM + 8
MASKED = -1e30
SCALE = 0.125 * math.log2(math.e)
BLOCK = 256
COLS = 256
TAG = 128


def normalise(rows, gain):
    x32 = rows.astype(jnp.float32)
    mean = jnp.mean(x32 * x32, axis=-1, keepdims=True)
    return (x32 * lax.rsqrt(mean + 1e-05) * gain).astype(jnp.bfloat16)


def dot(a, b, a_dim=1, b_dim=0):
    return lax.dot_general(
        a, b, (((a_dim,), (b_dim,)), ((), ())), preferred_element_type=jnp.float32
    )


def one_hot(pieces, width, count):
    tags = jnp.concatenate([piece[:, width:] for piece in pieces], axis=0).astype(jnp.float32)
    lane = lax.broadcasted_iota(jnp.int32, tags.shape, 1).astype(jnp.float32)
    parts = [(tags == lane + start).astype(jnp.float32) for start in range(0, count, TAG)]
    return jnp.concatenate(parts, axis=1).astype(jnp.bfloat16)


def query_rows(adj_ref, pieces, width):
    adjacency = adj_ref[...].astype(jnp.float32).astype(jnp.bfloat16)
    return dot(adjacency, one_hot(pieces, width, adjacency.shape[0]), 1, 1).astype(jnp.bfloat16)


class Work:
    def __init__(self, gain, w_ref, near, query_ref, acc_ref, top_ref, scratch):
        self.gain, self.w_ref, self.near = gain, w_ref, near
        self.query_ref, self.acc_ref, self.top_ref = query_ref, acc_ref, top_ref
        self.norm_ref, self.key_ref, self.val_ref, self.bias_ref, self.weight_ref = scratch
        heads, _, block = self.val_ref.shape
        ones = jnp.ones((heads, VAL_ROWS - HEAD_DIM, block), jnp.bfloat16)
        self.val_ref[:, HEAD_DIM:, :] = ones

    def normal(self, pieces):
        start = 0
        for piece in pieces:
            self.norm_ref[start : start + piece.shape[0], :] = normalise(piece[:, : self.gain.shape[1]], self.gain)
            start += piece.shape[0]
        return self.norm_ref[...]

    def project_queries(self, pieces):
        normed = self.normal(pieces)
        for start in range(0, normed.shape[1], COLS):
            part = dot(normed, self.w_ref[:, start : start + COLS]) * SCALE
            self.query_ref[:, start : start + COLS] = part.astype(jnp.bfloat16)

    def absorb(self, pieces, first):
        normed = self.normal(pieces)
        width = normed.shape[1]
        heads = width // HEAD_DIM
        for start in range(0, width, COLS):
            keys = dot(normed, self.w_ref[:, width + start : width + start + COLS])
            self.key_ref[:, start : start + COLS] = keys.astype(jnp.bfloat16)
        allowed = dot(one_hot(pieces, width, self.near.shape[0]), self.near)
        self.bias_ref[...] = (allowed - 1.0) * -MASKED
        for start in range(0, width, COLS):
            values = dot(normed, self.w_ref[:, 2 * width + start : 2 * width + start + COLS])
            values = values.astype(jnp.bfloat16).T
            for part in range(COLS // HEAD_DIM):
                rows = slice(part * HEAD_DIM, (part + 1) * HEAD_DIM)
                self.val_ref[start // HEAD_DIM + part, :HEAD_DIM, :] = values[rows]
        factors = []
        for head in range(heads):
            pair = slice(head // 2 * PAIR, head // 2 * PAIR + PAIR)
            query = self.query_ref[:, pair]
            lane = lax.broadcasted_iota(jnp.int32, query.shape, 1)
            query = jnp.where((lane // HEAD_DIM) == head % 2, query, jnp.zeros_like(query))
            scores = dot(self.key_ref[:, pair], query, 1, 1) + self.bias_ref[...]
            top = jnp.max(scores, axis=0, keepdims=True)
            if not first:
                before = self.top_ref[head : head + 1, :]
                top = jnp.maximum(top, before)
                factors.append(jnp.exp2(before - top))
            self.weight_ref[head] = jnp.exp2(scores - top).astype(jnp.bfloat16)
            self.top_ref[head : head + 1, :] = top
        for head in range(heads):
            summed = dot(self.val_ref[head], self.weight_ref[head])[:ACC_ROWS]
            if not first:
                summed = summed + self.acc_ref[head] * factors[head]
            self.acc_ref[head] = summed


def blocks_of(chunks, block):
    held = []
    for chunk in chunks:
        step = min(block, chunk.shape[0])
        held += [chunk[start : start + step, :] for start in range(0, chunk.shape[0], step)]
    per = block // held[0].shape[0]
    for start in range(0, len(held), per):
        yield held[start : start + per]


def first_kernel(queries, gain_ref, adj_ref, w_ref, *refs):
    count = len(refs) - 4 - 5
    chunks, rest = refs[:count], refs[count:]
    near_ref, query_ref, acc_ref, top_ref, *scratch = rest
    own = [ref[...] for ref in chunks[:queries]]
    near_ref[...] = query_rows(adj_ref, own, w_ref.shape[0])
    work = Work(gain_ref[...], w_ref, near_ref[...], query_ref, acc_ref, top_ref, scratch)
    work.project_queries(own)
    first = True
    for pieces in blocks_of(chunks[queries:], scratch[0].shape[0]):
        work.absorb(pieces, first)
        first = False


def next_kernel(near_ref, query_ref, acc_in, top_in, gain_ref, w_ref, *refs):
    count = len(refs) - 2 - 5
    chunks, rest = refs[:count], refs[count:]
    acc_ref, top_ref, *scratch = rest
    acc_ref[...] = acc_in[...]
    top_ref[...] = top_in[...]
    work = Work(gain_ref[...], w_ref, near_ref[...], query_ref, acc_ref, top_ref, scratch)
    for pieces in blocks_of(chunks, scratch[0].shape[0]):
        work.absorb(pieces, False)


def last_kernel(near_ref, query_ref, acc_in, top_in, gain_ref, w_ref, wo_ref, *refs):
    count = len(refs) - 4 - 5
    chunks, rest = refs[:count], refs[count:]
    out_ref, acc_ref, top_ref, att_ref, *scratch = rest
    acc_ref[...] = acc_in[...]
    top_ref[...] = top_in[...]
    work = Work(gain_ref[...], w_ref, near_ref[...], query_ref, acc_ref, top_ref, scratch)
    for pieces in blocks_of(chunks, scratch[0].shape[0]):
        work.absorb(pieces, False)
    for head in range(acc_ref.shape[0]):
        total = acc_ref[head, HEAD_DIM : HEAD_DIM + 1, :]
        part = acc_ref[head, :HEAD_DIM, :] / total
        att_ref[head * HEAD_DIM : (head + 1) * HEAD_DIM, :] = part.astype(jnp.bfloat16)
    attended = att_ref[...].T
    for start in range(0, attended.shape[1], COLS):
        out = dot(attended, wo_ref[:, start : start + COLS])
        out_ref[:, start : start + COLS] = out.astype(jnp.bfloat16)


def vmem(count):
    return [pl.BlockSpec(memory_space=pltpu.VMEM)] * count


def scratch(queries, heads):
    return [
        pltpu.VMEM((BLOCK, heads * HEAD_DIM), jnp.bfloat16),
        pltpu.VMEM((BLOCK, heads * HEAD_DIM), jnp.bfloat16),
        pltpu.VMEM((heads, VAL_ROWS, BLOCK), jnp.bfloat16),
        pltpu.VMEM((BLOCK, queries), jnp.float32),
        pltpu.VMEM((heads, BLOCK, queries), jnp.bfloat16),
    ]


def cost(queries, keys, width, more):
    flops = 2 * (2 * keys * width * width + 4 * queries * keys * width + more * queries * width * width)
    return pl.CostEstimate(flops=flops, bytes_accessed=8 * width * width, transcendentals=0)


PARAMS = pltpu.CompilerParams(vmem_limit_bytes=16 * 1024 * 1024)


def state_shapes(heads, queries):
    return (
        jax.ShapeDtypeStruct((heads, ACC_ROWS, queries), jnp.float32),
        jax.ShapeDtypeStruct((heads, queries), jnp.float32),
    )


def fetch_kernel(from_ref, after_ref, to_ref, sem):
    del after_ref
    copy = pltpu.make_async_copy(from_ref, to_ref, sem)
    copy.start()
    copy.wait()


def fetch(weights, after):
    return pl.pallas_call(
        fetch_kernel,
        out_shape=pltpu.VMEM(weights.shape, weights.dtype),
        in_specs=[pl.BlockSpec(memory_space=pltpu.HBM), pl.BlockSpec(memory_space=pl.ANY)],
        out_specs=pl.BlockSpec(memory_space=pl.ANY),
        scratch_shapes=[pltpu.SemaphoreType.DMA],
        compiler_params=pltpu.CompilerParams(vmem_limit_bytes=1024 * 1024),
        cost_estimate=pl.CostEstimate(flops=0, bytes_accessed=2 * weights.size * 2, transcendentals=0),
        name="fetch",
    )(weights, after)


def call_first(gain, adjacency, w_qkv, own, chunks):
    width, tiles = w_qkv.shape[0], adjacency.shape[0]
    queries = sum(chunk.shape[0] for chunk in own)
    heads = width // HEAD_DIM
    operands = (gain, adjacency, w_qkv, *own, *chunks)
    return pl.pallas_call(
        functools.partial(first_kernel, len(own)),
        out_shape=(
            jax.ShapeDtypeStruct((tiles, queries), jnp.bfloat16),
            jax.ShapeDtypeStruct((queries, width), jnp.bfloat16),
            *state_shapes(heads, queries),
        ),
        in_specs=vmem(len(operands)),
        out_specs=tuple(vmem(4)),
        scratch_shapes=scratch(queries, heads),
        compiler_params=PARAMS,
        cost_estimate=cost(queries, sum(c.shape[0] for c in chunks), width, 1),
        name="attend_first",
    )(*operands)


def call_next(near, query, acc, top, gain, w_qkv, chunks):
    queries, width = query.shape
    heads = width // HEAD_DIM
    operands = (near, query, acc, top, gain, w_qkv, *chunks)
    return pl.pallas_call(
        next_kernel,
        out_shape=state_shapes(heads, queries),
        in_specs=vmem(len(operands)),
        out_specs=tuple(vmem(2)),
        scratch_shapes=scratch(queries, heads),
        compiler_params=PARAMS,
        cost_estimate=cost(queries, sum(c.shape[0] for c in chunks), width, 0),
        name="attend_next",
    )(*operands)


def call_last(near, query, acc, top, gain, w_qkv, wo, chunks):
    queries, width = query.shape
    heads = width // HEAD_DIM
    operands = (near, query, acc, top, gain, w_qkv, wo, *chunks)
    return pl.pallas_call(
        last_kernel,
        out_shape=jax.ShapeDtypeStruct((queries, width), jnp.bfloat16),
        in_specs=vmem(len(operands)),
        out_specs=vmem(1)[0],
        scratch_shapes=[
            pltpu.VMEM((heads, ACC_ROWS, queries), jnp.float32),
            pltpu.VMEM((heads, queries), jnp.float32),
            pltpu.VMEM((width, queries), jnp.bfloat16),
            *scratch(queries, heads),
        ],
        compiler_params=PARAMS,
        cost_estimate=cost(queries, sum(c.shape[0] for c in chunks), width, 1),
        name="attend_last",
    )(*operands)


def on_device(cells_in, gain, w_qkv, w_out, tile_of_cell, tile_adjacent):
    genes, cell_dev, width = cells_in.shape
    head_devs, cell_devs = lax.axis_size("heads"), lax.axis_size("cells")
    sets = cell_devs // genes
    half = genes // 2
    gene = lax.rem(lax.axis_index("cells"), genes)
    same = [[s * genes + g for s in range(sets)] for g in range(genes)]

    def over_cells(value, step):
        return lax.ppermute(value, "cells", [(i, i ^ step) for i in range(cell_devs)])

    def over_heads(value, step):
        return lax.ppermute(value, "heads", [(i, i ^ step) for i in range(head_devs)])

    tags = jnp.broadcast_to(tile_of_cell.astype(jnp.bfloat16)[:, None], (cell_dev, TAG))

    def piece_for(k):
        rows = lax.dynamic_index_in_dim(cells_in, gene ^ k, 0, keepdims=False)
        return jnp.concatenate([rows, tags], axis=1)

    arrived = [piece_for(0)] + [None] * (genes - 1)
    for k in [*range(half, genes), *range(1, half)]:
        arrived[k] = over_cells(piece_for(k), k)
    own = [jnp.concatenate(arrived[:half], 0)]
    w_qkv, *late = lax.optimization_barrier((fetch(w_qkv, own[0]), *arrived[half:]))
    own.append(jnp.concatenate(late, 0))
    others, near_chunks = [[], []], []
    for i in range(2):
        held = own[i]
        if sets > 1:
            held = lax.all_gather(held, "cells", axis=0, axis_index_groups=same, tiled=True)
        near_chunks += [held, over_heads(held, 1)]
        for step in range(2, head_devs, 2):
            chunk = over_heads(held, step)
            others[i] += [chunk, over_heads(chunk, 1)] if i == 0 else [chunk, None]
    gain = gain.reshape(1, width)
    near, query, acc, top = call_first(gain, tile_adjacent, w_qkv, own, near_chunks)
    for step in range(2, head_devs, 2):
        chunk, acc = lax.optimization_barrier((others[1][step - 2], acc))
        others[1][step - 2 : step] = [chunk, over_heads(chunk, 1)]
    acc, top = call_next(near, query, acc, top, gain, w_qkv, others[0])
    out = call_last(near, query, acc, top, gain, w_qkv, w_out, others[1])
    out = out.reshape(genes, cell_dev, width)
    result = jnp.zeros_like(out)
    for k in [0, *range(half, genes), *range(1, half)]:
        piece = out[k] if k == 0 else over_cells(out[k], k)
        result = lax.dynamic_update_index_in_dim(result, piece, gene ^ k, 0)
    return result


def solution(mesh):
    return jax.shard_map(
        on_device,
        mesh=mesh,
        in_specs=(P(None, ("heads", "cells"), None), P(), P(), P(), P(("heads", "cells")), P()),
        out_specs=P(None, ("heads", "cells"), None),
        check_vma=False,
    )
```

time: 75.2 us -> 57.8 us (0.77)
  waiting for transfers between devices: 24.8 us -> 13.2 us
  starting transfers between devices: 32.1 us -> 25.8 us
    ppermute x12 -> x6, waiting for transfers between devices: 8.19 us -> 1.54 us  [over_heads(): lax.ppermute(value, 'heads', [(i, i ^ step) for i in range(head_devs)])]
    ppermute x17 -> x14, waiting for transfers between devices: 16.6 us -> 11.6 us  [over_cells(): lax.ppermute(value, 'cells', [(i, i ^ step) for i in range(cell_devs)])]
    ppermute x17 -> x14, starting transfers between devices: 26.8 us -> 22 us  [over_cells(): lax.ppermute(value, 'cells', [(i, i ^ step) for i in range(cell_devs)])]
    ppermute x12 -> x6, starting transfers between devices: 5.22 us -> 3.77 us  [over_heads(): lax.ppermute(value, 'heads', [(i, i ^ step) for i in range(head_devs)])]
    unnamed x15 -> x13, local copies, waits for them, and re-layouts: 3.6 us -> 2.83 us
    pallas_call x3 -> x4, Pallas kernels: 12.1 us -> 12.8 us  [the longest x1 5.93 us: call_first(): pl.pallas_call(functools.partial(first_kernel, len(own)), out_shape=(jax....]
  transfers between devices with their start and end apart: 29 -> 20, of which waited for: 13 -> 8; matrix products, arithmetic and copies ran while one was open for 1% -> 0% of each run, Pallas kernels for 12% -> 16%
where the time goes in v3:
time: 57.8 us; the launch traced here: 57.6 us
  starting transfers between devices  25.8 us (45%)
  waiting for transfers between devices  13.2 us (23%)
  Pallas kernels  12.8 us (22%)
  local copies, waits for them, and re-layouts  4.81 us (8%)
  other arithmetic  0.73 us (1%)
    ppermute x14, starting transfers between devices, over_cells(): lax.ppermute(value, 'cells', [(i, i ^ step) for i in range(cell_devs)])  22 us
    ppermute x14, waiting for transfers between devices, over_cells(): lax.ppermute(value, 'cells', [(i, i ^ step) for i in range(cell_devs)])  11.6 us
    pallas_call x1, Pallas kernels, call_first(): pl.pallas_call(functools.partial(first_kernel, len(own)), out_shape=(jax....  5.93 us
    ppermute x6, starting transfers between devices, over_heads(): lax.ppermute(value, 'heads', [(i, i ^ step) for i in range(head_devs)])  3.77 us
    pallas_call x1, Pallas kernels, call_last(): pl.pallas_call(last_kernel, out_shape=jax.ShapeDtypeStruct((queries, widt...  3.55 us
    pallas_call x1, Pallas kernels, call_next(): pl.pallas_call(next_kernel, out_shape=state_shapes(heads, queries), in_sp...  2.93 us
    unnamed x13, local copies, waits for them, and re-layouts  2.83 us
    ppermute x6, waiting for transfers between devices, over_heads(): lax.ppermute(value, 'heads', [(i, i ^ step) for i in range(head_devs)])  1.54 us
  transfers between devices with their start and end apart: 20, of which 8 were waited for; matrix products, arithmetic and copies ran while one was open for 0% of the time, Pallas kernels for 16%

profile of v3, /device:TPU:0, one launch (start us, length us, event | category | flops | bytes accessed | tf_op | source)
XLA Modules:
  0.0 57.6 jit_solution(11263106837807596086)
XLA Ops:
  0.0 0.7 %convert_element_type.3 = bf16[32]{0:T(256)(128)(2,1)S(1)} convert(s32[32]{0:T(128)} %param.10) | non-fusion elementwise | flops 32 | bytes 192 | tf_op jit(solution)/shard_map/convert_element_type | solution.py:279
  0.7 1.1 %dynamic-slice_bitcast_fusion = (bf16[32,1024]{1,0:T(8,128)(2,1)S(1)}, bf16[32,1024]{1,0:T(8,128)(2,1)S(1)}, bf16[32,1024]{1,0:T(8,128)(2,1)S(1)}, bf16[32,1024]...) fusion(bf16[8,32,1024]{2,1,0:T(8,128)(2,1)} %param.6, ...), kind=kLoop, calls=%fused_computation.17 | loop fusion | bytes 1048608 | tf_op jit(solution)/shard_map/jit(dynamic_index_in_dim)/squeeze | solution.py:282
  1.8 0.1 broadcast_in_dim.33
  1.9 3.0 %collective-permute-start = (bf16[32,1152]{1,0:T(8,128)(2,1)S(1)}, bf16[32,1152]{1,0:T(8,128)(2,1)S(1)}, u32[]{:S(2)}, u32[]{:S(2)}) collective-permute-start(bf16[32,1152]{1,0:T(8,128)(2,1)S(1)} %get-tuple-element.52), channel_id=1, source_target_pairs={{0,1},{1,0},{2,3},{3,2},{4,5},{5,4},{6,7},{7,6},{8,9},{9,8},{10,11... | collective-permute-start | bytes 221192 | tf_op jit(solution)/shard_map/ppermute | solution.py:274
  4.9 1.6 %collective-permute-start.1 = (bf16[32,1152]{1,0:T(8,128)(2,1)S(1)}, bf16[32,1152]{1,0:T(8,128)(2,1)S(1)}, u32[]{:S(2)}, u32[]{:S(2)}) collective-permute-start(bf16[32,1152]{1,0:T(8,128)(2,1)S(1)} %get-tuple-element.47), channel_id=1, source_target_pairs={{0,2},{1,3},{2,0},{3,1},{4,6},{5,7},{6,4},{7,5},{8,10},{9,11},{10,... | collective-permute-start | bytes 221192 | tf_op jit(solution)/shard_map/ppermute | solution.py:274
  6.5 0.0 collective-permute-start.2
  6.5 3.0 %collective-permute-start.3 = (bf16[32,1152]{1,0:T(8,128)(2,1)S(1)}, bf16[32,1152]{1,0:T(8,128)(2,1)S(1)}, u32[]{:S(2)}, u32[]{:S(2)}) collective-permute-start(bf16[32,1152]{1,0:T(8,128)(2,1)S(1)} %get-tuple-element.49), channel_id=1, source_target_pairs={{0,4},{1,5},{2,6},{3,7},{4,0},{5,1},{6,2},{7,3},{8,12},{9,13},{10,... | collective-permute-start | bytes 221192 | tf_op jit(solution)/shard_map/ppermute | solution.py:274
  9.5 1.3 %collective-permute-start.4 = (bf16[32,1152]{1,0:T(8,128)(2,1)S(1)}, bf16[32,1152]{1,0:T(8,128)(2,1)S(1)}, u32[]{:S(2)}, u32[]{:S(2)}) collective-permute-start(bf16[32,1152]{1,0:T(8,128)(2,1)S(1)} %get-tuple-element.50), channel_id=1, source_target_pairs={{0,5},{1,4},{2,7},{3,6},{4,1},{5,0},{6,3},{7,2},{8,13},{9,12},{10,... | collective-permute-start | bytes 221192 | tf_op jit(solution)/shard_map/ppermute | solution.py:274
  10.8 0.0 collective-permute-done
  10.8 3.6 %collective-permute-start.5 = (bf16[32,1152]{1,0:T(8,128)(2,1)S(1)}, bf16[32,1152]{1,0:T(8,128)(2,1)S(1)}, u32[]{:S(2)}, u32[]{:S(2)}) collective-permute-start(bf16[32,1152]{1,0:T(8,128)(2,1)S(1)} %get-tuple-element.51), channel_id=1, source_target_pairs={{0,6},{1,7},{2,4},{3,5},{4,2},{5,3},{6,0},{7,1},{8,14},{9,15},{10,... | collective-permute-start | bytes 221192 | tf_op jit(solution)/shard_map/ppermute | solution.py:274
  14.4 0.0 collective-permute-done.1
  14.4 0.0 collective-permute-start.6
  14.4 0.0 collective-permute-done.2
  14.4 1.7 %collective-permute-start.10 = (bf16[128,1152]{1,0:T(8,128)(2,1)S(1)}, bf16[128,1152]{1,0:T(8,128)(2,1)S(1)}, u32[]{:S(2)}, u32[]{:S(2)}) collective-permute-start(bf16[128,1152]{1,0:T(8,128)(2,1)S(1)} %pad_maximum_fusion.after_ref.refs_0_.refs_2_), channel_id=1, source_target_pairs={{0,16},{8,24},{16,0},{24,8},{1,17},{9,25},{17,1},{25,9},{2,18},{10... | collective-permute-start | bytes 884744 | tf_op jit(solution)/shard_map/ppermute | solution.py:277
  16.1 0.0 copy-start
  16.1 2.8 %copy-done = bf16[1024,3072]{1,0:T(8,128)(2,1)S(1)} copy-done((bf16[1024,3072]{1,0:T(8,128)(2,1)S(1)}, bf16[1024,3072]{1,0:T(8,128)(2,1)}, u32[]{:S(2)}) %copy-start) | copy-done | bytes 6291480
  18.9 0.0 copy-start.2
  18.9 0.0 copy-start.3
  18.9 0.4 fetch.1.w_ref
  19.4 0.0 collective-permute-done.3
  19.4 1.4 %collective-permute-done.4 = bf16[32,1152]{1,0:T(8,128)(2,1)S(1)} collective-permute-done((bf16[32,1152]{1,0:T(8,128)(2,1)S(1)}, bf16[32,1152]{1,0:T(8,128)(2,1)S(1)}, u32[]{:S(2)}, u32[]{:S(2)}) %collective-permute-start.4) | collective-permute-done | bytes 73760 | tf_op jit(solution)/shard_map/ppermute | solution.py:274
  20.8 0.0 collective-permute-done.5
  20.8 0.8 %collective-permute-done.6 = bf16[32,1152]{1,0:T(8,128)(2,1)S(1)} collective-permute-done((bf16[32,1152]{1,0:T(8,128)(2,1)S(1)}, bf16[32,1152]{1,0:T(8,128)(2,1)S(1)}, u32[]{:S(2)}, u32[]{:S(2)}) %collective-permute-start.6) | collective-permute-done | bytes 73760 | tf_op jit(solution)/shard_map/ppermute | solution.py:274
  21.6 0.1 collective-permute-start.8
  21.7 0.5 collective-permute-start.7
  22.2 1.5 %collective-permute-start.9 = (bf16[128,1152]{1,0:T(8,128)(2,1)S(1)}, bf16[128,1152]{1,0:T(8,128)(2,1)S(1)}, u32[]{:S(2)}, u32[]{:S(2)}) collective-permute-start(bf16[128,1152]{1,0:T(8,128)(2,1)S(1)} %constant_dynamic-update-slice_fusion.refs_1_.refs_4_), channel_id=1, source_target_pairs={{0,16},{8,24},{16,0},{24,8},{1,17},{9,25},{17,1},{25,9},{2,18},{10... | collective-permute-start | bytes 884744 | tf_op jit(solution)/shard_map/ppermute | solution.py:277
  23.7 0.0 collective-permute-done.10.refs_0_
  23.7 0.0 collective-permute-start.11
  23.7 0.0 collective-permute-done.8.refs_5_
  23.7 0.0 collective-permute-done.7.refs_3_
  23.7 0.0 copy-done.2
  23.7 0.0 copy-done.3
  23.7 5.9 %attend_first.1 = (bf16[256,256]{1,0:T(8,128)(2,1)S(1)}, bf16[256,1024]{1,0:T(8,128)(2,1)S(1)}, f32[16,72,256]{2,1,0:T(8,128)S(1)}, f32[16,256]{1,0:T(8,128)S(1)}) custom-call(f32[1,1024]{1,0:T(1,128)S(1)} %bitcast.35, s32[256,256]{1,0:T(8,128)S(1)} %copy-done.3, bf16[1024,3072]{1,0:T(8,128)(2,1)S(1)} %fetch.1.w_ref, ...), custom_call_target="tpu_custom_call" | custom-call | flops 3758096384 | bytes 8388608 | tf_op jit(solution)/shard_map/attend_first/pallas_call | solution.py:212
  29.6 1.5 %collective-permute-done.9.refs_0_ = bf16[128,1152]{1,0:T(8,128)(2,1)S(1)} collective-permute-done((bf16[128,1152]{1,0:T(8,128)(2,1)S(1)}, bf16[128,1152]{1,0:T(8,128)(2,1)S(1)}, u32[]{:S(2)}, u32[]{:S(2)}) %collective-permute-start.9) | collective-permute-done | bytes 294944 | tf_op jit(solution)/shard_map/ppermute | solution.py:277
  31.2 0.0 collective-permute-start.12
  31.2 0.0 collective-permute-done.11.refs_1_
  31.2 0.0 copy-start.1
  31.2 2.9 %attend_next.1 = (f32[16,72,256]{2,1,0:T(8,128)S(1)}, f32[16,256]{1,0:T(8,128)S(1)}) custom-call(bf16[256,256]{1,0:T(8,128)(2,1)S(1)} %get-tuple-element.23.near_ref, bf16[256,1024]{1,0:T(8,128)(2,1)S(1)} %get-tuple-element.24.query_ref, f32[16,72,256]{2,1,0:T(8,128)S(1)} %get-tuple-element.26.acc_in, f32[16,256]{1,0:T(8,128)S(1)} %get-tuple-element.27.top_in, ...), custom_call_target="tpu_custom_call" | custom-call | flops 1610612736 | bytes 8388608 | tf_op jit(solution)/shard_map/attend_next/pallas_call | solution.py:232
  34.1 0.0 collective-permute-done.12.refs_1_
  34.1 0.0 copy-done.1
  34.1 3.5 %attend_last.1 = bf16[256,1024]{1,0:T(8,128)(2,1)S(1)} custom-call(bf16[256,256]{1,0:T(8,128)(2,1)S(1)} %get-tuple-element.23.near_ref, bf16[256,1024]{1,0:T(8,128)(2,1)S(1)} %get-tuple-element.24.query_ref, f32[16,72,256]{2,1,0:T(8,128)S(1)} %get-tuple-element.28.acc_in, f32[16,256]{1,0:T(8,128)S(1)} %get-tuple-element.29.top_in, f32[1,1024]{1,0:T(1,128)S(1)} %bitcast.37, ...), custom_call_target="tpu_custom_call" | custom-call | flops 2147483648 | bytes 8388608 | tf_op jit(solution)/shard_map/attend_last/pallas_call | solution.py:248
  37.7 4.1 %collective-permute-start.13 = (bf16[32,1024]{1,0:T(8,128)(2,1)S(1)}, bf16[32,1024]{1,0:T(8,128)(2,1)S(1)}, u32[]{:S(2)}, u32[]{:S(2)}) collective-permute-start(bf16[32,1024]{1,0:T(8,128)(2,1)S(1)} %get-tuple-element.37), channel_id=1, source_target_pairs={{0,4},{1,5},{2,6},{3,7},{4,0},{5,1},{6,2},{7,3},{8,12},{9,13},{10,... | collective-permute-start | bytes 196616 | tf_op jit(solution)/shard_map/ppermute | solution.py:274
  41.8 0.1 broadcast_in_dim.32
  41.9 0.1 collective-permute-start.14
  42.0 1.5 %collective-permute-start.15 = (bf16[32,1024]{1,0:T(8,128)(2,1)S(1)}, bf16[32,1024]{1,0:T(8,128)(2,1)S(1)}, u32[]{:S(2)}, u32[]{:S(2)}) collective-permute-start(bf16[32,1024]{1,0:T(8,128)(2,1)S(1)} %get-tuple-element.35), channel_id=1, source_target_pairs={{0,6},{1,7},{2,4},{3,5},{4,2},{5,3},{6,0},{7,1},{8,14},{9,15},{10,... | collective-permute-start | bytes 196616 | tf_op jit(solution)/shard_map/ppermute | solution.py:274
  43.5 3.2 %collective-permute-start.16 = (bf16[32,1024]{1,0:T(8,128)(2,1)S(1)}, bf16[32,1024]{1,0:T(8,128)(2,1)S(1)}, u32[]{:S(2)}, u32[]{:S(2)}) collective-permute-start(bf16[32,1024]{1,0:T(8,128)(2,1)S(1)} %get-tuple-element.34), channel_id=1, source_target_pairs={{0,7},{1,6},{2,5},{3,4},{4,3},{5,2},{6,1},{7,0},{8,15},{9,14},{10,... | collective-permute-start | bytes 196616 | tf_op jit(solution)/shard_map/ppermute | solution.py:274
  46.7 0.6 %collective-permute-start.17 = (bf16[32,1024]{1,0:T(8,128)(2,1)S(1)}, bf16[32,1024]{1,0:T(8,128)(2,1)S(1)}, u32[]{:S(2)}, u32[]{:S(2)}) collective-permute-start(bf16[32,1024]{1,0:T(8,128)(2,1)S(1)} %get-tuple-element.33), channel_id=1, source_target_pairs={{0,1},{1,0},{2,3},{3,2},{4,5},{5,4},{6,7},{7,6},{8,9},{9,8},{10,11... | collective-permute-start | bytes 196616 | tf_op jit(solution)/shard_map/ppermute | solution.py:274
  47.3 2.5 %collective-permute-done.13 = bf16[32,1024]{1,0:T(8,128)(2,1)S(1)} collective-permute-done((bf16[32,1024]{1,0:T(8,128)(2,1)S(1)}, bf16[32,1024]{1,0:T(8,128)(2,1)S(1)}, u32[]{:S(2)}, u32[]{:S(2)}) %collective-permute-start.13) | collective-permute-done | bytes 65568 | tf_op jit(solution)/shard_map/ppermute | solution.py:274
  49.9 0.0 collective-permute-start.18
  49.9 1.9 %collective-permute-done.14 = bf16[32,1024]{1,0:T(8,128)(2,1)S(1)} collective-permute-done((bf16[32,1024]{1,0:T(8,128)(2,1)S(1)}, bf16[32,1024]{1,0:T(8,128)(2,1)S(1)}, u32[]{:S(2)}, u32[]{:S(2)}) %collective-permute-start.14) | collective-permute-done | bytes 65568 | tf_op jit(solution)/shard_map/ppermute | solution.py:274
  51.8 0.0 collective-permute-start.19
  51.8 0.0 collective-permute-done.15
  51.8 0.0 collective-permute-done.16
  51.8 1.0 %collective-permute-done.17 = bf16[32,1024]{1,0:T(8,128)(2,1)S(1)} collective-permute-done((bf16[32,1024]{1,0:T(8,128)(2,1)S(1)}, bf16[32,1024]{1,0:T(8,128)(2,1)S(1)}, u32[]{:S(2)}, u32[]{:S(2)}) %collective-permute-start.17) | collective-permute-done | bytes 65568 | tf_op jit(solution)/shard_map/ppermute | solution.py:274
  52.9 1.3 %collective-permute-done.18 = bf16[32,1024]{1,0:T(8,128)(2,1)S(1)} collective-permute-done((bf16[32,1024]{1,0:T(8,128)(2,1)S(1)}, bf16[32,1024]{1,0:T(8,128)(2,1)S(1)}, u32[]{:S(2)}, u32[]{:S(2)}) %collective-permute-start.18) | collective-permute-done | bytes 65568 | tf_op jit(solution)/shard_map/ppermute | solution.py:274
  54.2 0.0 copy-start.4
  54.2 2.7 %collective-permute-done.19 = bf16[32,1024]{1,0:T(8,128)(2,1)S(1)} collective-permute-done((bf16[32,1024]{1,0:T(8,128)(2,1)S(1)}, bf16[32,1024]{1,0:T(8,128)(2,1)S(1)}, u32[]{:S(2)}, u32[]{:S(2)}) %collective-permute-start.19) | collective-permute-done | bytes 65568 | tf_op jit(solution)/shard_map/ppermute | solution.py:274
  56.9 0.0 copy-done.4
  56.9 0.6 %bitcast_dynamic-update-slice_fusion = bf16[8,32,1024]{2,1,0:T(8,128)(2,1)} fusion(bf16[8,32,1024]{2,1,0:T(8,128)(2,1)} %copy-done.4, s32[]{:T(128)S(6)} %select_n.37, bf16[32,1024]{1,0:T(8,128)(2,1)S(1)} %collective-permute-done.19), kind=kLoop, calls=%fused_computation.10 | loop fusion | bytes 131076 | tf_op jit(solution)/shard_map/jit(dynamic_update_index_in_dim)/dynamic_update_slice | solution.py:311
  (14 shorter events, 0.2 us)
Async XLA Ops:
  1.9 8.9 %collective-permute-start = (bf16[32,1152]{1,0:T(8,128)(2,1)S(1)}, bf16[32,1152]{1,0:T(8,128)(2,1)S(1)}, u32[]{:S(2)}, u32[]{:S(2)}) collective-permute-start(bf16[32,1152]{1,0:T(8,128)(2,1)S(1)} %get-tuple-element.52), channel_id=1, source_target_pairs={{0,1},{1,0},{2,3},{3,2},{4,5},{5,4},{6,7},{7,6},{8,9},{9,8},{10,11... | collective-permute-start | bytes 221192 | tf_op jit(solution)/shard_map/ppermute | solution.py:274
  4.9 9.5 %collective-permute-start.1 = (bf16[32,1152]{1,0:T(8,128)(2,1)S(1)}, bf16[32,1152]{1,0:T(8,128)(2,1)S(1)}, u32[]{:S(2)}, u32[]{:S(2)}) collective-permute-start(bf16[32,1152]{1,0:T(8,128)(2,1)S(1)} %get-tuple-element.47), channel_id=1, source_target_pairs={{0,2},{1,3},{2,0},{3,1},{4,6},{5,7},{6,4},{7,5},{8,10},{9,11},{10,... | collective-permute-start | bytes 221192 | tf_op jit(solution)/shard_map/ppermute | solution.py:274
  6.5 7.9 %collective-permute-start.2 = (bf16[32,1152]{1,0:T(8,128)(2,1)S(1)}, bf16[32,1152]{1,0:T(8,128)(2,1)S(1)}, u32[]{:S(2)}, u32[]{:S(2)}) collective-permute-start(bf16[32,1152]{1,0:T(8,128)(2,1)S(1)} %get-tuple-element.48), channel_id=1, source_target_pairs={{0,3},{1,2},{2,1},{3,0},{4,7},{5,6},{6,5},{7,4},{8,11},{9,10},{10,... | collective-permute-start | bytes 221192 | tf_op jit(solution)/shard_map/ppermute | solution.py:274
  6.5 12.9 %collective-permute-start.3 = (bf16[32,1152]{1,0:T(8,128)(2,1)S(1)}, bf16[32,1152]{1,0:T(8,128)(2,1)S(1)}, u32[]{:S(2)}, u32[]{:S(2)}) collective-permute-start(bf16[32,1152]{1,0:T(8,128)(2,1)S(1)} %get-tuple-element.49), channel_id=1, source_target_pairs={{0,4},{1,5},{2,6},{3,7},{4,0},{5,1},{6,2},{7,3},{8,12},{9,13},{10,... | collective-permute-start | bytes 221192 | tf_op jit(solution)/shard_map/ppermute | solution.py:274
  9.5 11.3 %collective-permute-start.4 = (bf16[32,1152]{1,0:T(8,128)(2,1)S(1)}, bf16[32,1152]{1,0:T(8,128)(2,1)S(1)}, u32[]{:S(2)}, u32[]{:S(2)}) collective-permute-start(bf16[32,1152]{1,0:T(8,128)(2,1)S(1)} %get-tuple-element.50), channel_id=1, source_target_pairs={{0,5},{1,4},{2,7},{3,6},{4,1},{5,0},{6,3},{7,2},{8,13},{9,12},{10,... | collective-permute-start | bytes 221192 | tf_op jit(solution)/shard_map/ppermute | solution.py:274
  10.8 10.0 %collective-permute-start.5 = (bf16[32,1152]{1,0:T(8,128)(2,1)S(1)}, bf16[32,1152]{1,0:T(8,128)(2,1)S(1)}, u32[]{:S(2)}, u32[]{:S(2)}) collective-permute-start(bf16[32,1152]{1,0:T(8,128)(2,1)S(1)} %get-tuple-element.51), channel_id=1, source_target_pairs={{0,6},{1,7},{2,4},{3,5},{4,2},{5,3},{6,0},{7,1},{8,14},{9,15},{10,... | collective-permute-start | bytes 221192 | tf_op jit(solution)/shard_map/ppermute | solution.py:274
  14.4 7.2 %collective-permute-start.6 = (bf16[32,1152]{1,0:T(8,128)(2,1)S(1)}, bf16[32,1152]{1,0:T(8,128)(2,1)S(1)}, u32[]{:S(2)}, u32[]{:S(2)}) collective-permute-start(bf16[32,1152]{1,0:T(8,128)(2,1)S(1)} %get-tuple-element.46), channel_id=1, source_target_pairs={{0,7},{1,6},{2,5},{3,4},{4,3},{5,2},{6,1},{7,0},{8,15},{9,14},{10,... | collective-permute-start | bytes 221192 | tf_op jit(solution)/shard_map/ppermute | solution.py:274
  14.4 9.2 %collective-permute-start.10 = (bf16[128,1152]{1,0:T(8,128)(2,1)S(1)}, bf16[128,1152]{1,0:T(8,128)(2,1)S(1)}, u32[]{:S(2)}, u32[]{:S(2)}) collective-permute-start(bf16[128,1152]{1,0:T(8,128)(2,1)S(1)} %pad_maximum_fusion.after_ref.refs_0_.refs_2_), channel_id=1, source_target_pairs={{0,16},{8,24},{16,0},{24,8},{1,17},{9,25},{17,1},{25,9},{2,18},{10... | collective-permute-start | bytes 884744 | tf_op jit(solution)/shard_map/ppermute | solution.py:277
  16.1 2.8 %copy-start = (bf16[1024,3072]{1,0:T(8,128)(2,1)S(1)}, bf16[1024,3072]{1,0:T(8,128)(2,1)}, u32[]{:S(2)}) copy-start(bf16[1024,3072]{1,0:T(8,128)(2,1)} %from_ref.1) | copy-start | bytes 18874372
  18.9 4.8 %copy-start.2 = (f32[1024]{0:T(1024)S(1)}, f32[1024]{0:T(1024)}, u32[]{:S(2)}) copy-start(f32[1024]{0:T(1024)} %param.7) | copy-start | bytes 12292
  18.9 4.8 %copy-start.3 = (s32[256,256]{1,0:T(8,128)S(1)}, s32[256,256]{1,0:T(8,128)}, u32[]{:S(2)}) copy-start(s32[256,256]{1,0:T(8,128)} %adj_ref.1) | copy-start | bytes 786436
  21.6 2.1 %collective-permute-start.8 = (bf16[128,1152]{1,0:T(8,128)(2,1)S(1)}, bf16[128,1152]{1,0:T(8,128)(2,1)S(1)}, u32[]{:S(2)}, u32[]{:S(2)}) collective-permute-start(bf16[128,1152]{1,0:T(8,128)(2,1)S(1)} %constant_dynamic-update-slice_fusion.refs_1_.refs_4_), channel_id=1, source_target_pairs={{0,8},{8,0},{16,24},{24,16},{1,9},{9,1},{17,25},{25,17},{2,10},{10... | collective-permute-start | bytes 884744 | tf_op jit(solution)/shard_map/ppermute | solution.py:277
  21.7 2.0 %collective-permute-start.7 = (bf16[128,1152]{1,0:T(8,128)(2,1)S(1)}, bf16[128,1152]{1,0:T(8,128)(2,1)S(1)}, u32[]{:S(2)}, u32[]{:S(2)}) collective-permute-start(bf16[128,1152]{1,0:T(8,128)(2,1)S(1)} %pad_maximum_fusion.after_ref.refs_0_.refs_2_), channel_id=1, source_target_pairs={{0,8},{8,0},{16,24},{24,16},{1,9},{9,1},{17,25},{25,17},{2,10},{10... | collective-permute-start | bytes 884744 | tf_op jit(solution)/shard_map/ppermute | solution.py:277
  22.2 9.0 %collective-permute-start.9 = (bf16[128,1152]{1,0:T(8,128)(2,1)S(1)}, bf16[128,1152]{1,0:T(8,128)(2,1)S(1)}, u32[]{:S(2)}, u32[]{:S(2)}) collective-permute-start(bf16[128,1152]{1,0:T(8,128)(2,1)S(1)} %constant_dynamic-update-slice_fusion.refs_1_.refs_4_), channel_id=1, source_target_pairs={{0,16},{8,24},{16,0},{24,8},{1,17},{9,25},{17,1},{25,9},{2,18},{10... | collective-permute-start | bytes 884744 | tf_op jit(solution)/shard_map/ppermute | solution.py:277
  23.7 7.5 %collective-permute-start.11 = (bf16[128,1152]{1,0:T(8,128)(2,1)S(1)}, bf16[128,1152]{1,0:T(8,128)(2,1)S(1)}, u32[]{:S(2)}, u32[]{:S(2)}) collective-permute-start(bf16[128,1152]{1,0:T(8,128)(2,1)S(1)} %collective-permute-done.10.refs_0_), channel_id=1, source_target_pairs={{0,8},{8,0},{16,24},{24,16},{1,9},{9,1},{17,25},{25,17},{2,10},{10... | collective-permute-start | bytes 884744 | tf_op jit(solution)/shard_map/ppermute | solution.py:277
  31.2 2.9 %collective-permute-start.12 = (bf16[128,1152]{1,0:T(8,128)(2,1)S(1)}, bf16[128,1152]{1,0:T(8,128)(2,1)S(1)}, u32[]{:S(2)}, u32[]{:S(2)}) collective-permute-start(bf16[128,1152]{1,0:T(8,128)(2,1)S(1)} %collective-permute-done.9.refs_0_), channel_id=1, source_target_pairs={{0,8},{8,0},{16,24},{24,16},{1,9},{9,1},{17,25},{25,17},{2,10},{10... | collective-permute-start | bytes 884744 | tf_op jit(solution)/shard_map/ppermute | solution.py:277
  31.2 2.9 %copy-start.1 = (bf16[1024,1024]{1,0:T(8,128)(2,1)S(1)}, bf16[1024,1024]{1,0:T(8,128)(2,1)}, u32[]{:S(2)}) copy-start(bf16[1024,1024]{1,0:T(8,128)(2,1)} %wo_ref.1) | copy-start | bytes 6291460
  37.7 12.2 %collective-permute-start.13 = (bf16[32,1024]{1,0:T(8,128)(2,1)S(1)}, bf16[32,1024]{1,0:T(8,128)(2,1)S(1)}, u32[]{:S(2)}, u32[]{:S(2)}) collective-permute-start(bf16[32,1024]{1,0:T(8,128)(2,1)S(1)} %get-tuple-element.37), channel_id=1, source_target_pairs={{0,4},{1,5},{2,6},{3,7},{4,0},{5,1},{6,2},{7,3},{8,12},{9,13},{10,... | collective-permute-start | bytes 196616 | tf_op jit(solution)/shard_map/ppermute | solution.py:274
  41.9 9.8 %collective-permute-start.14 = (bf16[32,1024]{1,0:T(8,128)(2,1)S(1)}, bf16[32,1024]{1,0:T(8,128)(2,1)S(1)}, u32[]{:S(2)}, u32[]{:S(2)}) collective-permute-start(bf16[32,1024]{1,0:T(8,128)(2,1)S(1)} %get-tuple-element.36), channel_id=1, source_target_pairs={{0,5},{1,4},{2,7},{3,6},{4,1},{5,0},{6,3},{7,2},{8,13},{9,12},{10,... | collective-permute-start | bytes 196616 | tf_op jit(solution)/shard_map/ppermute | solution.py:274
  42.0 9.8 %collective-permute-start.15 = (bf16[32,1024]{1,0:T(8,128)(2,1)S(1)}, bf16[32,1024]{1,0:T(8,128)(2,1)S(1)}, u32[]{:S(2)}, u32[]{:S(2)}) collective-permute-start(bf16[32,1024]{1,0:T(8,128)(2,1)S(1)} %get-tuple-element.35), channel_id=1, source_target_pairs={{0,6},{1,7},{2,4},{3,5},{4,2},{5,3},{6,0},{7,1},{8,14},{9,15},{10,... | collective-permute-start | bytes 196616 | tf_op jit(solution)/shard_map/ppermute | solution.py:274
  43.5 8.3 %collective-permute-start.16 = (bf16[32,1024]{1,0:T(8,128)(2,1)S(1)}, bf16[32,1024]{1,0:T(8,128)(2,1)S(1)}, u32[]{:S(2)}, u32[]{:S(2)}) collective-permute-start(bf16[32,1024]{1,0:T(8,128)(2,1)S(1)} %get-tuple-element.34), channel_id=1, source_target_pairs={{0,7},{1,6},{2,5},{3,4},{4,3},{5,2},{6,1},{7,0},{8,15},{9,14},{10,... | collective-permute-start | bytes 196616 | tf_op jit(solution)/shard_map/ppermute | solution.py:274
  46.7 6.1 %collective-permute-start.17 = (bf16[32,1024]{1,0:T(8,128)(2,1)S(1)}, bf16[32,1024]{1,0:T(8,128)(2,1)S(1)}, u32[]{:S(2)}, u32[]{:S(2)}) collective-permute-start(bf16[32,1024]{1,0:T(8,128)(2,1)S(1)} %get-tuple-element.33), channel_id=1, source_target_pairs={{0,1},{1,0},{2,3},{3,2},{4,5},{5,4},{6,7},{7,6},{8,9},{9,8},{10,11... | collective-permute-start | bytes 196616 | tf_op jit(solution)/shard_map/ppermute | solution.py:274
  49.9 4.3 %collective-permute-start.18 = (bf16[32,1024]{1,0:T(8,128)(2,1)S(1)}, bf16[32,1024]{1,0:T(8,128)(2,1)S(1)}, u32[]{:S(2)}, u32[]{:S(2)}) collective-permute-start(bf16[32,1024]{1,0:T(8,128)(2,1)S(1)} %get-tuple-element.32), channel_id=1, source_target_pairs={{0,2},{1,3},{2,0},{3,1},{4,6},{5,7},{6,4},{7,5},{8,10},{9,11},{10,... | collective-permute-start | bytes 196616 | tf_op jit(solution)/shard_map/ppermute | solution.py:274
  51.8 5.2 %collective-permute-start.19 = (bf16[32,1024]{1,0:T(8,128)(2,1)S(1)}, bf16[32,1024]{1,0:T(8,128)(2,1)S(1)}, u32[]{:S(2)}, u32[]{:S(2)}) collective-permute-start(bf16[32,1024]{1,0:T(8,128)(2,1)S(1)} %get-tuple-element.31), channel_id=1, source_target_pairs={{0,3},{1,2},{2,1},{3,0},{4,7},{5,6},{6,5},{7,4},{8,11},{9,10},{10,... | collective-permute-start | bytes 196616 | tf_op jit(solution)/shard_map/ppermute | solution.py:274
  54.2 2.8 %copy-start.4 = (bf16[8,32,1024]{2,1,0:T(8,128)(2,1)}, bf16[8,32,1024]{2,1,0:T(8,128)(2,1)S(1)}, u32[]{:S(2)}) copy-start(bf16[8,32,1024]{2,1,0:T(8,128)(2,1)S(1)} %bitcast_dynamic-update-slice_fusion.1) | copy-start | bytes 1572868

commit v4 on v0

v4 whole, which is shorter than its diff:
```python
import math

import jax
import jax.numpy as jnp
from jax import lax
from jax.experimental import pallas as pl
from jax.experimental.pallas import tpu as pltpu
from jax.sharding import PartitionSpec as P

HEAD_DIM = 64
PAIR = 2 * HEAD_DIM
VAL_ROWS = PAIR + 16
ACC_ROWS = HEAD_DIM + 8
MASKED = -1e30
SCALE = 0.125 * math.log2(math.e)
COLS = 256
TAG = 128
BF16 = jnp.bfloat16
F32 = jnp.float32


def dot(a, b, a_dim=1, b_dim=0):
    return lax.dot_general(a, b, (((a_dim,), (b_dim,)), ((), ())), preferred_element_type=F32)


def one_hot(tags, count):
    tags = tags.astype(F32)
    lane = lax.broadcasted_iota(jnp.int32, tags.shape, 1).astype(F32)
    parts = [(tags == lane + start).astype(F32) for start in range(0, count, TAG)]
    return jnp.concatenate(parts, axis=1).astype(BF16)


class Stage:
    def __init__(self, env, pieces, queries, blocks, attend, fetch=False, finish=False, keep=()):
        self.pieces, self.queries, self.blocks = pieces, queries, blocks
        self.attend, self.fetch, self.finish, self.keep = attend, fetch, finish, keep
        self.width = env["w_hbm"].shape[0]
        self.tiles = env["adjacency_hbm"].shape[0]
        self.pairs = self.width // PAIR
        self.rows = {q: sum(size for _, _, size in pieces["q", q]) for q in {q for q, _ in attend}}
        self.cells = {b: sum(size for _, _, size in pieces["k", b]) for b in {b for _, b in attend}}
        self.block = max(self.cells.values())
        self.touched = sorted({q for q, _ in attend})
        ins = {"w_hbm", "gain_hbm", "adjacency_hbm"} if fetch else {"w"}
        if queries and not fetch:
            ins.add("adjacency")
        for group in [("q", q) for q in queries] + [("k", b) for b in {b for _, b in attend}]:
            ins |= {name for name, _, _ in pieces[group]}
        for q in self.touched:
            if q not in queries:
                ins |= {f"Q{q}", f"G{q}"}
            if f"acc{q}" in env:
                ins |= {f"acc{q}", f"top{q}"}
        for b in {b for _, b in attend} - set(blocks):
            ins |= {f"K{b}", f"V{b}"}
        if finish:
            ins.add("w_out")
        self.ins = sorted(ins)
        self.held = set(ins)
        shapes = {}
        for q in queries:
            shapes[f"Q{q}"] = ((self.pairs, 2 * self.rows[q], PAIR), BF16)
            shapes[f"G{q}"] = ((self.tiles, 2 * self.rows[q]), BF16)
        for q in self.touched:
            shapes[f"acc{q}"] = ((self.pairs, ACC_ROWS, 2 * self.rows[q]), F32)
            shapes[f"top{q}"] = ((self.pairs, 2 * self.rows[q]), F32)
        for b in blocks:
            shapes[f"K{b}"] = ((self.cells[b], self.width), BF16)
            shapes[f"V{b}"] = ((self.pairs, VAL_ROWS, self.cells[b]), BF16)
        outs, scratch = {}, {}
        for name, shape in shapes.items():
            stays = name[0] in "KV" and int(name[1:]) not in keep
            (scratch if finish or stays else outs)[name] = shape
        if finish:
            for q in self.touched:
                outs[f"out{q}"] = ((self.rows[q], self.width), BF16)
        self.outs, self.scratch = outs, scratch

    def body(self, *refs):
        count = len(self.ins)
        names = list(self.outs) + ["adjacency", "w"] * self.fetch + list(self.scratch)
        more = ["cells", "bias", "weights"] + ["attended"] * self.finish
        more += ["gain", "pairs_allowed", "sems"] * self.fetch
        self.read = dict(zip(self.ins, refs[:count]))
        self.write = dict(zip(names + more, refs[count:]))
        self.w = self.write["w"] if self.fetch else self.read["w"]
        if self.fetch:
            self.start_copies()
        for b in self.blocks:
            root = self.load_cells("k", b)
            if self.fetch and b == self.blocks[0]:
                self.take_weights(1)
            self.project_keys(b, root)
            if self.fetch and b == self.blocks[0]:
                self.take_weights(2)
            self.project_values(b, root)
        if self.fetch:
            self.take_weights(0)
        for q in self.queries:
            self.project_queries(q)
        self.attend_all()
        if self.finish:
            for q in self.touched:
                self.project_out(q)

    def ref(self, name):
        return self.write[name] if name in self.write else self.read[name]

    def rows_of(self, kind, index, columns):
        parts = self.pieces[kind, index]
        return [self.read[name][start : start + size, columns] for name, start, size in parts]

    def start_copies(self):
        width, sems = self.width, self.write["sems"]
        moves = [(self.read["gain_hbm"], self.write["gain"])]
        moves += [(self.read["adjacency_hbm"], self.write["pairs_allowed"])]
        for start in (width, 2 * width, 0):
            part = slice(start, start + width)
            moves.append((self.read["w_hbm"].at[:, part], self.write["w"].at[:, part]))
        copies = [pltpu.make_async_copy(*move, sems.at[i]) for i, move in enumerate(moves)]
        for copy in copies:
            copy.start()
        copies[0].wait()
        self.copies = {1: copies[2], 2: copies[3], 0: copies[4]}
        self.gain = self.write["gain"][...].T
        copies[1].wait()
        allowed = self.write["pairs_allowed"][...]
        self.write["adjacency"][...] = allowed.astype(F32).astype(BF16)

    def take_weights(self, part):
        self.copies[part].wait()
        columns = slice(part * self.width, (part + 1) * self.width)
        size = self.gain.shape[0]
        for i in range(self.width // size):
            rows = slice(i * size, (i + 1) * size)
            scaled = self.w[rows, columns].astype(F32) * self.gain[:, i : i + 1]
            self.w[rows, columns] = scaled.astype(BF16)

    def load_cells(self, kind, index):
        start, roots = 0, []
        for rows in self.rows_of(kind, index, slice(0, self.width)):
            self.write["cells"][start : start + rows.shape[0], :] = rows
            start += rows.shape[0]
            x32 = rows.astype(F32)
            roots.append(lax.rsqrt(jnp.mean(x32 * x32, axis=-1, keepdims=True) + 1e-05))
        return jnp.concatenate(roots, axis=0)

    def tags_of(self, kind, index):
        tags = jnp.concatenate(self.rows_of(kind, index, slice(self.width, None)), axis=0)
        return one_hot(tags, self.tiles)

    def project_queries(self, q):
        rows = self.rows[q]
        scale = self.load_cells("q", q) * SCALE
        cells = self.write["cells"][:rows, :]
        for start in range(0, self.width, COLS):
            query = (dot(cells, self.w[:, start : start + COLS]) * scale).astype(BF16)
            lane = lax.broadcasted_iota(jnp.int32, (rows, PAIR), 1)
            for part in range(COLS // PAIR):
                both = query[:, part * PAIR : (part + 1) * PAIR]
                pair = start // PAIR + part
                none = jnp.zeros_like(both)
                self.write[f"Q{q}"][pair, :rows, :] = jnp.where(lane < HEAD_DIM, both, none)
                self.write[f"Q{q}"][pair, rows:, :] = jnp.where(lane < HEAD_DIM, none, both)
        near = dot(self.ref("adjacency")[...], self.tags_of("q", q), 1, 1).astype(BF16)
        self.write[f"G{q}"][...] = jnp.concatenate([near, near], axis=1)

    def project_keys(self, b, root):
        cells = self.write["cells"][: self.cells[b], :]
        for start in range(0, self.width, COLS):
            part = slice(self.width + start, self.width + start + COLS)
            self.write[f"K{b}"][:, start : start + COLS] = (dot(cells, self.w[:, part]) * root).astype(BF16)

    def project_values(self, b, root):
        cells = self.write["cells"][: self.cells[b], :]
        ones = jnp.ones((self.pairs, VAL_ROWS - PAIR, self.cells[b]), BF16)
        self.write[f"V{b}"][:, PAIR:, :] = ones
        for start in range(0, self.width, COLS):
            part = slice(2 * self.width + start, 2 * self.width + start + COLS)
            values = (dot(cells, self.w[:, part]) * root).astype(BF16).T
            for i in range(COLS // PAIR):
                rows = values[i * PAIR : (i + 1) * PAIR]
                self.write[f"V{b}"][start // PAIR + i, :PAIR, :] = rows

    def attend_all(self):
        source = {q: self.read for q in self.touched if f"acc{q}" in self.held}
        before = None
        for turn, (q, b) in enumerate(self.attend):
            after = self.start_turn(q, b, source.get(q), turn % 2)
            source[q] = self.write
            for pair in range(self.pairs):
                self.weigh(after, pair)
                if before is not None:
                    self.add_values(before, pair)
            before = after
        for pair in range(self.pairs):
            self.add_values(before, pair)

    def start_turn(self, q, b, before, slot):
        cells = self.cells[b]
        bias_ref = self.write["bias"].at[slot, :cells]
        bias_ref[...] = (dot(self.tags_of("k", b), self.ref(f"G{q}")[...]) - 1.0) * -MASKED
        return (q, b, before, bias_ref, self.write["weights"].at[slot, :, :cells], {})

    def weigh(self, turn, pair):
        q, b, before, bias_ref, weight_ref, factors = turn
        keys = self.ref(f"K{b}")[:, pair * PAIR : (pair + 1) * PAIR]
        scores = dot(keys, self.ref(f"Q{q}")[pair], 1, 1) + bias_ref[...]
        top = jnp.max(scores, axis=0, keepdims=True)
        if before is not None:
            last = before[f"top{q}"][pair : pair + 1, :]
            top = jnp.maximum(top, last)
            factors[pair] = jnp.exp2(last - top)
        weight_ref[pair] = jnp.exp2(scores - top).astype(BF16)
        self.write[f"top{q}"][pair : pair + 1, :] = top

    def add_values(self, turn, pair):
        q, b, before, _, weight_ref, factors = turn
        half = self.rows[q]
        acc_ref = self.write[f"acc{q}"]
        summed = dot(self.ref(f"V{b}")[pair], weight_ref[pair])
        even, odd = summed[:HEAD_DIM, :half], summed[HEAD_DIM:PAIR, half:]
        both = jnp.concatenate([even, odd], axis=1)
        total = summed[PAIR : PAIR + ACC_ROWS - HEAD_DIM]
        if before is not None:
            both = both + before[f"acc{q}"][pair, :HEAD_DIM, :] * factors[pair]
            total = total + before[f"acc{q}"][pair, HEAD_DIM:, :] * factors[pair]
        acc_ref[pair, :HEAD_DIM, :] = both
        acc_ref[pair, HEAD_DIM:, :] = total

    def project_out(self, q):
        half = self.rows[q]
        acc_ref, att_ref = self.write[f"acc{q}"], self.write["attended"]
        for pair in range(self.pairs):
            total = acc_ref[pair, HEAD_DIM : HEAD_DIM + 1, :]
            part = (acc_ref[pair, :HEAD_DIM, :] / total).astype(BF16)
            row = pair * PAIR
            att_ref[row : row + HEAD_DIM, :] = part[:, :half]
            att_ref[row + HEAD_DIM : row + PAIR, :] = part[:, half:]
        attended = att_ref[...].T
        for start in range(0, self.width, COLS):
            out = dot(attended, self.read["w_out"][:, start : start + COLS]).astype(BF16)
            self.write[f"out{q}"][:, start : start + COLS] = out

    def call(self, env, name):
        vmem = pl.BlockSpec(memory_space=pltpu.VMEM)
        hbm = pl.BlockSpec(memory_space=pltpu.HBM)
        operands = [env[n] for n in self.ins]
        out_shape = [jax.ShapeDtypeStruct(*shape) for shape in self.outs.values()]
        out_specs = [vmem] * len(out_shape)
        rows = max(self.rows.values())
        scratch = [pltpu.VMEM(*shape) for shape in self.scratch.values()]
        scratch += [
            pltpu.VMEM((max(self.block, rows), self.width), BF16),
            pltpu.VMEM((2, self.block, 2 * rows), F32),
            pltpu.VMEM((2, self.pairs, self.block, 2 * rows), BF16),
        ]
        if self.finish:
            scratch.append(pltpu.VMEM((self.width, rows), BF16))
        if self.fetch:
            shape = (self.width, 3 * self.width)
            out_shape += [jax.ShapeDtypeStruct((self.tiles, self.tiles), BF16), pltpu.VMEM(shape, BF16)]
            out_specs += [vmem, vmem]
            scratch += [
                pltpu.VMEM(env["gain_hbm"].shape, F32),
                pltpu.VMEM((self.tiles, self.tiles), jnp.int32),
                pltpu.SemaphoreType.DMA((5,)),
            ]
        flops = 2 * self.width * (
            2 * sum(self.cells[b] for b in self.blocks) * self.width
            + (len(self.queries) + self.finish * len(self.touched)) * rows * self.width
            + 8 * sum(self.cells[b] for _, b in self.attend) * rows
        )
        outs = pl.pallas_call(
            self.body,
            out_shape=tuple(out_shape),
            in_specs=[hbm if n.endswith("_hbm") else vmem for n in self.ins],
            out_specs=tuple(out_specs),
            scratch_shapes=scratch,
            compiler_params=pltpu.CompilerParams(vmem_limit_bytes=16 * 1024 * 1024),
            cost_estimate=pl.CostEstimate(flops=flops, bytes_accessed=1 << 23, transcendentals=0),
            name=name,
        )(*operands)
        env.update(zip(list(self.outs) + ["adjacency", "w"] * self.fetch, outs))


def on_device(cells_in, gain, w_qkv, w_out, tile_of_cell, tile_adjacent):
    genes, cell_dev, width = cells_in.shape
    head_devs, cell_devs = lax.axis_size("heads"), lax.axis_size("cells")
    sets = cell_devs // genes
    half = genes // 2
    gene = lax.rem(lax.axis_index("cells"), genes)
    same = [[s * genes + g for s in range(sets)] for g in range(genes)]

    def over_cells(value, step):
        return lax.ppermute(value, "cells", [(i, i ^ step) for i in range(cell_devs)])

    def over_heads(value, step):
        return lax.ppermute(value, "heads", [(i, i ^ step) for i in range(head_devs)])

    tags = jnp.broadcast_to(tile_of_cell.astype(BF16)[:, None], (cell_dev, TAG))

    def piece_for(k):
        rows = lax.dynamic_index_in_dim(cells_in, gene ^ k, 0, keepdims=False)
        return jnp.concatenate([rows, tags], axis=1)

    order = [4, 1, 2, 0, 6, 5, 7, 3] if genes == 8 else list(range(genes))
    arrived = [over_cells(piece_for(k), k) if k else piece_for(0) for k in order]
    env = {"w_out": w_out}
    held = {"w_hbm": w_qkv, "gain_hbm": gain.reshape(-1, TAG), "adjacency_hbm": tile_adjacent}
    for name, value in held.items():
        env[name] = pltpu.with_memory_space_constraint(value, pltpu.HBM)
    pieces = {}
    rows = half * cell_dev

    def spread(group, own, beside):
        env[f"own{group}"] = own
        pieces["q", group] = [(f"own{group}", 0, rows)]
        held = own
        if sets > 1:
            held = lax.all_gather(own, "cells", axis=0, axis_index_groups=same, tiled=True)
        for step in range(0, head_devs, 2):
            env[f"chunk{group}{step}"] = over_heads(held, step) if step else held
            if step in beside:
                env[f"beside{group}{step}"] = over_heads(env[f"chunk{group}{step}"], 1)

    first = jnp.concatenate(arrived[:half], 0)
    steps = range(0, head_devs, 2)
    spread(0, first, steps)
    if sets == 1 and head_devs == 4:
        blocks = [["own0"], ["beside00", "own1"], ["beside10", "chunk02"], ["beside02", "chunk12"], ["beside12"]]
        for b, names in enumerate(blocks):
            pieces["k", b] = [(name, 0, rows) for name in names]
        Stage(env, pieces, [0], [0], [(0, 0)], fetch=True, keep=[0]).call(env, "first_group")
        env["w"], *late = lax.optimization_barrier((env["w"], *arrived[half:]))
        spread(1, jnp.concatenate(late, 0), [0])
        attend = [(0, 1), (1, 0), (1, 1), (0, 2), (1, 2)]
        Stage(env, pieces, [1], [1, 2], attend).call(env, "second_group")
        env["chunk12"], env["top1"] = lax.optimization_barrier((env["chunk12"], env["top1"]))
        env["beside12"] = over_heads(env["chunk12"], 1)
        Stage(env, pieces, [], [3], [(0, 3), (1, 3)]).call(env, "far")
        Stage(env, pieces, [], [4], [(0, 4), (1, 4)], finish=True).call(env, "last")
    else:
        spread(1, jnp.concatenate(arrived[half:], 0), steps)
        names = [f"{kind}{group}{step}" for group in range(2) for step in steps for kind in ("chunk", "beside")]
        for b, (name, s) in enumerate((name, s) for name in names for s in range(sets)):
            pieces["k", b] = [(name, s * rows, rows)]
        last = len(names) * sets - 1
        for b in range(last + 1):
            attend = [(0, b), (1, b)]
            stage = Stage(env, pieces, [] if b else [0, 1], [b], attend, fetch=b == 0, finish=b == last)
            stage.call(env, f"block_{b}")
    result = jnp.zeros_like(cells_in)
    for place, k in enumerate(order):
        start = place % half * cell_dev
        piece = env[f"out{place // half}"][start : start + cell_dev]
        piece = over_cells(piece, k) if k else piece
        result = lax.dynamic_update_index_in_dim(result, piece, gene ^ k, 0)
    return result


def solution(mesh):
    return jax.shard_map(
        on_device,
        mesh=mesh,
        in_specs=(P(None, ("heads", "cells"), None), P(), P(), P(), P(("heads", "cells")), P()),
        out_specs=P(None, ("heads", "cells"), None),
        check_vma=False,
    )
```

time: 224 us -> 53.7 us (0.24)
  blocking collectives: 70.4 us -> 0 us
  local copies, waits for them, and re-layouts: 50.1 us -> 2.03 us
  matrix products: 39.4 us -> 0 us
  other arithmetic: 27.6 us -> 0.73 us
  starting transfers between devices: 5.52 us -> 26.7 us
  Pallas kernels: 0 us -> 15 us
  between operations: 14.1 us -> 0.27 us
  waiting for transfers between devices: 13.9 us -> 8.74 us
    dot_general x10 -> x0, matrix products: 39.4 us -> none  [the longest x4 17.7 us: update(): jnp.einsum('ovn,onr->ovr', softmax_weights.astype(jnp.bfloat16), value_ma...]
    all_gather x1 -> x0, blocking collectives: 35.9 us -> none  [on_device(): tiles_all = lax.all_gather(tiles_here, 'cells', axis=0, tiled=True)]
    all_to_all x2 -> x0, blocking collectives: 30.2 us -> none  [the longest x1 19 us: on_device(): lax.all_to_all(attention_output, 'cells', split_axis=1, concat_axis=0, ti...]
    ppermute x0 -> x20, starting transfers between devices: none -> 26.7 us  [the longest x14 24 us: over_cells(): lax.ppermute(value, 'cells', [(i, i ^ step) for i in range(cell_devs)])]
    pallas_call x0 -> x4, Pallas kernels: none -> 15 us  [call(): pl.pallas_call(self.body, out_shape=tuple(out_shape), in_specs=[hbm if n....]
    reduce_sum x5 -> x0, other arithmetic: 14.3 us -> none  [the longest x4 13 us: update(): total = total * factor + jnp.sum(softmax_weights, axis=-1)]
    all_gather x1 -> x0, waiting for transfers between devices: 13.9 us -> none  [on_device(): rows_all = lax.all_gather(normed, 'heads', axis=1, tiled=True)]
    gather x5 -> x0, local copies, waits for them, and re-layouts: 12.8 us -> none  [the longest x4 9.31 us: update(): allowed = jnp.take(rowtile, key_tiles, axis=1) > 0]
  transfers between devices with their start and end apart: 2 -> 20, of which waited for: 1 -> 7; matrix products, arithmetic and copies ran while one was open for 8% -> 0% of each run, Pallas kernels for 0% -> 24%
where the time goes in v4:
time: 53.7 us; the launch traced here: 53.5 us
  starting transfers between devices  26.7 us (50%)
  Pallas kernels  15 us (28%)
  waiting for transfers between devices  8.74 us (16%)
  local copies, waits for them, and re-layouts  2.03 us (4%)
  other arithmetic  0.73 us (1%)
    ppermute x14, starting transfers between devices, over_cells(): lax.ppermute(value, 'cells', [(i, i ^ step) for i in range(cell_devs)])  24 us
    pallas_call x4, Pallas kernels, call(): pl.pallas_call(self.body, out_shape=tuple(out_shape), in_specs=[hbm if n....  15 us
    ppermute x14, waiting for transfers between devices, over_cells(): lax.ppermute(value, 'cells', [(i, i ^ step) for i in range(cell_devs)])  5.97 us
    ppermute x6, waiting for transfers between devices, over_heads(): lax.ppermute(value, 'heads', [(i, i ^ step) for i in range(head_devs)])  2.77 us
    ppermute x6, starting transfers between devices, over_heads(): lax.ppermute(value, 'heads', [(i, i ^ step) for i in range(head_devs)])  2.68 us
    squeeze x1, local copies, waits for them, and re-layouts, piece_for(): rows = lax.dynamic_index_in_dim(cells_in, gene ^ k, 0, keepdims=False)  1.1 us
  transfers between devices with their start and end apart: 20, of which 7 were waited for; matrix products, arithmetic and copies ran while one was open for 0% of the time, Pallas kernels for 24%

profile of v4, /device:TPU:0, one launch (start us, length us, event | category | flops | bytes accessed | tf_op | source)
XLA Modules:
  0.0 53.5 jit_solution(17505452674582047306)
XLA Ops:
  0.0 0.7 %convert_element_type.3 = bf16[32]{0:T(256)(128)(2,1)S(1)} convert(s32[32]{0:T(128)} %param.10) | non-fusion elementwise | flops 32 | bytes 192 | tf_op jit(solution)/shard_map/convert_element_type | solution.py:301
  0.7 1.1 %dynamic-slice_bitcast_fusion = (bf16[32,1024]{1,0:T(8,128)(2,1)S(1)}, bf16[32,1024]{1,0:T(8,128)(2,1)S(1)}, bf16[32,1024]{1,0:T(8,128)(2,1)S(1)}, bf16[32,1024]...) fusion(bf16[8,32,1024]{2,1,0:T(8,128)(2,1)} %param.6, ...), kind=kLoop, calls=%fused_computation.16 | loop fusion | bytes 1048608 | tf_op jit(solution)/shard_map/jit(dynamic_index_in_dim)/squeeze | solution.py:304
  1.8 0.1 broadcast_in_dim.35
  1.9 4.1 %collective-permute-start = (bf16[32,1152]{1,0:T(8,128)(2,1)S(1)}, bf16[32,1152]{1,0:T(8,128)(2,1)S(1)}, u32[]{:S(2)}, u32[]{:S(2)}) collective-permute-start(bf16[32,1152]{1,0:T(8,128)(2,1)S(1)} %get-tuple-element.80), channel_id=1, source_target_pairs={{0,4},{1,5},{2,6},{3,7},{4,0},{5,1},{6,2},{7,3},{8,12},{9,13},{10,... | collective-permute-start | bytes 221192 | tf_op jit(solution)/shard_map/ppermute | solution.py:296
  6.0 1.5 %collective-permute-start.1 = (bf16[32,1152]{1,0:T(8,128)(2,1)S(1)}, bf16[32,1152]{1,0:T(8,128)(2,1)S(1)}, u32[]{:S(2)}, u32[]{:S(2)}) collective-permute-start(bf16[32,1152]{1,0:T(8,128)(2,1)S(1)} %get-tuple-element.75), channel_id=1, source_target_pairs={{0,1},{1,0},{2,3},{3,2},{4,5},{5,4},{6,7},{7,6},{8,9},{9,8},{10,11... | collective-permute-start | bytes 221192 | tf_op jit(solution)/shard_map/ppermute | solution.py:296
  7.5 1.6 %collective-permute-start.2 = (bf16[32,1152]{1,0:T(8,128)(2,1)S(1)}, bf16[32,1152]{1,0:T(8,128)(2,1)S(1)}, u32[]{:S(2)}, u32[]{:S(2)}) collective-permute-start(bf16[32,1152]{1,0:T(8,128)(2,1)S(1)} %get-tuple-element.76), channel_id=1, source_target_pairs={{0,2},{1,3},{2,0},{3,1},{4,6},{5,7},{6,4},{7,5},{8,10},{9,11},{10,... | collective-permute-start | bytes 221192 | tf_op jit(solution)/shard_map/ppermute | solution.py:296
  9.1 0.2 collective-permute-start.4
  9.3 1.6 %collective-permute-start.5 = (bf16[32,1152]{1,0:T(8,128)(2,1)S(1)}, bf16[32,1152]{1,0:T(8,128)(2,1)S(1)}, u32[]{:S(2)}, u32[]{:S(2)}) collective-permute-start(bf16[32,1152]{1,0:T(8,128)(2,1)S(1)} %get-tuple-element.78), channel_id=1, source_target_pairs={{0,5},{1,4},{2,7},{3,6},{4,1},{5,0},{6,3},{7,2},{8,13},{9,12},{10,... | collective-permute-start | bytes 221192 | tf_op jit(solution)/shard_map/ppermute | solution.py:296
  10.9 0.0 collective-permute-done
  11.0 5.0 %collective-permute-start.6 = (bf16[32,1152]{1,0:T(8,128)(2,1)S(1)}, bf16[32,1152]{1,0:T(8,128)(2,1)S(1)}, u32[]{:S(2)}, u32[]{:S(2)}) collective-permute-start(bf16[32,1152]{1,0:T(8,128)(2,1)S(1)} %get-tuple-element.79), channel_id=1, source_target_pairs={{0,7},{1,6},{2,5},{3,4},{4,3},{5,2},{6,1},{7,0},{8,15},{9,14},{10,... | collective-permute-start | bytes 221192 | tf_op jit(solution)/shard_map/ppermute | solution.py:296
  15.9 0.0 collective-permute-done.1
  15.9 0.0 collective-permute-start.7
  15.9 0.0 collective-permute-done.2
  16.0 1.6 %collective-permute-start.9 = (bf16[128,1152]{1,0:T(8,128)(2,1)S(1)}, bf16[128,1152]{1,0:T(8,128)(2,1)S(1)}, u32[]{:S(2)}, u32[]{:S(2)}) collective-permute-start(bf16[128,1152]{1,0:T(8,128)(2,1)S(1)} %maximum_maximum_fusion.refs_2_.refs_9_), channel_id=1, source_target_pairs={{0,16},{8,24},{16,0},{24,8},{1,17},{9,25},{17,1},{25,9},{2,18},{10... | collective-permute-start | bytes 884744 | tf_op jit(solution)/shard_map/ppermute | solution.py:299
  17.5 4.6 %first_group.1 = (bf16[8,256,128]{2,1,0:T(8,128)(2,1)S(1)}, bf16[256,256]{1,0:T(8,128)(2,1)S(1)}, f32[8,72,256]{2,1,0:T(8,128)S(1)}, f32[8,256]{1,0:T(8,128)S(1)...) custom-call(s32[256,256]{1,0:T(8,128)} %refs_0_.1, ...), custom_call_target="tpu_custom_call" | custom-call | flops 1073741824 | bytes 8388608 | tf_op jit(solution)/shard_map/first_group/pallas_call | solution.py:274
  22.1 0.0 collective-permute-done.4
  22.1 0.0 collective-permute-done.5
  22.1 0.0 collective-permute-done.6
  22.1 0.0 collective-permute-done.7
  22.2 0.1 collective-permute-start.8
  22.3 0.5 collective-permute-start.3
  22.8 0.5 %collective-permute-start.11 = (bf16[128,1152]{1,0:T(8,128)(2,1)S(1)}, bf16[128,1152]{1,0:T(8,128)(2,1)S(1)}, u32[]{:S(2)}, u32[]{:S(2)}) collective-permute-start(bf16[128,1152]{1,0:T(8,128)(2,1)S(1)} %constant_dynamic-update-slice_fusion.refs_10_), channel_id=1, source_target_pairs={{0,16},{8,24},{16,0},{24,8},{1,17},{9,25},{17,1},{25,9},{2,18},{10... | collective-permute-start | bytes 884744 | tf_op jit(solution)/shard_map/ppermute | solution.py:299
  23.3 0.2 collective-permute-done.9.refs_8_
  23.5 0.0 collective-permute-start.10
  23.5 0.3 collective-permute-done.8.refs_7_
  23.9 0.4 collective-permute-done.3.refs_6_
  24.3 5.7 %second_group.1 = (bf16[8,256,128]{2,1,0:T(8,128)(2,1)S(1)}, bf16[256,256]{1,0:T(8,128)(2,1)S(1)}, f32[8,72,256]{2,1,0:T(8,128)S(1)}, f32[8,256]{1,0:T(8,128)S(1...) custom-call(bf16[256,256]{1,0:T(8,128)(2,1)S(1)} %get-tuple-element.32.refs_0_, ...), custom_call_target="tpu_custom_call" | custom-call | flops 4831838208 | bytes 8388608 | tf_op jit(solution)/shard_map/second_group/pallas_call | solution.py:274
  30.0 0.0 copy-start
  30.0 1.8 %collective-permute-done.11.refs_7_ = bf16[128,1152]{1,0:T(8,128)(2,1)S(1)} collective-permute-done((bf16[128,1152]{1,0:T(8,128)(2,1)S(1)}, bf16[128,1152]{1,0:T(8,128)(2,1)S(1)}, u32[]{:S(2)}, u32[]{:S(2)}) %collective-permute-start.11) | collective-permute-done | bytes 294944 | tf_op jit(solution)/shard_map/ppermute | solution.py:299
  31.8 0.0 collective-permute-start.12
  31.8 0.0 collective-permute-done.10.refs_6_
  31.8 2.6 %far.1 = (f32[8,72,256]{2,1,0:T(8,128)S(1)}, f32[8,256]{1,0:T(8,128)S(1)}, f32[8,72,256]{2,1,0:T(8,128)S(1)}, f32[8,256]{1,0:T(8,128)S(1)}) custom-call(bf16[256,256]{1,0:T(8,128)(2,1)S(1)} %get-tuple-element.32.refs_0_, bf16[256,256]{1,0:T(8,128)(2,1)S(1)} %get-tuple-element.45.refs_1_, bf16[8,256,128]{2,1,0:T(8,128)(2,1)S(1)} %get-tuple-element.34.refs_2_, ...), custom_call_target="tpu_custom_call" | custom-call | flops 2147483648 | bytes 8388608 | tf_op jit(solution)/shard_map/far/pallas_call | solution.py:274
  34.4 0.0 collective-permute-done.12.refs_6_
  34.5 0.0 copy-done
  34.5 2.1 %last.1 = (bf16[128,1024]{1,0:T(8,128)(2,1)S(1)}, bf16[128,1024]{1,0:T(8,128)(2,1)S(1)}) custom-call(bf16[256,256]{1,0:T(8,128)(2,1)S(1)} %get-tuple-element.32.refs_0_, bf16[256,256]{1,0:T(8,128)(2,1)S(1)} %get-tuple-element.45.refs_1_, bf16[8,256,128]{2,1,0:T(8,128)(2,1)S(1)} %get-tuple-element.34.refs_2_, ...), custom_call_target="tpu_custom_call" | custom-call | flops 1610612736 | bytes 8388608 | tf_op jit(solution)/shard_map/last/pallas_call | solution.py:274
  36.6 0.8 %collective-permute-start.13 = (bf16[32,1024]{1,0:T(8,128)(2,1)S(1)}, bf16[32,1024]{1,0:T(8,128)(2,1)S(1)}, u32[]{:S(2)}, u32[]{:S(2)}) collective-permute-start(bf16[32,1024]{1,0:T(8,128)(2,1)S(1)} %get-tuple-element.73), channel_id=1, source_target_pairs={{0,4},{1,5},{2,6},{3,7},{4,0},{5,1},{6,2},{7,3},{8,12},{9,13},{10,... | collective-permute-start | bytes 196616 | tf_op jit(solution)/shard_map/ppermute | solution.py:296
  37.4 1.1 %collective-permute-start.14 = (bf16[32,1024]{1,0:T(8,128)(2,1)S(1)}, bf16[32,1024]{1,0:T(8,128)(2,1)S(1)}, u32[]{:S(2)}, u32[]{:S(2)}) collective-permute-start(bf16[32,1024]{1,0:T(8,128)(2,1)S(1)} %get-tuple-element.72), channel_id=1, source_target_pairs={{0,1},{1,0},{2,3},{3,2},{4,5},{5,4},{6,7},{7,6},{8,9},{9,8},{10,11... | collective-permute-start | bytes 196616 | tf_op jit(solution)/shard_map/ppermute | solution.py:296
  38.5 1.7 %collective-permute-start.15 = (bf16[32,1024]{1,0:T(8,128)(2,1)S(1)}, bf16[32,1024]{1,0:T(8,128)(2,1)S(1)}, u32[]{:S(2)}, u32[]{:S(2)}) collective-permute-start(bf16[32,1024]{1,0:T(8,128)(2,1)S(1)} %get-tuple-element.71), channel_id=1, source_target_pairs={{0,2},{1,3},{2,0},{3,1},{4,6},{5,7},{6,4},{7,5},{8,10},{9,11},{10,... | collective-permute-start | bytes 196616 | tf_op jit(solution)/shard_map/ppermute | solution.py:296
  40.3 2.4 %collective-permute-start.16 = (bf16[32,1024]{1,0:T(8,128)(2,1)S(1)}, bf16[32,1024]{1,0:T(8,128)(2,1)S(1)}, u32[]{:S(2)}, u32[]{:S(2)}) collective-permute-start(bf16[32,1024]{1,0:T(8,128)(2,1)S(1)} %get-tuple-element.70), channel_id=1, source_target_pairs={{0,6},{1,7},{2,4},{3,5},{4,2},{5,3},{6,0},{7,1},{8,14},{9,15},{10,... | collective-permute-start | bytes 196616 | tf_op jit(solution)/shard_map/ppermute | solution.py:296
  42.6 0.4 collective-permute-start.17
  43.0 0.4 collective-permute-done.13
  43.5 3.5 %collective-permute-start.18 = (bf16[32,1024]{1,0:T(8,128)(2,1)S(1)}, bf16[32,1024]{1,0:T(8,128)(2,1)S(1)}, u32[]{:S(2)}, u32[]{:S(2)}) collective-permute-start(bf16[32,1024]{1,0:T(8,128)(2,1)S(1)} %get-tuple-element.68), channel_id=1, source_target_pairs={{0,7},{1,6},{2,5},{3,4},{4,3},{5,2},{6,1},{7,0},{8,15},{9,14},{10,... | collective-permute-start | bytes 196616 | tf_op jit(solution)/shard_map/ppermute | solution.py:296
  47.0 0.1 broadcast_in_dim.34
  47.1 0.0 collective-permute-done.14
  47.1 0.1 collective-permute-start.19
  47.2 0.0 collective-permute-done.15
  47.2 0.0 collective-permute-done.16
  47.3 4.3 %collective-permute-done.17 = bf16[32,1024]{1,0:T(8,128)(2,1)S(1)} collective-permute-done((bf16[32,1024]{1,0:T(8,128)(2,1)S(1)}, bf16[32,1024]{1,0:T(8,128)(2,1)S(1)}, u32[]{:S(2)}, u32[]{:S(2)}) %collective-permute-start.17) | collective-permute-done | bytes 65568 | tf_op jit(solution)/shard_map/ppermute | solution.py:296
  51.6 0.0 collective-permute-done.18
  51.6 0.0 copy-start.1
  51.7 1.2 %collective-permute-done.19 = bf16[32,1024]{1,0:T(8,128)(2,1)S(1)} collective-permute-done((bf16[32,1024]{1,0:T(8,128)(2,1)S(1)}, bf16[32,1024]{1,0:T(8,128)(2,1)S(1)}, u32[]{:S(2)}, u32[]{:S(2)}) %collective-permute-start.19) | collective-permute-done | bytes 65568 | tf_op jit(solution)/shard_map/ppermute | solution.py:296
  52.8 0.0 copy-done.1
  52.8 0.6 %bitcast_dynamic-update-slice_fusion = bf16[8,32,1024]{2,1,0:T(8,128)(2,1)} fusion(bf16[8,32,1024]{2,1,0:T(8,128)(2,1)} %copy-done.1, s32[]{:T(128)S(6)} %select_n.41, bf16[32,1024]{1,0:T(8,128)(2,1)S(1)} %collective-permute-done.19), kind=kLoop, calls=%fused_computation.8 | loop fusion | bytes 131076 | tf_op jit(solution)/shard_map/jit(dynamic_update_index_in_dim)/dynamic_update_slice | solution.py:358
  (15 shorter events, 0.2 us)
Async XLA Ops:
  1.9 9.1 %collective-permute-start = (bf16[32,1152]{1,0:T(8,128)(2,1)S(1)}, bf16[32,1152]{1,0:T(8,128)(2,1)S(1)}, u32[]{:S(2)}, u32[]{:S(2)}) collective-permute-start(bf16[32,1152]{1,0:T(8,128)(2,1)S(1)} %get-tuple-element.80), channel_id=1, source_target_pairs={{0,4},{1,5},{2,6},{3,7},{4,0},{5,1},{6,2},{7,3},{8,12},{9,13},{10,... | collective-permute-start | bytes 221192 | tf_op jit(solution)/shard_map/ppermute | solution.py:296
  6.0 9.9 %collective-permute-start.1 = (bf16[32,1152]{1,0:T(8,128)(2,1)S(1)}, bf16[32,1152]{1,0:T(8,128)(2,1)S(1)}, u32[]{:S(2)}, u32[]{:S(2)}) collective-permute-start(bf16[32,1152]{1,0:T(8,128)(2,1)S(1)} %get-tuple-element.75), channel_id=1, source_target_pairs={{0,1},{1,0},{2,3},{3,2},{4,5},{5,4},{6,7},{7,6},{8,9},{9,8},{10,11... | collective-permute-start | bytes 221192 | tf_op jit(solution)/shard_map/ppermute | solution.py:296
  7.5 8.4 %collective-permute-start.2 = (bf16[32,1152]{1,0:T(8,128)(2,1)S(1)}, bf16[32,1152]{1,0:T(8,128)(2,1)S(1)}, u32[]{:S(2)}, u32[]{:S(2)}) collective-permute-start(bf16[32,1152]{1,0:T(8,128)(2,1)S(1)} %get-tuple-element.76), channel_id=1, source_target_pairs={{0,2},{1,3},{2,0},{3,1},{4,6},{5,7},{6,4},{7,5},{8,10},{9,11},{10,... | collective-permute-start | bytes 221192 | tf_op jit(solution)/shard_map/ppermute | solution.py:296
  9.1 13.0 %collective-permute-start.4 = (bf16[32,1152]{1,0:T(8,128)(2,1)S(1)}, bf16[32,1152]{1,0:T(8,128)(2,1)S(1)}, u32[]{:S(2)}, u32[]{:S(2)}) collective-permute-start(bf16[32,1152]{1,0:T(8,128)(2,1)S(1)} %get-tuple-element.77), channel_id=1, source_target_pairs={{0,6},{1,7},{2,4},{3,5},{4,2},{5,3},{6,0},{7,1},{8,14},{9,15},{10,... | collective-permute-start | bytes 221192 | tf_op jit(solution)/shard_map/ppermute | solution.py:296
  9.3 12.8 %collective-permute-start.5 = (bf16[32,1152]{1,0:T(8,128)(2,1)S(1)}, bf16[32,1152]{1,0:T(8,128)(2,1)S(1)}, u32[]{:S(2)}, u32[]{:S(2)}) collective-permute-start(bf16[32,1152]{1,0:T(8,128)(2,1)S(1)} %get-tuple-element.78), channel_id=1, source_target_pairs={{0,5},{1,4},{2,7},{3,6},{4,1},{5,0},{6,3},{7,2},{8,13},{9,12},{10,... | collective-permute-start | bytes 221192 | tf_op jit(solution)/shard_map/ppermute | solution.py:296
  11.0 11.2 %collective-permute-start.6 = (bf16[32,1152]{1,0:T(8,128)(2,1)S(1)}, bf16[32,1152]{1,0:T(8,128)(2,1)S(1)}, u32[]{:S(2)}, u32[]{:S(2)}) collective-permute-start(bf16[32,1152]{1,0:T(8,128)(2,1)S(1)} %get-tuple-element.79), channel_id=1, source_target_pairs={{0,7},{1,6},{2,5},{3,4},{4,3},{5,2},{6,1},{7,0},{8,15},{9,14},{10,... | collective-permute-start | bytes 221192 | tf_op jit(solution)/shard_map/ppermute | solution.py:296
  15.9 6.2 %collective-permute-start.7 = (bf16[32,1152]{1,0:T(8,128)(2,1)S(1)}, bf16[32,1152]{1,0:T(8,128)(2,1)S(1)}, u32[]{:S(2)}, u32[]{:S(2)}) collective-permute-start(bf16[32,1152]{1,0:T(8,128)(2,1)S(1)} %get-tuple-element.74), channel_id=1, source_target_pairs={{0,3},{1,2},{2,1},{3,0},{4,7},{5,6},{6,5},{7,4},{8,11},{9,10},{10,... | collective-permute-start | bytes 221192 | tf_op jit(solution)/shard_map/ppermute | solution.py:296
  16.0 7.5 %collective-permute-start.9 = (bf16[128,1152]{1,0:T(8,128)(2,1)S(1)}, bf16[128,1152]{1,0:T(8,128)(2,1)S(1)}, u32[]{:S(2)}, u32[]{:S(2)}) collective-permute-start(bf16[128,1152]{1,0:T(8,128)(2,1)S(1)} %maximum_maximum_fusion.refs_2_.refs_9_), channel_id=1, source_target_pairs={{0,16},{8,24},{16,0},{24,8},{1,17},{9,25},{17,1},{25,9},{2,18},{10... | collective-permute-start | bytes 884744 | tf_op jit(solution)/shard_map/ppermute | solution.py:299
  22.2 1.6 %collective-permute-start.8 = (bf16[128,1152]{1,0:T(8,128)(2,1)S(1)}, bf16[128,1152]{1,0:T(8,128)(2,1)S(1)}, u32[]{:S(2)}, u32[]{:S(2)}) collective-permute-start(bf16[128,1152]{1,0:T(8,128)(2,1)S(1)} %constant_dynamic-update-slice_fusion.refs_10_), channel_id=1, source_target_pairs={{0,8},{8,0},{16,24},{24,16},{1,9},{9,1},{17,25},{25,17},{2,10},{10... | collective-permute-start | bytes 884744 | tf_op jit(solution)/shard_map/ppermute | solution.py:299
  22.3 2.0 %collective-permute-start.3 = (bf16[128,1152]{1,0:T(8,128)(2,1)S(1)}, bf16[128,1152]{1,0:T(8,128)(2,1)S(1)}, u32[]{:S(2)}, u32[]{:S(2)}) collective-permute-start(bf16[128,1152]{1,0:T(8,128)(2,1)S(1)} %maximum_maximum_fusion.refs_2_.refs_9_), channel_id=1, source_target_pairs={{0,8},{8,0},{16,24},{24,16},{1,9},{9,1},{17,25},{25,17},{2,10},{10... | collective-permute-start | bytes 884744 | tf_op jit(solution)/shard_map/ppermute | solution.py:299
  22.8 9.0 %collective-permute-start.11 = (bf16[128,1152]{1,0:T(8,128)(2,1)S(1)}, bf16[128,1152]{1,0:T(8,128)(2,1)S(1)}, u32[]{:S(2)}, u32[]{:S(2)}) collective-permute-start(bf16[128,1152]{1,0:T(8,128)(2,1)S(1)} %constant_dynamic-update-slice_fusion.refs_10_), channel_id=1, source_target_pairs={{0,16},{8,24},{16,0},{24,8},{1,17},{9,25},{17,1},{25,9},{2,18},{10... | collective-permute-start | bytes 884744 | tf_op jit(solution)/shard_map/ppermute | solution.py:299
  23.5 8.3 %collective-permute-start.10 = (bf16[128,1152]{1,0:T(8,128)(2,1)S(1)}, bf16[128,1152]{1,0:T(8,128)(2,1)S(1)}, u32[]{:S(2)}, u32[]{:S(2)}) collective-permute-start(bf16[128,1152]{1,0:T(8,128)(2,1)S(1)} %collective-permute-done.9.refs_8_), channel_id=1, source_target_pairs={{0,8},{8,0},{16,24},{24,16},{1,9},{9,1},{17,25},{25,17},{2,10},{10... | collective-permute-start | bytes 884744 | tf_op jit(solution)/shard_map/ppermute | solution.py:299
  30.0 4.5 %copy-start = (bf16[1024,1024]{1,0:T(8,128)(2,1)S(1)}, bf16[1024,1024]{1,0:T(8,128)(2,1)}, u32[]{:S(2)}) copy-start(bf16[1024,1024]{1,0:T(8,128)(2,1)} %refs_10_.1) | copy-start | bytes 6291460
  31.8 2.7 %collective-permute-start.12 = (bf16[128,1152]{1,0:T(8,128)(2,1)S(1)}, bf16[128,1152]{1,0:T(8,128)(2,1)S(1)}, u32[]{:S(2)}, u32[]{:S(2)}) collective-permute-start(bf16[128,1152]{1,0:T(8,128)(2,1)S(1)} %collective-permute-done.11.refs_7_), channel_id=1, source_target_pairs={{0,8},{8,0},{16,24},{24,16},{1,9},{9,1},{17,25},{25,17},{2,10},{10... | collective-permute-start | bytes 884744 | tf_op jit(solution)/shard_map/ppermute | solution.py:299
  36.6 6.9 %collective-permute-start.13 = (bf16[32,1024]{1,0:T(8,128)(2,1)S(1)}, bf16[32,1024]{1,0:T(8,128)(2,1)S(1)}, u32[]{:S(2)}, u32[]{:S(2)}) collective-permute-start(bf16[32,1024]{1,0:T(8,128)(2,1)S(1)} %get-tuple-element.73), channel_id=1, source_target_pairs={{0,4},{1,5},{2,6},{3,7},{4,0},{5,1},{6,2},{7,3},{8,12},{9,13},{10,... | collective-permute-start | bytes 196616 | tf_op jit(solution)/shard_map/ppermute | solution.py:296
  37.4 9.6 %collective-permute-start.14 = (bf16[32,1024]{1,0:T(8,128)(2,1)S(1)}, bf16[32,1024]{1,0:T(8,128)(2,1)S(1)}, u32[]{:S(2)}, u32[]{:S(2)}) collective-permute-start(bf16[32,1024]{1,0:T(8,128)(2,1)S(1)} %get-tuple-element.72), channel_id=1, source_target_pairs={{0,1},{1,0},{2,3},{3,2},{4,5},{5,4},{6,7},{7,6},{8,9},{9,8},{10,11... | collective-permute-start | bytes 196616 | tf_op jit(solution)/shard_map/ppermute | solution.py:296
  38.5 8.7 %collective-permute-start.15 = (bf16[32,1024]{1,0:T(8,128)(2,1)S(1)}, bf16[32,1024]{1,0:T(8,128)(2,1)S(1)}, u32[]{:S(2)}, u32[]{:S(2)}) collective-permute-start(bf16[32,1024]{1,0:T(8,128)(2,1)S(1)} %get-tuple-element.71), channel_id=1, source_target_pairs={{0,2},{1,3},{2,0},{3,1},{4,6},{5,7},{6,4},{7,5},{8,10},{9,11},{10,... | collective-permute-start | bytes 196616 | tf_op jit(solution)/shard_map/ppermute | solution.py:296
  40.3 7.0 %collective-permute-start.16 = (bf16[32,1024]{1,0:T(8,128)(2,1)S(1)}, bf16[32,1024]{1,0:T(8,128)(2,1)S(1)}, u32[]{:S(2)}, u32[]{:S(2)}) collective-permute-start(bf16[32,1024]{1,0:T(8,128)(2,1)S(1)} %get-tuple-element.70), channel_id=1, source_target_pairs={{0,6},{1,7},{2,4},{3,5},{4,2},{5,3},{6,0},{7,1},{8,14},{9,15},{10,... | collective-permute-start | bytes 196616 | tf_op jit(solution)/shard_map/ppermute | solution.py:296
  42.6 9.0 %collective-permute-start.17 = (bf16[32,1024]{1,0:T(8,128)(2,1)S(1)}, bf16[32,1024]{1,0:T(8,128)(2,1)S(1)}, u32[]{:S(2)}, u32[]{:S(2)}) collective-permute-start(bf16[32,1024]{1,0:T(8,128)(2,1)S(1)} %get-tuple-element.69), channel_id=1, source_target_pairs={{0,5},{1,4},{2,7},{3,6},{4,1},{5,0},{6,3},{7,2},{8,13},{9,12},{10,... | collective-permute-start | bytes 196616 | tf_op jit(solution)/shard_map/ppermute | solution.py:296
  43.5 8.1 %collective-permute-start.18 = (bf16[32,1024]{1,0:T(8,128)(2,1)S(1)}, bf16[32,1024]{1,0:T(8,128)(2,1)S(1)}, u32[]{:S(2)}, u32[]{:S(2)}) collective-permute-start(bf16[32,1024]{1,0:T(8,128)(2,1)S(1)} %get-tuple-element.68), channel_id=1, source_target_pairs={{0,7},{1,6},{2,5},{3,4},{4,3},{5,2},{6,1},{7,0},{8,15},{9,14},{10,... | collective-permute-start | bytes 196616 | tf_op jit(solution)/shard_map/ppermute | solution.py:296
  47.1 5.7 %collective-permute-start.19 = (bf16[32,1024]{1,0:T(8,128)(2,1)S(1)}, bf16[32,1024]{1,0:T(8,128)(2,1)S(1)}, u32[]{:S(2)}, u32[]{:S(2)}) collective-permute-start(bf16[32,1024]{1,0:T(8,128)(2,1)S(1)} %get-tuple-element.67), channel_id=1, source_target_pairs={{0,3},{1,2},{2,1},{3,0},{4,7},{5,6},{6,5},{7,4},{8,11},{9,10},{10,... | collective-permute-start | bytes 196616 | tf_op jit(solution)/shard_map/ppermute | solution.py:296
  51.6 1.2 %copy-start.1 = (bf16[8,32,1024]{2,1,0:T(8,128)(2,1)}, bf16[8,32,1024]{2,1,0:T(8,128)(2,1)S(1)}, u32[]{:S(2)}) copy-start(bf16[8,32,1024]{2,1,0:T(8,128)(2,1)S(1)} %bitcast_dynamic-update-slice_fusion.1) | copy-start | bytes 1572868

commit v5 on v4

--- a/solution.py
+++ b/solution.py
@@ -28,6 +28,72 @@
     lane = lax.broadcasted_iota(jnp.int32, tags.shape, 1).astype(F32)
     parts = [(tags == lane + start).astype(F32) for start in range(0, count, TAG)]
     return jnp.concatenate(parts, axis=1).astype(BF16)
+
+
+def pack_kernel(order, x_hbm, gain_hbm, tile_hbm, *refs):
+    out_refs, (cells_ref, gain_ref, tile_ref, sems) = refs[: len(order)], refs[len(order) :]
+    genes, rows, width = cells_ref.shape
+    gene = lax.rem(lax.axis_index("cells"), genes)
+    moves = [(gain_hbm, gain_ref), (tile_hbm, tile_ref)]
+    moves += [(x_hbm.at[gene ^ k], cells_ref.at[i]) for i, k in enumerate(order)]
+    copies = [pltpu.make_async_copy(*move, sems.at[i]) for i, move in enumerate(moves)]
+    for copy in copies:
+        copy.start()
+    for copy in copies:
+        copy.wait()
+    gain = gain_ref[...]
+    row = lax.broadcasted_iota(jnp.int32, (rows, rows), 0)
+    column = lax.broadcasted_iota(jnp.int32, (rows, rows), 1)
+    tiles = jnp.where(row == column, tile_ref[...].astype(F32), 0.0)
+    tags = jnp.broadcast_to(jnp.sum(tiles, axis=1, keepdims=True), (rows, TAG)).astype(BF16)
+    for i in range(genes):
+        x32 = cells_ref[i].astype(F32)
+        mean = jnp.mean(x32 * x32, axis=-1, keepdims=True)
+        out_refs[i][:, :width] = (x32 * lax.rsqrt(mean + 1e-05) * gain).astype(BF16)
+        out_refs[i][:, width:] = tags
+
+
+def pack(cells_in, gain, tiles, order):
+    genes, rows, width = cells_in.shape
+    operands = [cells_in, gain.reshape(1, width), tiles.reshape(1, rows)]
+    operands = [pltpu.with_memory_space_constraint(value, pltpu.HBM) for value in operands]
+    return pl.pallas_call(
+        lambda *refs: pack_kernel(order, *refs),
+        out_shape=[jax.ShapeDtypeStruct((rows, width + TAG), BF16)] * genes,
+        in_specs=[pl.BlockSpec(memory_space=pltpu.HBM)] * 3,
+        out_specs=[pl.BlockSpec(memory_space=pltpu.VMEM)] * genes,
+        scratch_shapes=[
+            pltpu.VMEM(cells_in.shape, BF16),
+            pltpu.VMEM((1, width), F32),
+            pltpu.VMEM((1, rows), jnp.int32),
+            pltpu.SemaphoreType.DMA((genes + 2,)),
+        ],
+        compiler_params=pltpu.CompilerParams(vmem_limit_bytes=4 * 1024 * 1024),
+        name="pack",
+    )(*operands)
+
+
+def unpack_kernel(order, *refs):
+    piece_refs, (out_hbm, sems) = refs[: len(order)], refs[len(order) :]
+    gene = lax.rem(lax.axis_index("cells"), len(order))
+    copies = []
+    for i, (k, piece_ref) in enumerate(zip(order, piece_refs)):
+        copies.append(pltpu.make_async_copy(piece_ref, out_hbm.at[gene ^ k], sems.at[i]))
+        copies[-1].start()
+    for copy in copies:
+        copy.wait()
+
+
+def unpack(pieces, order, shape):
+    return pl.pallas_call(
+        lambda *refs: unpack_kernel(order, *refs),
+        out_shape=jax.ShapeDtypeStruct(shape, BF16),
+        in_specs=[pl.BlockSpec(memory_space=pl.ANY)] * len(order),
+        out_specs=pl.BlockSpec(memory_space=pltpu.HBM),
+        scratch_shapes=[pltpu.SemaphoreType.DMA((len(order),))],
+        compiler_params=pltpu.CompilerParams(vmem_limit_bytes=1024 * 1024),
+        name="unpack",
+    )(*pieces)
 
 
 class Stage:
@@ -41,7 +107,7 @@
         self.cells = {b: sum(size for _, _, size in pieces["k", b]) for b in {b for _, b in attend}}
         self.block = max(self.cells.values())
         self.touched = sorted({q for q, _ in attend})
-        ins = {"w_hbm", "gain_hbm", "adjacency_hbm"} if fetch else {"w"}
+        ins = {"w_hbm", "adjacency_hbm"} if fetch else {"w"}
         if queries and not fetch:
             ins.add("adjacency")
         for group in [("q", q) for q in queries] + [("k", b) for b in {b for _, b in attend}]:
@@ -79,23 +145,23 @@
     def body(self, *refs):
         count = len(self.ins)
         names = list(self.outs) + ["adjacency", "w"] * self.fetch + list(self.scratch)
-        more = ["cells", "bias", "weights"] + ["attended"] * self.finish
-        more += ["gain", "pairs_allowed", "sems"] * self.fetch
+        more = ["bias", "weights"] + ["attended"] * self.finish
+        more += ["pairs_allowed", "sems"] * self.fetch
         self.read = dict(zip(self.ins, refs[:count]))
         self.write = dict(zip(names + more, refs[count:]))
         self.w = self.write["w"] if self.fetch else self.read["w"]
         if self.fetch:
             self.start_copies()
         for b in self.blocks:
-            root = self.load_cells("k", b)
+            cells = self.load_cells("k", b)
             if self.fetch and b == self.blocks[0]:
-                self.take_weights(1)
-            self.project_keys(b, root)
+                self.copies[1].wait()
+            self.project_keys(b, cells)
             if self.fetch and b == self.blocks[0]:
-                self.take_weights(2)
-            self.project_values(b, root)
+                self.copies[2].wait()
+            self.project_values(b, cells)
         if self.fetch:
-            self.take_weights(0)
+            self.copies[0].wait()
         for q in self.queries:
             self.project_queries(q)
         self.attend_all()
@@ -112,8 +178,7 @@
 
     def start_copies(self):
         width, sems = self.width, self.write["sems"]
-        moves = [(self.read["gain_hbm"], self.write["gain"])]
-        moves += [(self.read["adjacency_hbm"], self.write["pairs_allowed"])]
+        moves = [(self.read["adjacency_hbm"], self.write["pairs_allowed"])]
         for start in (width, 2 * width, 0):
             part = slice(start, start + width)
             moves.append((self.read["w_hbm"].at[:, part], self.write["w"].at[:, part]))
@@ -121,29 +186,12 @@
         for copy in copies:
             copy.start()
         copies[0].wait()
-        self.copies = {1: copies[2], 2: copies[3], 0: copies[4]}
-        self.gain = self.write["gain"][...].T
-        copies[1].wait()
+        self.copies = {1: copies[1], 2: copies[2], 0: copies[3]}
         allowed = self.write["pairs_allowed"][...]
         self.write["adjacency"][...] = allowed.astype(F32).astype(BF16)
 
-    def take_weights(self, part):
-        self.copies[part].wait()
-        columns = slice(part * self.width, (part + 1) * self.width)
-        size = self.gain.shape[0]
-        for i in range(self.width // size):
-            rows = slice(i * size, (i + 1) * size)
-            scaled = self.w[rows, columns].astype(F32) * self.gain[:, i : i + 1]
-            self.w[rows, columns] = scaled.astype(BF16)
-
     def load_cells(self, kind, index):
-        start, roots = 0, []
-        for rows in self.rows_of(kind, index, slice(0, self.width)):
-            self.write["cells"][start : start + rows.shape[0], :] = rows
-            start += rows.shape[0]
-            x32 = rows.astype(F32)
-            roots.append(lax.rsqrt(jnp.mean(x32 * x32, axis=-1, keepdims=True) + 1e-05))
-        return jnp.concatenate(roots, axis=0)
+        return jnp.concatenate(self.rows_of(kind, index, slice(0, self.width)), axis=0)
 
     def tags_of(self, kind, index):
         tags = jnp.concatenate(self.rows_of(kind, index, slice(self.width, None)), axis=0)
@@ -151,10 +199,9 @@
 
     def project_queries(self, q):
         rows = self.rows[q]
-        scale = self.load_cells("q", q) * SCALE
-        cells = self.write["cells"][:rows, :]
+        cells = self.load_cells("q", q)
         for start in range(0, self.width, COLS):
-            query = (dot(cells, self.w[:, start : start + COLS]) * scale).astype(BF16)
+            query = (dot(cells, self.w[:, start : start + COLS]) * SCALE).astype(BF16)
             lane = lax.broadcasted_iota(jnp.int32, (rows, PAIR), 1)
             for part in range(COLS // PAIR):
                 both = query[:, part * PAIR : (part + 1) * PAIR]
@@ -165,19 +212,17 @@
         near = dot(self.ref("adjacency")[...], self.tags_of("q", q), 1, 1).astype(BF16)
         self.write[f"G{q}"][...] = jnp.concatenate([near, near], axis=1)
 
-    def project_keys(self, b, root):
-        cells = self.write["cells"][: self.cells[b], :]
+    def project_keys(self, b, cells):
         for start in range(0, self.width, COLS):
             part = slice(self.width + start, self.width + start + COLS)
-            self.write[f"K{b}"][:, start : start + COLS] = (dot(cells, self.w[:, part]) * root).astype(BF16)
-
-    def project_values(self, b, root):
-        cells = self.write["cells"][: self.cells[b], :]
+            self.write[f"K{b}"][:, start : start + COLS] = dot(cells, self.w[:, part]).astype(BF16)
+
+    def project_values(self, b, cells):
         ones = jnp.ones((self.pairs, VAL_ROWS - PAIR, self.cells[b]), BF16)
         self.write[f"V{b}"][:, PAIR:, :] = ones
         for start in range(0, self.width, COLS):
             part = slice(2 * self.width + start, 2 * self.width + start + COLS)
-            values = (dot(cells, self.w[:, part]) * root).astype(BF16).T
+            values = dot(cells, self.w[:, part]).astype(BF16).T
             for i in range(COLS // PAIR):
                 rows = values[i * PAIR : (i + 1) * PAIR]
                 self.write[f"V{b}"][start // PAIR + i, :PAIR, :] = rows
@@ -251,7 +296,6 @@
         rows = max(self.rows.values())
         scratch = [pltpu.VMEM(*shape) for shape in self.scratch.values()]
         scratch += [
-            pltpu.VMEM((max(self.block, rows), self.width), BF16),
             pltpu.VMEM((2, self.block, 2 * rows), F32),
             pltpu.VMEM((2, self.pairs, self.block, 2 * rows), BF16),
         ]
@@ -262,9 +306,8 @@
             out_shape += [jax.ShapeDtypeStruct((self.tiles, self.tiles), BF16), pltpu.VMEM(shape, BF16)]
             out_specs += [vmem, vmem]
             scratch += [
-                pltpu.VMEM(env["gain_hbm"].shape, F32),
                 pltpu.VMEM((self.tiles, self.tiles), jnp.int32),
-                pltpu.SemaphoreType.DMA((5,)),
+                pltpu.SemaphoreType.DMA((4,)),
             ]
         flops = 2 * self.width * (
             2 * sum(self.cells[b] for b in self.blocks) * self.width
@@ -289,7 +332,6 @@
     head_devs, cell_devs = lax.axis_size("heads"), lax.axis_size("cells")
     sets = cell_devs // genes
     half = genes // 2
-    gene = lax.rem(lax.axis_index("cells"), genes)
     same = [[s * genes + g for s in range(sets)] for g in range(genes)]
 
     def over_cells(value, step):
@@ -298,16 +340,12 @@
     def over_heads(value, step):
         return lax.ppermute(value, "heads", [(i, i ^ step) for i in range(head_devs)])
 
-    tags = jnp.broadcast_to(tile_of_cell.astype(BF16)[:, None], (cell_dev, TAG))
-
-    def piece_for(k):
-        rows = lax.dynamic_index_in_dim(cells_in, gene ^ k, 0, keepdims=False)
-        return jnp.concatenate([rows, tags], axis=1)
-
-    order = [4, 1, 2, 0, 6, 5, 7, 3] if genes == 8 else list(range(genes))
-    arrived = [over_cells(piece_for(k), k) if k else piece_for(0) for k in order]
+    order = [4, 1, 3, 0, 5, 7, 6, 2] if genes == 8 else list(range(genes))
+    back = [0, 4, 1, 2, 6, 5, 7, 3] if genes == 8 else order
+    packed = pack(cells_in, gain, tile_of_cell, order)
+    arrived = [over_cells(piece, k) if k else piece for piece, k in zip(packed, order)]
     env = {"w_out": w_out}
-    held = {"w_hbm": w_qkv, "gain_hbm": gain.reshape(-1, TAG), "adjacency_hbm": tile_adjacent}
+    held = {"w_hbm": w_qkv, "adjacency_hbm": tile_adjacent}
     for name, value in held.items():
         env[name] = pltpu.with_memory_space_constraint(value, pltpu.HBM)
     pieces = {}
@@ -350,13 +388,13 @@
             attend = [(0, b), (1, b)]
             stage = Stage(env, pieces, [] if b else [0, 1], [b], attend, fetch=b == 0, finish=b == last)
             stage.call(env, f"block_{b}")
-    result = jnp.zeros_like(cells_in)
-    for place, k in enumerate(order):
+    returned = []
+    for k in back:
+        place = order.index(k)
         start = place % half * cell_dev
         piece = env[f"out{place // half}"][start : start + cell_dev]
-        piece = over_cells(piece, k) if k else piece
-        result = lax.dynamic_update_index_in_dim(result, piece, gene ^ k, 0)
-    return result
+        returned.append(over_cells(piece, k) if k else piece)
+    return unpack(returned, back, cells_in.shape)
 
 
 def solution(mesh):

time: 53.7 us -> 51.7 us (0.963)
  local copies, waits for them, and re-layouts: 2.03 us -> 0.14 us
  Pallas kernels: 15 us -> 16.6 us
  other arithmetic: 0.73 us -> 0 us
  waiting for transfers between devices: 8.74 us -> 8.12 us
    pallas_call x0 -> x2, Pallas kernels: none -> 2.24 us  [the longest x1 1.39 us: pack(): pl.pallas_call(lambda *refs: pack_kernel(order, *refs), out_shape=[jax.Sh...]
    ppermute x14, starting transfers between devices: 24 us -> 22.9 us  [over_cells(): lax.ppermute(value, 'cells', [(i, i ^ step) for i in range(cell_devs)])]
    squeeze x1 -> x0, local copies, waits for them, and re-layouts: 1.1 us -> none  [piece_for(): rows = lax.dynamic_index_in_dim(cells_in, gene ^ k, 0, keepdims=False)]
    ppermute x6, starting transfers between devices: 2.68 us -> 3.62 us  [over_heads(): lax.ppermute(value, 'heads', [(i, i ^ step) for i in range(head_devs)])]
    ppermute x6, waiting for transfers between devices: 2.77 us -> 1.89 us  [over_heads(): lax.ppermute(value, 'heads', [(i, i ^ step) for i in range(head_devs)])]
    dynamic_update_slice x8 -> x0, local copies, waits for them, and re-layouts: 0.71 us -> none  [on_device(): result = lax.dynamic_update_index_in_dim(result, piece, gene ^ k, 0)]
    convert_element_type x1 -> x0, other arithmetic: 0.66 us -> none  [on_device(): tags = jnp.broadcast_to(tile_of_cell.astype(BF16)[:, None], (cell_dev, TAG))]
    pallas_call x4, Pallas kernels: 15 us -> 14.3 us  [call(): pl.pallas_call(self.body, out_shape=tuple(out_shape), in_specs=[hbm if n....]
  transfers between devices with their start and end apart: 20 -> 20, of which waited for: 7 -> 6; matrix products, arithmetic and copies ran while one was open for 0% -> 0% of each run, Pallas kernels for 24% -> 24%
where the time goes in v5:
time: 51.7 us; the launch traced here: 51.5 us
  starting transfers between devices  26.5 us (51%)
  Pallas kernels  16.6 us (32%)
  waiting for transfers between devices  8.12 us (16%)
    ppermute x14, starting transfers between devices, over_cells(): lax.ppermute(value, 'cells', [(i, i ^ step) for i in range(cell_devs)])  22.9 us
    pallas_call x4, Pallas kernels, call(): pl.pallas_call(self.body, out_shape=tuple(out_shape), in_specs=[hbm if n....  14.3 us
    ppermute x14, waiting for transfers between devices, over_cells(): lax.ppermute(value, 'cells', [(i, i ^ step) for i in range(cell_devs)])  6.23 us
    ppermute x6, starting transfers between devices, over_heads(): lax.ppermute(value, 'heads', [(i, i ^ step) for i in range(head_devs)])  3.62 us
    ppermute x6, waiting for transfers between devices, over_heads(): lax.ppermute(value, 'heads', [(i, i ^ step) for i in range(head_devs)])  1.89 us
    pallas_call x1, Pallas kernels, pack(): pl.pallas_call(lambda *refs: pack_kernel(order, *refs), out_shape=[jax.Sh...  1.39 us
  transfers between devices with their start and end apart: 20, of which 6 were waited for; matrix products, arithmetic and copies ran while one was open for 0% of the time, Pallas kernels for 24%

profile of v5, /device:TPU:0, one launch (start us, length us, event | category | flops | bytes accessed | tf_op | source)
XLA Modules:
  0.0 51.5 jit_solution(4305153879342070089)
XLA Ops:
  0.0 1.4 %pack.1 = (bf16[32,1152]{1,0:T(8,128)(2,1)S(1)}, bf16[32,1152]{1,0:T(8,128)(2,1)S(1)}, bf16[32,1152]{1,0:T(8,128)(2,1)S(1)}, bf16[32,1152]{1,0:T(8,128)(2,1)S(1)...) custom-call(bf16[8,32,1024]{2,1,0:T(8,128)(2,1)} %refs_0_.2, ...), custom_call_target="tpu_custom_call" | custom-call | tf_op jit(solution)/shard_map/pack/pallas_call | solution.py:60
  1.4 4.1 %collective-permute-start = (bf16[32,1152]{1,0:T(8,128)(2,1)S(1)}, bf16[32,1152]{1,0:T(8,128)(2,1)S(1)}, u32[]{:S(2)}, u32[]{:S(2)}) collective-permute-start(bf16[32,1152]{1,0:T(8,128)(2,1)S(1)} %get-tuple-element.40), channel_id=1, source_target_pairs={{0,4},{1,5},{2,6},{3,7},{4,0},{5,1},{6,2},{7,3},{8,12},{9,13},{10,... | collective-permute-start | bytes 221192 | tf_op jit(solution)/shard_map/ppermute | solution.py:338
  5.5 1.5 %collective-permute-start.1 = (bf16[32,1152]{1,0:T(8,128)(2,1)S(1)}, bf16[32,1152]{1,0:T(8,128)(2,1)S(1)}, u32[]{:S(2)}, u32[]{:S(2)}) collective-permute-start(bf16[32,1152]{1,0:T(8,128)(2,1)S(1)} %get-tuple-element.41), channel_id=1, source_target_pairs={{0,1},{1,0},{2,3},{3,2},{4,5},{5,4},{6,7},{7,6},{8,9},{9,8},{10,11... | collective-permute-start | bytes 221192 | tf_op jit(solution)/shard_map/ppermute | solution.py:338
  7.0 1.5 %collective-permute-start.2 = (bf16[32,1152]{1,0:T(8,128)(2,1)S(1)}, bf16[32,1152]{1,0:T(8,128)(2,1)S(1)}, u32[]{:S(2)}, u32[]{:S(2)}) collective-permute-start(bf16[32,1152]{1,0:T(8,128)(2,1)S(1)} %get-tuple-element.42), channel_id=1, source_target_pairs={{0,3},{1,2},{2,1},{3,0},{4,7},{5,6},{6,5},{7,4},{8,11},{9,10},{10,... | collective-permute-start | bytes 221192 | tf_op jit(solution)/shard_map/ppermute | solution.py:338
  8.5 1.3 %collective-permute-start.4 = (bf16[32,1152]{1,0:T(8,128)(2,1)S(1)}, bf16[32,1152]{1,0:T(8,128)(2,1)S(1)}, u32[]{:S(2)}, u32[]{:S(2)}) collective-permute-start(bf16[32,1152]{1,0:T(8,128)(2,1)S(1)} %get-tuple-element.51), channel_id=1, source_target_pairs={{0,5},{1,4},{2,7},{3,6},{4,1},{5,0},{6,3},{7,2},{8,13},{9,12},{10,... | collective-permute-start | bytes 221192 | tf_op jit(solution)/shard_map/ppermute | solution.py:338
  9.8 2.4 %collective-permute-start.5 = (bf16[32,1152]{1,0:T(8,128)(2,1)S(1)}, bf16[32,1152]{1,0:T(8,128)(2,1)S(1)}, u32[]{:S(2)}, u32[]{:S(2)}) collective-permute-start(bf16[32,1152]{1,0:T(8,128)(2,1)S(1)} %get-tuple-element.52), channel_id=1, source_target_pairs={{0,7},{1,6},{2,5},{3,4},{4,3},{5,2},{6,1},{7,0},{8,15},{9,14},{10,... | collective-permute-start | bytes 221192 | tf_op jit(solution)/shard_map/ppermute | solution.py:338
  12.3 0.0 collective-permute-done
  12.3 1.3 %collective-permute-start.6 = (bf16[32,1152]{1,0:T(8,128)(2,1)S(1)}, bf16[32,1152]{1,0:T(8,128)(2,1)S(1)}, u32[]{:S(2)}, u32[]{:S(2)}) collective-permute-start(bf16[32,1152]{1,0:T(8,128)(2,1)S(1)} %get-tuple-element.53), channel_id=1, source_target_pairs={{0,6},{1,7},{2,4},{3,5},{4,2},{5,3},{6,0},{7,1},{8,14},{9,15},{10,... | collective-permute-start | bytes 221192 | tf_op jit(solution)/shard_map/ppermute | solution.py:338
  13.6 0.0 collective-permute-done.1
  13.6 0.1 collective-permute-start.7
  13.7 0.0 collective-permute-done.2
  13.8 1.6 %collective-permute-start.9 = (bf16[128,1152]{1,0:T(8,128)(2,1)S(1)}, bf16[128,1152]{1,0:T(8,128)(2,1)S(1)}, u32[]{:S(2)}, u32[]{:S(2)}) collective-permute-start(bf16[128,1152]{1,0:T(8,128)(2,1)S(1)} %constant_dynamic-update-slice_fusion.refs_1_.refs_9_), channel_id=1, source_target_pairs={{0,16},{8,24},{16,0},{24,8},{1,17},{9,25},{17,1},{25,9},{2,18},{10... | collective-permute-start | bytes 884744 | tf_op jit(solution)/shard_map/ppermute | solution.py:341
  15.3 4.0 %first_group.1 = (bf16[8,256,128]{2,1,0:T(8,128)(2,1)S(1)}, bf16[256,256]{1,0:T(8,128)(2,1)S(1)}, f32[8,72,256]{2,1,0:T(8,128)S(1)}, f32[8,256]{1,0:T(8,128)S(1)...) custom-call(s32[256,256]{1,0:T(8,128)} %refs_0_.3, ...), custom_call_target="tpu_custom_call" | custom-call | flops 1073741824 | bytes 8388608 | tf_op jit(solution)/shard_map/first_group/pallas_call | solution.py:317
  19.4 0.2 collective-permute-done.4
  19.5 0.0 collective-permute-done.5
  19.5 0.0 collective-permute-done.6
  19.5 0.2 collective-permute-done.7
  19.8 0.1 collective-permute-start.8
  19.9 0.5 collective-permute-start.3
  20.4 1.5 %collective-permute-start.11 = (bf16[128,1152]{1,0:T(8,128)(2,1)S(1)}, bf16[128,1152]{1,0:T(8,128)(2,1)S(1)}, u32[]{:S(2)}, u32[]{:S(2)}) collective-permute-start(bf16[128,1152]{1,0:T(8,128)(2,1)S(1)} %constant_dynamic-update-slice_fusion.4.refs_10_), channel_id=1, source_target_pairs={{0,16},{8,24},{16,0},{24,8},{1,17},{9,25},{17,1},{25,9},{2,18},{10... | collective-permute-start | bytes 884744 | tf_op jit(solution)/shard_map/ppermute | solution.py:341
  21.9 0.0 collective-permute-done.9.refs_8_
  21.9 0.0 collective-permute-start.10
  21.9 0.0 collective-permute-done.8.refs_7_
  21.9 0.0 collective-permute-done.3.refs_6_
  21.9 5.6 %second_group.1 = (bf16[8,256,128]{2,1,0:T(8,128)(2,1)S(1)}, bf16[256,256]{1,0:T(8,128)(2,1)S(1)}, f32[8,72,256]{2,1,0:T(8,128)S(1)}, f32[8,256]{1,0:T(8,128)S(1...) custom-call(bf16[256,256]{1,0:T(8,128)(2,1)S(1)} %get-tuple-element.44.refs_0_, ...), custom_call_target="tpu_custom_call" | custom-call | flops 4831838208 | bytes 8388608 | tf_op jit(solution)/shard_map/second_group/pallas_call | solution.py:317
  27.5 0.0 copy-start
  27.5 1.9 %collective-permute-done.11.refs_7_ = bf16[128,1152]{1,0:T(8,128)(2,1)S(1)} collective-permute-done((bf16[128,1152]{1,0:T(8,128)(2,1)S(1)}, bf16[128,1152]{1,0:T(8,128)(2,1)S(1)}, u32[]{:S(2)}, u32[]{:S(2)}) %collective-permute-start.11) | collective-permute-done | bytes 294944 | tf_op jit(solution)/shard_map/ppermute | solution.py:341
  29.4 0.0 collective-permute-start.12
  29.4 0.0 collective-permute-done.10.refs_6_
  29.4 2.6 %far.1 = (f32[8,72,256]{2,1,0:T(8,128)S(1)}, f32[8,256]{1,0:T(8,128)S(1)}, f32[8,72,256]{2,1,0:T(8,128)S(1)}, f32[8,256]{1,0:T(8,128)S(1)}) custom-call(bf16[256,256]{1,0:T(8,128)(2,1)S(1)} %get-tuple-element.44.refs_0_, bf16[256,256]{1,0:T(8,128)(2,1)S(1)} %get-tuple-element.61.refs_1_, bf16[8,256,128]{2,1,0:T(8,128)(2,1)S(1)} %get-tuple-element.46.refs_2_, ...), custom_call_target="tpu_custom_call" | custom-call | flops 2147483648 | bytes 8388608 | tf_op jit(solution)/shard_map/far/pallas_call | solution.py:317
  32.0 0.0 collective-permute-done.12.refs_6_
  32.0 0.0 copy-done
  32.0 2.1 %last.1 = (bf16[128,1024]{1,0:T(8,128)(2,1)S(1)}, bf16[128,1024]{1,0:T(8,128)(2,1)S(1)}) custom-call(bf16[256,256]{1,0:T(8,128)(2,1)S(1)} %get-tuple-element.44.refs_0_, bf16[256,256]{1,0:T(8,128)(2,1)S(1)} %get-tuple-element.61.refs_1_, bf16[8,256,128]{2,1,0:T(8,128)(2,1)S(1)} %get-tuple-element.46.refs_2_, ...), custom_call_target="tpu_custom_call" | custom-call | flops 1610612736 | bytes 8388608 | tf_op jit(solution)/shard_map/last/pallas_call | solution.py:317
  34.2 2.7 %collective-permute-start.13 = (bf16[32,1024]{1,0:T(8,128)(2,1)S(1)}, bf16[32,1024]{1,0:T(8,128)(2,1)S(1)}, u32[]{:S(2)}, u32[]{:S(2)}) collective-permute-start(bf16[32,1024]{1,0:T(8,128)(2,1)S(1)} %get-tuple-element.77), channel_id=1, source_target_pairs={{0,4},{1,5},{2,6},{3,7},{4,0},{5,1},{6,2},{7,3},{8,12},{9,13},{10,... | collective-permute-start | bytes 196616 | tf_op jit(solution)/shard_map/ppermute | solution.py:338
  36.9 1.5 %collective-permute-start.14 = (bf16[32,1024]{1,0:T(8,128)(2,1)S(1)}, bf16[32,1024]{1,0:T(8,128)(2,1)S(1)}, u32[]{:S(2)}, u32[]{:S(2)}) collective-permute-start(bf16[32,1024]{1,0:T(8,128)(2,1)S(1)} %get-tuple-element.76), channel_id=1, source_target_pairs={{0,1},{1,0},{2,3},{3,2},{4,5},{5,4},{6,7},{7,6},{8,9},{9,8},{10,11... | collective-permute-start | bytes 196616 | tf_op jit(solution)/shard_map/ppermute | solution.py:338
  38.5 0.1 collective-permute-start.15
  38.5 1.8 %collective-permute-start.16 = (bf16[32,1024]{1,0:T(8,128)(2,1)S(1)}, bf16[32,1024]{1,0:T(8,128)(2,1)S(1)}, u32[]{:S(2)}, u32[]{:S(2)}) collective-permute-start(bf16[32,1024]{1,0:T(8,128)(2,1)S(1)} %get-tuple-element.81), channel_id=1, source_target_pairs={{0,6},{1,7},{2,4},{3,5},{4,2},{5,3},{6,0},{7,1},{8,14},{9,15},{10,... | collective-permute-start | bytes 196616 | tf_op jit(solution)/shard_map/ppermute | solution.py:338
  40.4 1.6 %collective-permute-start.17 = (bf16[32,1024]{1,0:T(8,128)(2,1)S(1)}, bf16[32,1024]{1,0:T(8,128)(2,1)S(1)}, u32[]{:S(2)}, u32[]{:S(2)}) collective-permute-start(bf16[32,1024]{1,0:T(8,128)(2,1)S(1)} %get-tuple-element.80), channel_id=1, source_target_pairs={{0,5},{1,4},{2,7},{3,6},{4,1},{5,0},{6,3},{7,2},{8,13},{9,12},{10,... | collective-permute-start | bytes 196616 | tf_op jit(solution)/shard_map/ppermute | solution.py:338
  42.0 0.0 collective-permute-done.13.refs_1_
  42.0 2.7 %collective-permute-start.18 = (bf16[32,1024]{1,0:T(8,128)(2,1)S(1)}, bf16[32,1024]{1,0:T(8,128)(2,1)S(1)}, u32[]{:S(2)}, u32[]{:S(2)}) collective-permute-start(bf16[32,1024]{1,0:T(8,128)(2,1)S(1)} %get-tuple-element.79), channel_id=1, source_target_pairs={{0,7},{1,6},{2,5},{3,4},{4,3},{5,2},{6,1},{7,0},{8,15},{9,14},{10,... | collective-permute-start | bytes 196616 | tf_op jit(solution)/shard_map/ppermute | solution.py:338
  44.7 0.0 collective-permute-done.14.refs_2_
  44.7 0.1 collective-permute-start.19
  44.8 0.0 collective-permute-done.15.refs_3_
  44.8 0.4 collective-permute-done.16.refs_4_
  45.2 4.8 %collective-permute-done.17.refs_5_ = bf16[32,1024]{1,0:T(8,128)(2,1)S(1)} collective-permute-done((bf16[32,1024]{1,0:T(8,128)(2,1)S(1)}, bf16[32,1024]{1,0:T(8,128)(2,1)S(1)}, u32[]{:S(2)}, u32[]{:S(2)}) %collective-permute-start.17) | collective-permute-done | bytes 65568 | tf_op jit(solution)/shard_map/ppermute | solution.py:338
  50.0 0.0 collective-permute-done.18.refs_6_
  50.0 0.6 %collective-permute-done.19.refs_7_ = bf16[32,1024]{1,0:T(8,128)(2,1)S(1)} collective-permute-done((bf16[32,1024]{1,0:T(8,128)(2,1)S(1)}, bf16[32,1024]{1,0:T(8,128)(2,1)S(1)}, u32[]{:S(2)}, u32[]{:S(2)}) %collective-permute-start.19) | collective-permute-done | bytes 65568 | tf_op jit(solution)/shard_map/ppermute | solution.py:338
  50.6 0.8 %unpack.1 = bf16[8,32,1024]{2,1,0:T(8,128)(2,1)} custom-call(bf16[32,1024]{1,0:T(8,128)(2,1)S(1)} %get-tuple-element.78.refs_0_, bf16[32,1024]{1,0:T(8,128)(2,1)S(1)} %collective-permute-done.13.refs_1_, bf16[32,1024]{1,0:T(8,128)(2,1)S(1)} %collective-permute-done.14.refs_2_, bf16[32,1024]{1,0:T(8,128)(2,1)S(1)} %collective-permute-done.15.refs_3_, ...), custom_call_target="tpu_custom_call" | custom-call | tf_op jit(solution)/shard_map/unpack/pallas_call | solution.py:88
  (10 shorter events, 0.1 us)
Async XLA Ops:
  1.4 10.9 %collective-permute-start = (bf16[32,1152]{1,0:T(8,128)(2,1)S(1)}, bf16[32,1152]{1,0:T(8,128)(2,1)S(1)}, u32[]{:S(2)}, u32[]{:S(2)}) collective-permute-start(bf16[32,1152]{1,0:T(8,128)(2,1)S(1)} %get-tuple-element.40), channel_id=1, source_target_pairs={{0,4},{1,5},{2,6},{3,7},{4,0},{5,1},{6,2},{7,3},{8,12},{9,13},{10,... | collective-permute-start | bytes 221192 | tf_op jit(solution)/shard_map/ppermute | solution.py:338
  5.5 8.1 %collective-permute-start.1 = (bf16[32,1152]{1,0:T(8,128)(2,1)S(1)}, bf16[32,1152]{1,0:T(8,128)(2,1)S(1)}, u32[]{:S(2)}, u32[]{:S(2)}) collective-permute-start(bf16[32,1152]{1,0:T(8,128)(2,1)S(1)} %get-tuple-element.41), channel_id=1, source_target_pairs={{0,1},{1,0},{2,3},{3,2},{4,5},{5,4},{6,7},{7,6},{8,9},{9,8},{10,11... | collective-permute-start | bytes 221192 | tf_op jit(solution)/shard_map/ppermute | solution.py:338
  7.0 6.7 %collective-permute-start.2 = (bf16[32,1152]{1,0:T(8,128)(2,1)S(1)}, bf16[32,1152]{1,0:T(8,128)(2,1)S(1)}, u32[]{:S(2)}, u32[]{:S(2)}) collective-permute-start(bf16[32,1152]{1,0:T(8,128)(2,1)S(1)} %get-tuple-element.42), channel_id=1, source_target_pairs={{0,3},{1,2},{2,1},{3,0},{4,7},{5,6},{6,5},{7,4},{8,11},{9,10},{10,... | collective-permute-start | bytes 221192 | tf_op jit(solution)/shard_map/ppermute | solution.py:338
  8.5 11.0 %collective-permute-start.4 = (bf16[32,1152]{1,0:T(8,128)(2,1)S(1)}, bf16[32,1152]{1,0:T(8,128)(2,1)S(1)}, u32[]{:S(2)}, u32[]{:S(2)}) collective-permute-start(bf16[32,1152]{1,0:T(8,128)(2,1)S(1)} %get-tuple-element.51), channel_id=1, source_target_pairs={{0,5},{1,4},{2,7},{3,6},{4,1},{5,0},{6,3},{7,2},{8,13},{9,12},{10,... | collective-permute-start | bytes 221192 | tf_op jit(solution)/shard_map/ppermute | solution.py:338
  9.8 9.7 %collective-permute-start.5 = (bf16[32,1152]{1,0:T(8,128)(2,1)S(1)}, bf16[32,1152]{1,0:T(8,128)(2,1)S(1)}, u32[]{:S(2)}, u32[]{:S(2)}) collective-permute-start(bf16[32,1152]{1,0:T(8,128)(2,1)S(1)} %get-tuple-element.52), channel_id=1, source_target_pairs={{0,7},{1,6},{2,5},{3,4},{4,3},{5,2},{6,1},{7,0},{8,15},{9,14},{10,... | collective-permute-start | bytes 221192 | tf_op jit(solution)/shard_map/ppermute | solution.py:338
  12.3 7.3 %collective-permute-start.6 = (bf16[32,1152]{1,0:T(8,128)(2,1)S(1)}, bf16[32,1152]{1,0:T(8,128)(2,1)S(1)}, u32[]{:S(2)}, u32[]{:S(2)}) collective-permute-start(bf16[32,1152]{1,0:T(8,128)(2,1)S(1)} %get-tuple-element.53), channel_id=1, source_target_pairs={{0,6},{1,7},{2,4},{3,5},{4,2},{5,3},{6,0},{7,1},{8,14},{9,15},{10,... | collective-permute-start | bytes 221192 | tf_op jit(solution)/shard_map/ppermute | solution.py:338
  13.6 6.2 %collective-permute-start.7 = (bf16[32,1152]{1,0:T(8,128)(2,1)S(1)}, bf16[32,1152]{1,0:T(8,128)(2,1)S(1)}, u32[]{:S(2)}, u32[]{:S(2)}) collective-permute-start(bf16[32,1152]{1,0:T(8,128)(2,1)S(1)} %get-tuple-element.54), channel_id=1, source_target_pairs={{0,2},{1,3},{2,0},{3,1},{4,6},{5,7},{6,4},{7,5},{8,10},{9,11},{10,... | collective-permute-start | bytes 221192 | tf_op jit(solution)/shard_map/ppermute | solution.py:338
  13.8 8.1 %collective-permute-start.9 = (bf16[128,1152]{1,0:T(8,128)(2,1)S(1)}, bf16[128,1152]{1,0:T(8,128)(2,1)S(1)}, u32[]{:S(2)}, u32[]{:S(2)}) collective-permute-start(bf16[128,1152]{1,0:T(8,128)(2,1)S(1)} %constant_dynamic-update-slice_fusion.refs_1_.refs_9_), channel_id=1, source_target_pairs={{0,16},{8,24},{16,0},{24,8},{1,17},{9,25},{17,1},{25,9},{2,18},{10... | collective-permute-start | bytes 884744 | tf_op jit(solution)/shard_map/ppermute | solution.py:341
  19.8 2.1 %collective-permute-start.8 = (bf16[128,1152]{1,0:T(8,128)(2,1)S(1)}, bf16[128,1152]{1,0:T(8,128)(2,1)S(1)}, u32[]{:S(2)}, u32[]{:S(2)}) collective-permute-start(bf16[128,1152]{1,0:T(8,128)(2,1)S(1)} %constant_dynamic-update-slice_fusion.4.refs_10_), channel_id=1, source_target_pairs={{0,8},{8,0},{16,24},{24,16},{1,9},{9,1},{17,25},{25,17},{2,10},{10... | collective-permute-start | bytes 884744 | tf_op jit(solution)/shard_map/ppermute | solution.py:341
  19.9 2.0 %collective-permute-start.3 = (bf16[128,1152]{1,0:T(8,128)(2,1)S(1)}, bf16[128,1152]{1,0:T(8,128)(2,1)S(1)}, u32[]{:S(2)}, u32[]{:S(2)}) collective-permute-start(bf16[128,1152]{1,0:T(8,128)(2,1)S(1)} %constant_dynamic-update-slice_fusion.refs_1_.refs_9_), channel_id=1, source_target_pairs={{0,8},{8,0},{16,24},{24,16},{1,9},{9,1},{17,25},{25,17},{2,10},{10... | collective-permute-start | bytes 884744 | tf_op jit(solution)/shard_map/ppermute | solution.py:341
  20.4 9.0 %collective-permute-start.11 = (bf16[128,1152]{1,0:T(8,128)(2,1)S(1)}, bf16[128,1152]{1,0:T(8,128)(2,1)S(1)}, u32[]{:S(2)}, u32[]{:S(2)}) collective-permute-start(bf16[128,1152]{1,0:T(8,128)(2,1)S(1)} %constant_dynamic-update-slice_fusion.4.refs_10_), channel_id=1, source_target_pairs={{0,16},{8,24},{16,0},{24,8},{1,17},{9,25},{17,1},{25,9},{2,18},{10... | collective-permute-start | bytes 884744 | tf_op jit(solution)/shard_map/ppermute | solution.py:341
  21.9 7.5 %collective-permute-start.10 = (bf16[128,1152]{1,0:T(8,128)(2,1)S(1)}, bf16[128,1152]{1,0:T(8,128)(2,1)S(1)}, u32[]{:S(2)}, u32[]{:S(2)}) collective-permute-start(bf16[128,1152]{1,0:T(8,128)(2,1)S(1)} %collective-permute-done.9.refs_8_), channel_id=1, source_target_pairs={{0,8},{8,0},{16,24},{24,16},{1,9},{9,1},{17,25},{25,17},{2,10},{10... | collective-permute-start | bytes 884744 | tf_op jit(solution)/shard_map/ppermute | solution.py:341
  27.5 4.5 %copy-start = (bf16[1024,1024]{1,0:T(8,128)(2,1)S(1)}, bf16[1024,1024]{1,0:T(8,128)(2,1)}, u32[]{:S(2)}) copy-start(bf16[1024,1024]{1,0:T(8,128)(2,1)} %refs_10_.1) | copy-start | bytes 6291460
  29.4 2.6 %collective-permute-start.12 = (bf16[128,1152]{1,0:T(8,128)(2,1)S(1)}, bf16[128,1152]{1,0:T(8,128)(2,1)S(1)}, u32[]{:S(2)}, u32[]{:S(2)}) collective-permute-start(bf16[128,1152]{1,0:T(8,128)(2,1)S(1)} %collective-permute-done.11.refs_7_), channel_id=1, source_target_pairs={{0,8},{8,0},{16,24},{24,16},{1,9},{9,1},{17,25},{25,17},{2,10},{10... | collective-permute-start | bytes 884744 | tf_op jit(solution)/shard_map/ppermute | solution.py:341
  34.2 7.8 %collective-permute-start.13 = (bf16[32,1024]{1,0:T(8,128)(2,1)S(1)}, bf16[32,1024]{1,0:T(8,128)(2,1)S(1)}, u32[]{:S(2)}, u32[]{:S(2)}) collective-permute-start(bf16[32,1024]{1,0:T(8,128)(2,1)S(1)} %get-tuple-element.77), channel_id=1, source_target_pairs={{0,4},{1,5},{2,6},{3,7},{4,0},{5,1},{6,2},{7,3},{8,12},{9,13},{10,... | collective-permute-start | bytes 196616 | tf_op jit(solution)/shard_map/ppermute | solution.py:338
  36.9 7.8 %collective-permute-start.14 = (bf16[32,1024]{1,0:T(8,128)(2,1)S(1)}, bf16[32,1024]{1,0:T(8,128)(2,1)S(1)}, u32[]{:S(2)}, u32[]{:S(2)}) collective-permute-start(bf16[32,1024]{1,0:T(8,128)(2,1)S(1)} %get-tuple-element.76), channel_id=1, source_target_pairs={{0,1},{1,0},{2,3},{3,2},{4,5},{5,4},{6,7},{7,6},{8,9},{9,8},{10,11... | collective-permute-start | bytes 196616 | tf_op jit(solution)/shard_map/ppermute | solution.py:338
  38.5 6.4 %collective-permute-start.15 = (bf16[32,1024]{1,0:T(8,128)(2,1)S(1)}, bf16[32,1024]{1,0:T(8,128)(2,1)S(1)}, u32[]{:S(2)}, u32[]{:S(2)}) collective-permute-start(bf16[32,1024]{1,0:T(8,128)(2,1)S(1)} %get-tuple-element.82), channel_id=1, source_target_pairs={{0,2},{1,3},{2,0},{3,1},{4,6},{5,7},{6,4},{7,5},{8,10},{9,11},{10,... | collective-permute-start | bytes 196616 | tf_op jit(solution)/shard_map/ppermute | solution.py:338
  38.5 6.7 %collective-permute-start.16 = (bf16[32,1024]{1,0:T(8,128)(2,1)S(1)}, bf16[32,1024]{1,0:T(8,128)(2,1)S(1)}, u32[]{:S(2)}, u32[]{:S(2)}) collective-permute-start(bf16[32,1024]{1,0:T(8,128)(2,1)S(1)} %get-tuple-element.81), channel_id=1, source_target_pairs={{0,6},{1,7},{2,4},{3,5},{4,2},{5,3},{6,0},{7,1},{8,14},{9,15},{10,... | collective-permute-start | bytes 196616 | tf_op jit(solution)/shard_map/ppermute | solution.py:338
  40.4 9.7 %collective-permute-start.17 = (bf16[32,1024]{1,0:T(8,128)(2,1)S(1)}, bf16[32,1024]{1,0:T(8,128)(2,1)S(1)}, u32[]{:S(2)}, u32[]{:S(2)}) collective-permute-start(bf16[32,1024]{1,0:T(8,128)(2,1)S(1)} %get-tuple-element.80), channel_id=1, source_target_pairs={{0,5},{1,4},{2,7},{3,6},{4,1},{5,0},{6,3},{7,2},{8,13},{9,12},{10,... | collective-permute-start | bytes 196616 | tf_op jit(solution)/shard_map/ppermute | solution.py:338
  42.0 8.1 %collective-permute-start.18 = (bf16[32,1024]{1,0:T(8,128)(2,1)S(1)}, bf16[32,1024]{1,0:T(8,128)(2,1)S(1)}, u32[]{:S(2)}, u32[]{:S(2)}) collective-permute-start(bf16[32,1024]{1,0:T(8,128)(2,1)S(1)} %get-tuple-element.79), channel_id=1, source_target_pairs={{0,7},{1,6},{2,5},{3,4},{4,3},{5,2},{6,1},{7,0},{8,15},{9,14},{10,... | collective-permute-start | bytes 196616 | tf_op jit(solution)/shard_map/ppermute | solution.py:338
  44.7 6.0 %collective-permute-start.19 = (bf16[32,1024]{1,0:T(8,128)(2,1)S(1)}, bf16[32,1024]{1,0:T(8,128)(2,1)S(1)}, u32[]{:S(2)}, u32[]{:S(2)}) collective-permute-start(bf16[32,1024]{1,0:T(8,128)(2,1)S(1)} %get-tuple-element.75), channel_id=1, source_target_pairs={{0,3},{1,2},{2,1},{3,0},{4,7},{5,6},{6,5},{7,4},{8,11},{9,10},{10,... | collective-permute-start | bytes 196616 | tf_op jit(solution)/shard_map/ppermute | solution.py:338

commit v6 on v5

--- a/solution.py
+++ b/solution.py
@@ -14,7 +14,8 @@
 MASKED = -1e30
 SCALE = 0.125 * math.log2(math.e)
 COLS = 256
-TAG = 128
+ROWS, LANES = 16, 128
+MORE = 1
 BF16 = jnp.bfloat16
 F32 = jnp.float32
 
@@ -24,9 +25,8 @@
 
 
 def one_hot(tags, count):
-    tags = tags.astype(F32)
     lane = lax.broadcasted_iota(jnp.int32, tags.shape, 1).astype(F32)
-    parts = [(tags == lane + start).astype(F32) for start in range(0, count, TAG)]
+    parts = [(tags == lane + start).astype(F32) for start in range(0, count, LANES)]
     return jnp.concatenate(parts, axis=1).astype(BF16)
 
 
@@ -45,12 +45,23 @@
     row = lax.broadcasted_iota(jnp.int32, (rows, rows), 0)
     column = lax.broadcasted_iota(jnp.int32, (rows, rows), 1)
     tiles = jnp.where(row == column, tile_ref[...].astype(F32), 0.0)
-    tags = jnp.broadcast_to(jnp.sum(tiles, axis=1, keepdims=True), (rows, TAG)).astype(BF16)
+    tags = jnp.sum(tiles, axis=1, keepdims=True)
+    parts = rows // ROWS
+    lane = lax.broadcasted_iota(jnp.int32, (ROWS, LANES), 1) // (LANES // parts)
+    tag_tile = jnp.zeros((ROWS, LANES), F32)
+    for part in range(parts):
+        tag_tile = jnp.where(lane == part, tags[part * ROWS : (part + 1) * ROWS], tag_tile)
     for i in range(genes):
         x32 = cells_ref[i].astype(F32)
         mean = jnp.mean(x32 * x32, axis=-1, keepdims=True)
-        out_refs[i][:, :width] = (x32 * lax.rsqrt(mean + 1e-05) * gain).astype(BF16)
-        out_refs[i][:, width:] = tags
+        normed = (x32 * lax.rsqrt(mean + 1e-05) * gain).astype(BF16)
+        place = 0
+        for row in range(0, rows, ROWS):
+            for start in range(0, width, LANES):
+                tile = normed[row : row + ROWS, start : start + LANES]
+                out_refs[i][place : place + ROWS, :] = tile
+                place += ROWS
+        out_refs[i][place:, :] = tag_tile.astype(BF16)
 
 
 def pack(cells_in, gain, tiles, order):
@@ -59,7 +70,7 @@
     operands = [pltpu.with_memory_space_constraint(value, pltpu.HBM) for value in operands]
     return pl.pallas_call(
         lambda *refs: pack_kernel(order, *refs),
-        out_shape=[jax.ShapeDtypeStruct((rows, width + TAG), BF16)] * genes,
+        out_shape=[jax.ShapeDtypeStruct((rows * width // LANES + ROWS, LANES), BF16)] * genes,
         in_specs=[pl.BlockSpec(memory_space=pltpu.HBM)] * 3,
         out_specs=[pl.BlockSpec(memory_space=pltpu.VMEM)] * genes,
         scratch_shapes=[
@@ -101,6 +112,7 @@
         self.pieces, self.queries, self.blocks = pieces, queries, blocks
         self.attend, self.fetch, self.finish, self.keep = attend, fetch, finish, keep
         self.width = env["w_hbm"].shape[0]
+        self.piece = env["piece"]
         self.tiles = env["adjacency_hbm"].shape[0]
         self.pairs = self.width // PAIR
         self.rows = {q: sum(size for _, _, size in pieces["q", q]) for q in {q for q, _ in attend}}
@@ -145,25 +157,24 @@
     def body(self, *refs):
         count = len(self.ins)
         names = list(self.outs) + ["adjacency", "w"] * self.fetch + list(self.scratch)
-        more = ["bias", "weights"] + ["attended"] * self.finish
+        more = ["cells", "bias", "weights"] + ["attended"] * self.finish
         more += ["pairs_allowed", "sems"] * self.fetch
         self.read = dict(zip(self.ins, refs[:count]))
         self.write = dict(zip(names + more, refs[count:]))
         self.w = self.write["w"] if self.fetch else self.read["w"]
         if self.fetch:
             self.start_copies()
-        for b in self.blocks:
-            cells = self.load_cells("k", b)
-            if self.fetch and b == self.blocks[0]:
-                self.copies[1].wait()
-            self.project_keys(b, cells)
-            if self.fetch and b == self.blocks[0]:
-                self.copies[2].wait()
-            self.project_values(b, cells)
         if self.fetch:
             self.copies[0].wait()
         for q in self.queries:
             self.project_queries(q)
+        if self.fetch:
+            self.copies[1].wait()
+        for b in self.blocks:
+            cells = self.load_cells("k", b)
+            self.project_keys(b, cells)
+            if not self.fetch:
+                self.project_values(b, cells)
         self.attend_all()
         if self.finish:
             for q in self.touched:
@@ -172,30 +183,45 @@
     def ref(self, name):
         return self.write[name] if name in self.write else self.read[name]
 
-    def rows_of(self, kind, index, columns):
-        parts = self.pieces[kind, index]
-        return [self.read[name][start : start + size, columns] for name, start, size in parts]
+    def tiles_of(self, kind, index):
+        per = self.piece * self.width // LANES + ROWS
+        for name, start, size in self.pieces[kind, index]:
+            for piece in range(start // self.piece, (start + size) // self.piece):
+                yield self.read[name], piece * per
 
     def start_copies(self):
         width, sems = self.width, self.write["sems"]
         moves = [(self.read["adjacency_hbm"], self.write["pairs_allowed"])]
-        for start in (width, 2 * width, 0):
+        for start in (0, width, 2 * width):
             part = slice(start, start + width)
             moves.append((self.read["w_hbm"].at[:, part], self.write["w"].at[:, part]))
         copies = [pltpu.make_async_copy(*move, sems.at[i]) for i, move in enumerate(moves)]
         for copy in copies:
             copy.start()
         copies[0].wait()
-        self.copies = {1: copies[1], 2: copies[2], 0: copies[3]}
+        self.copies = copies[1:]
         allowed = self.write["pairs_allowed"][...]
         self.write["adjacency"][...] = allowed.astype(F32).astype(BF16)
 
     def load_cells(self, kind, index):
-        return jnp.concatenate(self.rows_of(kind, index, slice(0, self.width)), axis=0)
+        cells_ref, row = self.write["cells"], 0
+        for ref, place in self.tiles_of(kind, index):
+            for _ in range(self.piece // ROWS):
+                for start in range(0, self.width, LANES):
+                    cells_ref[row : row + ROWS, start : start + LANES] = ref[place : place + ROWS, :]
+                    place += ROWS
+                row += ROWS
+        return cells_ref[:row, :]
 
     def tags_of(self, kind, index):
-        tags = jnp.concatenate(self.rows_of(kind, index, slice(self.width, None)), axis=0)
-        return one_hot(tags, self.tiles)
+        tags, parts = [], self.piece // ROWS
+        for ref, place in self.tiles_of(kind, index):
+            place += self.piece * self.width // LANES
+            tile = ref[place : place + ROWS, :].astype(F32)
+            for part in range(parts):
+                column = part * (LANES // parts)
+                tags.append(jnp.broadcast_to(tile[:, column : column + 1], tile.shape))
+        return one_hot(jnp.concatenate(tags, axis=0), self.tiles)
 
     def project_queries(self, q):
         rows = self.rows[q]
@@ -209,7 +235,8 @@
                 none = jnp.zeros_like(both)
                 self.write[f"Q{q}"][pair, :rows, :] = jnp.where(lane < HEAD_DIM, both, none)
                 self.write[f"Q{q}"][pair, rows:, :] = jnp.where(lane < HEAD_DIM, none, both)
-        near = dot(self.ref("adjacency")[...], self.tags_of("q", q), 1, 1).astype(BF16)
+        near = dot(self.ref("adjacency")[...], self.tags_of("q", q), 1, 1)
+        near = ((1.0 - near) * MASKED).astype(BF16)
         self.write[f"G{q}"][...] = jnp.concatenate([near, near], axis=1)
 
     def project_keys(self, b, cells):
@@ -230,21 +257,32 @@
     def attend_all(self):
         source = {q: self.read for q in self.touched if f"acc{q}" in self.held}
         before = None
+        late = self.blocks if self.fetch else []
         for turn, (q, b) in enumerate(self.attend):
             after = self.start_turn(q, b, source.get(q), turn % 2)
             source[q] = self.write
             for pair in range(self.pairs):
                 self.weigh(after, pair)
+                if before is not None and late:
+                    late = self.project_late_values(late)
                 if before is not None:
                     self.add_values(before, pair)
             before = after
+        if late:
+            self.project_late_values(late)
         for pair in range(self.pairs):
             self.add_values(before, pair)
+
+    def project_late_values(self, late):
+        self.copies[2].wait()
+        for b in late:
+            self.project_values(b, self.load_cells("k", b))
+        return []
 
     def start_turn(self, q, b, before, slot):
         cells = self.cells[b]
         bias_ref = self.write["bias"].at[slot, :cells]
-        bias_ref[...] = (dot(self.tags_of("k", b), self.ref(f"G{q}")[...]) - 1.0) * -MASKED
+        bias_ref[...] = dot(self.tags_of("k", b), self.ref(f"G{q}")[...])
         return (q, b, before, bias_ref, self.write["weights"].at[slot, :, :cells], {})
 
     def weigh(self, turn, pair):
@@ -296,6 +334,7 @@
         rows = max(self.rows.values())
         scratch = [pltpu.VMEM(*shape) for shape in self.scratch.values()]
         scratch += [
+            pltpu.VMEM((max(self.block, rows), self.width), BF16),
             pltpu.VMEM((2, self.block, 2 * rows), F32),
             pltpu.VMEM((2, self.pairs, self.block, 2 * rows), BF16),
         ]
@@ -340,11 +379,11 @@
     def over_heads(value, step):
         return lax.ppermute(value, "heads", [(i, i ^ step) for i in range(head_devs)])
 
-    order = [4, 1, 3, 0, 5, 7, 6, 2] if genes == 8 else list(range(genes))
+    order = [4, 1, 3, 0, 2, 6, 5, 7] if genes == 8 else list(range(genes))
     back = [0, 4, 1, 2, 6, 5, 7, 3] if genes == 8 else order
     packed = pack(cells_in, gain, tile_of_cell, order)
     arrived = [over_cells(piece, k) if k else piece for piece, k in zip(packed, order)]
-    env = {"w_out": w_out}
+    env = {"w_out": w_out, "piece": cell_dev}
     held = {"w_hbm": w_qkv, "adjacency_hbm": tile_adjacent}
     for name, value in held.items():
         env[name] = pltpu.with_memory_space_constraint(value, pltpu.HBM)
@@ -353,7 +392,6 @@
 
     def spread(group, own, beside):
         env[f"own{group}"] = own
-        pieces["q", group] = [(f"own{group}", 0, rows)]
         held = own
         if sets > 1:
             held = lax.all_gather(own, "cells", axis=0, axis_index_groups=same, tiled=True)
@@ -362,15 +400,23 @@
             if step in beside:
                 env[f"beside{group}{step}"] = over_heads(env[f"chunk{group}{step}"], 1)
 
-    first = jnp.concatenate(arrived[:half], 0)
+    shallow = sets == 1 and head_devs == 4
+    cut = half + MORE if shallow else half
+    first = jnp.concatenate(arrived[:cut], 0)
+    more = (cut - half) * cell_dev
+    pieces["q", 0] = [("own0", 0, rows)]
+    pieces["q", 1] = [("own0", rows, more)] * (more > 0) + [("own1", 0, rows - more)]
     steps = range(0, head_devs, 2)
     spread(0, first, steps)
-    if sets == 1 and head_devs == 4:
+    if shallow:
+        def env_rows(name):
+            return rows + (more if "0" == name.lstrip("ownchunkbeside")[0] else -more)
+
         blocks = [["own0"], ["beside00", "own1"], ["beside10", "chunk02"], ["beside02", "chunk12"], ["beside12"]]
         for b, names in enumerate(blocks):
-            pieces["k", b] = [(name, 0, rows) for name in names]
+            pieces["k", b] = [(name, 0, env_rows(name)) for name in names]
         Stage(env, pieces, [0], [0], [(0, 0)], fetch=True, keep=[0]).call(env, "first_group")
-        env["w"], *late = lax.optimization_barrier((env["w"], *arrived[half:]))
+        env["w"], *late = lax.optimization_barrier((env["w"], *arrived[cut:]))
         spread(1, jnp.concatenate(late, 0), [0])
         attend = [(0, 1), (1, 0), (1, 1), (0, 2), (1, 2)]
         Stage(env, pieces, [1], [1, 2], attend).call(env, "second_group")

time: 51.7 us -> 50.6 us (0.979)
  waiting for transfers between devices: 8.12 us -> 6.66 us
    ppermute x6, waiting for transfers between devices: 1.89 us -> 1.1 us  [over_heads(): lax.ppermute(value, 'heads', [(i, i ^ step) for i in range(head_devs)])]
    ppermute x14, waiting for transfers between devices: 6.23 us -> 5.56 us  [over_cells(): lax.ppermute(value, 'cells', [(i, i ^ step) for i in range(cell_devs)])]
  transfers between devices with their start and end apart: 20 -> 20, of which waited for: 6 -> 4; matrix products, arithmetic and copies ran while one was open for 0% -> 0% of each run, Pallas kernels for 24% -> 25%
where the time goes in v6:
time: 50.6 us; the launch traced here: 50.4 us
  starting transfers between devices  26.6 us (53%)
  Pallas kernels  16.8 us (33%)
  waiting for transfers between devices  6.66 us (13%)
    ppermute x14, starting transfers between devices, over_cells(): lax.ppermute(value, 'cells', [(i, i ^ step) for i in range(cell_devs)])  22.9 us
    pallas_call x4, Pallas kernels, call(): pl.pallas_call(self.body, out_shape=tuple(out_shape), in_specs=[hbm if n....  14.6 us
    ppermute x14, waiting for transfers between devices, over_cells(): lax.ppermute(value, 'cells', [(i, i ^ step) for i in range(cell_devs)])  5.56 us
    ppermute x6, starting transfers between devices, over_heads(): lax.ppermute(value, 'heads', [(i, i ^ step) for i in range(head_devs)])  3.75 us
    pallas_call x1, Pallas kernels, pack(): pl.pallas_call(lambda *refs: pack_kernel(order, *refs), out_shape=[jax.Sh...  1.39 us
    ppermute x6, waiting for transfers between devices, over_heads(): lax.ppermute(value, 'heads', [(i, i ^ step) for i in range(head_devs)])  1.1 us
  transfers between devices with their start and end apart: 20, of which 4 were waited for; matrix products, arithmetic and copies ran while one was open for 0% of the time, Pallas kernels for 25%

profile of v6, /device:TPU:0, one launch (start us, length us, event | category | flops | bytes accessed | tf_op | source)
XLA Modules:
  0.0 50.4 jit_solution(10902046960633177179)
XLA Ops:
  0.0 1.4 %pack.1 = (bf16[272,128]{1,0:T(8,128)(2,1)S(1)}, bf16[272,128]{1,0:T(8,128)(2,1)S(1)}, bf16[272,128]{1,0:T(8,128)(2,1)S(1)}, bf16[272,128]{1,0:T(8,128)(2,1)S(1)...) custom-call(bf16[8,32,1024]{2,1,0:T(8,128)(2,1)} %refs_0_.2, ...), custom_call_target="tpu_custom_call" | custom-call | tf_op jit(solution)/shard_map/pack/pallas_call | solution.py:71
  1.4 4.1 %collective-permute-start = (bf16[272,128]{1,0:T(8,128)(2,1)S(1)}, bf16[272,128]{1,0:T(8,128)(2,1)S(1)}, u32[]{:S(2)}, u32[]{:S(2)}) collective-permute-start(bf16[272,128]{1,0:T(8,128)(2,1)S(1)} %get-tuple-element.39), channel_id=1, source_target_pairs={{0,4},{1,5},{2,6},{3,7},{4,0},{5,1},{6,2},{7,3},{8,12},{9,13},{10,... | collective-permute-start | bytes 208904 | tf_op jit(solution)/shard_map/ppermute | solution.py:377
  5.5 1.5 %collective-permute-start.1 = (bf16[272,128]{1,0:T(8,128)(2,1)S(1)}, bf16[272,128]{1,0:T(8,128)(2,1)S(1)}, u32[]{:S(2)}, u32[]{:S(2)}) collective-permute-start(bf16[272,128]{1,0:T(8,128)(2,1)S(1)} %get-tuple-element.40), channel_id=1, source_target_pairs={{0,1},{1,0},{2,3},{3,2},{4,5},{5,4},{6,7},{7,6},{8,9},{9,8},{10,11... | collective-permute-start | bytes 208904 | tf_op jit(solution)/shard_map/ppermute | solution.py:377
  7.0 1.5 %collective-permute-start.2 = (bf16[272,128]{1,0:T(8,128)(2,1)S(1)}, bf16[272,128]{1,0:T(8,128)(2,1)S(1)}, u32[]{:S(2)}, u32[]{:S(2)}) collective-permute-start(bf16[272,128]{1,0:T(8,128)(2,1)S(1)} %get-tuple-element.41), channel_id=1, source_target_pairs={{0,3},{1,2},{2,1},{3,0},{4,7},{5,6},{6,5},{7,4},{8,11},{9,10},{10,... | collective-permute-start | bytes 208904 | tf_op jit(solution)/shard_map/ppermute | solution.py:377
  8.5 0.4 collective-permute-start.3
  9.0 1.3 %collective-permute-start.5 = (bf16[272,128]{1,0:T(8,128)(2,1)S(1)}, bf16[272,128]{1,0:T(8,128)(2,1)S(1)}, u32[]{:S(2)}, u32[]{:S(2)}) collective-permute-start(bf16[272,128]{1,0:T(8,128)(2,1)S(1)} %get-tuple-element.51), channel_id=1, source_target_pairs={{0,6},{1,7},{2,4},{3,5},{4,2},{5,3},{6,0},{7,1},{8,14},{9,15},{10,... | collective-permute-start | bytes 208904 | tf_op jit(solution)/shard_map/ppermute | solution.py:377
  10.3 0.0 collective-permute-done
  10.3 2.6 %collective-permute-start.6 = (bf16[272,128]{1,0:T(8,128)(2,1)S(1)}, bf16[272,128]{1,0:T(8,128)(2,1)S(1)}, u32[]{:S(2)}, u32[]{:S(2)}) collective-permute-start(bf16[272,128]{1,0:T(8,128)(2,1)S(1)} %get-tuple-element.52), channel_id=1, source_target_pairs={{0,5},{1,4},{2,7},{3,6},{4,1},{5,0},{6,3},{7,2},{8,13},{9,12},{10,... | collective-permute-start | bytes 208904 | tf_op jit(solution)/shard_map/ppermute | solution.py:377
  13.0 0.0 collective-permute-done.1
  13.0 0.9 %collective-permute-start.7 = (bf16[272,128]{1,0:T(8,128)(2,1)S(1)}, bf16[272,128]{1,0:T(8,128)(2,1)S(1)}, u32[]{:S(2)}, u32[]{:S(2)}) collective-permute-start(bf16[272,128]{1,0:T(8,128)(2,1)S(1)} %get-tuple-element.53), channel_id=1, source_target_pairs={{0,7},{1,6},{2,5},{3,4},{4,3},{5,2},{6,1},{7,0},{8,15},{9,14},{10,... | collective-permute-start | bytes 208904 | tf_op jit(solution)/shard_map/ppermute | solution.py:377
  14.0 0.0 collective-permute-done.2
  14.0 0.0 collective-permute-done.3
  14.0 1.6 %collective-permute-start.9 = (bf16[1360,128]{1,0:T(8,128)(2,1)S(1)}, bf16[1360,128]{1,0:T(8,128)(2,1)S(1)}, u32[]{:S(2)}, u32[]{:S(2)}) collective-permute-start(bf16[1360,128]{1,0:T(8,128)(2,1)S(1)} %constant_dynamic-update-slice_fusion.refs_1_.refs_9_), channel_id=1, source_target_pairs={{0,16},{8,24},{16,0},{24,8},{1,17},{9,25},{17,1},{25,9},{2,18},{10... | collective-permute-start | bytes 1044488 | tf_op jit(solution)/shard_map/ppermute | solution.py:380
  15.6 0.0 collective-permute-start.4
  15.6 4.1 %first_group.1 = (bf16[8,256,128]{2,1,0:T(8,128)(2,1)S(1)}, bf16[256,256]{1,0:T(8,128)(2,1)S(1)}, f32[8,72,256]{2,1,0:T(8,128)S(1)}, f32[8,256]{1,0:T(8,128)S(1)...) custom-call(s32[256,256]{1,0:T(8,128)} %refs_0_.3, ...), custom_call_target="tpu_custom_call" | custom-call | flops 1275068416 | bytes 8388608 | tf_op jit(solution)/shard_map/first_group/pallas_call | solution.py:356
  19.7 0.0 collective-permute-done.5
  19.7 0.9 %collective-permute-done.6 = bf16[272,128]{1,0:T(8,128)(2,1)S(1)} collective-permute-done((bf16[272,128]{1,0:T(8,128)(2,1)S(1)}, bf16[272,128]{1,0:T(8,128)(2,1)S(1)}, u32[]{:S(2)}, u32[]{:S(2)}) %collective-permute-start.6) | collective-permute-done | bytes 69664 | tf_op jit(solution)/shard_map/ppermute | solution.py:377
  20.6 0.0 collective-permute-done.7
  20.7 0.1 collective-permute-start.8
  20.8 1.6 %collective-permute-start.11 = (bf16[816,128]{1,0:T(8,128)(2,1)S(1)}, bf16[816,128]{1,0:T(8,128)(2,1)S(1)}, u32[]{:S(2)}, u32[]{:S(2)}) collective-permute-start(bf16[816,128]{1,0:T(8,128)(2,1)S(1)} %constant_dynamic-update-slice_fusion.5.refs_10_), channel_id=1, source_target_pairs={{0,16},{8,24},{16,0},{24,8},{1,17},{9,25},{17,1},{25,9},{2,18},{10... | collective-permute-start | bytes 626696 | tf_op jit(solution)/shard_map/ppermute | solution.py:380
  22.3 1.1 %collective-permute-done.9.refs_8_ = bf16[1360,128]{1,0:T(8,128)(2,1)S(1)} collective-permute-done((bf16[1360,128]{1,0:T(8,128)(2,1)S(1)}, bf16[1360,128]{1,0:T(8,128)(2,1)S(1)}, u32[]{:S(2)}, u32[]{:S(2)}) %collective-permute-start.9) | collective-permute-done | bytes 348192 | tf_op jit(solution)/shard_map/ppermute | solution.py:380
  23.4 0.0 collective-permute-start.10
  23.4 0.0 collective-permute-done.8.refs_7_
  23.4 0.0 collective-permute-done.4.refs_6_
  23.4 5.8 %second_group.1 = (bf16[8,256,128]{2,1,0:T(8,128)(2,1)S(1)}, bf16[256,256]{1,0:T(8,128)(2,1)S(1)}, f32[8,72,256]{2,1,0:T(8,128)S(1)}, f32[8,256]{1,0:T(8,128)S(1...) custom-call(bf16[256,256]{1,0:T(8,128)(2,1)S(1)} %get-tuple-element.44.refs_0_, ...), custom_call_target="tpu_custom_call" | custom-call | flops 4898947072 | bytes 8388608 | tf_op jit(solution)/shard_map/second_group/pallas_call | solution.py:356
  29.2 0.0 copy-start
  29.2 0.0 collective-permute-done.11.refs_7_
  29.2 0.6 %collective-permute-start.12 = (bf16[816,128]{1,0:T(8,128)(2,1)S(1)}, bf16[816,128]{1,0:T(8,128)(2,1)S(1)}, u32[]{:S(2)}, u32[]{:S(2)}) collective-permute-start(bf16[816,128]{1,0:T(8,128)(2,1)S(1)} %collective-permute-done.11.refs_7_), channel_id=1, source_target_pairs={{0,8},{8,0},{16,24},{24,16},{1,9},{9,1},{17,25},{25,17},{2,10},{10... | collective-permute-start | bytes 626696 | tf_op jit(solution)/shard_map/ppermute | solution.py:380
  29.8 0.0 collective-permute-done.10.refs_6_
  29.8 2.6 %far.1 = (f32[8,72,256]{2,1,0:T(8,128)S(1)}, f32[8,256]{1,0:T(8,128)S(1)}, f32[8,72,256]{2,1,0:T(8,128)S(1)}, f32[8,256]{1,0:T(8,128)S(1)}) custom-call(bf16[256,256]{1,0:T(8,128)(2,1)S(1)} %get-tuple-element.44.refs_0_, bf16[256,256]{1,0:T(8,128)(2,1)S(1)} %get-tuple-element.59.refs_1_, bf16[8,256,128]{2,1,0:T(8,128)(2,1)S(1)} %get-tuple-element.46.refs_2_, ...), custom_call_target="tpu_custom_call" | custom-call | flops 2147483648 | bytes 8388608 | tf_op jit(solution)/shard_map/far/pallas_call | solution.py:356
  32.4 0.0 collective-permute-done.12.refs_6_
  32.4 0.0 copy-done
  32.4 2.2 %last.1 = (bf16[128,1024]{1,0:T(8,128)(2,1)S(1)}, bf16[128,1024]{1,0:T(8,128)(2,1)S(1)}) custom-call(bf16[256,256]{1,0:T(8,128)(2,1)S(1)} %get-tuple-element.44.refs_0_, bf16[256,256]{1,0:T(8,128)(2,1)S(1)} %get-tuple-element.59.refs_1_, bf16[8,256,128]{2,1,0:T(8,128)(2,1)S(1)} %get-tuple-element.46.refs_2_, ...), custom_call_target="tpu_custom_call" | custom-call | flops 1342177280 | bytes 8388608 | tf_op jit(solution)/shard_map/last/pallas_call | solution.py:356
  34.6 1.7 %collective-permute-start.13 = (bf16[32,1024]{1,0:T(8,128)(2,1)S(1)}, bf16[32,1024]{1,0:T(8,128)(2,1)S(1)}, u32[]{:S(2)}, u32[]{:S(2)}) collective-permute-start(bf16[32,1024]{1,0:T(8,128)(2,1)S(1)} %get-tuple-element.75), channel_id=1, source_target_pairs={{0,4},{1,5},{2,6},{3,7},{4,0},{5,1},{6,2},{7,3},{8,12},{9,13},{10,... | collective-permute-start | bytes 196616 | tf_op jit(solution)/shard_map/ppermute | solution.py:377
  36.3 1.6 %collective-permute-start.14 = (bf16[32,1024]{1,0:T(8,128)(2,1)S(1)}, bf16[32,1024]{1,0:T(8,128)(2,1)S(1)}, u32[]{:S(2)}, u32[]{:S(2)}) collective-permute-start(bf16[32,1024]{1,0:T(8,128)(2,1)S(1)} %get-tuple-element.74), channel_id=1, source_target_pairs={{0,1},{1,0},{2,3},{3,2},{4,5},{5,4},{6,7},{7,6},{8,9},{9,8},{10,11... | collective-permute-start | bytes 196616 | tf_op jit(solution)/shard_map/ppermute | solution.py:377
  37.9 0.4 collective-permute-start.15
  38.3 1.4 %collective-permute-start.16 = (bf16[32,1024]{1,0:T(8,128)(2,1)S(1)}, bf16[32,1024]{1,0:T(8,128)(2,1)S(1)}, u32[]{:S(2)}, u32[]{:S(2)}) collective-permute-start(bf16[32,1024]{1,0:T(8,128)(2,1)S(1)} %get-tuple-element.79), channel_id=1, source_target_pairs={{0,6},{1,7},{2,4},{3,5},{4,2},{5,3},{6,0},{7,1},{8,14},{9,15},{10,... | collective-permute-start | bytes 196616 | tf_op jit(solution)/shard_map/ppermute | solution.py:377
  39.7 1.7 %collective-permute-start.17 = (bf16[32,1024]{1,0:T(8,128)(2,1)S(1)}, bf16[32,1024]{1,0:T(8,128)(2,1)S(1)}, u32[]{:S(2)}, u32[]{:S(2)}) collective-permute-start(bf16[32,1024]{1,0:T(8,128)(2,1)S(1)} %get-tuple-element.78), channel_id=1, source_target_pairs={{0,5},{1,4},{2,7},{3,6},{4,1},{5,0},{6,3},{7,2},{8,13},{9,12},{10,... | collective-permute-start | bytes 196616 | tf_op jit(solution)/shard_map/ppermute | solution.py:377
  41.4 0.0 collective-permute-done.13.refs_1_
  41.4 2.8 %collective-permute-start.18 = (bf16[32,1024]{1,0:T(8,128)(2,1)S(1)}, bf16[32,1024]{1,0:T(8,128)(2,1)S(1)}, u32[]{:S(2)}, u32[]{:S(2)}) collective-permute-start(bf16[32,1024]{1,0:T(8,128)(2,1)S(1)} %get-tuple-element.77), channel_id=1, source_target_pairs={{0,7},{1,6},{2,5},{3,4},{4,3},{5,2},{6,1},{7,0},{8,15},{9,14},{10,... | collective-permute-start | bytes 196616 | tf_op jit(solution)/shard_map/ppermute | solution.py:377
  44.1 0.0 collective-permute-done.14.refs_2_
  44.1 0.8 %collective-permute-start.19 = (bf16[32,1024]{1,0:T(8,128)(2,1)S(1)}, bf16[32,1024]{1,0:T(8,128)(2,1)S(1)}, u32[]{:S(2)}, u32[]{:S(2)}) collective-permute-start(bf16[32,1024]{1,0:T(8,128)(2,1)S(1)} %get-tuple-element.73), channel_id=1, source_target_pairs={{0,3},{1,2},{2,1},{3,0},{4,7},{5,6},{6,5},{7,4},{8,11},{9,10},{10,... | collective-permute-start | bytes 196616 | tf_op jit(solution)/shard_map/ppermute | solution.py:377
  45.0 0.0 collective-permute-done.15.refs_3_
  45.0 0.0 collective-permute-done.16.refs_4_
  45.0 4.2 %collective-permute-done.17.refs_5_ = bf16[32,1024]{1,0:T(8,128)(2,1)S(1)} collective-permute-done((bf16[32,1024]{1,0:T(8,128)(2,1)S(1)}, bf16[32,1024]{1,0:T(8,128)(2,1)S(1)}, u32[]{:S(2)}, u32[]{:S(2)}) %collective-permute-start.17) | collective-permute-done | bytes 65568 | tf_op jit(solution)/shard_map/ppermute | solution.py:377
  49.1 0.0 collective-permute-done.18.refs_6_
  49.1 0.4 collective-permute-done.19.refs_7_
  49.6 0.8 %unpack.1 = bf16[8,32,1024]{2,1,0:T(8,128)(2,1)} custom-call(bf16[32,1024]{1,0:T(8,128)(2,1)S(1)} %get-tuple-element.76.refs_0_, bf16[32,1024]{1,0:T(8,128)(2,1)S(1)} %collective-permute-done.13.refs_1_, bf16[32,1024]{1,0:T(8,128)(2,1)S(1)} %collective-permute-done.14.refs_2_, bf16[32,1024]{1,0:T(8,128)(2,1)S(1)} %collective-permute-done.15.refs_3_, ...), custom_call_target="tpu_custom_call" | custom-call | tf_op jit(solution)/shard_map/unpack/pallas_call | solution.py:99
  (10 shorter events, 0.1 us)
Async XLA Ops:
  1.4 8.9 %collective-permute-start = (bf16[272,128]{1,0:T(8,128)(2,1)S(1)}, bf16[272,128]{1,0:T(8,128)(2,1)S(1)}, u32[]{:S(2)}, u32[]{:S(2)}) collective-permute-start(bf16[272,128]{1,0:T(8,128)(2,1)S(1)} %get-tuple-element.39), channel_id=1, source_target_pairs={{0,4},{1,5},{2,6},{3,7},{4,0},{5,1},{6,2},{7,3},{8,12},{9,13},{10,... | collective-permute-start | bytes 208904 | tf_op jit(solution)/shard_map/ppermute | solution.py:377
  5.5 7.5 %collective-permute-start.1 = (bf16[272,128]{1,0:T(8,128)(2,1)S(1)}, bf16[272,128]{1,0:T(8,128)(2,1)S(1)}, u32[]{:S(2)}, u32[]{:S(2)}) collective-permute-start(bf16[272,128]{1,0:T(8,128)(2,1)S(1)} %get-tuple-element.40), channel_id=1, source_target_pairs={{0,1},{1,0},{2,3},{3,2},{4,5},{5,4},{6,7},{7,6},{8,9},{9,8},{10,11... | collective-permute-start | bytes 208904 | tf_op jit(solution)/shard_map/ppermute | solution.py:377
  7.0 6.9 %collective-permute-start.2 = (bf16[272,128]{1,0:T(8,128)(2,1)S(1)}, bf16[272,128]{1,0:T(8,128)(2,1)S(1)}, u32[]{:S(2)}, u32[]{:S(2)}) collective-permute-start(bf16[272,128]{1,0:T(8,128)(2,1)S(1)} %get-tuple-element.41), channel_id=1, source_target_pairs={{0,3},{1,2},{2,1},{3,0},{4,7},{5,6},{6,5},{7,4},{8,11},{9,10},{10,... | collective-permute-start | bytes 208904 | tf_op jit(solution)/shard_map/ppermute | solution.py:377
  8.5 5.5 %collective-permute-start.3 = (bf16[272,128]{1,0:T(8,128)(2,1)S(1)}, bf16[272,128]{1,0:T(8,128)(2,1)S(1)}, u32[]{:S(2)}, u32[]{:S(2)}) collective-permute-start(bf16[272,128]{1,0:T(8,128)(2,1)S(1)} %get-tuple-element.43), channel_id=1, source_target_pairs={{0,2},{1,3},{2,0},{3,1},{4,6},{5,7},{6,4},{7,5},{8,10},{9,11},{10,... | collective-permute-start | bytes 208904 | tf_op jit(solution)/shard_map/ppermute | solution.py:377
  9.0 10.7 %collective-permute-start.5 = (bf16[272,128]{1,0:T(8,128)(2,1)S(1)}, bf16[272,128]{1,0:T(8,128)(2,1)S(1)}, u32[]{:S(2)}, u32[]{:S(2)}) collective-permute-start(bf16[272,128]{1,0:T(8,128)(2,1)S(1)} %get-tuple-element.51), channel_id=1, source_target_pairs={{0,6},{1,7},{2,4},{3,5},{4,2},{5,3},{6,0},{7,1},{8,14},{9,15},{10,... | collective-permute-start | bytes 208904 | tf_op jit(solution)/shard_map/ppermute | solution.py:377
  10.3 10.3 %collective-permute-start.6 = (bf16[272,128]{1,0:T(8,128)(2,1)S(1)}, bf16[272,128]{1,0:T(8,128)(2,1)S(1)}, u32[]{:S(2)}, u32[]{:S(2)}) collective-permute-start(bf16[272,128]{1,0:T(8,128)(2,1)S(1)} %get-tuple-element.52), channel_id=1, source_target_pairs={{0,5},{1,4},{2,7},{3,6},{4,1},{5,0},{6,3},{7,2},{8,13},{9,12},{10,... | collective-permute-start | bytes 208904 | tf_op jit(solution)/shard_map/ppermute | solution.py:377
  13.0 7.6 %collective-permute-start.7 = (bf16[272,128]{1,0:T(8,128)(2,1)S(1)}, bf16[272,128]{1,0:T(8,128)(2,1)S(1)}, u32[]{:S(2)}, u32[]{:S(2)}) collective-permute-start(bf16[272,128]{1,0:T(8,128)(2,1)S(1)} %get-tuple-element.53), channel_id=1, source_target_pairs={{0,7},{1,6},{2,5},{3,4},{4,3},{5,2},{6,1},{7,0},{8,15},{9,14},{10,... | collective-permute-start | bytes 208904 | tf_op jit(solution)/shard_map/ppermute | solution.py:377
  14.0 9.4 %collective-permute-start.9 = (bf16[1360,128]{1,0:T(8,128)(2,1)S(1)}, bf16[1360,128]{1,0:T(8,128)(2,1)S(1)}, u32[]{:S(2)}, u32[]{:S(2)}) collective-permute-start(bf16[1360,128]{1,0:T(8,128)(2,1)S(1)} %constant_dynamic-update-slice_fusion.refs_1_.refs_9_), channel_id=1, source_target_pairs={{0,16},{8,24},{16,0},{24,8},{1,17},{9,25},{17,1},{25,9},{2,18},{10... | collective-permute-start | bytes 1044488 | tf_op jit(solution)/shard_map/ppermute | solution.py:380
  15.6 7.8 %collective-permute-start.4 = (bf16[1360,128]{1,0:T(8,128)(2,1)S(1)}, bf16[1360,128]{1,0:T(8,128)(2,1)S(1)}, u32[]{:S(2)}, u32[]{:S(2)}) collective-permute-start(bf16[1360,128]{1,0:T(8,128)(2,1)S(1)} %constant_dynamic-update-slice_fusion.refs_1_.refs_9_), channel_id=1, source_target_pairs={{0,8},{8,0},{16,24},{24,16},{1,9},{9,1},{17,25},{25,17},{2,10},{10... | collective-permute-start | bytes 1044488 | tf_op jit(solution)/shard_map/ppermute | solution.py:380
  20.7 2.7 %collective-permute-start.8 = (bf16[816,128]{1,0:T(8,128)(2,1)S(1)}, bf16[816,128]{1,0:T(8,128)(2,1)S(1)}, u32[]{:S(2)}, u32[]{:S(2)}) collective-permute-start(bf16[816,128]{1,0:T(8,128)(2,1)S(1)} %constant_dynamic-update-slice_fusion.5.refs_10_), channel_id=1, source_target_pairs={{0,8},{8,0},{16,24},{24,16},{1,9},{9,1},{17,25},{25,17},{2,10},{10... | collective-permute-start | bytes 626696 | tf_op jit(solution)/shard_map/ppermute | solution.py:380
  20.8 8.4 %collective-permute-start.11 = (bf16[816,128]{1,0:T(8,128)(2,1)S(1)}, bf16[816,128]{1,0:T(8,128)(2,1)S(1)}, u32[]{:S(2)}, u32[]{:S(2)}) collective-permute-start(bf16[816,128]{1,0:T(8,128)(2,1)S(1)} %constant_dynamic-update-slice_fusion.5.refs_10_), channel_id=1, source_target_pairs={{0,16},{8,24},{16,0},{24,8},{1,17},{9,25},{17,1},{25,9},{2,18},{10... | collective-permute-start | bytes 626696 | tf_op jit(solution)/shard_map/ppermute | solution.py:380
  23.4 6.4 %collective-permute-start.10 = (bf16[1360,128]{1,0:T(8,128)(2,1)S(1)}, bf16[1360,128]{1,0:T(8,128)(2,1)S(1)}, u32[]{:S(2)}, u32[]{:S(2)}) collective-permute-start(bf16[1360,128]{1,0:T(8,128)(2,1)S(1)} %collective-permute-done.9.refs_8_), channel_id=1, source_target_pairs={{0,8},{8,0},{16,24},{24,16},{1,9},{9,1},{17,25},{25,17},{2,10},{10... | collective-permute-start | bytes 1044488 | tf_op jit(solution)/shard_map/ppermute | solution.py:380
  29.2 3.2 %copy-start = (bf16[1024,1024]{1,0:T(8,128)(2,1)S(1)}, bf16[1024,1024]{1,0:T(8,128)(2,1)}, u32[]{:S(2)}) copy-start(bf16[1024,1024]{1,0:T(8,128)(2,1)} %refs_10_.1) | copy-start | bytes 6291460
  29.2 3.1 %collective-permute-start.12 = (bf16[816,128]{1,0:T(8,128)(2,1)S(1)}, bf16[816,128]{1,0:T(8,128)(2,1)S(1)}, u32[]{:S(2)}, u32[]{:S(2)}) collective-permute-start(bf16[816,128]{1,0:T(8,128)(2,1)S(1)} %collective-permute-done.11.refs_7_), channel_id=1, source_target_pairs={{0,8},{8,0},{16,24},{24,16},{1,9},{9,1},{17,25},{25,17},{2,10},{10... | collective-permute-start | bytes 626696 | tf_op jit(solution)/shard_map/ppermute | solution.py:380
  34.6 6.8 %collective-permute-start.13 = (bf16[32,1024]{1,0:T(8,128)(2,1)S(1)}, bf16[32,1024]{1,0:T(8,128)(2,1)S(1)}, u32[]{:S(2)}, u32[]{:S(2)}) collective-permute-start(bf16[32,1024]{1,0:T(8,128)(2,1)S(1)} %get-tuple-element.75), channel_id=1, source_target_pairs={{0,4},{1,5},{2,6},{3,7},{4,0},{5,1},{6,2},{7,3},{8,12},{9,13},{10,... | collective-permute-start | bytes 196616 | tf_op jit(solution)/shard_map/ppermute | solution.py:377
  36.3 7.8 %collective-permute-start.14 = (bf16[32,1024]{1,0:T(8,128)(2,1)S(1)}, bf16[32,1024]{1,0:T(8,128)(2,1)S(1)}, u32[]{:S(2)}, u32[]{:S(2)}) collective-permute-start(bf16[32,1024]{1,0:T(8,128)(2,1)S(1)} %get-tuple-element.74), channel_id=1, source_target_pairs={{0,1},{1,0},{2,3},{3,2},{4,5},{5,4},{6,7},{7,6},{8,9},{9,8},{10,11... | collective-permute-start | bytes 196616 | tf_op jit(solution)/shard_map/ppermute | solution.py:377
  37.9 7.1 %collective-permute-start.15 = (bf16[32,1024]{1,0:T(8,128)(2,1)S(1)}, bf16[32,1024]{1,0:T(8,128)(2,1)S(1)}, u32[]{:S(2)}, u32[]{:S(2)}) collective-permute-start(bf16[32,1024]{1,0:T(8,128)(2,1)S(1)} %get-tuple-element.80), channel_id=1, source_target_pairs={{0,2},{1,3},{2,0},{3,1},{4,6},{5,7},{6,4},{7,5},{8,10},{9,11},{10,... | collective-permute-start | bytes 196616 | tf_op jit(solution)/shard_map/ppermute | solution.py:377
  38.3 6.6 %collective-permute-start.16 = (bf16[32,1024]{1,0:T(8,128)(2,1)S(1)}, bf16[32,1024]{1,0:T(8,128)(2,1)S(1)}, u32[]{:S(2)}, u32[]{:S(2)}) collective-permute-start(bf16[32,1024]{1,0:T(8,128)(2,1)S(1)} %get-tuple-element.79), channel_id=1, source_target_pairs={{0,6},{1,7},{2,4},{3,5},{4,2},{5,3},{6,0},{7,1},{8,14},{9,15},{10,... | collective-permute-start | bytes 196616 | tf_op jit(solution)/shard_map/ppermute | solution.py:377
  39.7 9.4 %collective-permute-start.17 = (bf16[32,1024]{1,0:T(8,128)(2,1)S(1)}, bf16[32,1024]{1,0:T(8,128)(2,1)S(1)}, u32[]{:S(2)}, u32[]{:S(2)}) collective-permute-start(bf16[32,1024]{1,0:T(8,128)(2,1)S(1)} %get-tuple-element.78), channel_id=1, source_target_pairs={{0,5},{1,4},{2,7},{3,6},{4,1},{5,0},{6,3},{7,2},{8,13},{9,12},{10,... | collective-permute-start | bytes 196616 | tf_op jit(solution)/shard_map/ppermute | solution.py:377
  41.4 7.8 %collective-permute-start.18 = (bf16[32,1024]{1,0:T(8,128)(2,1)S(1)}, bf16[32,1024]{1,0:T(8,128)(2,1)S(1)}, u32[]{:S(2)}, u32[]{:S(2)}) collective-permute-start(bf16[32,1024]{1,0:T(8,128)(2,1)S(1)} %get-tuple-element.77), channel_id=1, source_target_pairs={{0,7},{1,6},{2,5},{3,4},{4,3},{5,2},{6,1},{7,0},{8,15},{9,14},{10,... | collective-permute-start | bytes 196616 | tf_op jit(solution)/shard_map/ppermute | solution.py:377
  44.1 5.4 %collective-permute-start.19 = (bf16[32,1024]{1,0:T(8,128)(2,1)S(1)}, bf16[32,1024]{1,0:T(8,128)(2,1)S(1)}, u32[]{:S(2)}, u32[]{:S(2)}) collective-permute-start(bf16[32,1024]{1,0:T(8,128)(2,1)S(1)} %get-tuple-element.73), channel_id=1, source_target_pairs={{0,3},{1,2},{2,1},{3,0},{4,7},{5,6},{6,5},{7,4},{8,11},{9,10},{10,... | collective-permute-start | bytes 196616 | tf_op jit(solution)/shard_map/ppermute | solution.py:377

commit v7 on v6

--- a/solution.py
+++ b/solution.py
@@ -168,13 +168,12 @@
             self.copies[0].wait()
         for q in self.queries:
             self.project_queries(q)
+        self.late = self.fetch and len(self.attend) == 1
         if self.fetch:
             self.copies[1].wait()
-        for b in self.blocks:
-            cells = self.load_cells("k", b)
-            self.project_keys(b, cells)
-            if not self.fetch:
-                self.project_values(b, cells)
+            if not self.late:
+                self.copies[2].wait()
+        self.plan()
         self.attend_all()
         if self.finish:
             for q in self.touched:
@@ -203,15 +202,15 @@
         allowed = self.write["pairs_allowed"][...]
         self.write["adjacency"][...] = allowed.astype(F32).astype(BF16)
 
-    def load_cells(self, kind, index):
-        cells_ref, row = self.write["cells"], 0
+    def load_cells(self, kind, index, slot=0):
+        cells_ref, row = self.write["cells"].at[slot], 0
         for ref, place in self.tiles_of(kind, index):
             for _ in range(self.piece // ROWS):
                 for start in range(0, self.width, LANES):
                     cells_ref[row : row + ROWS, start : start + LANES] = ref[place : place + ROWS, :]
                     place += ROWS
                 row += ROWS
-        return cells_ref[:row, :]
+        return lambda: cells_ref[:row, :]
 
     def tags_of(self, kind, index):
         tags, parts = [], self.piece // ROWS
@@ -225,7 +224,7 @@
 
     def project_queries(self, q):
         rows = self.rows[q]
-        cells = self.load_cells("q", q)
+        cells = self.load_cells("q", q)()
         for start in range(0, self.width, COLS):
             query = (dot(cells, self.w[:, start : start + COLS]) * SCALE).astype(BF16)
             lane = lax.broadcasted_iota(jnp.int32, (rows, PAIR), 1)
@@ -239,45 +238,53 @@
         near = ((1.0 - near) * MASKED).astype(BF16)
         self.write[f"G{q}"][...] = jnp.concatenate([near, near], axis=1)
 
-    def project_keys(self, b, cells):
-        for start in range(0, self.width, COLS):
-            part = slice(self.width + start, self.width + start + COLS)
-            self.write[f"K{b}"][:, start : start + COLS] = dot(cells, self.w[:, part]).astype(BF16)
-
-    def project_values(self, b, cells):
-        ones = jnp.ones((self.pairs, VAL_ROWS - PAIR, self.cells[b]), BF16)
-        self.write[f"V{b}"][:, PAIR:, :] = ones
-        for start in range(0, self.width, COLS):
-            part = slice(2 * self.width + start, 2 * self.width + start + COLS)
-            values = dot(cells, self.w[:, part]).astype(BF16).T
-            for i in range(COLS // PAIR):
-                rows = values[i * PAIR : (i + 1) * PAIR]
-                self.write[f"V{b}"][start // PAIR + i, :PAIR, :] = rows
+    def plan(self):
+        self.due = {}
+        order = [b for _, b in self.attend]
+        for b in self.blocks:
+            turn = order.index(b)
+            cells = self.load_cells("k", b, self.blocks.index(b))
+            for start in range(0, self.width, COLS):
+                self.due.setdefault(turn, []).append((self.project_keys, b, cells, start))
+                self.due.setdefault(turn + 1, []).append((self.project_values, b, cells, start))
+
+    def run_due(self, turn, step=0, steps=1):
+        tasks = self.due.get(turn, [])
+        for task, *operands in tasks[len(tasks) * step // steps : len(tasks) * (step + 1) // steps]:
+            task(*operands)
+
+    def project_keys(self, b, cells, start):
+        part = slice(self.width + start, self.width + start + COLS)
+        self.write[f"K{b}"][:, start : start + COLS] = dot(cells(), self.w[:, part]).astype(BF16)
+
+    def project_values(self, b, cells, start):
+        part = slice(2 * self.width + start, 2 * self.width + start + COLS)
+        values = dot(cells(), self.w[:, part]).astype(BF16).T
+        for i in range(COLS // PAIR):
+            pair = start // PAIR + i
+            self.write[f"V{b}"][pair, :PAIR, :] = values[i * PAIR : (i + 1) * PAIR]
+            ones = jnp.ones((VAL_ROWS - PAIR, self.cells[b]), BF16)
+            self.write[f"V{b}"][pair, PAIR:, :] = ones
 
     def attend_all(self):
         source = {q: self.read for q in self.touched if f"acc{q}" in self.held}
         before = None
-        late = self.blocks if self.fetch else []
+        self.run_due(0)
         for turn, (q, b) in enumerate(self.attend):
             after = self.start_turn(q, b, source.get(q), turn % 2)
             source[q] = self.write
             for pair in range(self.pairs):
                 self.weigh(after, pair)
-                if before is not None and late:
-                    late = self.project_late_values(late)
+                if not self.late:
+                    self.run_due(turn + 1, pair, self.pairs)
                 if before is not None:
                     self.add_values(before, pair)
             before = after
-        if late:
-            self.project_late_values(late)
+        if self.late:
+            self.copies[2].wait()
+            self.run_due(len(self.attend))
         for pair in range(self.pairs):
             self.add_values(before, pair)
-
-    def project_late_values(self, late):
-        self.copies[2].wait()
-        for b in late:
-            self.project_values(b, self.load_cells("k", b))
-        return []
 
     def start_turn(self, q, b, before, slot):
         cells = self.cells[b]
@@ -334,7 +341,7 @@
         rows = max(self.rows.values())
         scratch = [pltpu.VMEM(*shape) for shape in self.scratch.values()]
         scratch += [
-            pltpu.VMEM((max(self.block, rows), self.width), BF16),
+            pltpu.VMEM((max(len(self.blocks), 1), max(self.block, rows), self.width), BF16),
             pltpu.VMEM((2, self.block, 2 * rows), F32),
             pltpu.VMEM((2, self.pairs, self.block, 2 * rows), BF16),
         ]

time: 50.6 us -> 50.3 us (level)
  transfers between devices with their start and end apart: 20 -> 20, of which waited for: 4 -> 4; matrix products, arithmetic and copies ran while one was open for 0% -> 0% of each run, Pallas kernels for 25% -> 24%
where the time goes in v7:
time: 50.3 us; the launch traced here: 50.2 us
  starting transfers between devices  26.6 us (53%)
  Pallas kernels  16.6 us (33%)
  waiting for transfers between devices  6.65 us (13%)
    ppermute x14, starting transfers between devices, over_cells(): lax.ppermute(value, 'cells', [(i, i ^ step) for i in range(cell_devs)])  22.9 us
    pallas_call x4, Pallas kernels, call(): pl.pallas_call(self.body, out_shape=tuple(out_shape), in_specs=[hbm if n....  14.3 us
    ppermute x14, waiting for transfers between devices, over_cells(): lax.ppermute(value, 'cells', [(i, i ^ step) for i in range(cell_devs)])  5.56 us
    ppermute x6, starting transfers between devices, over_heads(): lax.ppermute(value, 'heads', [(i, i ^ step) for i in range(head_devs)])  3.75 us
    pallas_call x1, Pallas kernels, pack(): pl.pallas_call(lambda *refs: pack_kernel(order, *refs), out_shape=[jax.Sh...  1.39 us
    ppermute x6, waiting for transfers between devices, over_heads(): lax.ppermute(value, 'heads', [(i, i ^ step) for i in range(head_devs)])  1.1 us
  transfers between devices with their start and end apart: 20, of which 4 were waited for; matrix products, arithmetic and copies ran while one was open for 0% of the time, Pallas kernels for 24%

profile of v7, /device:TPU:0, one launch (start us, length us, event | category | flops | bytes accessed | tf_op | source)
XLA Modules:
  0.0 50.2 jit_solution(10165404260280560301)
XLA Ops:
  0.0 1.4 %pack.1 = (bf16[272,128]{1,0:T(8,128)(2,1)S(1)}, bf16[272,128]{1,0:T(8,128)(2,1)S(1)}, bf16[272,128]{1,0:T(8,128)(2,1)S(1)}, bf16[272,128]{1,0:T(8,128)(2,1)S(1)...) custom-call(bf16[8,32,1024]{2,1,0:T(8,128)(2,1)} %refs_0_.2, ...), custom_call_target="tpu_custom_call" | custom-call | tf_op jit(solution)/shard_map/pack/pallas_call | solution.py:71
  1.4 4.1 %collective-permute-start = (bf16[272,128]{1,0:T(8,128)(2,1)S(1)}, bf16[272,128]{1,0:T(8,128)(2,1)S(1)}, u32[]{:S(2)}, u32[]{:S(2)}) collective-permute-start(bf16[272,128]{1,0:T(8,128)(2,1)S(1)} %get-tuple-element.39), channel_id=1, source_target_pairs={{0,4},{1,5},{2,6},{3,7},{4,0},{5,1},{6,2},{7,3},{8,12},{9,13},{10,... | collective-permute-start | bytes 208904 | tf_op jit(solution)/shard_map/ppermute | solution.py:384
  5.5 1.5 %collective-permute-start.1 = (bf16[272,128]{1,0:T(8,128)(2,1)S(1)}, bf16[272,128]{1,0:T(8,128)(2,1)S(1)}, u32[]{:S(2)}, u32[]{:S(2)}) collective-permute-start(bf16[272,128]{1,0:T(8,128)(2,1)S(1)} %get-tuple-element.40), channel_id=1, source_target_pairs={{0,1},{1,0},{2,3},{3,2},{4,5},{5,4},{6,7},{7,6},{8,9},{9,8},{10,11... | collective-permute-start | bytes 208904 | tf_op jit(solution)/shard_map/ppermute | solution.py:384
  7.0 1.5 %collective-permute-start.2 = (bf16[272,128]{1,0:T(8,128)(2,1)S(1)}, bf16[272,128]{1,0:T(8,128)(2,1)S(1)}, u32[]{:S(2)}, u32[]{:S(2)}) collective-permute-start(bf16[272,128]{1,0:T(8,128)(2,1)S(1)} %get-tuple-element.41), channel_id=1, source_target_pairs={{0,3},{1,2},{2,1},{3,0},{4,7},{5,6},{6,5},{7,4},{8,11},{9,10},{10,... | collective-permute-start | bytes 208904 | tf_op jit(solution)/shard_map/ppermute | solution.py:384
  8.5 0.4 collective-permute-start.3
  9.0 1.3 %collective-permute-start.5 = (bf16[272,128]{1,0:T(8,128)(2,1)S(1)}, bf16[272,128]{1,0:T(8,128)(2,1)S(1)}, u32[]{:S(2)}, u32[]{:S(2)}) collective-permute-start(bf16[272,128]{1,0:T(8,128)(2,1)S(1)} %get-tuple-element.51), channel_id=1, source_target_pairs={{0,6},{1,7},{2,4},{3,5},{4,2},{5,3},{6,0},{7,1},{8,14},{9,15},{10,... | collective-permute-start | bytes 208904 | tf_op jit(solution)/shard_map/ppermute | solution.py:384
  10.3 0.0 collective-permute-done
  10.3 2.6 %collective-permute-start.6 = (bf16[272,128]{1,0:T(8,128)(2,1)S(1)}, bf16[272,128]{1,0:T(8,128)(2,1)S(1)}, u32[]{:S(2)}, u32[]{:S(2)}) collective-permute-start(bf16[272,128]{1,0:T(8,128)(2,1)S(1)} %get-tuple-element.52), channel_id=1, source_target_pairs={{0,5},{1,4},{2,7},{3,6},{4,1},{5,0},{6,3},{7,2},{8,13},{9,12},{10,... | collective-permute-start | bytes 208904 | tf_op jit(solution)/shard_map/ppermute | solution.py:384
  13.0 0.0 collective-permute-done.1
  13.0 0.9 %collective-permute-start.7 = (bf16[272,128]{1,0:T(8,128)(2,1)S(1)}, bf16[272,128]{1,0:T(8,128)(2,1)S(1)}, u32[]{:S(2)}, u32[]{:S(2)}) collective-permute-start(bf16[272,128]{1,0:T(8,128)(2,1)S(1)} %get-tuple-element.53), channel_id=1, source_target_pairs={{0,7},{1,6},{2,5},{3,4},{4,3},{5,2},{6,1},{7,0},{8,15},{9,14},{10,... | collective-permute-start | bytes 208904 | tf_op jit(solution)/shard_map/ppermute | solution.py:384
  14.0 0.0 collective-permute-done.2
  14.0 0.0 collective-permute-done.3
  14.0 1.6 %collective-permute-start.9 = (bf16[1360,128]{1,0:T(8,128)(2,1)S(1)}, bf16[1360,128]{1,0:T(8,128)(2,1)S(1)}, u32[]{:S(2)}, u32[]{:S(2)}) collective-permute-start(bf16[1360,128]{1,0:T(8,128)(2,1)S(1)} %constant_dynamic-update-slice_fusion.refs_1_.refs_9_), channel_id=1, source_target_pairs={{0,16},{8,24},{16,0},{24,8},{1,17},{9,25},{17,1},{25,9},{2,18},{10... | collective-permute-start | bytes 1044488 | tf_op jit(solution)/shard_map/ppermute | solution.py:387
  15.6 0.0 collective-permute-start.4
  15.6 4.0 %first_group.1 = (bf16[8,256,128]{2,1,0:T(8,128)(2,1)S(1)}, bf16[256,256]{1,0:T(8,128)(2,1)S(1)}, f32[8,72,256]{2,1,0:T(8,128)S(1)}, f32[8,256]{1,0:T(8,128)S(1)...) custom-call(s32[256,256]{1,0:T(8,128)} %refs_0_.3, ...), custom_call_target="tpu_custom_call" | custom-call | flops 1275068416 | bytes 8388608 | tf_op jit(solution)/shard_map/first_group/pallas_call | solution.py:363
  19.6 0.0 collective-permute-done.5
  19.7 1.0 %collective-permute-done.6 = bf16[272,128]{1,0:T(8,128)(2,1)S(1)} collective-permute-done((bf16[272,128]{1,0:T(8,128)(2,1)S(1)}, bf16[272,128]{1,0:T(8,128)(2,1)S(1)}, u32[]{:S(2)}, u32[]{:S(2)}) %collective-permute-start.6) | collective-permute-done | bytes 69664 | tf_op jit(solution)/shard_map/ppermute | solution.py:384
  20.6 0.0 collective-permute-done.7
  20.7 0.1 collective-permute-start.8
  20.8 1.6 %collective-permute-start.11 = (bf16[816,128]{1,0:T(8,128)(2,1)S(1)}, bf16[816,128]{1,0:T(8,128)(2,1)S(1)}, u32[]{:S(2)}, u32[]{:S(2)}) collective-permute-start(bf16[816,128]{1,0:T(8,128)(2,1)S(1)} %constant_dynamic-update-slice_fusion.5.refs_10_), channel_id=1, source_target_pairs={{0,16},{8,24},{16,0},{24,8},{1,17},{9,25},{17,1},{25,9},{2,18},{10... | collective-permute-start | bytes 626696 | tf_op jit(solution)/shard_map/ppermute | solution.py:387
  22.3 1.1 %collective-permute-done.9.refs_8_ = bf16[1360,128]{1,0:T(8,128)(2,1)S(1)} collective-permute-done((bf16[1360,128]{1,0:T(8,128)(2,1)S(1)}, bf16[1360,128]{1,0:T(8,128)(2,1)S(1)}, u32[]{:S(2)}, u32[]{:S(2)}) %collective-permute-start.9) | collective-permute-done | bytes 348192 | tf_op jit(solution)/shard_map/ppermute | solution.py:387
  23.4 0.0 collective-permute-start.10
  23.4 0.0 collective-permute-done.8.refs_7_
  23.4 0.0 collective-permute-done.4.refs_6_
  23.4 5.6 %second_group.1 = (bf16[8,256,128]{2,1,0:T(8,128)(2,1)S(1)}, bf16[256,256]{1,0:T(8,128)(2,1)S(1)}, f32[8,72,256]{2,1,0:T(8,128)S(1)}, f32[8,256]{1,0:T(8,128)S(1...) custom-call(bf16[256,256]{1,0:T(8,128)(2,1)S(1)} %get-tuple-element.44.refs_0_, ...), custom_call_target="tpu_custom_call" | custom-call | flops 4898947072 | bytes 8388608 | tf_op jit(solution)/shard_map/second_group/pallas_call | solution.py:363
  29.0 0.0 copy-start
  29.0 0.0 collective-permute-done.11.refs_7_
  29.0 0.6 %collective-permute-start.12 = (bf16[816,128]{1,0:T(8,128)(2,1)S(1)}, bf16[816,128]{1,0:T(8,128)(2,1)S(1)}, u32[]{:S(2)}, u32[]{:S(2)}) collective-permute-start(bf16[816,128]{1,0:T(8,128)(2,1)S(1)} %collective-permute-done.11.refs_7_), channel_id=1, source_target_pairs={{0,8},{8,0},{16,24},{24,16},{1,9},{9,1},{17,25},{25,17},{2,10},{10... | collective-permute-start | bytes 626696 | tf_op jit(solution)/shard_map/ppermute | solution.py:387
  29.6 0.0 collective-permute-done.10.refs_6_
  29.6 2.5 %far.1 = (f32[8,72,256]{2,1,0:T(8,128)S(1)}, f32[8,256]{1,0:T(8,128)S(1)}, f32[8,72,256]{2,1,0:T(8,128)S(1)}, f32[8,256]{1,0:T(8,128)S(1)}) custom-call(bf16[256,256]{1,0:T(8,128)(2,1)S(1)} %get-tuple-element.44.refs_0_, bf16[256,256]{1,0:T(8,128)(2,1)S(1)} %get-tuple-element.59.refs_1_, bf16[8,256,128]{2,1,0:T(8,128)(2,1)S(1)} %get-tuple-element.46.refs_2_, ...), custom_call_target="tpu_custom_call" | custom-call | flops 2147483648 | bytes 8388608 | tf_op jit(solution)/shard_map/far/pallas_call | solution.py:363
  32.1 0.0 collective-permute-done.12.refs_6_
  32.1 0.0 copy-done
  32.1 2.2 %last.1 = (bf16[128,1024]{1,0:T(8,128)(2,1)S(1)}, bf16[128,1024]{1,0:T(8,128)(2,1)S(1)}) custom-call(bf16[256,256]{1,0:T(8,128)(2,1)S(1)} %get-tuple-element.44.refs_0_, bf16[256,256]{1,0:T(8,128)(2,1)S(1)} %get-tuple-element.59.refs_1_, bf16[8,256,128]{2,1,0:T(8,128)(2,1)S(1)} %get-tuple-element.46.refs_2_, ...), custom_call_target="tpu_custom_call" | custom-call | flops 1342177280 | bytes 8388608 | tf_op jit(solution)/shard_map/last/pallas_call | solution.py:363
  34.4 1.7 %collective-permute-start.13 = (bf16[32,1024]{1,0:T(8,128)(2,1)S(1)}, bf16[32,1024]{1,0:T(8,128)(2,1)S(1)}, u32[]{:S(2)}, u32[]{:S(2)}) collective-permute-start(bf16[32,1024]{1,0:T(8,128)(2,1)S(1)} %get-tuple-element.75), channel_id=1, source_target_pairs={{0,4},{1,5},{2,6},{3,7},{4,0},{5,1},{6,2},{7,3},{8,12},{9,13},{10,... | collective-permute-start | bytes 196616 | tf_op jit(solution)/shard_map/ppermute | solution.py:384
  36.1 1.6 %collective-permute-start.14 = (bf16[32,1024]{1,0:T(8,128)(2,1)S(1)}, bf16[32,1024]{1,0:T(8,128)(2,1)S(1)}, u32[]{:S(2)}, u32[]{:S(2)}) collective-permute-start(bf16[32,1024]{1,0:T(8,128)(2,1)S(1)} %get-tuple-element.74), channel_id=1, source_target_pairs={{0,1},{1,0},{2,3},{3,2},{4,5},{5,4},{6,7},{7,6},{8,9},{9,8},{10,11... | collective-permute-start | bytes 196616 | tf_op jit(solution)/shard_map/ppermute | solution.py:384
  37.7 0.4 collective-permute-start.15
  38.1 1.4 %collective-permute-start.16 = (bf16[32,1024]{1,0:T(8,128)(2,1)S(1)}, bf16[32,1024]{1,0:T(8,128)(2,1)S(1)}, u32[]{:S(2)}, u32[]{:S(2)}) collective-permute-start(bf16[32,1024]{1,0:T(8,128)(2,1)S(1)} %get-tuple-element.79), channel_id=1, source_target_pairs={{0,6},{1,7},{2,4},{3,5},{4,2},{5,3},{6,0},{7,1},{8,14},{9,15},{10,... | collective-permute-start | bytes 196616 | tf_op jit(solution)/shard_map/ppermute | solution.py:384
  39.5 1.7 %collective-permute-start.17 = (bf16[32,1024]{1,0:T(8,128)(2,1)S(1)}, bf16[32,1024]{1,0:T(8,128)(2,1)S(1)}, u32[]{:S(2)}, u32[]{:S(2)}) collective-permute-start(bf16[32,1024]{1,0:T(8,128)(2,1)S(1)} %get-tuple-element.78), channel_id=1, source_target_pairs={{0,5},{1,4},{2,7},{3,6},{4,1},{5,0},{6,3},{7,2},{8,13},{9,12},{10,... | collective-permute-start | bytes 196616 | tf_op jit(solution)/shard_map/ppermute | solution.py:384
  41.1 0.0 collective-permute-done.13.refs_1_
  41.1 2.7 %collective-permute-start.18 = (bf16[32,1024]{1,0:T(8,128)(2,1)S(1)}, bf16[32,1024]{1,0:T(8,128)(2,1)S(1)}, u32[]{:S(2)}, u32[]{:S(2)}) collective-permute-start(bf16[32,1024]{1,0:T(8,128)(2,1)S(1)} %get-tuple-element.77), channel_id=1, source_target_pairs={{0,7},{1,6},{2,5},{3,4},{4,3},{5,2},{6,1},{7,0},{8,15},{9,14},{10,... | collective-permute-start | bytes 196616 | tf_op jit(solution)/shard_map/ppermute | solution.py:384
  43.9 0.0 collective-permute-done.14.refs_2_
  43.9 0.9 %collective-permute-start.19 = (bf16[32,1024]{1,0:T(8,128)(2,1)S(1)}, bf16[32,1024]{1,0:T(8,128)(2,1)S(1)}, u32[]{:S(2)}, u32[]{:S(2)}) collective-permute-start(bf16[32,1024]{1,0:T(8,128)(2,1)S(1)} %get-tuple-element.73), channel_id=1, source_target_pairs={{0,3},{1,2},{2,1},{3,0},{4,7},{5,6},{6,5},{7,4},{8,11},{9,10},{10,... | collective-permute-start | bytes 196616 | tf_op jit(solution)/shard_map/ppermute | solution.py:384
  44.8 0.0 collective-permute-done.15.refs_3_
  44.8 0.0 collective-permute-done.16.refs_4_
  44.8 4.1 %collective-permute-done.17.refs_5_ = bf16[32,1024]{1,0:T(8,128)(2,1)S(1)} collective-permute-done((bf16[32,1024]{1,0:T(8,128)(2,1)S(1)}, bf16[32,1024]{1,0:T(8,128)(2,1)S(1)}, u32[]{:S(2)}, u32[]{:S(2)}) %collective-permute-start.17) | collective-permute-done | bytes 65568 | tf_op jit(solution)/shard_map/ppermute | solution.py:384
  48.9 0.0 collective-permute-done.18.refs_6_
  48.9 0.4 collective-permute-done.19.refs_7_
  49.3 0.8 %unpack.1 = bf16[8,32,1024]{2,1,0:T(8,128)(2,1)} custom-call(bf16[32,1024]{1,0:T(8,128)(2,1)S(1)} %get-tuple-element.76.refs_0_, bf16[32,1024]{1,0:T(8,128)(2,1)S(1)} %collective-permute-done.13.refs_1_, bf16[32,1024]{1,0:T(8,128)(2,1)S(1)} %collective-permute-done.14.refs_2_, bf16[32,1024]{1,0:T(8,128)(2,1)S(1)} %collective-permute-done.15.refs_3_, ...), custom_call_target="tpu_custom_call" | custom-call | tf_op jit(solution)/shard_map/unpack/pallas_call | solution.py:99
  (10 shorter events, 0.1 us)
Async XLA Ops:
  1.4 8.9 %collective-permute-start = (bf16[272,128]{1,0:T(8,128)(2,1)S(1)}, bf16[272,128]{1,0:T(8,128)(2,1)S(1)}, u32[]{:S(2)}, u32[]{:S(2)}) collective-permute-start(bf16[272,128]{1,0:T(8,128)(2,1)S(1)} %get-tuple-element.39), channel_id=1, source_target_pairs={{0,4},{1,5},{2,6},{3,7},{4,0},{5,1},{6,2},{7,3},{8,12},{9,13},{10,... | collective-permute-start | bytes 208904 | tf_op jit(solution)/shard_map/ppermute | solution.py:384
  5.5 7.5 %collective-permute-start.1 = (bf16[272,128]{1,0:T(8,128)(2,1)S(1)}, bf16[272,128]{1,0:T(8,128)(2,1)S(1)}, u32[]{:S(2)}, u32[]{:S(2)}) collective-permute-start(bf16[272,128]{1,0:T(8,128)(2,1)S(1)} %get-tuple-element.40), channel_id=1, source_target_pairs={{0,1},{1,0},{2,3},{3,2},{4,5},{5,4},{6,7},{7,6},{8,9},{9,8},{10,11... | collective-permute-start | bytes 208904 | tf_op jit(solution)/shard_map/ppermute | solution.py:384
  7.0 6.9 %collective-permute-start.2 = (bf16[272,128]{1,0:T(8,128)(2,1)S(1)}, bf16[272,128]{1,0:T(8,128)(2,1)S(1)}, u32[]{:S(2)}, u32[]{:S(2)}) collective-permute-start(bf16[272,128]{1,0:T(8,128)(2,1)S(1)} %get-tuple-element.41), channel_id=1, source_target_pairs={{0,3},{1,2},{2,1},{3,0},{4,7},{5,6},{6,5},{7,4},{8,11},{9,10},{10,... | collective-permute-start | bytes 208904 | tf_op jit(solution)/shard_map/ppermute | solution.py:384
  8.5 5.5 %collective-permute-start.3 = (bf16[272,128]{1,0:T(8,128)(2,1)S(1)}, bf16[272,128]{1,0:T(8,128)(2,1)S(1)}, u32[]{:S(2)}, u32[]{:S(2)}) collective-permute-start(bf16[272,128]{1,0:T(8,128)(2,1)S(1)} %get-tuple-element.43), channel_id=1, source_target_pairs={{0,2},{1,3},{2,0},{3,1},{4,6},{5,7},{6,4},{7,5},{8,10},{9,11},{10,... | collective-permute-start | bytes 208904 | tf_op jit(solution)/shard_map/ppermute | solution.py:384
  9.0 10.7 %collective-permute-start.5 = (bf16[272,128]{1,0:T(8,128)(2,1)S(1)}, bf16[272,128]{1,0:T(8,128)(2,1)S(1)}, u32[]{:S(2)}, u32[]{:S(2)}) collective-permute-start(bf16[272,128]{1,0:T(8,128)(2,1)S(1)} %get-tuple-element.51), channel_id=1, source_target_pairs={{0,6},{1,7},{2,4},{3,5},{4,2},{5,3},{6,0},{7,1},{8,14},{9,15},{10,... | collective-permute-start | bytes 208904 | tf_op jit(solution)/shard_map/ppermute | solution.py:384
  10.3 10.3 %collective-permute-start.6 = (bf16[272,128]{1,0:T(8,128)(2,1)S(1)}, bf16[272,128]{1,0:T(8,128)(2,1)S(1)}, u32[]{:S(2)}, u32[]{:S(2)}) collective-permute-start(bf16[272,128]{1,0:T(8,128)(2,1)S(1)} %get-tuple-element.52), channel_id=1, source_target_pairs={{0,5},{1,4},{2,7},{3,6},{4,1},{5,0},{6,3},{7,2},{8,13},{9,12},{10,... | collective-permute-start | bytes 208904 | tf_op jit(solution)/shard_map/ppermute | solution.py:384
  13.0 7.6 %collective-permute-start.7 = (bf16[272,128]{1,0:T(8,128)(2,1)S(1)}, bf16[272,128]{1,0:T(8,128)(2,1)S(1)}, u32[]{:S(2)}, u32[]{:S(2)}) collective-permute-start(bf16[272,128]{1,0:T(8,128)(2,1)S(1)} %get-tuple-element.53), channel_id=1, source_target_pairs={{0,7},{1,6},{2,5},{3,4},{4,3},{5,2},{6,1},{7,0},{8,15},{9,14},{10,... | collective-permute-start | bytes 208904 | tf_op jit(solution)/shard_map/ppermute | solution.py:384
  14.0 9.4 %collective-permute-start.9 = (bf16[1360,128]{1,0:T(8,128)(2,1)S(1)}, bf16[1360,128]{1,0:T(8,128)(2,1)S(1)}, u32[]{:S(2)}, u32[]{:S(2)}) collective-permute-start(bf16[1360,128]{1,0:T(8,128)(2,1)S(1)} %constant_dynamic-update-slice_fusion.refs_1_.refs_9_), channel_id=1, source_target_pairs={{0,16},{8,24},{16,0},{24,8},{1,17},{9,25},{17,1},{25,9},{2,18},{10... | collective-permute-start | bytes 1044488 | tf_op jit(solution)/shard_map/ppermute | solution.py:387
  15.6 7.8 %collective-permute-start.4 = (bf16[1360,128]{1,0:T(8,128)(2,1)S(1)}, bf16[1360,128]{1,0:T(8,128)(2,1)S(1)}, u32[]{:S(2)}, u32[]{:S(2)}) collective-permute-start(bf16[1360,128]{1,0:T(8,128)(2,1)S(1)} %constant_dynamic-update-slice_fusion.refs_1_.refs_9_), channel_id=1, source_target_pairs={{0,8},{8,0},{16,24},{24,16},{1,9},{9,1},{17,25},{25,17},{2,10},{10... | collective-permute-start | bytes 1044488 | tf_op jit(solution)/shard_map/ppermute | solution.py:387
  20.7 2.7 %collective-permute-start.8 = (bf16[816,128]{1,0:T(8,128)(2,1)S(1)}, bf16[816,128]{1,0:T(8,128)(2,1)S(1)}, u32[]{:S(2)}, u32[]{:S(2)}) collective-permute-start(bf16[816,128]{1,0:T(8,128)(2,1)S(1)} %constant_dynamic-update-slice_fusion.5.refs_10_), channel_id=1, source_target_pairs={{0,8},{8,0},{16,24},{24,16},{1,9},{9,1},{17,25},{25,17},{2,10},{10... | collective-permute-start | bytes 626696 | tf_op jit(solution)/shard_map/ppermute | solution.py:387
  20.8 8.3 %collective-permute-start.11 = (bf16[816,128]{1,0:T(8,128)(2,1)S(1)}, bf16[816,128]{1,0:T(8,128)(2,1)S(1)}, u32[]{:S(2)}, u32[]{:S(2)}) collective-permute-start(bf16[816,128]{1,0:T(8,128)(2,1)S(1)} %constant_dynamic-update-slice_fusion.5.refs_10_), channel_id=1, source_target_pairs={{0,16},{8,24},{16,0},{24,8},{1,17},{9,25},{17,1},{25,9},{2,18},{10... | collective-permute-start | bytes 626696 | tf_op jit(solution)/shard_map/ppermute | solution.py:387
  23.4 6.2 %collective-permute-start.10 = (bf16[1360,128]{1,0:T(8,128)(2,1)S(1)}, bf16[1360,128]{1,0:T(8,128)(2,1)S(1)}, u32[]{:S(2)}, u32[]{:S(2)}) collective-permute-start(bf16[1360,128]{1,0:T(8,128)(2,1)S(1)} %collective-permute-done.9.refs_8_), channel_id=1, source_target_pairs={{0,8},{8,0},{16,24},{24,16},{1,9},{9,1},{17,25},{25,17},{2,10},{10... | collective-permute-start | bytes 1044488 | tf_op jit(solution)/shard_map/ppermute | solution.py:387
  29.0 3.1 %copy-start = (bf16[1024,1024]{1,0:T(8,128)(2,1)S(1)}, bf16[1024,1024]{1,0:T(8,128)(2,1)}, u32[]{:S(2)}) copy-start(bf16[1024,1024]{1,0:T(8,128)(2,1)} %refs_10_.1) | copy-start | bytes 6291460
  29.0 3.1 %collective-permute-start.12 = (bf16[816,128]{1,0:T(8,128)(2,1)S(1)}, bf16[816,128]{1,0:T(8,128)(2,1)S(1)}, u32[]{:S(2)}, u32[]{:S(2)}) collective-permute-start(bf16[816,128]{1,0:T(8,128)(2,1)S(1)} %collective-permute-done.11.refs_7_), channel_id=1, source_target_pairs={{0,8},{8,0},{16,24},{24,16},{1,9},{9,1},{17,25},{25,17},{2,10},{10... | collective-permute-start | bytes 626696 | tf_op jit(solution)/shard_map/ppermute | solution.py:387
  34.4 6.8 %collective-permute-start.13 = (bf16[32,1024]{1,0:T(8,128)(2,1)S(1)}, bf16[32,1024]{1,0:T(8,128)(2,1)S(1)}, u32[]{:S(2)}, u32[]{:S(2)}) collective-permute-start(bf16[32,1024]{1,0:T(8,128)(2,1)S(1)} %get-tuple-element.75), channel_id=1, source_target_pairs={{0,4},{1,5},{2,6},{3,7},{4,0},{5,1},{6,2},{7,3},{8,12},{9,13},{10,... | collective-permute-start | bytes 196616 | tf_op jit(solution)/shard_map/ppermute | solution.py:384
  36.1 7.8 %collective-permute-start.14 = (bf16[32,1024]{1,0:T(8,128)(2,1)S(1)}, bf16[32,1024]{1,0:T(8,128)(2,1)S(1)}, u32[]{:S(2)}, u32[]{:S(2)}) collective-permute-start(bf16[32,1024]{1,0:T(8,128)(2,1)S(1)} %get-tuple-element.74), channel_id=1, source_target_pairs={{0,1},{1,0},{2,3},{3,2},{4,5},{5,4},{6,7},{7,6},{8,9},{9,8},{10,11... | collective-permute-start | bytes 196616 | tf_op jit(solution)/shard_map/ppermute | solution.py:384
  37.7 7.0 %collective-permute-start.15 = (bf16[32,1024]{1,0:T(8,128)(2,1)S(1)}, bf16[32,1024]{1,0:T(8,128)(2,1)S(1)}, u32[]{:S(2)}, u32[]{:S(2)}) collective-permute-start(bf16[32,1024]{1,0:T(8,128)(2,1)S(1)} %get-tuple-element.80), channel_id=1, source_target_pairs={{0,2},{1,3},{2,0},{3,1},{4,6},{5,7},{6,4},{7,5},{8,10},{9,11},{10,... | collective-permute-start | bytes 196616 | tf_op jit(solution)/shard_map/ppermute | solution.py:384
  38.1 6.6 %collective-permute-start.16 = (bf16[32,1024]{1,0:T(8,128)(2,1)S(1)}, bf16[32,1024]{1,0:T(8,128)(2,1)S(1)}, u32[]{:S(2)}, u32[]{:S(2)}) collective-permute-start(bf16[32,1024]{1,0:T(8,128)(2,1)S(1)} %get-tuple-element.79), channel_id=1, source_target_pairs={{0,6},{1,7},{2,4},{3,5},{4,2},{5,3},{6,0},{7,1},{8,14},{9,15},{10,... | collective-permute-start | bytes 196616 | tf_op jit(solution)/shard_map/ppermute | solution.py:384
  39.5 9.4 %collective-permute-start.17 = (bf16[32,1024]{1,0:T(8,128)(2,1)S(1)}, bf16[32,1024]{1,0:T(8,128)(2,1)S(1)}, u32[]{:S(2)}, u32[]{:S(2)}) collective-permute-start(bf16[32,1024]{1,0:T(8,128)(2,1)S(1)} %get-tuple-element.78), channel_id=1, source_target_pairs={{0,5},{1,4},{2,7},{3,6},{4,1},{5,0},{6,3},{7,2},{8,13},{9,12},{10,... | collective-permute-start | bytes 196616 | tf_op jit(solution)/shard_map/ppermute | solution.py:384
  41.1 7.7 %collective-permute-start.18 = (bf16[32,1024]{1,0:T(8,128)(2,1)S(1)}, bf16[32,1024]{1,0:T(8,128)(2,1)S(1)}, u32[]{:S(2)}, u32[]{:S(2)}) collective-permute-start(bf16[32,1024]{1,0:T(8,128)(2,1)S(1)} %get-tuple-element.77), channel_id=1, source_target_pairs={{0,7},{1,6},{2,5},{3,4},{4,3},{5,2},{6,1},{7,0},{8,15},{9,14},{10,... | collective-permute-start | bytes 196616 | tf_op jit(solution)/shard_map/ppermute | solution.py:384
  43.9 5.4 %collective-permute-start.19 = (bf16[32,1024]{1,0:T(8,128)(2,1)S(1)}, bf16[32,1024]{1,0:T(8,128)(2,1)S(1)}, u32[]{:S(2)}, u32[]{:S(2)}) collective-permute-start(bf16[32,1024]{1,0:T(8,128)(2,1)S(1)} %get-tuple-element.73), channel_id=1, source_target_pairs={{0,3},{1,2},{2,1},{3,0},{4,7},{5,6},{6,5},{7,4},{8,11},{9,10},{10,... | collective-permute-start | bytes 196616 | tf_op jit(solution)/shard_map/ppermute | solution.py:384

commit v8 on v7

--- a/solution.py
+++ b/solution.py
@@ -12,6 +12,7 @@
 VAL_ROWS = PAIR + 16
 ACC_ROWS = HEAD_DIM + 8
 MASKED = -1e30
+LOWEST_TOP = -1e29
 SCALE = 0.125 * math.log2(math.e)
 COLS = 256
 ROWS, LANES = 16, 128
@@ -301,6 +302,8 @@
             last = before[f"top{q}"][pair : pair + 1, :]
             top = jnp.maximum(top, last)
             factors[pair] = jnp.exp2(last - top)
+        else:
+            top = jnp.maximum(top, LOWEST_TOP)
         weight_ref[pair] = jnp.exp2(scores - top).astype(BF16)
         self.write[f"top{q}"][pair : pair + 1, :] = top
 

time: 50.3 us -> 50.3 us (level)
  no operation moved by 1% of the time
where the time goes in v8:
time: 50.3 us; the launch traced here: 50.2 us
  starting transfers between devices  26.6 us (53%)
  Pallas kernels  16.6 us (33%)
  waiting for transfers between devices  6.66 us (13%)
    ppermute x14, starting transfers between devices, over_cells(): lax.ppermute(value, 'cells', [(i, i ^ step) for i in range(cell_devs)])  22.9 us
    pallas_call x4, Pallas kernels, call(): pl.pallas_call(self.body, out_shape=tuple(out_shape), in_specs=[hbm if n....  14.3 us
    ppermute x14, waiting for transfers between devices, over_cells(): lax.ppermute(value, 'cells', [(i, i ^ step) for i in range(cell_devs)])  5.56 us
    ppermute x6, starting transfers between devices, over_heads(): lax.ppermute(value, 'heads', [(i, i ^ step) for i in range(head_devs)])  3.75 us
    pallas_call x1, Pallas kernels, pack(): pl.pallas_call(lambda *refs: pack_kernel(order, *refs), out_shape=[jax.Sh...  1.39 us
    ppermute x6, waiting for transfers between devices, over_heads(): lax.ppermute(value, 'heads', [(i, i ^ step) for i in range(head_devs)])  1.1 us
  transfers between devices with their start and end apart: 20, of which 4 were waited for; matrix products, arithmetic and copies ran while one was open for 0% of the time, Pallas kernels for 24%

profile of v8, /device:TPU:0, one launch (start us, length us, event | category | flops | bytes accessed | tf_op | source)
XLA Modules:
  0.0 50.2 jit_solution(10910846088261041419)
XLA Ops:
  0.0 1.4 %pack.1 = (bf16[272,128]{1,0:T(8,128)(2,1)S(1)}, bf16[272,128]{1,0:T(8,128)(2,1)S(1)}, bf16[272,128]{1,0:T(8,128)(2,1)S(1)}, bf16[272,128]{1,0:T(8,128)(2,1)S(1)...) custom-call(bf16[8,32,1024]{2,1,0:T(8,128)(2,1)} %refs_0_.2, ...), custom_call_target="tpu_custom_call" | custom-call | tf_op jit(solution)/shard_map/pack/pallas_call | solution.py:72
  1.4 4.1 %collective-permute-start = (bf16[272,128]{1,0:T(8,128)(2,1)S(1)}, bf16[272,128]{1,0:T(8,128)(2,1)S(1)}, u32[]{:S(2)}, u32[]{:S(2)}) collective-permute-start(bf16[272,128]{1,0:T(8,128)(2,1)S(1)} %get-tuple-element.39), channel_id=1, source_target_pairs={{0,4},{1,5},{2,6},{3,7},{4,0},{5,1},{6,2},{7,3},{8,12},{9,13},{10,... | collective-permute-start | bytes 208904 | tf_op jit(solution)/shard_map/ppermute | solution.py:387
  5.5 1.5 %collective-permute-start.1 = (bf16[272,128]{1,0:T(8,128)(2,1)S(1)}, bf16[272,128]{1,0:T(8,128)(2,1)S(1)}, u32[]{:S(2)}, u32[]{:S(2)}) collective-permute-start(bf16[272,128]{1,0:T(8,128)(2,1)S(1)} %get-tuple-element.40), channel_id=1, source_target_pairs={{0,1},{1,0},{2,3},{3,2},{4,5},{5,4},{6,7},{7,6},{8,9},{9,8},{10,11... | collective-permute-start | bytes 208904 | tf_op jit(solution)/shard_map/ppermute | solution.py:387
  7.0 1.5 %collective-permute-start.2 = (bf16[272,128]{1,0:T(8,128)(2,1)S(1)}, bf16[272,128]{1,0:T(8,128)(2,1)S(1)}, u32[]{:S(2)}, u32[]{:S(2)}) collective-permute-start(bf16[272,128]{1,0:T(8,128)(2,1)S(1)} %get-tuple-element.41), channel_id=1, source_target_pairs={{0,3},{1,2},{2,1},{3,0},{4,7},{5,6},{6,5},{7,4},{8,11},{9,10},{10,... | collective-permute-start | bytes 208904 | tf_op jit(solution)/shard_map/ppermute | solution.py:387
  8.5 0.4 collective-permute-start.3
  9.0 1.3 %collective-permute-start.5 = (bf16[272,128]{1,0:T(8,128)(2,1)S(1)}, bf16[272,128]{1,0:T(8,128)(2,1)S(1)}, u32[]{:S(2)}, u32[]{:S(2)}) collective-permute-start(bf16[272,128]{1,0:T(8,128)(2,1)S(1)} %get-tuple-element.51), channel_id=1, source_target_pairs={{0,6},{1,7},{2,4},{3,5},{4,2},{5,3},{6,0},{7,1},{8,14},{9,15},{10,... | collective-permute-start | bytes 208904 | tf_op jit(solution)/shard_map/ppermute | solution.py:387
  10.3 0.0 collective-permute-done
  10.3 2.6 %collective-permute-start.6 = (bf16[272,128]{1,0:T(8,128)(2,1)S(1)}, bf16[272,128]{1,0:T(8,128)(2,1)S(1)}, u32[]{:S(2)}, u32[]{:S(2)}) collective-permute-start(bf16[272,128]{1,0:T(8,128)(2,1)S(1)} %get-tuple-element.52), channel_id=1, source_target_pairs={{0,5},{1,4},{2,7},{3,6},{4,1},{5,0},{6,3},{7,2},{8,13},{9,12},{10,... | collective-permute-start | bytes 208904 | tf_op jit(solution)/shard_map/ppermute | solution.py:387
  13.0 0.0 collective-permute-done.1
  13.0 0.9 %collective-permute-start.7 = (bf16[272,128]{1,0:T(8,128)(2,1)S(1)}, bf16[272,128]{1,0:T(8,128)(2,1)S(1)}, u32[]{:S(2)}, u32[]{:S(2)}) collective-permute-start(bf16[272,128]{1,0:T(8,128)(2,1)S(1)} %get-tuple-element.53), channel_id=1, source_target_pairs={{0,7},{1,6},{2,5},{3,4},{4,3},{5,2},{6,1},{7,0},{8,15},{9,14},{10,... | collective-permute-start | bytes 208904 | tf_op jit(solution)/shard_map/ppermute | solution.py:387
  14.0 0.0 collective-permute-done.2
  14.0 0.0 collective-permute-done.3
  14.0 1.6 %collective-permute-start.9 = (bf16[1360,128]{1,0:T(8,128)(2,1)S(1)}, bf16[1360,128]{1,0:T(8,128)(2,1)S(1)}, u32[]{:S(2)}, u32[]{:S(2)}) collective-permute-start(bf16[1360,128]{1,0:T(8,128)(2,1)S(1)} %constant_dynamic-update-slice_fusion.refs_1_.refs_9_), channel_id=1, source_target_pairs={{0,16},{8,24},{16,0},{24,8},{1,17},{9,25},{17,1},{25,9},{2,18},{10... | collective-permute-start | bytes 1044488 | tf_op jit(solution)/shard_map/ppermute | solution.py:390
  15.6 0.0 collective-permute-start.4
  15.6 4.1 %first_group.1 = (bf16[8,256,128]{2,1,0:T(8,128)(2,1)S(1)}, bf16[256,256]{1,0:T(8,128)(2,1)S(1)}, f32[8,72,256]{2,1,0:T(8,128)S(1)}, f32[8,256]{1,0:T(8,128)S(1)...) custom-call(s32[256,256]{1,0:T(8,128)} %refs_0_.3, ...), custom_call_target="tpu_custom_call" | custom-call | flops 1275068416 | bytes 8388608 | tf_op jit(solution)/shard_map/first_group/pallas_call | solution.py:366
  19.6 0.0 collective-permute-done.5
  19.7 1.0 %collective-permute-done.6 = bf16[272,128]{1,0:T(8,128)(2,1)S(1)} collective-permute-done((bf16[272,128]{1,0:T(8,128)(2,1)S(1)}, bf16[272,128]{1,0:T(8,128)(2,1)S(1)}, u32[]{:S(2)}, u32[]{:S(2)}) %collective-permute-start.6) | collective-permute-done | bytes 69664 | tf_op jit(solution)/shard_map/ppermute | solution.py:387
  20.6 0.0 collective-permute-done.7
  20.7 0.1 collective-permute-start.8
  20.8 1.6 %collective-permute-start.11 = (bf16[816,128]{1,0:T(8,128)(2,1)S(1)}, bf16[816,128]{1,0:T(8,128)(2,1)S(1)}, u32[]{:S(2)}, u32[]{:S(2)}) collective-permute-start(bf16[816,128]{1,0:T(8,128)(2,1)S(1)} %constant_dynamic-update-slice_fusion.5.refs_10_), channel_id=1, source_target_pairs={{0,16},{8,24},{16,0},{24,8},{1,17},{9,25},{17,1},{25,9},{2,18},{10... | collective-permute-start | bytes 626696 | tf_op jit(solution)/shard_map/ppermute | solution.py:390
  22.3 1.1 %collective-permute-done.9.refs_8_ = bf16[1360,128]{1,0:T(8,128)(2,1)S(1)} collective-permute-done((bf16[1360,128]{1,0:T(8,128)(2,1)S(1)}, bf16[1360,128]{1,0:T(8,128)(2,1)S(1)}, u32[]{:S(2)}, u32[]{:S(2)}) %collective-permute-start.9) | collective-permute-done | bytes 348192 | tf_op jit(solution)/shard_map/ppermute | solution.py:390
  23.4 0.0 collective-permute-start.10
  23.4 0.0 collective-permute-done.8.refs_7_
  23.4 0.0 collective-permute-done.4.refs_6_
  23.4 5.6 %second_group.1 = (bf16[8,256,128]{2,1,0:T(8,128)(2,1)S(1)}, bf16[256,256]{1,0:T(8,128)(2,1)S(1)}, f32[8,72,256]{2,1,0:T(8,128)S(1)}, f32[8,256]{1,0:T(8,128)S(1...) custom-call(bf16[256,256]{1,0:T(8,128)(2,1)S(1)} %get-tuple-element.44.refs_0_, ...), custom_call_target="tpu_custom_call" | custom-call | flops 4898947072 | bytes 8388608 | tf_op jit(solution)/shard_map/second_group/pallas_call | solution.py:366
  29.0 0.0 copy-start
  29.0 0.0 collective-permute-done.11.refs_7_
  29.0 0.6 %collective-permute-start.12 = (bf16[816,128]{1,0:T(8,128)(2,1)S(1)}, bf16[816,128]{1,0:T(8,128)(2,1)S(1)}, u32[]{:S(2)}, u32[]{:S(2)}) collective-permute-start(bf16[816,128]{1,0:T(8,128)(2,1)S(1)} %collective-permute-done.11.refs_7_), channel_id=1, source_target_pairs={{0,8},{8,0},{16,24},{24,16},{1,9},{9,1},{17,25},{25,17},{2,10},{10... | collective-permute-start | bytes 626696 | tf_op jit(solution)/shard_map/ppermute | solution.py:390
  29.6 0.0 collective-permute-done.10.refs_6_
  29.6 2.5 %far.1 = (f32[8,72,256]{2,1,0:T(8,128)S(1)}, f32[8,256]{1,0:T(8,128)S(1)}, f32[8,72,256]{2,1,0:T(8,128)S(1)}, f32[8,256]{1,0:T(8,128)S(1)}) custom-call(bf16[256,256]{1,0:T(8,128)(2,1)S(1)} %get-tuple-element.44.refs_0_, bf16[256,256]{1,0:T(8,128)(2,1)S(1)} %get-tuple-element.59.refs_1_, bf16[8,256,128]{2,1,0:T(8,128)(2,1)S(1)} %get-tuple-element.46.refs_2_, ...), custom_call_target="tpu_custom_call" | custom-call | flops 2147483648 | bytes 8388608 | tf_op jit(solution)/shard_map/far/pallas_call | solution.py:366
  32.1 0.0 collective-permute-done.12.refs_6_
  32.1 0.0 copy-done
  32.1 2.2 %last.1 = (bf16[128,1024]{1,0:T(8,128)(2,1)S(1)}, bf16[128,1024]{1,0:T(8,128)(2,1)S(1)}) custom-call(bf16[256,256]{1,0:T(8,128)(2,1)S(1)} %get-tuple-element.44.refs_0_, bf16[256,256]{1,0:T(8,128)(2,1)S(1)} %get-tuple-element.59.refs_1_, bf16[8,256,128]{2,1,0:T(8,128)(2,1)S(1)} %get-tuple-element.46.refs_2_, ...), custom_call_target="tpu_custom_call" | custom-call | flops 1342177280 | bytes 8388608 | tf_op jit(solution)/shard_map/last/pallas_call | solution.py:366
  34.4 1.7 %collective-permute-start.13 = (bf16[32,1024]{1,0:T(8,128)(2,1)S(1)}, bf16[32,1024]{1,0:T(8,128)(2,1)S(1)}, u32[]{:S(2)}, u32[]{:S(2)}) collective-permute-start(bf16[32,1024]{1,0:T(8,128)(2,1)S(1)} %get-tuple-element.75), channel_id=1, source_target_pairs={{0,4},{1,5},{2,6},{3,7},{4,0},{5,1},{6,2},{7,3},{8,12},{9,13},{10,... | collective-permute-start | bytes 196616 | tf_op jit(solution)/shard_map/ppermute | solution.py:387
  36.1 1.6 %collective-permute-start.14 = (bf16[32,1024]{1,0:T(8,128)(2,1)S(1)}, bf16[32,1024]{1,0:T(8,128)(2,1)S(1)}, u32[]{:S(2)}, u32[]{:S(2)}) collective-permute-start(bf16[32,1024]{1,0:T(8,128)(2,1)S(1)} %get-tuple-element.74), channel_id=1, source_target_pairs={{0,1},{1,0},{2,3},{3,2},{4,5},{5,4},{6,7},{7,6},{8,9},{9,8},{10,11... | collective-permute-start | bytes 196616 | tf_op jit(solution)/shard_map/ppermute | solution.py:387
  37.7 0.4 collective-permute-start.15
  38.1 1.4 %collective-permute-start.16 = (bf16[32,1024]{1,0:T(8,128)(2,1)S(1)}, bf16[32,1024]{1,0:T(8,128)(2,1)S(1)}, u32[]{:S(2)}, u32[]{:S(2)}) collective-permute-start(bf16[32,1024]{1,0:T(8,128)(2,1)S(1)} %get-tuple-element.79), channel_id=1, source_target_pairs={{0,6},{1,7},{2,4},{3,5},{4,2},{5,3},{6,0},{7,1},{8,14},{9,15},{10,... | collective-permute-start | bytes 196616 | tf_op jit(solution)/shard_map/ppermute | solution.py:387
  39.5 1.7 %collective-permute-start.17 = (bf16[32,1024]{1,0:T(8,128)(2,1)S(1)}, bf16[32,1024]{1,0:T(8,128)(2,1)S(1)}, u32[]{:S(2)}, u32[]{:S(2)}) collective-permute-start(bf16[32,1024]{1,0:T(8,128)(2,1)S(1)} %get-tuple-element.78), channel_id=1, source_target_pairs={{0,5},{1,4},{2,7},{3,6},{4,1},{5,0},{6,3},{7,2},{8,13},{9,12},{10,... | collective-permute-start | bytes 196616 | tf_op jit(solution)/shard_map/ppermute | solution.py:387
  41.1 0.0 collective-permute-done.13.refs_1_
  41.1 2.7 %collective-permute-start.18 = (bf16[32,1024]{1,0:T(8,128)(2,1)S(1)}, bf16[32,1024]{1,0:T(8,128)(2,1)S(1)}, u32[]{:S(2)}, u32[]{:S(2)}) collective-permute-start(bf16[32,1024]{1,0:T(8,128)(2,1)S(1)} %get-tuple-element.77), channel_id=1, source_target_pairs={{0,7},{1,6},{2,5},{3,4},{4,3},{5,2},{6,1},{7,0},{8,15},{9,14},{10,... | collective-permute-start | bytes 196616 | tf_op jit(solution)/shard_map/ppermute | solution.py:387
  43.9 0.0 collective-permute-done.14.refs_2_
  43.9 0.9 %collective-permute-start.19 = (bf16[32,1024]{1,0:T(8,128)(2,1)S(1)}, bf16[32,1024]{1,0:T(8,128)(2,1)S(1)}, u32[]{:S(2)}, u32[]{:S(2)}) collective-permute-start(bf16[32,1024]{1,0:T(8,128)(2,1)S(1)} %get-tuple-element.73), channel_id=1, source_target_pairs={{0,3},{1,2},{2,1},{3,0},{4,7},{5,6},{6,5},{7,4},{8,11},{9,10},{10,... | collective-permute-start | bytes 196616 | tf_op jit(solution)/shard_map/ppermute | solution.py:387
  44.7 0.0 collective-permute-done.15.refs_3_
  44.8 0.0 collective-permute-done.16.refs_4_
  44.8 4.1 %collective-permute-done.17.refs_5_ = bf16[32,1024]{1,0:T(8,128)(2,1)S(1)} collective-permute-done((bf16[32,1024]{1,0:T(8,128)(2,1)S(1)}, bf16[32,1024]{1,0:T(8,128)(2,1)S(1)}, u32[]{:S(2)}, u32[]{:S(2)}) %collective-permute-start.17) | collective-permute-done | bytes 65568 | tf_op jit(solution)/shard_map/ppermute | solution.py:387
  48.9 0.0 collective-permute-done.18.refs_6_
  48.9 0.4 collective-permute-done.19.refs_7_
  49.3 0.8 %unpack.1 = bf16[8,32,1024]{2,1,0:T(8,128)(2,1)} custom-call(bf16[32,1024]{1,0:T(8,128)(2,1)S(1)} %get-tuple-element.76.refs_0_, bf16[32,1024]{1,0:T(8,128)(2,1)S(1)} %collective-permute-done.13.refs_1_, bf16[32,1024]{1,0:T(8,128)(2,1)S(1)} %collective-permute-done.14.refs_2_, bf16[32,1024]{1,0:T(8,128)(2,1)S(1)} %collective-permute-done.15.refs_3_, ...), custom_call_target="tpu_custom_call" | custom-call | tf_op jit(solution)/shard_map/unpack/pallas_call | solution.py:100
  (10 shorter events, 0.1 us)
Async XLA Ops:
  1.4 8.9 %collective-permute-start = (bf16[272,128]{1,0:T(8,128)(2,1)S(1)}, bf16[272,128]{1,0:T(8,128)(2,1)S(1)}, u32[]{:S(2)}, u32[]{:S(2)}) collective-permute-start(bf16[272,128]{1,0:T(8,128)(2,1)S(1)} %get-tuple-element.39), channel_id=1, source_target_pairs={{0,4},{1,5},{2,6},{3,7},{4,0},{5,1},{6,2},{7,3},{8,12},{9,13},{10,... | collective-permute-start | bytes 208904 | tf_op jit(solution)/shard_map/ppermute | solution.py:387
  5.5 7.5 %collective-permute-start.1 = (bf16[272,128]{1,0:T(8,128)(2,1)S(1)}, bf16[272,128]{1,0:T(8,128)(2,1)S(1)}, u32[]{:S(2)}, u32[]{:S(2)}) collective-permute-start(bf16[272,128]{1,0:T(8,128)(2,1)S(1)} %get-tuple-element.40), channel_id=1, source_target_pairs={{0,1},{1,0},{2,3},{3,2},{4,5},{5,4},{6,7},{7,6},{8,9},{9,8},{10,11... | collective-permute-start | bytes 208904 | tf_op jit(solution)/shard_map/ppermute | solution.py:387
  7.0 6.9 %collective-permute-start.2 = (bf16[272,128]{1,0:T(8,128)(2,1)S(1)}, bf16[272,128]{1,0:T(8,128)(2,1)S(1)}, u32[]{:S(2)}, u32[]{:S(2)}) collective-permute-start(bf16[272,128]{1,0:T(8,128)(2,1)S(1)} %get-tuple-element.41), channel_id=1, source_target_pairs={{0,3},{1,2},{2,1},{3,0},{4,7},{5,6},{6,5},{7,4},{8,11},{9,10},{10,... | collective-permute-start | bytes 208904 | tf_op jit(solution)/shard_map/ppermute | solution.py:387
  8.5 5.5 %collective-permute-start.3 = (bf16[272,128]{1,0:T(8,128)(2,1)S(1)}, bf16[272,128]{1,0:T(8,128)(2,1)S(1)}, u32[]{:S(2)}, u32[]{:S(2)}) collective-permute-start(bf16[272,128]{1,0:T(8,128)(2,1)S(1)} %get-tuple-element.43), channel_id=1, source_target_pairs={{0,2},{1,3},{2,0},{3,1},{4,6},{5,7},{6,4},{7,5},{8,10},{9,11},{10,... | collective-permute-start | bytes 208904 | tf_op jit(solution)/shard_map/ppermute | solution.py:387
  9.0 10.7 %collective-permute-start.5 = (bf16[272,128]{1,0:T(8,128)(2,1)S(1)}, bf16[272,128]{1,0:T(8,128)(2,1)S(1)}, u32[]{:S(2)}, u32[]{:S(2)}) collective-permute-start(bf16[272,128]{1,0:T(8,128)(2,1)S(1)} %get-tuple-element.51), channel_id=1, source_target_pairs={{0,6},{1,7},{2,4},{3,5},{4,2},{5,3},{6,0},{7,1},{8,14},{9,15},{10,... | collective-permute-start | bytes 208904 | tf_op jit(solution)/shard_map/ppermute | solution.py:387
  10.3 10.3 %collective-permute-start.6 = (bf16[272,128]{1,0:T(8,128)(2,1)S(1)}, bf16[272,128]{1,0:T(8,128)(2,1)S(1)}, u32[]{:S(2)}, u32[]{:S(2)}) collective-permute-start(bf16[272,128]{1,0:T(8,128)(2,1)S(1)} %get-tuple-element.52), channel_id=1, source_target_pairs={{0,5},{1,4},{2,7},{3,6},{4,1},{5,0},{6,3},{7,2},{8,13},{9,12},{10,... | collective-permute-start | bytes 208904 | tf_op jit(solution)/shard_map/ppermute | solution.py:387
  13.0 7.6 %collective-permute-start.7 = (bf16[272,128]{1,0:T(8,128)(2,1)S(1)}, bf16[272,128]{1,0:T(8,128)(2,1)S(1)}, u32[]{:S(2)}, u32[]{:S(2)}) collective-permute-start(bf16[272,128]{1,0:T(8,128)(2,1)S(1)} %get-tuple-element.53), channel_id=1, source_target_pairs={{0,7},{1,6},{2,5},{3,4},{4,3},{5,2},{6,1},{7,0},{8,15},{9,14},{10,... | collective-permute-start | bytes 208904 | tf_op jit(solution)/shard_map/ppermute | solution.py:387
  14.0 9.4 %collective-permute-start.9 = (bf16[1360,128]{1,0:T(8,128)(2,1)S(1)}, bf16[1360,128]{1,0:T(8,128)(2,1)S(1)}, u32[]{:S(2)}, u32[]{:S(2)}) collective-permute-start(bf16[1360,128]{1,0:T(8,128)(2,1)S(1)} %constant_dynamic-update-slice_fusion.refs_1_.refs_9_), channel_id=1, source_target_pairs={{0,16},{8,24},{16,0},{24,8},{1,17},{9,25},{17,1},{25,9},{2,18},{10... | collective-permute-start | bytes 1044488 | tf_op jit(solution)/shard_map/ppermute | solution.py:390
  15.6 7.8 %collective-permute-start.4 = (bf16[1360,128]{1,0:T(8,128)(2,1)S(1)}, bf16[1360,128]{1,0:T(8,128)(2,1)S(1)}, u32[]{:S(2)}, u32[]{:S(2)}) collective-permute-start(bf16[1360,128]{1,0:T(8,128)(2,1)S(1)} %constant_dynamic-update-slice_fusion.refs_1_.refs_9_), channel_id=1, source_target_pairs={{0,8},{8,0},{16,24},{24,16},{1,9},{9,1},{17,25},{25,17},{2,10},{10... | collective-permute-start | bytes 1044488 | tf_op jit(solution)/shard_map/ppermute | solution.py:390
  20.7 2.7 %collective-permute-start.8 = (bf16[816,128]{1,0:T(8,128)(2,1)S(1)}, bf16[816,128]{1,0:T(8,128)(2,1)S(1)}, u32[]{:S(2)}, u32[]{:S(2)}) collective-permute-start(bf16[816,128]{1,0:T(8,128)(2,1)S(1)} %constant_dynamic-update-slice_fusion.5.refs_10_), channel_id=1, source_target_pairs={{0,8},{8,0},{16,24},{24,16},{1,9},{9,1},{17,25},{25,17},{2,10},{10... | collective-permute-start | bytes 626696 | tf_op jit(solution)/shard_map/ppermute | solution.py:390
  20.8 8.3 %collective-permute-start.11 = (bf16[816,128]{1,0:T(8,128)(2,1)S(1)}, bf16[816,128]{1,0:T(8,128)(2,1)S(1)}, u32[]{:S(2)}, u32[]{:S(2)}) collective-permute-start(bf16[816,128]{1,0:T(8,128)(2,1)S(1)} %constant_dynamic-update-slice_fusion.5.refs_10_), channel_id=1, source_target_pairs={{0,16},{8,24},{16,0},{24,8},{1,17},{9,25},{17,1},{25,9},{2,18},{10... | collective-permute-start | bytes 626696 | tf_op jit(solution)/shard_map/ppermute | solution.py:390
  23.4 6.2 %collective-permute-start.10 = (bf16[1360,128]{1,0:T(8,128)(2,1)S(1)}, bf16[1360,128]{1,0:T(8,128)(2,1)S(1)}, u32[]{:S(2)}, u32[]{:S(2)}) collective-permute-start(bf16[1360,128]{1,0:T(8,128)(2,1)S(1)} %collective-permute-done.9.refs_8_), channel_id=1, source_target_pairs={{0,8},{8,0},{16,24},{24,16},{1,9},{9,1},{17,25},{25,17},{2,10},{10... | collective-permute-start | bytes 1044488 | tf_op jit(solution)/shard_map/ppermute | solution.py:390
  29.0 3.1 %copy-start = (bf16[1024,1024]{1,0:T(8,128)(2,1)S(1)}, bf16[1024,1024]{1,0:T(8,128)(2,1)}, u32[]{:S(2)}) copy-start(bf16[1024,1024]{1,0:T(8,128)(2,1)} %refs_10_.1) | copy-start | bytes 6291460
  29.0 3.1 %collective-permute-start.12 = (bf16[816,128]{1,0:T(8,128)(2,1)S(1)}, bf16[816,128]{1,0:T(8,128)(2,1)S(1)}, u32[]{:S(2)}, u32[]{:S(2)}) collective-permute-start(bf16[816,128]{1,0:T(8,128)(2,1)S(1)} %collective-permute-done.11.refs_7_), channel_id=1, source_target_pairs={{0,8},{8,0},{16,24},{24,16},{1,9},{9,1},{17,25},{25,17},{2,10},{10... | collective-permute-start | bytes 626696 | tf_op jit(solution)/shard_map/ppermute | solution.py:390
  34.4 6.8 %collective-permute-start.13 = (bf16[32,1024]{1,0:T(8,128)(2,1)S(1)}, bf16[32,1024]{1,0:T(8,128)(2,1)S(1)}, u32[]{:S(2)}, u32[]{:S(2)}) collective-permute-start(bf16[32,1024]{1,0:T(8,128)(2,1)S(1)} %get-tuple-element.75), channel_id=1, source_target_pairs={{0,4},{1,5},{2,6},{3,7},{4,0},{5,1},{6,2},{7,3},{8,12},{9,13},{10,... | collective-permute-start | bytes 196616 | tf_op jit(solution)/shard_map/ppermute | solution.py:387
  36.1 7.8 %collective-permute-start.14 = (bf16[32,1024]{1,0:T(8,128)(2,1)S(1)}, bf16[32,1024]{1,0:T(8,128)(2,1)S(1)}, u32[]{:S(2)}, u32[]{:S(2)}) collective-permute-start(bf16[32,1024]{1,0:T(8,128)(2,1)S(1)} %get-tuple-element.74), channel_id=1, source_target_pairs={{0,1},{1,0},{2,3},{3,2},{4,5},{5,4},{6,7},{7,6},{8,9},{9,8},{10,11... | collective-permute-start | bytes 196616 | tf_op jit(solution)/shard_map/ppermute | solution.py:387
  37.7 7.0 %collective-permute-start.15 = (bf16[32,1024]{1,0:T(8,128)(2,1)S(1)}, bf16[32,1024]{1,0:T(8,128)(2,1)S(1)}, u32[]{:S(2)}, u32[]{:S(2)}) collective-permute-start(bf16[32,1024]{1,0:T(8,128)(2,1)S(1)} %get-tuple-element.80), channel_id=1, source_target_pairs={{0,2},{1,3},{2,0},{3,1},{4,6},{5,7},{6,4},{7,5},{8,10},{9,11},{10,... | collective-permute-start | bytes 196616 | tf_op jit(solution)/shard_map/ppermute | solution.py:387
  38.1 6.6 %collective-permute-start.16 = (bf16[32,1024]{1,0:T(8,128)(2,1)S(1)}, bf16[32,1024]{1,0:T(8,128)(2,1)S(1)}, u32[]{:S(2)}, u32[]{:S(2)}) collective-permute-start(bf16[32,1024]{1,0:T(8,128)(2,1)S(1)} %get-tuple-element.79), channel_id=1, source_target_pairs={{0,6},{1,7},{2,4},{3,5},{4,2},{5,3},{6,0},{7,1},{8,14},{9,15},{10,... | collective-permute-start | bytes 196616 | tf_op jit(solution)/shard_map/ppermute | solution.py:387
  39.5 9.4 %collective-permute-start.17 = (bf16[32,1024]{1,0:T(8,128)(2,1)S(1)}, bf16[32,1024]{1,0:T(8,128)(2,1)S(1)}, u32[]{:S(2)}, u32[]{:S(2)}) collective-permute-start(bf16[32,1024]{1,0:T(8,128)(2,1)S(1)} %get-tuple-element.78), channel_id=1, source_target_pairs={{0,5},{1,4},{2,7},{3,6},{4,1},{5,0},{6,3},{7,2},{8,13},{9,12},{10,... | collective-permute-start | bytes 196616 | tf_op jit(solution)/shard_map/ppermute | solution.py:387
  41.1 7.7 %collective-permute-start.18 = (bf16[32,1024]{1,0:T(8,128)(2,1)S(1)}, bf16[32,1024]{1,0:T(8,128)(2,1)S(1)}, u32[]{:S(2)}, u32[]{:S(2)}) collective-permute-start(bf16[32,1024]{1,0:T(8,128)(2,1)S(1)} %get-tuple-element.77), channel_id=1, source_target_pairs={{0,7},{1,6},{2,5},{3,4},{4,3},{5,2},{6,1},{7,0},{8,15},{9,14},{10,... | collective-permute-start | bytes 196616 | tf_op jit(solution)/shard_map/ppermute | solution.py:387
  43.9 5.4 %collective-permute-start.19 = (bf16[32,1024]{1,0:T(8,128)(2,1)S(1)}, bf16[32,1024]{1,0:T(8,128)(2,1)S(1)}, u32[]{:S(2)}, u32[]{:S(2)}) collective-permute-start(bf16[32,1024]{1,0:T(8,128)(2,1)S(1)} %get-tuple-element.73), channel_id=1, source_target_pairs={{0,3},{1,2},{2,1},{3,0},{4,7},{5,6},{6,5},{7,4},{8,11},{9,10},{10,... | collective-permute-start | bytes 196616 | tf_op jit(solution)/shard_map/ppermute | solution.py:387

commit v9 on v8

--- a/solution.py
+++ b/solution.py
@@ -35,8 +35,8 @@
     out_refs, (cells_ref, gain_ref, tile_ref, sems) = refs[: len(order)], refs[len(order) :]
     genes, rows, width = cells_ref.shape
     gene = lax.rem(lax.axis_index("cells"), genes)
-    moves = [(gain_hbm, gain_ref), (tile_hbm, tile_ref)]
-    moves += [(x_hbm.at[gene ^ k], cells_ref.at[i]) for i, k in enumerate(order)]
+    moves = [(x_hbm.at[gene ^ k], cells_ref.at[i]) for i, k in enumerate(order)]
+    moves += [(gain_hbm, gain_ref), (tile_hbm, tile_ref)]
     copies = [pltpu.make_async_copy(*move, sems.at[i]) for i, move in enumerate(moves)]
     for copy in copies:
         copy.start()

time: 50.3 us -> 50.3 us (level)
  no operation moved by 1% of the time
where the time goes in v9:
time: 50.3 us; the launch traced here: 50.1 us
  starting transfers between devices  26.6 us (53%)
  Pallas kernels  16.5 us (33%)
  waiting for transfers between devices  6.64 us (13%)
    ppermute x14, starting transfers between devices, over_cells(): lax.ppermute(value, 'cells', [(i, i ^ step) for i in range(cell_devs)])  22.9 us
    pallas_call x4, Pallas kernels, call(): pl.pallas_call(self.body, out_shape=tuple(out_shape), in_specs=[hbm if n....  14.3 us
    ppermute x14, waiting for transfers between devices, over_cells(): lax.ppermute(value, 'cells', [(i, i ^ step) for i in range(cell_devs)])  5.55 us
    ppermute x6, starting transfers between devices, over_heads(): lax.ppermute(value, 'heads', [(i, i ^ step) for i in range(head_devs)])  3.76 us
    pallas_call x1, Pallas kernels, pack(): pl.pallas_call(lambda *refs: pack_kernel(order, *refs), out_shape=[jax.Sh...  1.36 us
    ppermute x6, waiting for transfers between devices, over_heads(): lax.ppermute(value, 'heads', [(i, i ^ step) for i in range(head_devs)])  1.1 us
  transfers between devices with their start and end apart: 20, of which 4 were waited for; matrix products, arithmetic and copies ran while one was open for 0% of the time, Pallas kernels for 24%

profile of v9, /device:TPU:0, one launch (start us, length us, event | category | flops | bytes accessed | tf_op | source)
XLA Modules:
  0.0 50.1 jit_solution(14382115048958675445)
XLA Ops:
  0.0 1.4 %pack.1 = (bf16[272,128]{1,0:T(8,128)(2,1)S(1)}, bf16[272,128]{1,0:T(8,128)(2,1)S(1)}, bf16[272,128]{1,0:T(8,128)(2,1)S(1)}, bf16[272,128]{1,0:T(8,128)(2,1)S(1)...) custom-call(bf16[8,32,1024]{2,1,0:T(8,128)(2,1)} %refs_0_.2, ...), custom_call_target="tpu_custom_call" | custom-call | tf_op jit(solution)/shard_map/pack/pallas_call | solution.py:72
  1.4 4.1 %collective-permute-start = (bf16[272,128]{1,0:T(8,128)(2,1)S(1)}, bf16[272,128]{1,0:T(8,128)(2,1)S(1)}, u32[]{:S(2)}, u32[]{:S(2)}) collective-permute-start(bf16[272,128]{1,0:T(8,128)(2,1)S(1)} %get-tuple-element.39), channel_id=1, source_target_pairs={{0,4},{1,5},{2,6},{3,7},{4,0},{5,1},{6,2},{7,3},{8,12},{9,13},{10,... | collective-permute-start | bytes 208904 | tf_op jit(solution)/shard_map/ppermute | solution.py:387
  5.5 1.5 %collective-permute-start.1 = (bf16[272,128]{1,0:T(8,128)(2,1)S(1)}, bf16[272,128]{1,0:T(8,128)(2,1)S(1)}, u32[]{:S(2)}, u32[]{:S(2)}) collective-permute-start(bf16[272,128]{1,0:T(8,128)(2,1)S(1)} %get-tuple-element.40), channel_id=1, source_target_pairs={{0,1},{1,0},{2,3},{3,2},{4,5},{5,4},{6,7},{7,6},{8,9},{9,8},{10,11... | collective-permute-start | bytes 208904 | tf_op jit(solution)/shard_map/ppermute | solution.py:387
  7.0 1.5 %collective-permute-start.2 = (bf16[272,128]{1,0:T(8,128)(2,1)S(1)}, bf16[272,128]{1,0:T(8,128)(2,1)S(1)}, u32[]{:S(2)}, u32[]{:S(2)}) collective-permute-start(bf16[272,128]{1,0:T(8,128)(2,1)S(1)} %get-tuple-element.41), channel_id=1, source_target_pairs={{0,3},{1,2},{2,1},{3,0},{4,7},{5,6},{6,5},{7,4},{8,11},{9,10},{10,... | collective-permute-start | bytes 208904 | tf_op jit(solution)/shard_map/ppermute | solution.py:387
  8.5 0.4 collective-permute-start.3
  9.0 1.3 %collective-permute-start.5 = (bf16[272,128]{1,0:T(8,128)(2,1)S(1)}, bf16[272,128]{1,0:T(8,128)(2,1)S(1)}, u32[]{:S(2)}, u32[]{:S(2)}) collective-permute-start(bf16[272,128]{1,0:T(8,128)(2,1)S(1)} %get-tuple-element.51), channel_id=1, source_target_pairs={{0,6},{1,7},{2,4},{3,5},{4,2},{5,3},{6,0},{7,1},{8,14},{9,15},{10,... | collective-permute-start | bytes 208904 | tf_op jit(solution)/shard_map/ppermute | solution.py:387
  10.3 0.0 collective-permute-done
  10.3 2.6 %collective-permute-start.6 = (bf16[272,128]{1,0:T(8,128)(2,1)S(1)}, bf16[272,128]{1,0:T(8,128)(2,1)S(1)}, u32[]{:S(2)}, u32[]{:S(2)}) collective-permute-start(bf16[272,128]{1,0:T(8,128)(2,1)S(1)} %get-tuple-element.52), channel_id=1, source_target_pairs={{0,5},{1,4},{2,7},{3,6},{4,1},{5,0},{6,3},{7,2},{8,13},{9,12},{10,... | collective-permute-start | bytes 208904 | tf_op jit(solution)/shard_map/ppermute | solution.py:387
  13.0 0.0 collective-permute-done.1
  13.0 0.9 %collective-permute-start.7 = (bf16[272,128]{1,0:T(8,128)(2,1)S(1)}, bf16[272,128]{1,0:T(8,128)(2,1)S(1)}, u32[]{:S(2)}, u32[]{:S(2)}) collective-permute-start(bf16[272,128]{1,0:T(8,128)(2,1)S(1)} %get-tuple-element.53), channel_id=1, source_target_pairs={{0,7},{1,6},{2,5},{3,4},{4,3},{5,2},{6,1},{7,0},{8,15},{9,14},{10,... | collective-permute-start | bytes 208904 | tf_op jit(solution)/shard_map/ppermute | solution.py:387
  13.9 0.0 collective-permute-done.2
  14.0 0.0 collective-permute-done.3
  14.0 1.6 %collective-permute-start.9 = (bf16[1360,128]{1,0:T(8,128)(2,1)S(1)}, bf16[1360,128]{1,0:T(8,128)(2,1)S(1)}, u32[]{:S(2)}, u32[]{:S(2)}) collective-permute-start(bf16[1360,128]{1,0:T(8,128)(2,1)S(1)} %constant_dynamic-update-slice_fusion.refs_1_.refs_9_), channel_id=1, source_target_pairs={{0,16},{8,24},{16,0},{24,8},{1,17},{9,25},{17,1},{25,9},{2,18},{10... | collective-permute-start | bytes 1044488 | tf_op jit(solution)/shard_map/ppermute | solution.py:390
  15.6 0.0 collective-permute-start.4
  15.6 4.1 %first_group.1 = (bf16[8,256,128]{2,1,0:T(8,128)(2,1)S(1)}, bf16[256,256]{1,0:T(8,128)(2,1)S(1)}, f32[8,72,256]{2,1,0:T(8,128)S(1)}, f32[8,256]{1,0:T(8,128)S(1)...) custom-call(s32[256,256]{1,0:T(8,128)} %refs_0_.3, ...), custom_call_target="tpu_custom_call" | custom-call | flops 1275068416 | bytes 8388608 | tf_op jit(solution)/shard_map/first_group/pallas_call | solution.py:366
  19.6 0.0 collective-permute-done.5
  19.6 1.0 %collective-permute-done.6 = bf16[272,128]{1,0:T(8,128)(2,1)S(1)} collective-permute-done((bf16[272,128]{1,0:T(8,128)(2,1)S(1)}, bf16[272,128]{1,0:T(8,128)(2,1)S(1)}, u32[]{:S(2)}, u32[]{:S(2)}) %collective-permute-start.6) | collective-permute-done | bytes 69664 | tf_op jit(solution)/shard_map/ppermute | solution.py:387
  20.6 0.0 collective-permute-done.7
  20.7 0.1 collective-permute-start.8
  20.7 1.6 %collective-permute-start.11 = (bf16[816,128]{1,0:T(8,128)(2,1)S(1)}, bf16[816,128]{1,0:T(8,128)(2,1)S(1)}, u32[]{:S(2)}, u32[]{:S(2)}) collective-permute-start(bf16[816,128]{1,0:T(8,128)(2,1)S(1)} %constant_dynamic-update-slice_fusion.5.refs_10_), channel_id=1, source_target_pairs={{0,16},{8,24},{16,0},{24,8},{1,17},{9,25},{17,1},{25,9},{2,18},{10... | collective-permute-start | bytes 626696 | tf_op jit(solution)/shard_map/ppermute | solution.py:390
  22.3 1.1 %collective-permute-done.9.refs_8_ = bf16[1360,128]{1,0:T(8,128)(2,1)S(1)} collective-permute-done((bf16[1360,128]{1,0:T(8,128)(2,1)S(1)}, bf16[1360,128]{1,0:T(8,128)(2,1)S(1)}, u32[]{:S(2)}, u32[]{:S(2)}) %collective-permute-start.9) | collective-permute-done | bytes 348192 | tf_op jit(solution)/shard_map/ppermute | solution.py:390
  23.4 0.0 collective-permute-start.10
  23.4 0.0 collective-permute-done.8.refs_7_
  23.4 0.0 collective-permute-done.4.refs_6_
  23.4 5.6 %second_group.1 = (bf16[8,256,128]{2,1,0:T(8,128)(2,1)S(1)}, bf16[256,256]{1,0:T(8,128)(2,1)S(1)}, f32[8,72,256]{2,1,0:T(8,128)S(1)}, f32[8,256]{1,0:T(8,128)S(1...) custom-call(bf16[256,256]{1,0:T(8,128)(2,1)S(1)} %get-tuple-element.44.refs_0_, ...), custom_call_target="tpu_custom_call" | custom-call | flops 4898947072 | bytes 8388608 | tf_op jit(solution)/shard_map/second_group/pallas_call | solution.py:366
  29.0 0.0 copy-start
  29.0 0.0 collective-permute-done.11.refs_7_
  29.0 0.6 %collective-permute-start.12 = (bf16[816,128]{1,0:T(8,128)(2,1)S(1)}, bf16[816,128]{1,0:T(8,128)(2,1)S(1)}, u32[]{:S(2)}, u32[]{:S(2)}) collective-permute-start(bf16[816,128]{1,0:T(8,128)(2,1)S(1)} %collective-permute-done.11.refs_7_), channel_id=1, source_target_pairs={{0,8},{8,0},{16,24},{24,16},{1,9},{9,1},{17,25},{25,17},{2,10},{10... | collective-permute-start | bytes 626696 | tf_op jit(solution)/shard_map/ppermute | solution.py:390
  29.6 0.0 collective-permute-done.10.refs_6_
  29.6 2.5 %far.1 = (f32[8,72,256]{2,1,0:T(8,128)S(1)}, f32[8,256]{1,0:T(8,128)S(1)}, f32[8,72,256]{2,1,0:T(8,128)S(1)}, f32[8,256]{1,0:T(8,128)S(1)}) custom-call(bf16[256,256]{1,0:T(8,128)(2,1)S(1)} %get-tuple-element.44.refs_0_, bf16[256,256]{1,0:T(8,128)(2,1)S(1)} %get-tuple-element.59.refs_1_, bf16[8,256,128]{2,1,0:T(8,128)(2,1)S(1)} %get-tuple-element.46.refs_2_, ...), custom_call_target="tpu_custom_call" | custom-call | flops 2147483648 | bytes 8388608 | tf_op jit(solution)/shard_map/far/pallas_call | solution.py:366
  32.1 0.0 collective-permute-done.12.refs_6_
  32.1 0.0 copy-done
  32.1 2.2 %last.1 = (bf16[128,1024]{1,0:T(8,128)(2,1)S(1)}, bf16[128,1024]{1,0:T(8,128)(2,1)S(1)}) custom-call(bf16[256,256]{1,0:T(8,128)(2,1)S(1)} %get-tuple-element.44.refs_0_, bf16[256,256]{1,0:T(8,128)(2,1)S(1)} %get-tuple-element.59.refs_1_, bf16[8,256,128]{2,1,0:T(8,128)(2,1)S(1)} %get-tuple-element.46.refs_2_, ...), custom_call_target="tpu_custom_call" | custom-call | flops 1342177280 | bytes 8388608 | tf_op jit(solution)/shard_map/last/pallas_call | solution.py:366
  34.3 1.7 %collective-permute-start.13 = (bf16[32,1024]{1,0:T(8,128)(2,1)S(1)}, bf16[32,1024]{1,0:T(8,128)(2,1)S(1)}, u32[]{:S(2)}, u32[]{:S(2)}) collective-permute-start(bf16[32,1024]{1,0:T(8,128)(2,1)S(1)} %get-tuple-element.75), channel_id=1, source_target_pairs={{0,4},{1,5},{2,6},{3,7},{4,0},{5,1},{6,2},{7,3},{8,12},{9,13},{10,... | collective-permute-start | bytes 196616 | tf_op jit(solution)/shard_map/ppermute | solution.py:387
  36.1 1.6 %collective-permute-start.14 = (bf16[32,1024]{1,0:T(8,128)(2,1)S(1)}, bf16[32,1024]{1,0:T(8,128)(2,1)S(1)}, u32[]{:S(2)}, u32[]{:S(2)}) collective-permute-start(bf16[32,1024]{1,0:T(8,128)(2,1)S(1)} %get-tuple-element.74), channel_id=1, source_target_pairs={{0,1},{1,0},{2,3},{3,2},{4,5},{5,4},{6,7},{7,6},{8,9},{9,8},{10,11... | collective-permute-start | bytes 196616 | tf_op jit(solution)/shard_map/ppermute | solution.py:387
  37.7 0.4 collective-permute-start.15
  38.1 1.4 %collective-permute-start.16 = (bf16[32,1024]{1,0:T(8,128)(2,1)S(1)}, bf16[32,1024]{1,0:T(8,128)(2,1)S(1)}, u32[]{:S(2)}, u32[]{:S(2)}) collective-permute-start(bf16[32,1024]{1,0:T(8,128)(2,1)S(1)} %get-tuple-element.79), channel_id=1, source_target_pairs={{0,6},{1,7},{2,4},{3,5},{4,2},{5,3},{6,0},{7,1},{8,14},{9,15},{10,... | collective-permute-start | bytes 196616 | tf_op jit(solution)/shard_map/ppermute | solution.py:387
  39.4 1.7 %collective-permute-start.17 = (bf16[32,1024]{1,0:T(8,128)(2,1)S(1)}, bf16[32,1024]{1,0:T(8,128)(2,1)S(1)}, u32[]{:S(2)}, u32[]{:S(2)}) collective-permute-start(bf16[32,1024]{1,0:T(8,128)(2,1)S(1)} %get-tuple-element.78), channel_id=1, source_target_pairs={{0,5},{1,4},{2,7},{3,6},{4,1},{5,0},{6,3},{7,2},{8,13},{9,12},{10,... | collective-permute-start | bytes 196616 | tf_op jit(solution)/shard_map/ppermute | solution.py:387
  41.1 0.0 collective-permute-done.13.refs_1_
  41.1 2.8 %collective-permute-start.18 = (bf16[32,1024]{1,0:T(8,128)(2,1)S(1)}, bf16[32,1024]{1,0:T(8,128)(2,1)S(1)}, u32[]{:S(2)}, u32[]{:S(2)}) collective-permute-start(bf16[32,1024]{1,0:T(8,128)(2,1)S(1)} %get-tuple-element.77), channel_id=1, source_target_pairs={{0,7},{1,6},{2,5},{3,4},{4,3},{5,2},{6,1},{7,0},{8,15},{9,14},{10,... | collective-permute-start | bytes 196616 | tf_op jit(solution)/shard_map/ppermute | solution.py:387
  43.9 0.0 collective-permute-done.14.refs_2_
  43.9 0.9 %collective-permute-start.19 = (bf16[32,1024]{1,0:T(8,128)(2,1)S(1)}, bf16[32,1024]{1,0:T(8,128)(2,1)S(1)}, u32[]{:S(2)}, u32[]{:S(2)}) collective-permute-start(bf16[32,1024]{1,0:T(8,128)(2,1)S(1)} %get-tuple-element.73), channel_id=1, source_target_pairs={{0,3},{1,2},{2,1},{3,0},{4,7},{5,6},{6,5},{7,4},{8,11},{9,10},{10,... | collective-permute-start | bytes 196616 | tf_op jit(solution)/shard_map/ppermute | solution.py:387
  44.7 0.0 collective-permute-done.15.refs_3_
  44.7 0.0 collective-permute-done.16.refs_4_
  44.7 4.1 %collective-permute-done.17.refs_5_ = bf16[32,1024]{1,0:T(8,128)(2,1)S(1)} collective-permute-done((bf16[32,1024]{1,0:T(8,128)(2,1)S(1)}, bf16[32,1024]{1,0:T(8,128)(2,1)S(1)}, u32[]{:S(2)}, u32[]{:S(2)}) %collective-permute-start.17) | collective-permute-done | bytes 65568 | tf_op jit(solution)/shard_map/ppermute | solution.py:387
  48.8 0.0 collective-permute-done.18.refs_6_
  48.9 0.4 collective-permute-done.19.refs_7_
  49.3 0.8 %unpack.1 = bf16[8,32,1024]{2,1,0:T(8,128)(2,1)} custom-call(bf16[32,1024]{1,0:T(8,128)(2,1)S(1)} %get-tuple-element.76.refs_0_, bf16[32,1024]{1,0:T(8,128)(2,1)S(1)} %collective-permute-done.13.refs_1_, bf16[32,1024]{1,0:T(8,128)(2,1)S(1)} %collective-permute-done.14.refs_2_, bf16[32,1024]{1,0:T(8,128)(2,1)S(1)} %collective-permute-done.15.refs_3_, ...), custom_call_target="tpu_custom_call" | custom-call | tf_op jit(solution)/shard_map/unpack/pallas_call | solution.py:100
  (10 shorter events, 0.1 us)
Async XLA Ops:
  1.4 8.9 %collective-permute-start = (bf16[272,128]{1,0:T(8,128)(2,1)S(1)}, bf16[272,128]{1,0:T(8,128)(2,1)S(1)}, u32[]{:S(2)}, u32[]{:S(2)}) collective-permute-start(bf16[272,128]{1,0:T(8,128)(2,1)S(1)} %get-tuple-element.39), channel_id=1, source_target_pairs={{0,4},{1,5},{2,6},{3,7},{4,0},{5,1},{6,2},{7,3},{8,12},{9,13},{10,... | collective-permute-start | bytes 208904 | tf_op jit(solution)/shard_map/ppermute | solution.py:387
  5.5 7.5 %collective-permute-start.1 = (bf16[272,128]{1,0:T(8,128)(2,1)S(1)}, bf16[272,128]{1,0:T(8,128)(2,1)S(1)}, u32[]{:S(2)}, u32[]{:S(2)}) collective-permute-start(bf16[272,128]{1,0:T(8,128)(2,1)S(1)} %get-tuple-element.40), channel_id=1, source_target_pairs={{0,1},{1,0},{2,3},{3,2},{4,5},{5,4},{6,7},{7,6},{8,9},{9,8},{10,11... | collective-permute-start | bytes 208904 | tf_op jit(solution)/shard_map/ppermute | solution.py:387
  7.0 6.9 %collective-permute-start.2 = (bf16[272,128]{1,0:T(8,128)(2,1)S(1)}, bf16[272,128]{1,0:T(8,128)(2,1)S(1)}, u32[]{:S(2)}, u32[]{:S(2)}) collective-permute-start(bf16[272,128]{1,0:T(8,128)(2,1)S(1)} %get-tuple-element.41), channel_id=1, source_target_pairs={{0,3},{1,2},{2,1},{3,0},{4,7},{5,6},{6,5},{7,4},{8,11},{9,10},{10,... | collective-permute-start | bytes 208904 | tf_op jit(solution)/shard_map/ppermute | solution.py:387
  8.5 5.5 %collective-permute-start.3 = (bf16[272,128]{1,0:T(8,128)(2,1)S(1)}, bf16[272,128]{1,0:T(8,128)(2,1)S(1)}, u32[]{:S(2)}, u32[]{:S(2)}) collective-permute-start(bf16[272,128]{1,0:T(8,128)(2,1)S(1)} %get-tuple-element.43), channel_id=1, source_target_pairs={{0,2},{1,3},{2,0},{3,1},{4,6},{5,7},{6,4},{7,5},{8,10},{9,11},{10,... | collective-permute-start | bytes 208904 | tf_op jit(solution)/shard_map/ppermute | solution.py:387
  9.0 10.7 %collective-permute-start.5 = (bf16[272,128]{1,0:T(8,128)(2,1)S(1)}, bf16[272,128]{1,0:T(8,128)(2,1)S(1)}, u32[]{:S(2)}, u32[]{:S(2)}) collective-permute-start(bf16[272,128]{1,0:T(8,128)(2,1)S(1)} %get-tuple-element.51), channel_id=1, source_target_pairs={{0,6},{1,7},{2,4},{3,5},{4,2},{5,3},{6,0},{7,1},{8,14},{9,15},{10,... | collective-permute-start | bytes 208904 | tf_op jit(solution)/shard_map/ppermute | solution.py:387
  10.3 10.3 %collective-permute-start.6 = (bf16[272,128]{1,0:T(8,128)(2,1)S(1)}, bf16[272,128]{1,0:T(8,128)(2,1)S(1)}, u32[]{:S(2)}, u32[]{:S(2)}) collective-permute-start(bf16[272,128]{1,0:T(8,128)(2,1)S(1)} %get-tuple-element.52), channel_id=1, source_target_pairs={{0,5},{1,4},{2,7},{3,6},{4,1},{5,0},{6,3},{7,2},{8,13},{9,12},{10,... | collective-permute-start | bytes 208904 | tf_op jit(solution)/shard_map/ppermute | solution.py:387
  13.0 7.6 %collective-permute-start.7 = (bf16[272,128]{1,0:T(8,128)(2,1)S(1)}, bf16[272,128]{1,0:T(8,128)(2,1)S(1)}, u32[]{:S(2)}, u32[]{:S(2)}) collective-permute-start(bf16[272,128]{1,0:T(8,128)(2,1)S(1)} %get-tuple-element.53), channel_id=1, source_target_pairs={{0,7},{1,6},{2,5},{3,4},{4,3},{5,2},{6,1},{7,0},{8,15},{9,14},{10,... | collective-permute-start | bytes 208904 | tf_op jit(solution)/shard_map/ppermute | solution.py:387
  14.0 9.4 %collective-permute-start.9 = (bf16[1360,128]{1,0:T(8,128)(2,1)S(1)}, bf16[1360,128]{1,0:T(8,128)(2,1)S(1)}, u32[]{:S(2)}, u32[]{:S(2)}) collective-permute-start(bf16[1360,128]{1,0:T(8,128)(2,1)S(1)} %constant_dynamic-update-slice_fusion.refs_1_.refs_9_), channel_id=1, source_target_pairs={{0,16},{8,24},{16,0},{24,8},{1,17},{9,25},{17,1},{25,9},{2,18},{10... | collective-permute-start | bytes 1044488 | tf_op jit(solution)/shard_map/ppermute | solution.py:390
  15.6 7.8 %collective-permute-start.4 = (bf16[1360,128]{1,0:T(8,128)(2,1)S(1)}, bf16[1360,128]{1,0:T(8,128)(2,1)S(1)}, u32[]{:S(2)}, u32[]{:S(2)}) collective-permute-start(bf16[1360,128]{1,0:T(8,128)(2,1)S(1)} %constant_dynamic-update-slice_fusion.refs_1_.refs_9_), channel_id=1, source_target_pairs={{0,8},{8,0},{16,24},{24,16},{1,9},{9,1},{17,25},{25,17},{2,10},{10... | collective-permute-start | bytes 1044488 | tf_op jit(solution)/shard_map/ppermute | solution.py:390
  20.7 2.7 %collective-permute-start.8 = (bf16[816,128]{1,0:T(8,128)(2,1)S(1)}, bf16[816,128]{1,0:T(8,128)(2,1)S(1)}, u32[]{:S(2)}, u32[]{:S(2)}) collective-permute-start(bf16[816,128]{1,0:T(8,128)(2,1)S(1)} %constant_dynamic-update-slice_fusion.5.refs_10_), channel_id=1, source_target_pairs={{0,8},{8,0},{16,24},{24,16},{1,9},{9,1},{17,25},{25,17},{2,10},{10... | collective-permute-start | bytes 626696 | tf_op jit(solution)/shard_map/ppermute | solution.py:390
  20.7 8.3 %collective-permute-start.11 = (bf16[816,128]{1,0:T(8,128)(2,1)S(1)}, bf16[816,128]{1,0:T(8,128)(2,1)S(1)}, u32[]{:S(2)}, u32[]{:S(2)}) collective-permute-start(bf16[816,128]{1,0:T(8,128)(2,1)S(1)} %constant_dynamic-update-slice_fusion.5.refs_10_), channel_id=1, source_target_pairs={{0,16},{8,24},{16,0},{24,8},{1,17},{9,25},{17,1},{25,9},{2,18},{10... | collective-permute-start | bytes 626696 | tf_op jit(solution)/shard_map/ppermute | solution.py:390
  23.4 6.2 %collective-permute-start.10 = (bf16[1360,128]{1,0:T(8,128)(2,1)S(1)}, bf16[1360,128]{1,0:T(8,128)(2,1)S(1)}, u32[]{:S(2)}, u32[]{:S(2)}) collective-permute-start(bf16[1360,128]{1,0:T(8,128)(2,1)S(1)} %collective-permute-done.9.refs_8_), channel_id=1, source_target_pairs={{0,8},{8,0},{16,24},{24,16},{1,9},{9,1},{17,25},{25,17},{2,10},{10... | collective-permute-start | bytes 1044488 | tf_op jit(solution)/shard_map/ppermute | solution.py:390
  29.0 3.1 %copy-start = (bf16[1024,1024]{1,0:T(8,128)(2,1)S(1)}, bf16[1024,1024]{1,0:T(8,128)(2,1)}, u32[]{:S(2)}) copy-start(bf16[1024,1024]{1,0:T(8,128)(2,1)} %refs_10_.1) | copy-start | bytes 6291460
  29.0 3.1 %collective-permute-start.12 = (bf16[816,128]{1,0:T(8,128)(2,1)S(1)}, bf16[816,128]{1,0:T(8,128)(2,1)S(1)}, u32[]{:S(2)}, u32[]{:S(2)}) collective-permute-start(bf16[816,128]{1,0:T(8,128)(2,1)S(1)} %collective-permute-done.11.refs_7_), channel_id=1, source_target_pairs={{0,8},{8,0},{16,24},{24,16},{1,9},{9,1},{17,25},{25,17},{2,10},{10... | collective-permute-start | bytes 626696 | tf_op jit(solution)/shard_map/ppermute | solution.py:390
  34.3 6.8 %collective-permute-start.13 = (bf16[32,1024]{1,0:T(8,128)(2,1)S(1)}, bf16[32,1024]{1,0:T(8,128)(2,1)S(1)}, u32[]{:S(2)}, u32[]{:S(2)}) collective-permute-start(bf16[32,1024]{1,0:T(8,128)(2,1)S(1)} %get-tuple-element.75), channel_id=1, source_target_pairs={{0,4},{1,5},{2,6},{3,7},{4,0},{5,1},{6,2},{7,3},{8,12},{9,13},{10,... | collective-permute-start | bytes 196616 | tf_op jit(solution)/shard_map/ppermute | solution.py:387
  36.1 7.8 %collective-permute-start.14 = (bf16[32,1024]{1,0:T(8,128)(2,1)S(1)}, bf16[32,1024]{1,0:T(8,128)(2,1)S(1)}, u32[]{:S(2)}, u32[]{:S(2)}) collective-permute-start(bf16[32,1024]{1,0:T(8,128)(2,1)S(1)} %get-tuple-element.74), channel_id=1, source_target_pairs={{0,1},{1,0},{2,3},{3,2},{4,5},{5,4},{6,7},{7,6},{8,9},{9,8},{10,11... | collective-permute-start | bytes 196616 | tf_op jit(solution)/shard_map/ppermute | solution.py:387
  37.7 7.0 %collective-permute-start.15 = (bf16[32,1024]{1,0:T(8,128)(2,1)S(1)}, bf16[32,1024]{1,0:T(8,128)(2,1)S(1)}, u32[]{:S(2)}, u32[]{:S(2)}) collective-permute-start(bf16[32,1024]{1,0:T(8,128)(2,1)S(1)} %get-tuple-element.80), channel_id=1, source_target_pairs={{0,2},{1,3},{2,0},{3,1},{4,6},{5,7},{6,4},{7,5},{8,10},{9,11},{10,... | collective-permute-start | bytes 196616 | tf_op jit(solution)/shard_map/ppermute | solution.py:387
  38.1 6.6 %collective-permute-start.16 = (bf16[32,1024]{1,0:T(8,128)(2,1)S(1)}, bf16[32,1024]{1,0:T(8,128)(2,1)S(1)}, u32[]{:S(2)}, u32[]{:S(2)}) collective-permute-start(bf16[32,1024]{1,0:T(8,128)(2,1)S(1)} %get-tuple-element.79), channel_id=1, source_target_pairs={{0,6},{1,7},{2,4},{3,5},{4,2},{5,3},{6,0},{7,1},{8,14},{9,15},{10,... | collective-permute-start | bytes 196616 | tf_op jit(solution)/shard_map/ppermute | solution.py:387
  39.4 9.4 %collective-permute-start.17 = (bf16[32,1024]{1,0:T(8,128)(2,1)S(1)}, bf16[32,1024]{1,0:T(8,128)(2,1)S(1)}, u32[]{:S(2)}, u32[]{:S(2)}) collective-permute-start(bf16[32,1024]{1,0:T(8,128)(2,1)S(1)} %get-tuple-element.78), channel_id=1, source_target_pairs={{0,5},{1,4},{2,7},{3,6},{4,1},{5,0},{6,3},{7,2},{8,13},{9,12},{10,... | collective-permute-start | bytes 196616 | tf_op jit(solution)/shard_map/ppermute | solution.py:387
  41.1 7.7 %collective-permute-start.18 = (bf16[32,1024]{1,0:T(8,128)(2,1)S(1)}, bf16[32,1024]{1,0:T(8,128)(2,1)S(1)}, u32[]{:S(2)}, u32[]{:S(2)}) collective-permute-start(bf16[32,1024]{1,0:T(8,128)(2,1)S(1)} %get-tuple-element.77), channel_id=1, source_target_pairs={{0,7},{1,6},{2,5},{3,4},{4,3},{5,2},{6,1},{7,0},{8,15},{9,14},{10,... | collective-permute-start | bytes 196616 | tf_op jit(solution)/shard_map/ppermute | solution.py:387
  43.9 5.4 %collective-permute-start.19 = (bf16[32,1024]{1,0:T(8,128)(2,1)S(1)}, bf16[32,1024]{1,0:T(8,128)(2,1)S(1)}, u32[]{:S(2)}, u32[]{:S(2)}) collective-permute-start(bf16[32,1024]{1,0:T(8,128)(2,1)S(1)} %get-tuple-element.73), channel_id=1, source_target_pairs={{0,3},{1,2},{2,1},{3,0},{4,7},{5,6},{6,5},{7,4},{8,11},{9,10},{10,... | collective-permute-start | bytes 196616 | tf_op jit(solution)/shard_map/ppermute | solution.py:387

commit v10 on v9

--- a/solution.py
+++ b/solution.py
@@ -389,7 +389,7 @@
     def over_heads(value, step):
         return lax.ppermute(value, "heads", [(i, i ^ step) for i in range(head_devs)])
 
-    order = [4, 1, 3, 0, 2, 6, 5, 7] if genes == 8 else list(range(genes))
+    order = [4, 1, 3, 2, 0, 6, 5, 7] if genes == 8 else list(range(genes))
     back = [0, 4, 1, 2, 6, 5, 7, 3] if genes == 8 else order
     packed = pack(cells_in, gain, tile_of_cell, order)
     arrived = [over_cells(piece, k) if k else piece for piece, k in zip(packed, order)]

time: 50.3 us -> 50.3 us (level)
  no operation moved by 1% of the time
where the time goes in v10:
time: 50.3 us; the launch traced here: 50.2 us
  starting transfers between devices  26.6 us (53%)
  Pallas kernels  16.5 us (33%)
  waiting for transfers between devices  6.68 us (13%)
    ppermute x14, starting transfers between devices, over_cells(): lax.ppermute(value, 'cells', [(i, i ^ step) for i in range(cell_devs)])  22.9 us
    pallas_call x4, Pallas kernels, call(): pl.pallas_call(self.body, out_shape=tuple(out_shape), in_specs=[hbm if n....  14.3 us
    ppermute x14, waiting for transfers between devices, over_cells(): lax.ppermute(value, 'cells', [(i, i ^ step) for i in range(cell_devs)])  5.58 us
    ppermute x6, starting transfers between devices, over_heads(): lax.ppermute(value, 'heads', [(i, i ^ step) for i in range(head_devs)])  3.76 us
    pallas_call x1, Pallas kernels, pack(): pl.pallas_call(lambda *refs: pack_kernel(order, *refs), out_shape=[jax.Sh...  1.36 us
    ppermute x6, waiting for transfers between devices, over_heads(): lax.ppermute(value, 'heads', [(i, i ^ step) for i in range(head_devs)])  1.1 us
  transfers between devices with their start and end apart: 20, of which 4 were waited for; matrix products, arithmetic and copies ran while one was open for 0% of the time, Pallas kernels for 24%

profile of v10, /device:TPU:0, one launch (start us, length us, event | category | flops | bytes accessed | tf_op | source)
XLA Modules:
  0.0 50.2 jit_solution(17863222967764416229)
XLA Ops:
  0.0 1.4 %pack.1 = (bf16[272,128]{1,0:T(8,128)(2,1)S(1)}, bf16[272,128]{1,0:T(8,128)(2,1)S(1)}, bf16[272,128]{1,0:T(8,128)(2,1)S(1)}, bf16[272,128]{1,0:T(8,128)(2,1)S(1)...) custom-call(bf16[8,32,1024]{2,1,0:T(8,128)(2,1)} %refs_0_.2, ...), custom_call_target="tpu_custom_call" | custom-call | tf_op jit(solution)/shard_map/pack/pallas_call | solution.py:72
  1.4 4.1 %collective-permute-start = (bf16[272,128]{1,0:T(8,128)(2,1)S(1)}, bf16[272,128]{1,0:T(8,128)(2,1)S(1)}, u32[]{:S(2)}, u32[]{:S(2)}) collective-permute-start(bf16[272,128]{1,0:T(8,128)(2,1)S(1)} %get-tuple-element.39), channel_id=1, source_target_pairs={{0,4},{1,5},{2,6},{3,7},{4,0},{5,1},{6,2},{7,3},{8,12},{9,13},{10,... | collective-permute-start | bytes 208904 | tf_op jit(solution)/shard_map/ppermute | solution.py:387
  5.5 1.5 %collective-permute-start.1 = (bf16[272,128]{1,0:T(8,128)(2,1)S(1)}, bf16[272,128]{1,0:T(8,128)(2,1)S(1)}, u32[]{:S(2)}, u32[]{:S(2)}) collective-permute-start(bf16[272,128]{1,0:T(8,128)(2,1)S(1)} %get-tuple-element.40), channel_id=1, source_target_pairs={{0,1},{1,0},{2,3},{3,2},{4,5},{5,4},{6,7},{7,6},{8,9},{9,8},{10,11... | collective-permute-start | bytes 208904 | tf_op jit(solution)/shard_map/ppermute | solution.py:387
  7.0 1.5 %collective-permute-start.2 = (bf16[272,128]{1,0:T(8,128)(2,1)S(1)}, bf16[272,128]{1,0:T(8,128)(2,1)S(1)}, u32[]{:S(2)}, u32[]{:S(2)}) collective-permute-start(bf16[272,128]{1,0:T(8,128)(2,1)S(1)} %get-tuple-element.41), channel_id=1, source_target_pairs={{0,3},{1,2},{2,1},{3,0},{4,7},{5,6},{6,5},{7,4},{8,11},{9,10},{10,... | collective-permute-start | bytes 208904 | tf_op jit(solution)/shard_map/ppermute | solution.py:387
  8.5 0.4 collective-permute-start.3
  9.0 1.3 %collective-permute-start.5 = (bf16[272,128]{1,0:T(8,128)(2,1)S(1)}, bf16[272,128]{1,0:T(8,128)(2,1)S(1)}, u32[]{:S(2)}, u32[]{:S(2)}) collective-permute-start(bf16[272,128]{1,0:T(8,128)(2,1)S(1)} %get-tuple-element.51), channel_id=1, source_target_pairs={{0,6},{1,7},{2,4},{3,5},{4,2},{5,3},{6,0},{7,1},{8,14},{9,15},{10,... | collective-permute-start | bytes 208904 | tf_op jit(solution)/shard_map/ppermute | solution.py:387
  10.3 0.0 collective-permute-done
  10.3 2.6 %collective-permute-start.6 = (bf16[272,128]{1,0:T(8,128)(2,1)S(1)}, bf16[272,128]{1,0:T(8,128)(2,1)S(1)}, u32[]{:S(2)}, u32[]{:S(2)}) collective-permute-start(bf16[272,128]{1,0:T(8,128)(2,1)S(1)} %get-tuple-element.52), channel_id=1, source_target_pairs={{0,5},{1,4},{2,7},{3,6},{4,1},{5,0},{6,3},{7,2},{8,13},{9,12},{10,... | collective-permute-start | bytes 208904 | tf_op jit(solution)/shard_map/ppermute | solution.py:387
  13.0 0.0 collective-permute-done.1
  13.0 0.9 %collective-permute-start.7 = (bf16[272,128]{1,0:T(8,128)(2,1)S(1)}, bf16[272,128]{1,0:T(8,128)(2,1)S(1)}, u32[]{:S(2)}, u32[]{:S(2)}) collective-permute-start(bf16[272,128]{1,0:T(8,128)(2,1)S(1)} %get-tuple-element.53), channel_id=1, source_target_pairs={{0,7},{1,6},{2,5},{3,4},{4,3},{5,2},{6,1},{7,0},{8,15},{9,14},{10,... | collective-permute-start | bytes 208904 | tf_op jit(solution)/shard_map/ppermute | solution.py:387
  13.9 0.0 collective-permute-done.2
  14.0 0.0 collective-permute-done.3
  14.0 1.6 %collective-permute-start.9 = (bf16[1360,128]{1,0:T(8,128)(2,1)S(1)}, bf16[1360,128]{1,0:T(8,128)(2,1)S(1)}, u32[]{:S(2)}, u32[]{:S(2)}) collective-permute-start(bf16[1360,128]{1,0:T(8,128)(2,1)S(1)} %constant_dynamic-update-slice_fusion.refs_1_.refs_9_), channel_id=1, source_target_pairs={{0,16},{8,24},{16,0},{24,8},{1,17},{9,25},{17,1},{25,9},{2,18},{10... | collective-permute-start | bytes 1044488 | tf_op jit(solution)/shard_map/ppermute | solution.py:390
  15.6 0.0 collective-permute-start.4
  15.6 4.1 %first_group.1 = (bf16[8,256,128]{2,1,0:T(8,128)(2,1)S(1)}, bf16[256,256]{1,0:T(8,128)(2,1)S(1)}, f32[8,72,256]{2,1,0:T(8,128)S(1)}, f32[8,256]{1,0:T(8,128)S(1)...) custom-call(s32[256,256]{1,0:T(8,128)} %refs_0_.3, ...), custom_call_target="tpu_custom_call" | custom-call | flops 1275068416 | bytes 8388608 | tf_op jit(solution)/shard_map/first_group/pallas_call | solution.py:366
  19.6 0.0 collective-permute-done.5
  19.6 1.0 %collective-permute-done.6 = bf16[272,128]{1,0:T(8,128)(2,1)S(1)} collective-permute-done((bf16[272,128]{1,0:T(8,128)(2,1)S(1)}, bf16[272,128]{1,0:T(8,128)(2,1)S(1)}, u32[]{:S(2)}, u32[]{:S(2)}) %collective-permute-start.6) | collective-permute-done | bytes 69664 | tf_op jit(solution)/shard_map/ppermute | solution.py:387
  20.6 0.0 collective-permute-done.7
  20.7 0.1 collective-permute-start.8
  20.7 1.6 %collective-permute-start.11 = (bf16[816,128]{1,0:T(8,128)(2,1)S(1)}, bf16[816,128]{1,0:T(8,128)(2,1)S(1)}, u32[]{:S(2)}, u32[]{:S(2)}) collective-permute-start(bf16[816,128]{1,0:T(8,128)(2,1)S(1)} %constant_dynamic-update-slice_fusion.5.refs_10_), channel_id=1, source_target_pairs={{0,16},{8,24},{16,0},{24,8},{1,17},{9,25},{17,1},{25,9},{2,18},{10... | collective-permute-start | bytes 626696 | tf_op jit(solution)/shard_map/ppermute | solution.py:390
  22.3 1.1 %collective-permute-done.9.refs_8_ = bf16[1360,128]{1,0:T(8,128)(2,1)S(1)} collective-permute-done((bf16[1360,128]{1,0:T(8,128)(2,1)S(1)}, bf16[1360,128]{1,0:T(8,128)(2,1)S(1)}, u32[]{:S(2)}, u32[]{:S(2)}) %collective-permute-start.9) | collective-permute-done | bytes 348192 | tf_op jit(solution)/shard_map/ppermute | solution.py:390
  23.4 0.0 collective-permute-start.10
  23.4 0.0 collective-permute-done.8.refs_7_
  23.4 0.0 collective-permute-done.4.refs_6_
  23.4 5.6 %second_group.1 = (bf16[8,256,128]{2,1,0:T(8,128)(2,1)S(1)}, bf16[256,256]{1,0:T(8,128)(2,1)S(1)}, f32[8,72,256]{2,1,0:T(8,128)S(1)}, f32[8,256]{1,0:T(8,128)S(1...) custom-call(bf16[256,256]{1,0:T(8,128)(2,1)S(1)} %get-tuple-element.44.refs_0_, ...), custom_call_target="tpu_custom_call" | custom-call | flops 4898947072 | bytes 8388608 | tf_op jit(solution)/shard_map/second_group/pallas_call | solution.py:366
  29.0 0.0 copy-start
  29.0 0.0 collective-permute-done.11.refs_7_
  29.0 0.6 %collective-permute-start.12 = (bf16[816,128]{1,0:T(8,128)(2,1)S(1)}, bf16[816,128]{1,0:T(8,128)(2,1)S(1)}, u32[]{:S(2)}, u32[]{:S(2)}) collective-permute-start(bf16[816,128]{1,0:T(8,128)(2,1)S(1)} %collective-permute-done.11.refs_7_), channel_id=1, source_target_pairs={{0,8},{8,0},{16,24},{24,16},{1,9},{9,1},{17,25},{25,17},{2,10},{10... | collective-permute-start | bytes 626696 | tf_op jit(solution)/shard_map/ppermute | solution.py:390
  29.6 0.0 collective-permute-done.10.refs_6_
  29.6 2.5 %far.1 = (f32[8,72,256]{2,1,0:T(8,128)S(1)}, f32[8,256]{1,0:T(8,128)S(1)}, f32[8,72,256]{2,1,0:T(8,128)S(1)}, f32[8,256]{1,0:T(8,128)S(1)}) custom-call(bf16[256,256]{1,0:T(8,128)(2,1)S(1)} %get-tuple-element.44.refs_0_, bf16[256,256]{1,0:T(8,128)(2,1)S(1)} %get-tuple-element.59.refs_1_, bf16[8,256,128]{2,1,0:T(8,128)(2,1)S(1)} %get-tuple-element.46.refs_2_, ...), custom_call_target="tpu_custom_call" | custom-call | flops 2147483648 | bytes 8388608 | tf_op jit(solution)/shard_map/far/pallas_call | solution.py:366
  32.1 0.0 collective-permute-done.12.refs_6_
  32.1 0.0 copy-done
  32.1 2.2 %last.1 = (bf16[128,1024]{1,0:T(8,128)(2,1)S(1)}, bf16[128,1024]{1,0:T(8,128)(2,1)S(1)}) custom-call(bf16[256,256]{1,0:T(8,128)(2,1)S(1)} %get-tuple-element.44.refs_0_, bf16[256,256]{1,0:T(8,128)(2,1)S(1)} %get-tuple-element.59.refs_1_, bf16[8,256,128]{2,1,0:T(8,128)(2,1)S(1)} %get-tuple-element.46.refs_2_, ...), custom_call_target="tpu_custom_call" | custom-call | flops 1342177280 | bytes 8388608 | tf_op jit(solution)/shard_map/last/pallas_call | solution.py:366
  34.3 1.7 %collective-permute-start.13 = (bf16[32,1024]{1,0:T(8,128)(2,1)S(1)}, bf16[32,1024]{1,0:T(8,128)(2,1)S(1)}, u32[]{:S(2)}, u32[]{:S(2)}) collective-permute-start(bf16[32,1024]{1,0:T(8,128)(2,1)S(1)} %get-tuple-element.76), channel_id=1, source_target_pairs={{0,4},{1,5},{2,6},{3,7},{4,0},{5,1},{6,2},{7,3},{8,12},{9,13},{10,... | collective-permute-start | bytes 196616 | tf_op jit(solution)/shard_map/ppermute | solution.py:387
  36.1 1.6 %collective-permute-start.14 = (bf16[32,1024]{1,0:T(8,128)(2,1)S(1)}, bf16[32,1024]{1,0:T(8,128)(2,1)S(1)}, u32[]{:S(2)}, u32[]{:S(2)}) collective-permute-start(bf16[32,1024]{1,0:T(8,128)(2,1)S(1)} %get-tuple-element.75), channel_id=1, source_target_pairs={{0,1},{1,0},{2,3},{3,2},{4,5},{5,4},{6,7},{7,6},{8,9},{9,8},{10,11... | collective-permute-start | bytes 196616 | tf_op jit(solution)/shard_map/ppermute | solution.py:387
  37.7 0.3 collective-permute-start.15
  38.0 1.4 %collective-permute-start.16 = (bf16[32,1024]{1,0:T(8,128)(2,1)S(1)}, bf16[32,1024]{1,0:T(8,128)(2,1)S(1)}, u32[]{:S(2)}, u32[]{:S(2)}) collective-permute-start(bf16[32,1024]{1,0:T(8,128)(2,1)S(1)} %get-tuple-element.79), channel_id=1, source_target_pairs={{0,6},{1,7},{2,4},{3,5},{4,2},{5,3},{6,0},{7,1},{8,14},{9,15},{10,... | collective-permute-start | bytes 196616 | tf_op jit(solution)/shard_map/ppermute | solution.py:387
  39.4 1.7 %collective-permute-start.17 = (bf16[32,1024]{1,0:T(8,128)(2,1)S(1)}, bf16[32,1024]{1,0:T(8,128)(2,1)S(1)}, u32[]{:S(2)}, u32[]{:S(2)}) collective-permute-start(bf16[32,1024]{1,0:T(8,128)(2,1)S(1)} %get-tuple-element.78), channel_id=1, source_target_pairs={{0,5},{1,4},{2,7},{3,6},{4,1},{5,0},{6,3},{7,2},{8,13},{9,12},{10,... | collective-permute-start | bytes 196616 | tf_op jit(solution)/shard_map/ppermute | solution.py:387
  41.1 0.0 collective-permute-done.13.refs_1_
  41.1 2.8 %collective-permute-start.18 = (bf16[32,1024]{1,0:T(8,128)(2,1)S(1)}, bf16[32,1024]{1,0:T(8,128)(2,1)S(1)}, u32[]{:S(2)}, u32[]{:S(2)}) collective-permute-start(bf16[32,1024]{1,0:T(8,128)(2,1)S(1)} %get-tuple-element.77), channel_id=1, source_target_pairs={{0,7},{1,6},{2,5},{3,4},{4,3},{5,2},{6,1},{7,0},{8,15},{9,14},{10,... | collective-permute-start | bytes 196616 | tf_op jit(solution)/shard_map/ppermute | solution.py:387
  43.9 0.0 collective-permute-done.14.refs_2_
  43.9 0.9 %collective-permute-start.19 = (bf16[32,1024]{1,0:T(8,128)(2,1)S(1)}, bf16[32,1024]{1,0:T(8,128)(2,1)S(1)}, u32[]{:S(2)}, u32[]{:S(2)}) collective-permute-start(bf16[32,1024]{1,0:T(8,128)(2,1)S(1)} %get-tuple-element.73), channel_id=1, source_target_pairs={{0,3},{1,2},{2,1},{3,0},{4,7},{5,6},{6,5},{7,4},{8,11},{9,10},{10,... | collective-permute-start | bytes 196616 | tf_op jit(solution)/shard_map/ppermute | solution.py:387
  44.7 0.0 collective-permute-done.15.refs_3_
  44.7 0.0 collective-permute-done.16.refs_4_
  44.7 4.2 %collective-permute-done.17.refs_5_ = bf16[32,1024]{1,0:T(8,128)(2,1)S(1)} collective-permute-done((bf16[32,1024]{1,0:T(8,128)(2,1)S(1)}, bf16[32,1024]{1,0:T(8,128)(2,1)S(1)}, u32[]{:S(2)}, u32[]{:S(2)}) %collective-permute-start.17) | collective-permute-done | bytes 65568 | tf_op jit(solution)/shard_map/ppermute | solution.py:387
  48.9 0.0 collective-permute-done.18.refs_6_
  48.9 0.4 collective-permute-done.19.refs_7_
  49.3 0.8 %unpack.1 = bf16[8,32,1024]{2,1,0:T(8,128)(2,1)} custom-call(bf16[32,1024]{1,0:T(8,128)(2,1)S(1)} %get-tuple-element.80.refs_0_, bf16[32,1024]{1,0:T(8,128)(2,1)S(1)} %collective-permute-done.13.refs_1_, bf16[32,1024]{1,0:T(8,128)(2,1)S(1)} %collective-permute-done.14.refs_2_, bf16[32,1024]{1,0:T(8,128)(2,1)S(1)} %collective-permute-done.15.refs_3_, ...), custom_call_target="tpu_custom_call" | custom-call | tf_op jit(solution)/shard_map/unpack/pallas_call | solution.py:100
  (10 shorter events, 0.1 us)
Async XLA Ops:
  1.4 8.9 %collective-permute-start = (bf16[272,128]{1,0:T(8,128)(2,1)S(1)}, bf16[272,128]{1,0:T(8,128)(2,1)S(1)}, u32[]{:S(2)}, u32[]{:S(2)}) collective-permute-start(bf16[272,128]{1,0:T(8,128)(2,1)S(1)} %get-tuple-element.39), channel_id=1, source_target_pairs={{0,4},{1,5},{2,6},{3,7},{4,0},{5,1},{6,2},{7,3},{8,12},{9,13},{10,... | collective-permute-start | bytes 208904 | tf_op jit(solution)/shard_map/ppermute | solution.py:387
  5.5 7.5 %collective-permute-start.1 = (bf16[272,128]{1,0:T(8,128)(2,1)S(1)}, bf16[272,128]{1,0:T(8,128)(2,1)S(1)}, u32[]{:S(2)}, u32[]{:S(2)}) collective-permute-start(bf16[272,128]{1,0:T(8,128)(2,1)S(1)} %get-tuple-element.40), channel_id=1, source_target_pairs={{0,1},{1,0},{2,3},{3,2},{4,5},{5,4},{6,7},{7,6},{8,9},{9,8},{10,11... | collective-permute-start | bytes 208904 | tf_op jit(solution)/shard_map/ppermute | solution.py:387
  7.0 6.9 %collective-permute-start.2 = (bf16[272,128]{1,0:T(8,128)(2,1)S(1)}, bf16[272,128]{1,0:T(8,128)(2,1)S(1)}, u32[]{:S(2)}, u32[]{:S(2)}) collective-permute-start(bf16[272,128]{1,0:T(8,128)(2,1)S(1)} %get-tuple-element.41), channel_id=1, source_target_pairs={{0,3},{1,2},{2,1},{3,0},{4,7},{5,6},{6,5},{7,4},{8,11},{9,10},{10,... | collective-permute-start | bytes 208904 | tf_op jit(solution)/shard_map/ppermute | solution.py:387
  8.5 5.4 %collective-permute-start.3 = (bf16[272,128]{1,0:T(8,128)(2,1)S(1)}, bf16[272,128]{1,0:T(8,128)(2,1)S(1)}, u32[]{:S(2)}, u32[]{:S(2)}) collective-permute-start(bf16[272,128]{1,0:T(8,128)(2,1)S(1)} %get-tuple-element.42), channel_id=1, source_target_pairs={{0,2},{1,3},{2,0},{3,1},{4,6},{5,7},{6,4},{7,5},{8,10},{9,11},{10,... | collective-permute-start | bytes 208904 | tf_op jit(solution)/shard_map/ppermute | solution.py:387
  9.0 10.7 %collective-permute-start.5 = (bf16[272,128]{1,0:T(8,128)(2,1)S(1)}, bf16[272,128]{1,0:T(8,128)(2,1)S(1)}, u32[]{:S(2)}, u32[]{:S(2)}) collective-permute-start(bf16[272,128]{1,0:T(8,128)(2,1)S(1)} %get-tuple-element.51), channel_id=1, source_target_pairs={{0,6},{1,7},{2,4},{3,5},{4,2},{5,3},{6,0},{7,1},{8,14},{9,15},{10,... | collective-permute-start | bytes 208904 | tf_op jit(solution)/shard_map/ppermute | solution.py:387
  10.3 10.3 %collective-permute-start.6 = (bf16[272,128]{1,0:T(8,128)(2,1)S(1)}, bf16[272,128]{1,0:T(8,128)(2,1)S(1)}, u32[]{:S(2)}, u32[]{:S(2)}) collective-permute-start(bf16[272,128]{1,0:T(8,128)(2,1)S(1)} %get-tuple-element.52), channel_id=1, source_target_pairs={{0,5},{1,4},{2,7},{3,6},{4,1},{5,0},{6,3},{7,2},{8,13},{9,12},{10,... | collective-permute-start | bytes 208904 | tf_op jit(solution)/shard_map/ppermute | solution.py:387
  13.0 7.6 %collective-permute-start.7 = (bf16[272,128]{1,0:T(8,128)(2,1)S(1)}, bf16[272,128]{1,0:T(8,128)(2,1)S(1)}, u32[]{:S(2)}, u32[]{:S(2)}) collective-permute-start(bf16[272,128]{1,0:T(8,128)(2,1)S(1)} %get-tuple-element.53), channel_id=1, source_target_pairs={{0,7},{1,6},{2,5},{3,4},{4,3},{5,2},{6,1},{7,0},{8,15},{9,14},{10,... | collective-permute-start | bytes 208904 | tf_op jit(solution)/shard_map/ppermute | solution.py:387
  14.0 9.4 %collective-permute-start.9 = (bf16[1360,128]{1,0:T(8,128)(2,1)S(1)}, bf16[1360,128]{1,0:T(8,128)(2,1)S(1)}, u32[]{:S(2)}, u32[]{:S(2)}) collective-permute-start(bf16[1360,128]{1,0:T(8,128)(2,1)S(1)} %constant_dynamic-update-slice_fusion.refs_1_.refs_9_), channel_id=1, source_target_pairs={{0,16},{8,24},{16,0},{24,8},{1,17},{9,25},{17,1},{25,9},{2,18},{10... | collective-permute-start | bytes 1044488 | tf_op jit(solution)/shard_map/ppermute | solution.py:390
  15.6 7.8 %collective-permute-start.4 = (bf16[1360,128]{1,0:T(8,128)(2,1)S(1)}, bf16[1360,128]{1,0:T(8,128)(2,1)S(1)}, u32[]{:S(2)}, u32[]{:S(2)}) collective-permute-start(bf16[1360,128]{1,0:T(8,128)(2,1)S(1)} %constant_dynamic-update-slice_fusion.refs_1_.refs_9_), channel_id=1, source_target_pairs={{0,8},{8,0},{16,24},{24,16},{1,9},{9,1},{17,25},{25,17},{2,10},{10... | collective-permute-start | bytes 1044488 | tf_op jit(solution)/shard_map/ppermute | solution.py:390
  20.7 2.7 %collective-permute-start.8 = (bf16[816,128]{1,0:T(8,128)(2,1)S(1)}, bf16[816,128]{1,0:T(8,128)(2,1)S(1)}, u32[]{:S(2)}, u32[]{:S(2)}) collective-permute-start(bf16[816,128]{1,0:T(8,128)(2,1)S(1)} %constant_dynamic-update-slice_fusion.5.refs_10_), channel_id=1, source_target_pairs={{0,8},{8,0},{16,24},{24,16},{1,9},{9,1},{17,25},{25,17},{2,10},{10... | collective-permute-start | bytes 626696 | tf_op jit(solution)/shard_map/ppermute | solution.py:390
  20.7 8.3 %collective-permute-start.11 = (bf16[816,128]{1,0:T(8,128)(2,1)S(1)}, bf16[816,128]{1,0:T(8,128)(2,1)S(1)}, u32[]{:S(2)}, u32[]{:S(2)}) collective-permute-start(bf16[816,128]{1,0:T(8,128)(2,1)S(1)} %constant_dynamic-update-slice_fusion.5.refs_10_), channel_id=1, source_target_pairs={{0,16},{8,24},{16,0},{24,8},{1,17},{9,25},{17,1},{25,9},{2,18},{10... | collective-permute-start | bytes 626696 | tf_op jit(solution)/shard_map/ppermute | solution.py:390
  23.4 6.2 %collective-permute-start.10 = (bf16[1360,128]{1,0:T(8,128)(2,1)S(1)}, bf16[1360,128]{1,0:T(8,128)(2,1)S(1)}, u32[]{:S(2)}, u32[]{:S(2)}) collective-permute-start(bf16[1360,128]{1,0:T(8,128)(2,1)S(1)} %collective-permute-done.9.refs_8_), channel_id=1, source_target_pairs={{0,8},{8,0},{16,24},{24,16},{1,9},{9,1},{17,25},{25,17},{2,10},{10... | collective-permute-start | bytes 1044488 | tf_op jit(solution)/shard_map/ppermute | solution.py:390
  29.0 3.1 %copy-start = (bf16[1024,1024]{1,0:T(8,128)(2,1)S(1)}, bf16[1024,1024]{1,0:T(8,128)(2,1)}, u32[]{:S(2)}) copy-start(bf16[1024,1024]{1,0:T(8,128)(2,1)} %refs_10_.1) | copy-start | bytes 6291460
  29.0 3.1 %collective-permute-start.12 = (bf16[816,128]{1,0:T(8,128)(2,1)S(1)}, bf16[816,128]{1,0:T(8,128)(2,1)S(1)}, u32[]{:S(2)}, u32[]{:S(2)}) collective-permute-start(bf16[816,128]{1,0:T(8,128)(2,1)S(1)} %collective-permute-done.11.refs_7_), channel_id=1, source_target_pairs={{0,8},{8,0},{16,24},{24,16},{1,9},{9,1},{17,25},{25,17},{2,10},{10... | collective-permute-start | bytes 626696 | tf_op jit(solution)/shard_map/ppermute | solution.py:390
  34.3 6.8 %collective-permute-start.13 = (bf16[32,1024]{1,0:T(8,128)(2,1)S(1)}, bf16[32,1024]{1,0:T(8,128)(2,1)S(1)}, u32[]{:S(2)}, u32[]{:S(2)}) collective-permute-start(bf16[32,1024]{1,0:T(8,128)(2,1)S(1)} %get-tuple-element.76), channel_id=1, source_target_pairs={{0,4},{1,5},{2,6},{3,7},{4,0},{5,1},{6,2},{7,3},{8,12},{9,13},{10,... | collective-permute-start | bytes 196616 | tf_op jit(solution)/shard_map/ppermute | solution.py:387
  36.1 7.8 %collective-permute-start.14 = (bf16[32,1024]{1,0:T(8,128)(2,1)S(1)}, bf16[32,1024]{1,0:T(8,128)(2,1)S(1)}, u32[]{:S(2)}, u32[]{:S(2)}) collective-permute-start(bf16[32,1024]{1,0:T(8,128)(2,1)S(1)} %get-tuple-element.75), channel_id=1, source_target_pairs={{0,1},{1,0},{2,3},{3,2},{4,5},{5,4},{6,7},{7,6},{8,9},{9,8},{10,11... | collective-permute-start | bytes 196616 | tf_op jit(solution)/shard_map/ppermute | solution.py:387
  37.7 7.1 %collective-permute-start.15 = (bf16[32,1024]{1,0:T(8,128)(2,1)S(1)}, bf16[32,1024]{1,0:T(8,128)(2,1)S(1)}, u32[]{:S(2)}, u32[]{:S(2)}) collective-permute-start(bf16[32,1024]{1,0:T(8,128)(2,1)S(1)} %get-tuple-element.74), channel_id=1, source_target_pairs={{0,2},{1,3},{2,0},{3,1},{4,6},{5,7},{6,4},{7,5},{8,10},{9,11},{10,... | collective-permute-start | bytes 196616 | tf_op jit(solution)/shard_map/ppermute | solution.py:387
  38.0 6.7 %collective-permute-start.16 = (bf16[32,1024]{1,0:T(8,128)(2,1)S(1)}, bf16[32,1024]{1,0:T(8,128)(2,1)S(1)}, u32[]{:S(2)}, u32[]{:S(2)}) collective-permute-start(bf16[32,1024]{1,0:T(8,128)(2,1)S(1)} %get-tuple-element.79), channel_id=1, source_target_pairs={{0,6},{1,7},{2,4},{3,5},{4,2},{5,3},{6,0},{7,1},{8,14},{9,15},{10,... | collective-permute-start | bytes 196616 | tf_op jit(solution)/shard_map/ppermute | solution.py:387
  39.4 9.5 %collective-permute-start.17 = (bf16[32,1024]{1,0:T(8,128)(2,1)S(1)}, bf16[32,1024]{1,0:T(8,128)(2,1)S(1)}, u32[]{:S(2)}, u32[]{:S(2)}) collective-permute-start(bf16[32,1024]{1,0:T(8,128)(2,1)S(1)} %get-tuple-element.78), channel_id=1, source_target_pairs={{0,5},{1,4},{2,7},{3,6},{4,1},{5,0},{6,3},{7,2},{8,13},{9,12},{10,... | collective-permute-start | bytes 196616 | tf_op jit(solution)/shard_map/ppermute | solution.py:387
  41.1 7.8 %collective-permute-start.18 = (bf16[32,1024]{1,0:T(8,128)(2,1)S(1)}, bf16[32,1024]{1,0:T(8,128)(2,1)S(1)}, u32[]{:S(2)}, u32[]{:S(2)}) collective-permute-start(bf16[32,1024]{1,0:T(8,128)(2,1)S(1)} %get-tuple-element.77), channel_id=1, source_target_pairs={{0,7},{1,6},{2,5},{3,4},{4,3},{5,2},{6,1},{7,0},{8,15},{9,14},{10,... | collective-permute-start | bytes 196616 | tf_op jit(solution)/shard_map/ppermute | solution.py:387
  43.9 5.5 %collective-permute-start.19 = (bf16[32,1024]{1,0:T(8,128)(2,1)S(1)}, bf16[32,1024]{1,0:T(8,128)(2,1)S(1)}, u32[]{:S(2)}, u32[]{:S(2)}) collective-permute-start(bf16[32,1024]{1,0:T(8,128)(2,1)S(1)} %get-tuple-element.73), channel_id=1, source_target_pairs={{0,3},{1,2},{2,1},{3,0},{4,7},{5,6},{6,5},{7,4},{8,11},{9,10},{10,... | collective-permute-start | bytes 196616 | tf_op jit(solution)/shard_map/ppermute | solution.py:387
